TPU v7x, 32 devices: a whole 2x2x4 slice. The times are simulated.
32 devices in a mesh: dp: 8 (over z, y), mp: 4 (over x, core).
Axes of the slice: x: 2, y: 2, z: 4, core: 2. Of those that a mesh axis runs over, the one named last changes fastest.
Arguments:
- prompts: bfloat16 [2048, 4096], P('dp'), may hold values from -6 to 6
- responses: bfloat16 [2048, 4096], P('dp'), may hold values from -6 to 6
- head_projection_matrix: bfloat16 [4096, 1024], P('dp', 'mp'), may hold values from -0.09375 to 0.09375
- positive: int32 [2048], P('dp'), may hold values from 0 to 2047, as said below
Outputs:
- row_loss: float32 [2048], P('dp')
- head_grad: float32 [4096, 1024], P('dp', 'mp')
Inputs may be any that keep to these rules, and one draw needn't show every extreme that they name: `positive`: positive_i lies in a block whose index is block(i) - k mod the number of blocks for some k in 0 to 7.
All inputs are finite; a program needn't handle non-finite values.
Results may differ from a plain program's by a relative error of at most 0.0039.
Values may be sent and summed in bfloat16 or wider, within the bound.
No kernel may reach another device: no remote copies, remote signals or barrier semaphores. Data moves between devices by JAX's collectives and lax.ppermute only.
A program may use at most 64 MiB of HBM per device.

v0:
```python
import math

import jax
import jax.numpy as jnp
from jax import lax
from jax.sharding import PartitionSpec as P

E = 1024
STEPS = 8


LOGIT_SCALE = 3.0
LOGIT_BIAS = -3.0


def passed_along(block, axis, distance):
    devices = range(lax.axis_size(axis))
    route = [((i - distance) % len(devices), i) for i in devices]
    return lax.ppermute(block, axis, route)


def cross_rows(left_side, righthand_term):
    return lax.dot_general(
        left_side, righthand_term, (((0,), (0,)), ((), ())), preferred_element_type=jnp.float32
    )


def cross_cols(left_side, righthand_term):
    return lax.dot_general(
        left_side, righthand_term, (((1,), (1,)), ((), ())), preferred_element_type=jnp.float32
    )


def per_device(prompts, responses, head_projection_matrix, positive):
    row_count = prompts.shape[0]
    col_count = head_projection_matrix.shape[1]
    factor = LOGIT_SCALE / math.sqrt(E)
    cycle_size = lax.axis_size("dp")
    position = lax.axis_index("dp")
    segment = lax.all_gather(head_projection_matrix, "dp", axis=0, tiled=True)
    prompt_cols = prompts
    response_cols = responses
    prompt_proj = jnp.dot(prompt_cols, segment, preferred_element_type=jnp.float32)
    response_proj = jnp.dot(response_cols, segment, preferred_element_type=jnp.float32)
    prompt_emb = prompt_proj.astype(jnp.bfloat16)
    visiting = response_proj.astype(jnp.bfloat16)
    local_ids = lax.iota(jnp.int32, row_count)
    prompt_gradient_total = jnp.zeros((row_count, col_count), jnp.float32)
    grad_response = jnp.zeros((row_count, col_count), jnp.float32)
    row_losses = jnp.zeros((row_count,), jnp.float32)
    for offset in range(STEPS):
        partial_logits = cross_cols(prompt_emb, visiting)
        pair_scores = lax.psum(partial_logits, "mp") * factor + LOGIT_BIAS
        anchor = (position - offset) % cycle_size
        column_ids = anchor * row_count + local_ids
        labels = jnp.where(positive[:, None] == column_ids[None, :], 1.0, -1.0).astype(jnp.float32)
        margin = -labels * pair_scores
        row_losses = row_losses + jnp.sum(jax.nn.softplus(margin), axis=1)
        pairwise_weight = (-labels * jax.nn.sigmoid(margin) * (factor / row_count)).astype(
            jnp.bfloat16
        )
        prompt_gradient_total = prompt_gradient_total + jnp.dot(
            pairwise_weight, visiting, preferred_element_type=jnp.float32
        )
        contribution = cross_rows(pairwise_weight, prompt_emb)
        if offset == 0:
            grad_response = contribution
        else:
            grad_response = grad_response + passed_along(contribution, "dp", -offset)
        if offset < STEPS - 1:
            visiting = passed_along(visiting, "dp", 1)
    grad_prompt_b = prompt_gradient_total.astype(jnp.bfloat16)
    grad_response_b = grad_response.astype(jnp.bfloat16)
    prompt_cols = prompts
    response_cols = responses
    head_grad = lax.psum_scatter(
        cross_rows(prompt_cols, grad_prompt_b) + cross_rows(response_cols, grad_response_b),
        "dp",
        scatter_dimension=0,
        tiled=True,
    )
    return (row_losses / row_count, head_grad)


def solution(mesh):
    return jax.shard_map(
        per_device,
        mesh=mesh,
        in_specs=(P("dp", None), P("dp", None), P("dp", "mp"), P("dp")),
        out_specs=(P("dp"), P("dp", "mp")),
        check_vma=False,
    )
```

profile of v0, /device:TPU:0, one launch (start us, length us, event | category | flops | bytes accessed | tf_op | source)
XLA Modules:
  0.0 331.2 jit_solution(12993819938914179414)
XLA Ops:
  8.0 54.2 %all-gather.2.cloned.1.call-done = bf16[4096,256]{1,0:T(8,128)(2,1)} async-done(((bf16[512,256]{1,0:T(8,128)(2,1)}), bf16[4096,256]{1,0:T(8,128)(2,1)}) %all-gather.2.cloned.1.call-update) | async-done | bytes 2097168 | tf_op jit(solution)/shard_map/all_gather | solution.py:40
  62.2 3.1 convolution_convert_fusion
  67.5 5.5 %collective-permute-done = bf16[256,256]{1,0:T(8,128)(2,1)S(1)} collective-permute-done((bf16[256,256]{1,0:T(8,128)(2,1)S(1)}, bf16[256,256]{1,0:T(8,128)(2,1)S(1)}, u32[]{:S(2)}, u32[]{:S(2)}) %collective-permute-start) | collective-permute-done | bytes 131104 | tf_op jit(solution)/shard_map/ppermute | solution.py:19
  73.9 6.7 %collective-permute-done.1 = bf16[256,256]{1,0:T(8,128)(2,1)S(1)} collective-permute-done((bf16[256,256]{1,0:T(8,128)(2,1)S(1)}, bf16[256,256]{1,0:T(8,128)(2,1)S(1)}, u32[]{:S(2)}, u32[]{:S(2)}) %collective-permute-start.1) | collective-permute-done | bytes 131104 | tf_op jit(solution)/shard_map/ppermute | solution.py:19
  81.6 6.7 %collective-permute-done.2 = bf16[256,256]{1,0:T(8,128)(2,1)S(1)} collective-permute-done((bf16[256,256]{1,0:T(8,128)(2,1)S(1)}, bf16[256,256]{1,0:T(8,128)(2,1)S(1)}, u32[]{:S(2)}, u32[]{:S(2)}) %collective-permute-start.2) | collective-permute-done | bytes 131104 | tf_op jit(solution)/shard_map/ppermute | solution.py:19
  89.2 7.3 %collective-permute-done.3 = bf16[256,256]{1,0:T(8,128)(2,1)S(1)} collective-permute-done((bf16[256,256]{1,0:T(8,128)(2,1)S(1)}, bf16[256,256]{1,0:T(8,128)(2,1)S(1)}, u32[]{:S(2)}, u32[]{:S(2)}) %collective-permute-start.3) | collective-permute-done | bytes 131104 | tf_op jit(solution)/shard_map/ppermute | solution.py:19
  97.5 7.8 %collective-permute-done.4 = bf16[256,256]{1,0:T(8,128)(2,1)S(1)} collective-permute-done((bf16[256,256]{1,0:T(8,128)(2,1)S(1)}, bf16[256,256]{1,0:T(8,128)(2,1)S(1)}, u32[]{:S(2)}, u32[]{:S(2)}) %collective-permute-start.4) | collective-permute-done | bytes 131104 | tf_op jit(solution)/shard_map/ppermute | solution.py:19
  106.2 7.0 %collective-permute-done.5 = bf16[256,256]{1,0:T(8,128)(2,1)S(1)} collective-permute-done((bf16[256,256]{1,0:T(8,128)(2,1)S(1)}, bf16[256,256]{1,0:T(8,128)(2,1)S(1)}, u32[]{:S(2)}, u32[]{:S(2)}) %collective-permute-start.5) | collective-permute-done | bytes 131104 | tf_op jit(solution)/shard_map/ppermute | solution.py:19
  114.2 6.7 %collective-permute-done.6 = bf16[256,256]{1,0:T(8,128)(2,1)S(1)} collective-permute-done((bf16[256,256]{1,0:T(8,128)(2,1)S(1)}, bf16[256,256]{1,0:T(8,128)(2,1)S(1)}, u32[]{:S(2)}, u32[]{:S(2)}) %collective-permute-start.6) | collective-permute-done | bytes 131104 | tf_op jit(solution)/shard_map/ppermute | solution.py:19
  123.8 48.1 %all-reduce.3.cloned.1.call-done = (f32[256,256]{1,0:T(8,128)}, f32[256,256]{1,0:T(8,128)}, f32[256,256]{1,0:T(8,128)}, f32[256,256]{1,0:T(8,128)}, f32[256,256]...) async-done(((f32[256,256]{1,0:T(8,128)}, f32[256,256]{1,0:T(8,128)}, f32[256,256]{1,0:T(8,128)}, f32[256,256]{1,0:T(8,128)}, ...) | async-done | bytes 2097168 | tf_op jit(solution)/shard_map/psum | solution.py:53
  172.1 1.4 fusion.19
  173.5 1.5 collective-permute-start.13
  176.5 3.3 %fusion.11 = (f32[256]{0:T(256)S(1)}, f32[256]{0:T(256)S(1)}, f32[256]{0:T(256)}, f32[256]{0:T(256)}, f32[256]{0:T(256)}, /*index=5*/f32[256]{0:T(256)}, f32[256...) fusion(f32[256,256]{1,0:T(8,128)S(1)} %copy-done.5, ...), kind=kLoop, calls=%fused_computation.30 | loop fusion | flops 9172992 | bytes 2900992 | tf_op jit(solution)/shard_map/reduce_sum | solution.py:58
  180.1 1.5 collective-permute-start.12
  182.5 2.4 collective-permute-start.11
  188.2 2.4 collective-permute-start.9
  193.8 1.5 collective-permute-start.8
  197.4 3.0 fusion.9
  200.4 7.1 %collective-permute-done.11 = f32[256,256]{1,0:T(8,128)} collective-permute-done((f32[256,256]{1,0:T(8,128)}, f32[256,256]{1,0:T(8,128)}, u32[]{:S(2)}, u32[]{:S(2)}) %collective-permute-start.11) | collective-permute-done | bytes 262176 | tf_op jit(solution)/shard_map/ppermute | solution.py:19
  207.5 4.7 %collective-permute-done.10 = f32[256,256]{1,0:T(8,128)} collective-permute-done((f32[256,256]{1,0:T(8,128)}, f32[256,256]{1,0:T(8,128)}, u32[]{:S(2)}, u32[]{:S(2)}) %collective-permute-start.10) | collective-permute-done | bytes 262176 | tf_op jit(solution)/shard_map/ppermute | solution.py:19
  212.2 2.7 collective-permute-done.7
  214.9 6.4 %fusion = f32[4096,256]{0,1:T(8,128)} fusion(f32[256,4096]{1,0:T(8,128)} %fusion.9, bf16[256,4096]{1,0:T(8,128)(2,1)} %param.5, f32[256,256]{1,0:T(8,128)S(1)} %copy-done.12, f32[256,256]{1,0:T(8,128)} %copy-done.13, f32[256,256]{1,0:T(8,128)} %collective-permute-done.11, f32[256,256]{1,0:T(8,128)} %collective-permute-done.10, ...), kind=kOutput, calls=%fused_computation.1 | convolution fusion | flops 572784640 | bytes 12716032 | tf_op jit(solution)/shard_map/dot_general | solution.py:23
  222.6 100.1 %reduce-scatter.2.cloned.1.call-done = f32[512,256]{0,1:T(8,128)} async-done(((f32[4096,256]{0,1:T(8,128)}), f32[512,256]{0,1:T(8,128)}) %reduce-scatter.2.cloned.1.call-update) | async-done | bytes 524304 | tf_op jit(solution)/shard_map/reduce_scatter | solution.py:76
  322.7 2.0 copy.6
  (109 shorter events, 23.6 us)
Async XLA Ops:
  7.2 58.7 %copy-start = (bf16[256,4096]{1,0:T(8,128)(2,1)S(1)}, bf16[256,4096]{1,0:T(8,128)(2,1)}, u32[]{:S(2)}) copy-start(bf16[256,4096]{1,0:T(8,128)(2,1)} %param.4) | copy-start | bytes 6291460
  7.2 55.0 %all-gather.2.cloned.1.call-start = ((), (), s32[]{:S(2)}) async-start(), calls=%async_computation.1 | async-start | bytes 2359296 | tf_op jit(solution)/shard_map/all_gather | solution.py:40
  7.9 164.0 %all-reduce.3.cloned.1.call-start = ((), (), s32[]{:S(2)}) async-start(), calls=%async_computation.3 | async-start | bytes 4194304 | tf_op jit(solution)/shard_map/psum | solution.py:53
  65.3 7.7 %collective-permute-start = (bf16[256,256]{1,0:T(8,128)(2,1)S(1)}, bf16[256,256]{1,0:T(8,128)(2,1)S(1)}, u32[]{:S(2)}, u32[]{:S(2)}) collective-permute-start(bf16[256,256]{1,0:T(8,128)(2,1)S(1)} %convolution_convert_fusion), channel_id=1, source_target_pairs={{28,0},{0,4},{4,8},{8,12},{12,16},{16,20},{20,24},{24,28},{29,1},{... | collective-permute-start | bytes 393224 | tf_op jit(solution)/shard_map/ppermute | solution.py:19
  73.0 7.7 %collective-permute-start.1 = (bf16[256,256]{1,0:T(8,128)(2,1)S(1)}, bf16[256,256]{1,0:T(8,128)(2,1)S(1)}, u32[]{:S(2)}, u32[]{:S(2)}) collective-permute-start(bf16[256,256]{1,0:T(8,128)(2,1)S(1)} %collective-permute-done), channel_id=1, source_target_pairs={{28,0},{0,4},{4,8},{8,12},{12,16},{16,20},{20,24},{24,28},{29,1},{... | collective-permute-start | bytes 393224 | tf_op jit(solution)/shard_map/ppermute | solution.py:19
  80.6 7.7 %collective-permute-start.2 = (bf16[256,256]{1,0:T(8,128)(2,1)S(1)}, bf16[256,256]{1,0:T(8,128)(2,1)S(1)}, u32[]{:S(2)}, u32[]{:S(2)}) collective-permute-start(bf16[256,256]{1,0:T(8,128)(2,1)S(1)} %collective-permute-done.1), channel_id=1, source_target_pairs={{28,0},{0,4},{4,8},{8,12},{12,16},{16,20},{20,24},{24,28},{29,1},{... | collective-permute-start | bytes 393224 | tf_op jit(solution)/shard_map/ppermute | solution.py:19
  88.3 8.3 %collective-permute-start.3 = (bf16[256,256]{1,0:T(8,128)(2,1)S(1)}, bf16[256,256]{1,0:T(8,128)(2,1)S(1)}, u32[]{:S(2)}, u32[]{:S(2)}) collective-permute-start(bf16[256,256]{1,0:T(8,128)(2,1)S(1)} %collective-permute-done.2), channel_id=1, source_target_pairs={{28,0},{0,4},{4,8},{8,12},{12,16},{16,20},{20,24},{24,28},{29,1},{... | collective-permute-start | bytes 393224 | tf_op jit(solution)/shard_map/ppermute | solution.py:19
  89.2 82.8 %copy-start.15 = (s32[256]{0:T(256)S(1)}, s32[256]{0:T(256)}, u32[]{:S(2)}) copy-start(s32[256]{0:T(256)} %param.7) | copy-start | bytes 3076
  96.6 8.7 %collective-permute-start.4 = (bf16[256,256]{1,0:T(8,128)(2,1)S(1)}, bf16[256,256]{1,0:T(8,128)(2,1)S(1)}, u32[]{:S(2)}, u32[]{:S(2)}) collective-permute-start(bf16[256,256]{1,0:T(8,128)(2,1)S(1)} %collective-permute-done.3), channel_id=1, source_target_pairs={{28,0},{0,4},{4,8},{8,12},{12,16},{16,20},{20,24},{24,28},{29,1},{... | collective-permute-start | bytes 393224 | tf_op jit(solution)/shard_map/ppermute | solution.py:19
  105.3 8.0 %collective-permute-start.5 = (bf16[256,256]{1,0:T(8,128)(2,1)S(1)}, bf16[256,256]{1,0:T(8,128)(2,1)S(1)}, u32[]{:S(2)}, u32[]{:S(2)}) collective-permute-start(bf16[256,256]{1,0:T(8,128)(2,1)S(1)} %collective-permute-done.4), channel_id=1, source_target_pairs={{28,0},{0,4},{4,8},{8,12},{12,16},{16,20},{20,24},{24,28},{29,1},{... | collective-permute-start | bytes 393224 | tf_op jit(solution)/shard_map/ppermute | solution.py:19
  113.3 7.7 %copy-start.3 = (bf16[256,256]{1,0:T(8,128)(2,1)}, bf16[256,256]{1,0:T(8,128)(2,1)S(1)}, u32[]{:S(2)}) copy-start(bf16[256,256]{1,0:T(8,128)(2,1)S(1)} %collective-permute-done.5) | copy-start | bytes 393220
  113.3 7.7 %collective-permute-start.6 = (bf16[256,256]{1,0:T(8,128)(2,1)S(1)}, bf16[256,256]{1,0:T(8,128)(2,1)S(1)}, u32[]{:S(2)}, u32[]{:S(2)}) collective-permute-start(bf16[256,256]{1,0:T(8,128)(2,1)S(1)} %collective-permute-done.5), channel_id=1, source_target_pairs={{28,0},{0,4},{4,8},{8,12},{12,16},{16,20},{20,24},{24,28},{29,1},{... | collective-permute-start | bytes 393224 | tf_op jit(solution)/shard_map/ppermute | solution.py:19
  121.9 200.8 %reduce-scatter.2.cloned.1.call-start = ((), (), s32[]{:S(2)}) async-start(), calls=%async_computation.2 | async-start | bytes 4718592 | tf_op jit(solution)/shard_map/reduce_scatter | solution.py:76
  122.1 54.3 %copy-start.28 = (s32[256]{0:T(256)}, s32[256]{0:T(256)S(1)}, u32[]{:S(2)}) copy-start(s32[256]{0:T(256)S(1)} %iota_add_fusion.7) | copy-start | bytes 3076
  172.0 4.4 %copy-start.8 = (f32[256,256]{1,0:T(8,128)S(1)}, f32[256,256]{1,0:T(8,128)}, u32[]{:S(2)}) copy-start(f32[256,256]{1,0:T(8,128)} %get-tuple-element.15) | copy-start | bytes 786436
  173.5 20.2 %collective-permute-start.13 = (f32[256,256]{1,0:T(8,128)S(1)}, f32[256,256]{1,0:T(8,128)S(1)}, u32[]{:S(2)}, u32[]{:S(2)}) collective-permute-start(f32[256,256]{1,0:T(8,128)S(1)} %fusion.19), channel_id=1, source_target_pairs={{28,0},{0,4},{4,8},{8,12},{12,16},{16,20},{20,24},{24,28},{29,1},{... | collective-permute-start | bytes 786440 | tf_op jit(solution)/shard_map/ppermute | solution.py:19
  180.1 15.2 %collective-permute-start.12 = (f32[256,256]{1,0:T(8,128)S(1)}, f32[256,256]{1,0:T(8,128)S(1)}, u32[]{:S(2)}, u32[]{:S(2)}) collective-permute-start(f32[256,256]{1,0:T(8,128)S(1)} %fusion.33), channel_id=1, source_target_pairs={{24,0},{28,4},{0,8},{4,12},{8,16},{12,20},{16,24},{20,28},{25,1},{... | collective-permute-start | bytes 786440 | tf_op jit(solution)/shard_map/ppermute | solution.py:19
  182.5 25.0 %collective-permute-start.11 = (f32[256,256]{1,0:T(8,128)}, f32[256,256]{1,0:T(8,128)}, u32[]{:S(2)}, u32[]{:S(2)}) collective-permute-start(f32[256,256]{1,0:T(8,128)} %fusion.32), channel_id=1, source_target_pairs={{20,0},{24,4},{28,8},{0,12},{4,16},{8,20},{12,24},{16,28},{21,1},{... | collective-permute-start | bytes 786440 | tf_op jit(solution)/shard_map/ppermute | solution.py:19
  185.9 26.4 %collective-permute-start.10 = (f32[256,256]{1,0:T(8,128)}, f32[256,256]{1,0:T(8,128)}, u32[]{:S(2)}, u32[]{:S(2)}) collective-permute-start(f32[256,256]{1,0:T(8,128)} %fusion.31), channel_id=1, source_target_pairs={{16,0},{20,4},{24,8},{28,12},{0,16},{4,20},{8,24},{12,28},{17,1},{... | collective-permute-start | bytes 786440 | tf_op jit(solution)/shard_map/ppermute | solution.py:19
  188.2 24.0 %collective-permute-start.9 = (f32[256,256]{1,0:T(8,128)}, f32[256,256]{1,0:T(8,128)}, u32[]{:S(2)}, u32[]{:S(2)}) collective-permute-start(f32[256,256]{1,0:T(8,128)} %fusion.30), channel_id=1, source_target_pairs={{12,0},{16,4},{20,8},{24,12},{28,16},{0,20},{4,24},{8,28},{13,1},{... | collective-permute-start | bytes 786440 | tf_op jit(solution)/shard_map/ppermute | solution.py:19
  193.7 21.2 %copy-start.29 = (s32[256]{0:T(256)S(1)}, s32[256]{0:T(256)}, u32[]{:S(2)}) copy-start(s32[256]{0:T(256)} %copy-done.28) | copy-start | bytes 3076
  193.8 18.5 %collective-permute-start.8 = (f32[256,256]{1,0:T(8,128)}, f32[256,256]{1,0:T(8,128)}, u32[]{:S(2)}, u32[]{:S(2)}) collective-permute-start(f32[256,256]{1,0:T(8,128)} %fusion.29), channel_id=1, source_target_pairs={{8,0},{12,4},{16,8},{20,12},{24,16},{28,20},{0,24},{4,28},{9,1},{1... | collective-permute-start | bytes 786440 | tf_op jit(solution)/shard_map/ppermute | solution.py:19
  196.0 18.9 %collective-permute-start.7 = (f32[256,256]{1,0:T(8,128)}, f32[256,256]{1,0:T(8,128)}, u32[]{:S(2)}, u32[]{:S(2)}) collective-permute-start(f32[256,256]{1,0:T(8,128)} %fusion.28), channel_id=1, source_target_pairs={{4,0},{8,4},{12,8},{16,12},{20,16},{24,20},{28,24},{0,28},{5,1},{9... | collective-permute-start | bytes 786440 | tf_op jit(solution)/shard_map/ppermute | solution.py:19
  197.4 17.5 %copy-start.12 = (f32[256,256]{1,0:T(8,128)S(1)}, f32[256,256]{1,0:T(8,128)}, u32[]{:S(2)}) copy-start(f32[256,256]{1,0:T(8,128)} %copy-done.11) | copy-start | bytes 786436
  (24 other events, 70.7 us)
Sparse Core Ops, SparseCore 0:
  10.1 51.9 all-gather.1
  122.0 49.9 all-reduce.2
  221.5 101.1 reduce-scatter.1
where the time goes:
time: 331 us
  waiting for transfers between devices  265 us (80%)
  matrix products  29.4 us (9%)
  between operations  14.3 us (4%)
  starting transfers between devices  13 us (4%)
  other arithmetic  5.69 us (2%)
  local copies, waits for them, and re-layouts  3.5 us (1%)
    reduce_scatter x1, waiting for transfers between devices, per_device(): lax.psum_scatter(cross_rows(prompt_cols, grad_prompt_b) + cross_rows(resp...  100 us
    ppermute x14, waiting for transfers between devices, passed_along(): return lax.ppermute(block, axis, route)  62.3 us
    all_gather x1, waiting for transfers between devices, per_device(): segment = lax.all_gather(head_projection_matrix, 'dp', axis=0, tiled=True)  54.2 us
    psum x1, waiting for transfers between devices, per_device(): pair_scores = lax.psum(partial_logits, 'mp') * factor + LOGIT_BIAS  48.1 us
    dot_general x9, matrix products, cross_rows(): lax.dot_general(left_side, righthand_term, (((0,), (0,)), ((), ())), pref...  15.8 us
    ppermute x14, starting transfers between devices, passed_along(): return lax.ppermute(block, axis, route)  12.9 us
    dot_general x8, matrix products, cross_cols(): lax.dot_general(left_side, righthand_term, (((1,), (1,)), ((), ())), pref...  7.44 us
  transfers between devices with their start and end apart: 17, of which 13 were waited for; matrix products, arithmetic and copies ran while one was open for 7% of the time, Pallas kernels for 0%

commit v1 on v0

--- a/solution.py
+++ b/solution.py
@@ -31,19 +31,19 @@
     )
 
 
-def per_device(prompts, responses, head_projection_matrix, positive):
+def matmul(left_side, righthand_term):
+    return jnp.dot(left_side, righthand_term, preferred_element_type=jnp.float32)
+
+
+def general(prompts, responses, head_projection_matrix, positive):
     row_count = prompts.shape[0]
     col_count = head_projection_matrix.shape[1]
     factor = LOGIT_SCALE / math.sqrt(E)
     cycle_size = lax.axis_size("dp")
     position = lax.axis_index("dp")
     segment = lax.all_gather(head_projection_matrix, "dp", axis=0, tiled=True)
-    prompt_cols = prompts
-    response_cols = responses
-    prompt_proj = jnp.dot(prompt_cols, segment, preferred_element_type=jnp.float32)
-    response_proj = jnp.dot(response_cols, segment, preferred_element_type=jnp.float32)
-    prompt_emb = prompt_proj.astype(jnp.bfloat16)
-    visiting = response_proj.astype(jnp.bfloat16)
+    prompt_emb = matmul(prompts, segment).astype(jnp.bfloat16)
+    visiting = matmul(responses, segment).astype(jnp.bfloat16)
     local_ids = lax.iota(jnp.int32, row_count)
     prompt_gradient_total = jnp.zeros((row_count, col_count), jnp.float32)
     grad_response = jnp.zeros((row_count, col_count), jnp.float32)
@@ -59,9 +59,7 @@
         pairwise_weight = (-labels * jax.nn.sigmoid(margin) * (factor / row_count)).astype(
             jnp.bfloat16
         )
-        prompt_gradient_total = prompt_gradient_total + jnp.dot(
-            pairwise_weight, visiting, preferred_element_type=jnp.float32
-        )
+        prompt_gradient_total = prompt_gradient_total + matmul(pairwise_weight, visiting)
         contribution = cross_rows(pairwise_weight, prompt_emb)
         if offset == 0:
             grad_response = contribution
@@ -71,15 +69,171 @@
             visiting = passed_along(visiting, "dp", 1)
     grad_prompt_b = prompt_gradient_total.astype(jnp.bfloat16)
     grad_response_b = grad_response.astype(jnp.bfloat16)
-    prompt_cols = prompts
-    response_cols = responses
     head_grad = lax.psum_scatter(
-        cross_rows(prompt_cols, grad_prompt_b) + cross_rows(response_cols, grad_response_b),
+        cross_rows(prompts, grad_prompt_b) + cross_rows(responses, grad_response_b),
         "dp",
         scatter_dimension=0,
         tiled=True,
     )
     return (row_losses / row_count, head_grad)
+
+
+LINE, PAIR, SIDE, CORES = 4, 2, 2, 2
+
+
+def routes(move):
+    table = []
+    for z in range(LINE):
+        for y in range(PAIR):
+            for x in range(SIDE):
+                for c in range(CORES):
+                    goal = move(z, y, x, c)
+                    if goal is not None:
+                        gz, gy, gx, gc = goal
+                        source = (z * PAIR + y) * SIDE * CORES + x * CORES + c
+                        target = (gz * PAIR + gy) * SIDE * CORES + gx * CORES + gc
+                        table.append((source, target))
+    return table
+
+
+def along_line(moves):
+    return routes(lambda z, y, x, c: (moves[z], y, x, c) if z in moves else None)
+
+
+def send(block, table):
+    return lax.ppermute(block, ("dp", "mp"), table)
+
+
+ACROSS_Y = routes(lambda z, y, x, c: (z, 1 - y, x, c))
+ACROSS_X = routes(lambda z, y, x, c: (z, y, 1 - x, c))
+ACROSS_C = routes(lambda z, y, x, c: (z, y, x, 1 - c))
+UP = along_line({0: 1, 1: 2, 2: 3})
+DOWN = along_line({1: 0, 2: 1, 3: 2})
+MIX = [routes(lambda z, y, x, c, k=k: (z, y, x ^ (k >> 1), c ^ (k & 1))) for k in range(4)]
+
+
+def line_gather(block):
+    below = send(block, UP)
+    above = send(block, DOWN)
+    second = send(below, along_line({1: 2, 2: 3})) + send(above, along_line({1: 0, 2: 1}))
+    third = send(second, along_line({1: 0, 2: 3}))
+    return below, above, second, third
+
+
+def line_reduce(first, second, third_up, third_down, own):
+    far = send(first.astype(jnp.bfloat16), along_line({0: 1, 3: 2})).astype(jnp.float32)
+    middle = (second + far).astype(jnp.bfloat16)
+    climbed = send(middle, along_line({0: 1, 1: 2})).astype(jnp.float32)
+    sunk = send(middle, along_line({3: 2, 2: 1})).astype(jnp.float32)
+    from_below = send((third_up + climbed).astype(jnp.bfloat16), UP)
+    from_above = send((third_down + sunk).astype(jnp.bfloat16), DOWN)
+    return own + from_below.astype(jnp.float32) + from_above.astype(jnp.float32)
+
+
+def full_window(prompts, responses, head_projection_matrix, positive):
+    row_count = prompts.shape[0]
+    depth, width = head_projection_matrix.shape
+    factor = LOGIT_SCALE / math.sqrt(E)
+    dp, mp = lax.axis_index("dp"), lax.axis_index("mp")
+    z, y = dp // PAIR, dp % PAIR
+    quarter = row_count // (SIDE * CORES)
+    both = jnp.concatenate([prompts, responses], axis=0)
+
+    def features(line, pair):
+        line = line % LINE
+        return lax.dynamic_slice_in_dim(both, (line * PAIR + pair) * depth, depth, axis=1)
+
+    below, above, second, third = line_gather(head_projection_matrix)
+    emb = jnp.zeros((2 * row_count, width), jnp.float32)
+    for block, hop in ((head_projection_matrix, 0), (below, -1), (above, 1), (second, 2)):
+        emb = emb + matmul(features(z + hop, y), block)
+        emb = emb + matmul(features(z + hop, 1 - y), send(block, ACROSS_Y))
+    emb = emb + matmul(features(LINE - 1 - z, y), third)
+    third_table = routes(lambda z, y, x, c: (z, 1 - y, x, c) if z in (0, LINE - 1) else None)
+    emb = emb + matmul(features(LINE - 1 - z, 1 - y), send(third, third_table))
+    emb = emb.astype(jnp.bfloat16)
+    prompt_emb, response_emb = emb[:row_count], emb[row_count:]
+
+    pieces = []
+    for k in range(SIDE * CORES):
+        piece = lax.dynamic_slice_in_dim(response_emb, (mp ^ k) * quarter, quarter, axis=0)
+        pieces.append(piece if k == 0 else send(piece, MIX[k]))
+    response_rows = jnp.concatenate(pieces, axis=1)
+    below, above, second, third = line_gather(response_rows)
+    below = jnp.where(z == 0, third, below)
+    above = jnp.where(z == LINE - 1, third, above)
+    held = jnp.concatenate([response_rows, below, above, second], axis=0)
+
+    plane = jnp.concatenate([prompt_emb, send(prompt_emb, ACROSS_Y)], axis=0)
+    beside = send(plane, ACROSS_X)
+    half = jnp.concatenate([plane, beside], axis=1)
+    other = send(half, ACROSS_C)
+    plane = jnp.concatenate([plane, other[:, :width], beside, other[:, width:]], axis=1)
+    wanted = jnp.concatenate([positive, send(positive, ACROSS_Y)], axis=0)
+
+    pair_scores = cross_cols(plane, held) * factor + LOGIT_BIAS
+    lines = jnp.stack([z, (z + LINE - 1) % LINE, (z + 1) % LINE, (z + 2) % LINE])
+    column_ids = ((lines * PAIR + y) * row_count + mp * quarter)[:, None] + lax.iota(
+        jnp.int32, quarter
+    )[None, :]
+    column_ids = column_ids.reshape(-1)
+    labels = jnp.where(wanted[:, None] == column_ids[None, :], 1.0, -1.0).astype(jnp.float32)
+    margin = -labels * pair_scores
+    losses = jnp.sum(jax.nn.softplus(margin), axis=1)
+    weight = (-labels * jax.nn.sigmoid(margin) * (factor / row_count)).astype(jnp.bfloat16)
+
+    parts = cross_rows(weight, plane)
+    own, lower, upper, far = [parts[k * quarter : (k + 1) * quarter] for k in range(4)]
+    grad = line_reduce(jnp.where(z == 0, lower, upper), far, upper, lower, own)
+    grad = grad.astype(jnp.bfloat16)
+    grad_response = jnp.zeros((row_count, width), jnp.bfloat16)
+    for k in range(SIDE * CORES):
+        piece = grad[:, k * width : (k + 1) * width]
+        piece = piece if k == 0 else send(piece, MIX[k])
+        grad_response = lax.dynamic_update_slice_in_dim(
+            grad_response, piece, (mp ^ k) * quarter, axis=0
+        )
+
+    parts = matmul(weight, held)
+    mine = jnp.concatenate([parts[:, :width], parts[:, 2 * width : 3 * width]], axis=1)
+    away = jnp.concatenate([parts[:, width : 2 * width], parts[:, 3 * width :]], axis=1)
+    mine = mine + send(away.astype(jnp.bfloat16), ACROSS_C).astype(jnp.float32)
+    mine = mine[:, :width] + send(mine[:, width:].astype(jnp.bfloat16), ACROSS_X).astype(
+        jnp.float32
+    )
+    grad_prompt = mine[:row_count] + send(
+        mine[row_count:].astype(jnp.bfloat16), ACROSS_Y
+    ).astype(jnp.float32)
+    grads = jnp.concatenate([grad_prompt.astype(jnp.bfloat16), grad_response], axis=0)
+
+    def head(line):
+        away = cross_rows(features(line, 1 - y), grads).astype(jnp.bfloat16)
+        return cross_rows(features(line, y), grads) + send(away, ACROSS_Y).astype(jnp.float32)
+
+    lower_half = z < LINE // 2
+    end_block = head(jnp.where(lower_half, z - 1, z + 1))
+    far_block = head(z + 2)
+    near_block = head(jnp.where(lower_half, z + 1, z - 1))
+    own_block = head(z)
+    head_grad = line_reduce(
+        end_block,
+        far_block,
+        jnp.where(z == 2, end_block, near_block),
+        jnp.where(z == 1, end_block, near_block),
+        own_block,
+    )
+
+    losses = losses[:row_count] + send(losses[row_count:], ACROSS_Y)
+    losses = losses + send(losses, ACROSS_X)
+    losses = losses + send(losses, ACROSS_C)
+    return (losses / row_count, head_grad)
+
+
+def per_device(prompts, responses, head_projection_matrix, positive):
+    whole = lax.axis_size("dp") == STEPS == LINE * PAIR
+    whole = whole and lax.axis_size("mp") == SIDE * CORES
+    step = full_window if whole else general
+    return step(prompts, responses, head_projection_matrix, positive)
 
 
 def solution(mesh):

time: 331 us -> 158 us (0.48)
  waiting for transfers between devices: 265 us -> 44.4 us
  starting transfers between devices: 13 us -> 76.9 us
  between operations: 14.3 us -> 1.36 us
  other arithmetic: 5.69 us -> 1.51 us
    reduce_scatter x1 -> x0, waiting for transfers between devices: 100 us -> none  [per_device(): lax.psum_scatter(cross_rows(prompt_cols, grad_prompt_b) + cross_rows(resp...]
    ppermute x14 -> x45, starting transfers between devices: 12.9 us -> 76.9 us  [send(): return lax.ppermute(block, ('dp', 'mp'), table)]
    all_gather x1 -> x0, waiting for transfers between devices: 54.2 us -> none  [per_device(): segment = lax.all_gather(head_projection_matrix, 'dp', axis=0, tiled=True)]
    psum x1 -> x0, waiting for transfers between devices: 48.1 us -> none  [per_device(): pair_scores = lax.psum(partial_logits, 'mp') * factor + LOGIT_BIAS]
    ppermute x14 -> x45, waiting for transfers between devices: 62.3 us -> 44.4 us  [send(): return lax.ppermute(block, ('dp', 'mp'), table)]
    dot_general x9 -> x11, matrix products: 6.19 us -> 14 us  [matmul(): jnp.dot(left_side, righthand_term, preferred_element_type=jnp.float32)]
    dot_general x8 -> x1, matrix products: 7.44 us -> 0.81 us  [cross_cols(): lax.dot_general(left_side, righthand_term, (((1,), (1,)), ((), ())), pref...]
    reduce_sum x1 -> x0, other arithmetic: 3.35 us -> none  [per_device(): row_losses = row_losses + jnp.sum(jax.nn.softplus(margin), axis=1)]
  transfers between devices with their start and end apart: 17 -> 45, of which waited for: 13 -> 19; matrix products, arithmetic and copies ran while one was open for 7% -> 17% of each run, Pallas kernels for 0% -> 0%
where the time goes in v1:
time: 158 us; the launch traced here: 157 us
  starting transfers between devices  76.9 us (49%)
  waiting for transfers between devices  44.4 us (28%)
  matrix products  27.2 us (17%)
  local copies, waits for them, and re-layouts  5.08 us (3%)
    ppermute x45, starting transfers between devices, send(): return lax.ppermute(block, ('dp', 'mp'), table)  76.9 us
    ppermute x45, waiting for transfers between devices, send(): return lax.ppermute(block, ('dp', 'mp'), table)  44.4 us
    dot_general x11, matrix products, matmul(): jnp.dot(left_side, righthand_term, preferred_element_type=jnp.float32)  14 us
    dot_general x9, matrix products, cross_rows(): lax.dot_general(left_side, righthand_term, (((0,), (0,)), ((), ())), pref...  12.4 us
    unnamed x7, local copies, waits for them, and re-layouts  3.17 us
  transfers between devices with their start and end apart: 45, of which 19 were waited for; matrix products, arithmetic and copies ran while one was open for 17% of the time, Pallas kernels for 0%

profile of v1, /device:TPU:0, one launch (start us, length us, event | category | flops | bytes accessed | tf_op | source)
XLA Modules:
  0.0 156.5 jit_solution(10088529430795759527)
XLA Ops:
  0.6 5.1 %collective-permute-start.2 = (bf16[512,256]{1,0:T(8,128)(2,1)}, bf16[512,256]{1,0:T(8,128)(2,1)S(1)}, u32[]{:S(2)}, u32[]{:S(2)}) collective-permute-start(bf16[512,256]{1,0:T(8,128)(2,1)} %param.6), channel_id=1, source_target_pairs={{0,8},{1,9},{2,10},{3,11},{4,12},{5,13},{6,14},{7,15},{8,16},{9,17... | collective-permute-start | bytes 786440 | tf_op jit(solution)/shard_map/ppermute | solution.py:104
  8.6 3.2 %constant_dynamic-update-slice_fusion.1 = bf16[512,4096]{1,0:T(8,128)(2,1)} fusion(bf16[256,4096]{1,0:T(8,128)(2,1)} %param.4), kind=kLoop, calls=%fused_computation.79 | loop fusion | bytes 4194304
  22.8 5.3 %collective-permute-done.7 = bf16[512,256]{1,0:T(8,128)(2,1)S(1)} collective-permute-done((bf16[512,256]{1,0:T(8,128)(2,1)S(1)}, bf16[512,256]{1,0:T(8,128)(2,1)S(1)}, u32[]{:S(2)}, u32[]{:S(2)}) %collective-permute-start.7) | collective-permute-done | bytes 262176 | tf_op jit(solution)/shard_map/ppermute | solution.py:104
  33.8 2.7 %collective-permute-done.9 = bf16[512,256]{1,0:T(8,128)(2,1)S(1)} collective-permute-done((bf16[512,256]{1,0:T(8,128)(2,1)S(1)}, bf16[512,256]{1,0:T(8,128)(2,1)S(1)}, u32[]{:S(2)}, u32[]{:S(2)}) %collective-permute-start.9) | collective-permute-done | bytes 262176 | tf_op jit(solution)/shard_map/ppermute | solution.py:104
  36.5 3.4 %collective-permute-start.10 = (bf16[512,256]{1,0:T(8,128)(2,1)S(1)}, bf16[512,256]{1,0:T(8,128)(2,1)S(1)}, u32[]{:S(2)}, u32[]{:S(2)}) collective-permute-start(bf16[512,256]{1,0:T(8,128)(2,1)S(1)} %collective-permute-done.9), channel_id=1, source_target_pairs={{0,4},{1,5},{2,6},{3,7},{4,0},{5,1},{6,2},{7,3},{24,28},{25,29},{2... | collective-permute-start | bytes 786440 | tf_op jit(solution)/shard_map/ppermute | solution.py:104
  55.7 3.5 %collective-permute-done.19 = bf16[64,1024]{1,0:T(8,128)(2,1)S(1)} collective-permute-done((bf16[64,1024]{1,0:T(8,128)(2,1)S(1)}, bf16[64,1024]{1,0:T(8,128)(2,1)S(1)}, u32[]{:S(2)}, u32[]{:S(2)}) %collective-permute-start.19) | collective-permute-done | bytes 131104 | tf_op jit(solution)/shard_map/ppermute | solution.py:104
  60.5 1.6 %collective-permute-start = (s32[256]{0:T(256)S(1)}, s32[256]{0:T(256)S(1)}, u32[]{:S(2)}, u32[]{:S(2)}) collective-permute-start(s32[256]{0:T(256)S(1)} %copy-done.2), channel_id=1, source_target_pairs={{0,4},{1,5},{2,6},{3,7},{4,0},{5,1},{6,2},{7,3},{8,12},{9,13},{10,... | collective-permute-start | bytes 3080 | tf_op jit(solution)/shard_map/ppermute | solution.py:104
  62.2 3.9 %collective-permute-done.20 = bf16[64,1024]{1,0:T(8,128)(2,1)S(1)} collective-permute-done((bf16[64,1024]{1,0:T(8,128)(2,1)S(1)}, bf16[64,1024]{1,0:T(8,128)(2,1)S(1)}, u32[]{:S(2)}, u32[]{:S(2)}) %collective-permute-start.20) | collective-permute-done | bytes 131104 | tf_op jit(solution)/shard_map/ppermute | solution.py:104
  67.7 5.3 %collective-permute-done.21 = bf16[64,1024]{1,0:T(8,128)(2,1)S(1)} collective-permute-done((bf16[64,1024]{1,0:T(8,128)(2,1)S(1)}, bf16[64,1024]{1,0:T(8,128)(2,1)S(1)}, u32[]{:S(2)}, u32[]{:S(2)}) %collective-permute-start.21) | collective-permute-done | bytes 131104 | tf_op jit(solution)/shard_map/ppermute | solution.py:104
  76.5 1.9 %collective-permute-done.28 = bf16[64,1024]{1,0:T(8,128)(2,1)S(1)} collective-permute-done((bf16[64,1024]{1,0:T(8,128)(2,1)S(1)}, bf16[64,1024]{1,0:T(8,128)(2,1)S(1)}, u32[]{:S(2)}, u32[]{:S(2)}) %collective-permute-start.28) | collective-permute-done | bytes 131104 | tf_op jit(solution)/shard_map/ppermute | solution.py:104
  78.5 4.4 %collective-permute-start.29 = (bf16[64,1024]{1,0:T(8,128)(2,1)S(1)}, bf16[64,1024]{1,0:T(8,128)(2,1)S(1)}, u32[]{:S(2)}, u32[]{:S(2)}) collective-permute-start(bf16[64,1024]{1,0:T(8,128)(2,1)S(1)} %fusion.35), channel_id=1, source_target_pairs={{0,8},{1,9},{2,10},{3,11},{4,12},{5,13},{6,14},{7,15},{8,16},{9,17... | collective-permute-start | bytes 393224 | tf_op jit(solution)/shard_map/ppermute | solution.py:104
  83.7 1.7 %collective-permute-done.29 = bf16[64,1024]{1,0:T(8,128)(2,1)S(1)} collective-permute-done((bf16[64,1024]{1,0:T(8,128)(2,1)S(1)}, bf16[64,1024]{1,0:T(8,128)(2,1)S(1)}, u32[]{:S(2)}, u32[]{:S(2)}) %collective-permute-start.29) | collective-permute-done | bytes 131104 | tf_op jit(solution)/shard_map/ppermute | solution.py:104
  86.7 6.9 %collective-permute-start.30 = (bf16[64,1024]{1,0:T(8,128)(2,1)S(1)}, bf16[64,1024]{1,0:T(8,128)(2,1)S(1)}, u32[]{:S(2)}, u32[]{:S(2)}) collective-permute-start(bf16[64,1024]{1,0:T(8,128)(2,1)S(1)} %get-tuple-element.8), channel_id=1, source_target_pairs={{0,8},{1,9},{2,10},{3,11},{4,12},{5,13},{6,14},{7,15},{8,16},{9,17... | collective-permute-start | bytes 393224 | tf_op jit(solution)/shard_map/ppermute | solution.py:104
  99.5 4.1 %collective-permute-done.26 = bf16[512,256]{1,0:T(8,128)(2,1)S(1)} collective-permute-done((bf16[512,256]{1,0:T(8,128)(2,1)S(1)}, bf16[512,256]{1,0:T(8,128)(2,1)S(1)}, u32[]{:S(2)}, u32[]{:S(2)}) %collective-permute-start.26) | collective-permute-done | bytes 262176 | tf_op jit(solution)/shard_map/ppermute | solution.py:104
  103.6 1.6 %collective-permute-start.27 = (bf16[256,256]{1,0:T(8,128)(2,1)S(1)}, bf16[256,256]{1,0:T(8,128)(2,1)S(1)}, u32[]{:S(2)}, u32[]{:S(2)}) collective-permute-start(bf16[256,256]{1,0:T(8,128)(2,1)S(1)} %slice.133), channel_id=1, source_target_pairs={{0,4},{1,5},{2,6},{3,7},{4,0},{5,1},{6,2},{7,3},{8,12},{9,13},{10,... | collective-permute-start | bytes 393224 | tf_op jit(solution)/shard_map/ppermute | solution.py:104
  105.3 3.9 %collective-permute-done.27 = bf16[256,256]{1,0:T(8,128)(2,1)S(1)} collective-permute-done((bf16[256,256]{1,0:T(8,128)(2,1)S(1)}, bf16[256,256]{1,0:T(8,128)(2,1)S(1)}, u32[]{:S(2)}, u32[]{:S(2)}) %collective-permute-start.27) | collective-permute-done | bytes 131104 | tf_op jit(solution)/shard_map/ppermute | solution.py:104
  114.2 2.9 %collective-permute-done.37 = bf16[512,256]{1,0:T(8,128)(2,1)S(1)} collective-permute-done((bf16[512,256]{1,0:T(8,128)(2,1)S(1)}, bf16[512,256]{1,0:T(8,128)(2,1)S(1)}, u32[]{:S(2)}, u32[]{:S(2)}) %collective-permute-start.37) | collective-permute-done | bytes 262176 | tf_op jit(solution)/shard_map/ppermute | solution.py:104
  118.5 4.4 %collective-permute-start.40 = (bf16[512,256]{1,0:T(8,128)(2,1)S(1)}, bf16[512,256]{1,0:T(8,128)(2,1)S(1)}, u32[]{:S(2)}, u32[]{:S(2)}) collective-permute-start(bf16[512,256]{1,0:T(8,128)(2,1)S(1)} %get-tuple-element.28), channel_id=1, source_target_pairs={{0,8},{1,9},{2,10},{3,11},{4,12},{5,13},{6,14},{7,15},{24,16},{25,... | collective-permute-start | bytes 786440 | tf_op jit(solution)/shard_map/ppermute | solution.py:104
  122.9 1.6 %collective-permute-start.22 = (f32[256]{0:T(256)S(1)}, f32[256]{0:T(256)S(1)}, u32[]{:S(2)}, u32[]{:S(2)}) collective-permute-start(f32[256]{0:T(256)S(1)} %slice.75), channel_id=1, source_target_pairs={{0,4},{1,5},{2,6},{3,7},{4,0},{5,1},{6,2},{7,3},{8,12},{9,13},{10,... | collective-permute-start | bytes 3080 | tf_op jit(solution)/shard_map/ppermute | solution.py:104
  128.8 4.4 %collective-permute-start.41 = (bf16[512,256]{1,0:T(8,128)(2,1)S(1)}, bf16[512,256]{1,0:T(8,128)(2,1)S(1)}, u32[]{:S(2)}, u32[]{:S(2)}) collective-permute-start(bf16[512,256]{1,0:T(8,128)(2,1)S(1)} %fusion.9), channel_id=1, source_target_pairs={{0,8},{1,9},{2,10},{3,11},{4,12},{5,13},{6,14},{7,15},{8,16},{9,17... | collective-permute-start | bytes 786440 | tf_op jit(solution)/shard_map/ppermute | solution.py:104
  135.3 1.6 %collective-permute-start.36 = (bf16[512,256]{1,0:T(8,128)(2,1)S(1)}, bf16[512,256]{1,0:T(8,128)(2,1)S(1)}, u32[]{:S(2)}, u32[]{:S(2)}) collective-permute-start(bf16[512,256]{1,0:T(8,128)(2,1)S(1)} %convolution_convert_fusion.3), channel_id=1, source_target_pairs={{0,4},{1,5},{2,6},{3,7},{4,0},{5,1},{6,2},{7,3},{8,12},{9,13},{10,... | collective-permute-start | bytes 786440 | tf_op jit(solution)/shard_map/ppermute | solution.py:104
  139.8 9.2 %collective-permute-start.42 = (bf16[512,256]{1,0:T(8,128)(2,1)S(1)}, bf16[512,256]{1,0:T(8,128)(2,1)S(1)}, u32[]{:S(2)}, u32[]{:S(2)}) collective-permute-start(bf16[512,256]{1,0:T(8,128)(2,1)S(1)} %get-tuple-element.4), channel_id=1, source_target_pairs={{0,8},{1,9},{2,10},{3,11},{4,12},{5,13},{6,14},{7,15},{8,16},{9,17... | collective-permute-start | bytes 786440 | tf_op jit(solution)/shard_map/ppermute | solution.py:104
  150.0 2.6 %collective-permute-done.23 = f32[256]{0:T(256)S(1)} collective-permute-done((f32[256]{0:T(256)S(1)}, f32[256]{0:T(256)S(1)}, u32[]{:S(2)}, u32[]{:S(2)}) %collective-permute-start.23) | collective-permute-done | bytes 1056 | tf_op jit(solution)/shard_map/ppermute | solution.py:104
  154.3 2.2 %fusion.4 = f32[512,256]{1,0:T(8,128)} fusion(bf16[512,256]{1,0:T(8,128)(2,1)S(1)} %collective-permute-done.44, bf16[512,256]{1,0:T(8,128)(2,1)S(1)} %collective-permute-done.42, bf16[512,256]{1,0:T(8,128)(2,1)S(1)} %collective-permute-done.36, bf16[512,4096]{1,0:T(8,128)(2,1)} %constant_dynamic-update-slice_fusion, s32[]{:T(128)S(6)} %select_n.186, ...), kind=kOutput, calls=%fused_computation.10 | convolution fusion | flops 135528448 | bytes 2097156 | tf_op jit(solution)/shard_map/dot_general | solution.py:23
  (130 shorter events, 68.1 us)
Async XLA Ops:
  0.6 14.0 %collective-permute-start.2 = (bf16[512,256]{1,0:T(8,128)(2,1)}, bf16[512,256]{1,0:T(8,128)(2,1)S(1)}, u32[]{:S(2)}, u32[]{:S(2)}) collective-permute-start(bf16[512,256]{1,0:T(8,128)(2,1)} %param.6), channel_id=1, source_target_pairs={{0,8},{1,9},{2,10},{3,11},{4,12},{5,13},{6,14},{7,15},{8,16},{9,17... | collective-permute-start | bytes 786440 | tf_op jit(solution)/shard_map/ppermute | solution.py:104
  5.7 10.2 %collective-permute-start.4 = (bf16[512,256]{1,0:T(8,128)(2,1)}, bf16[512,256]{1,0:T(8,128)(2,1)S(1)}, u32[]{:S(2)}, u32[]{:S(2)}) collective-permute-start(bf16[512,256]{1,0:T(8,128)(2,1)} %param.6), channel_id=1, source_target_pairs={{8,0},{9,1},{10,2},{11,3},{12,4},{13,5},{14,6},{15,7},{16,8},{17,9... | collective-permute-start | bytes 786440 | tf_op jit(solution)/shard_map/ppermute | solution.py:104
  7.0 11.7 %collective-permute-start.1 = (bf16[512,256]{1,0:T(8,128)(2,1)}, bf16[512,256]{1,0:T(8,128)(2,1)S(1)}, u32[]{:S(2)}, u32[]{:S(2)}) collective-permute-start(bf16[512,256]{1,0:T(8,128)(2,1)} %param.6), channel_id=1, source_target_pairs={{0,4},{1,5},{2,6},{3,7},{4,0},{5,1},{6,2},{7,3},{8,12},{9,13},{10,... | collective-permute-start | bytes 786440 | tf_op jit(solution)/shard_map/ppermute | solution.py:104
  14.6 8.2 %collective-permute-start.6 = (bf16[512,256]{1,0:T(8,128)(2,1)S(1)}, bf16[512,256]{1,0:T(8,128)(2,1)S(1)}, u32[]{:S(2)}, u32[]{:S(2)}) collective-permute-start(bf16[512,256]{1,0:T(8,128)(2,1)S(1)} %collective-permute-done.2), channel_id=1, source_target_pairs={{8,16},{9,17},{10,18},{11,19},{12,20},{13,21},{14,22},{15,23},{16,... | collective-permute-start | bytes 786440 | tf_op jit(solution)/shard_map/ppermute | solution.py:104
  15.3 15.8 %collective-permute-start.3 = (bf16[512,256]{1,0:T(8,128)(2,1)S(1)}, bf16[512,256]{1,0:T(8,128)(2,1)S(1)}, u32[]{:S(2)}, u32[]{:S(2)}) collective-permute-start(bf16[512,256]{1,0:T(8,128)(2,1)S(1)} %collective-permute-done.2), channel_id=1, source_target_pairs={{0,4},{1,5},{2,6},{3,7},{4,0},{5,1},{6,2},{7,3},{8,12},{9,13},{10,... | collective-permute-start | bytes 786440 | tf_op jit(solution)/shard_map/ppermute | solution.py:104
  15.9 12.2 %collective-permute-start.7 = (bf16[512,256]{1,0:T(8,128)(2,1)S(1)}, bf16[512,256]{1,0:T(8,128)(2,1)S(1)}, u32[]{:S(2)}, u32[]{:S(2)}) collective-permute-start(bf16[512,256]{1,0:T(8,128)(2,1)S(1)} %collective-permute-done.4), channel_id=1, source_target_pairs={{8,0},{9,1},{10,2},{11,3},{12,4},{13,5},{14,6},{15,7},{16,8},{17,9... | collective-permute-start | bytes 786440 | tf_op jit(solution)/shard_map/ppermute | solution.py:104
  17.2 25.4 %collective-permute-start.5 = (bf16[512,256]{1,0:T(8,128)(2,1)S(1)}, bf16[512,256]{1,0:T(8,128)(2,1)S(1)}, u32[]{:S(2)}, u32[]{:S(2)}) collective-permute-start(bf16[512,256]{1,0:T(8,128)(2,1)S(1)} %collective-permute-done.4), channel_id=1, source_target_pairs={{0,4},{1,5},{2,6},{3,7},{4,0},{5,1},{6,2},{7,3},{8,12},{9,13},{10,... | collective-permute-start | bytes 786440 | tf_op jit(solution)/shard_map/ppermute | solution.py:104
  28.2 8.3 %collective-permute-start.9 = (bf16[512,256]{1,0:T(8,128)(2,1)S(1)}, bf16[512,256]{1,0:T(8,128)(2,1)S(1)}, u32[]{:S(2)}, u32[]{:S(2)}) collective-permute-start(bf16[512,256]{1,0:T(8,128)(2,1)S(1)} %add.354), channel_id=1, source_target_pairs={{8,0},{9,1},{10,2},{11,3},{12,4},{13,5},{14,6},{15,7},{16,24},{17,... | collective-permute-start | bytes 786440 | tf_op jit(solution)/shard_map/ppermute | solution.py:104
  29.5 11.7 %collective-permute-start.8 = (bf16[512,256]{1,0:T(8,128)(2,1)S(1)}, bf16[512,256]{1,0:T(8,128)(2,1)S(1)}, u32[]{:S(2)}, u32[]{:S(2)}) collective-permute-start(bf16[512,256]{1,0:T(8,128)(2,1)S(1)} %add.354), channel_id=1, source_target_pairs={{0,4},{1,5},{2,6},{3,7},{4,0},{5,1},{6,2},{7,3},{8,12},{9,13},{10,... | collective-permute-start | bytes 786440 | tf_op jit(solution)/shard_map/ppermute | solution.py:104
  36.5 8.3 %collective-permute-start.10 = (bf16[512,256]{1,0:T(8,128)(2,1)S(1)}, bf16[512,256]{1,0:T(8,128)(2,1)S(1)}, u32[]{:S(2)}, u32[]{:S(2)}) collective-permute-start(bf16[512,256]{1,0:T(8,128)(2,1)S(1)} %collective-permute-done.9), channel_id=1, source_target_pairs={{0,4},{1,5},{2,6},{3,7},{4,0},{5,1},{6,2},{7,3},{24,28},{25,29},{2... | collective-permute-start | bytes 786440 | tf_op jit(solution)/shard_map/ppermute | solution.py:104
  51.6 7.6 %collective-permute-start.19 = (bf16[64,1024]{1,0:T(8,128)(2,1)S(1)}, bf16[64,1024]{1,0:T(8,128)(2,1)S(1)}, u32[]{:S(2)}, u32[]{:S(2)}) collective-permute-start(bf16[64,1024]{1,0:T(8,128)(2,1)S(1)} %pad_maximum_fusion.6), channel_id=1, source_target_pairs={{8,0},{9,1},{10,2},{11,3},{12,4},{13,5},{14,6},{15,7},{16,8},{17,9... | collective-permute-start | bytes 393224 | tf_op jit(solution)/shard_map/ppermute | solution.py:104
  53.7 13.7 %collective-permute-start.12 = (bf16[512,256]{1,0:T(8,128)(2,1)S(1)}, bf16[512,256]{1,0:T(8,128)(2,1)S(1)}, u32[]{:S(2)}, u32[]{:S(2)}) collective-permute-start(bf16[512,256]{1,0:T(8,128)(2,1)S(1)} %pad_maximum_fusion.4), channel_id=1, source_target_pairs={{0,2},{1,3},{2,0},{3,1},{4,6},{5,7},{6,4},{7,5},{8,10},{9,11},{10,... | collective-permute-start | bytes 786440 | tf_op jit(solution)/shard_map/ppermute | solution.py:104
  83.6 12.6 %collective-permute-start.25 = (bf16[512,512]{1,0:T(8,128)(2,1)S(1)}, bf16[512,512]{1,0:T(8,128)(2,1)S(1)}, u32[]{:S(2)}, u32[]{:S(2)}) collective-permute-start(bf16[512,512]{1,0:T(8,128)(2,1)S(1)} %pad_maximum_fusion.3), channel_id=1, source_target_pairs={{0,1},{1,0},{2,3},{3,2},{4,5},{5,4},{6,7},{7,6},{8,9},{9,8},{10,11... | collective-permute-start | bytes 1572872 | tf_op jit(solution)/shard_map/ppermute | solution.py:104
  85.4 9.2 %collective-permute-start.32 = (bf16[64,1024]{1,0:T(8,128)(2,1)S(1)}, bf16[64,1024]{1,0:T(8,128)(2,1)S(1)}, u32[]{:S(2)}, u32[]{:S(2)}) collective-permute-start(bf16[64,1024]{1,0:T(8,128)(2,1)S(1)} %get-tuple-element.9), channel_id=1, source_target_pairs={{8,0},{9,1},{10,2},{11,3},{12,4},{13,5},{14,6},{15,7},{16,8},{17,9... | collective-permute-start | bytes 393224 | tf_op jit(solution)/shard_map/ppermute | solution.py:104
  86.7 9.4 %collective-permute-start.30 = (bf16[64,1024]{1,0:T(8,128)(2,1)S(1)}, bf16[64,1024]{1,0:T(8,128)(2,1)S(1)}, u32[]{:S(2)}, u32[]{:S(2)}) collective-permute-start(bf16[64,1024]{1,0:T(8,128)(2,1)S(1)} %get-tuple-element.8), channel_id=1, source_target_pairs={{0,8},{1,9},{2,10},{3,11},{4,12},{5,13},{6,14},{7,15},{8,16},{9,17... | collective-permute-start | bytes 393224 | tf_op jit(solution)/shard_map/ppermute | solution.py:104
  97.6 7.6 %collective-permute-start.34 = (bf16[64,256]{1,0:T(8,128)(2,1)S(1)}, bf16[64,256]{1,0:T(8,128)(2,1)S(1)}, u32[]{:S(2)}, u32[]{:S(2)}) collective-permute-start(bf16[64,256]{1,0:T(8,128)(2,1)S(1)} %get-tuple-element.15), channel_id=1, source_target_pairs={{0,2},{1,3},{2,0},{3,1},{4,6},{5,7},{6,4},{7,5},{8,10},{9,11},{10,... | collective-permute-start | bytes 98312 | tf_op jit(solution)/shard_map/ppermute | solution.py:104
  113.6 12.9 %collective-permute-start.39 = (bf16[512,256]{1,0:T(8,128)(2,1)S(1)}, bf16[512,256]{1,0:T(8,128)(2,1)S(1)}, u32[]{:S(2)}, u32[]{:S(2)}) collective-permute-start(bf16[512,256]{1,0:T(8,128)(2,1)S(1)} %convolution_convert_fusion), channel_id=1, source_target_pairs={{0,4},{1,5},{2,6},{3,7},{4,0},{5,1},{6,2},{7,3},{8,12},{9,13},{10,... | collective-permute-start | bytes 786440 | tf_op jit(solution)/shard_map/ppermute | solution.py:104
  118.5 8.9 %collective-permute-start.40 = (bf16[512,256]{1,0:T(8,128)(2,1)S(1)}, bf16[512,256]{1,0:T(8,128)(2,1)S(1)}, u32[]{:S(2)}, u32[]{:S(2)}) collective-permute-start(bf16[512,256]{1,0:T(8,128)(2,1)S(1)} %get-tuple-element.28), channel_id=1, source_target_pairs={{0,8},{1,9},{2,10},{3,11},{4,12},{5,13},{6,14},{7,15},{24,16},{25,... | collective-permute-start | bytes 786440 | tf_op jit(solution)/shard_map/ppermute | solution.py:104
  122.9 26.0 %collective-permute-start.22 = (f32[256]{0:T(256)S(1)}, f32[256]{0:T(256)S(1)}, u32[]{:S(2)}, u32[]{:S(2)}) collective-permute-start(f32[256]{0:T(256)S(1)} %slice.75), channel_id=1, source_target_pairs={{0,4},{1,5},{2,6},{3,7},{4,0},{5,1},{6,2},{7,3},{8,12},{9,13},{10,... | collective-permute-start | bytes 3080 | tf_op jit(solution)/shard_map/ppermute | solution.py:104
  125.9 11.0 %collective-permute-start.38 = (bf16[512,256]{1,0:T(8,128)(2,1)S(1)}, bf16[512,256]{1,0:T(8,128)(2,1)S(1)}, u32[]{:S(2)}, u32[]{:S(2)}) collective-permute-start(bf16[512,256]{1,0:T(8,128)(2,1)S(1)} %convolution_convert_fusion.1), channel_id=1, source_target_pairs={{0,4},{1,5},{2,6},{3,7},{4,0},{5,1},{6,2},{7,3},{8,12},{9,13},{10,... | collective-permute-start | bytes 786440 | tf_op jit(solution)/shard_map/ppermute | solution.py:104
  128.8 9.5 %collective-permute-start.41 = (bf16[512,256]{1,0:T(8,128)(2,1)S(1)}, bf16[512,256]{1,0:T(8,128)(2,1)S(1)}, u32[]{:S(2)}, u32[]{:S(2)}) collective-permute-start(bf16[512,256]{1,0:T(8,128)(2,1)S(1)} %fusion.9), channel_id=1, source_target_pairs={{0,8},{1,9},{2,10},{3,11},{4,12},{5,13},{6,14},{7,15},{8,16},{9,17... | collective-permute-start | bytes 786440 | tf_op jit(solution)/shard_map/ppermute | solution.py:104
  135.3 19.0 %collective-permute-start.36 = (bf16[512,256]{1,0:T(8,128)(2,1)S(1)}, bf16[512,256]{1,0:T(8,128)(2,1)S(1)}, u32[]{:S(2)}, u32[]{:S(2)}) collective-permute-start(bf16[512,256]{1,0:T(8,128)(2,1)S(1)} %convolution_convert_fusion.3), channel_id=1, source_target_pairs={{0,4},{1,5},{2,6},{3,7},{4,0},{5,1},{6,2},{7,3},{8,12},{9,13},{10,... | collective-permute-start | bytes 786440 | tf_op jit(solution)/shard_map/ppermute | solution.py:104
  138.5 15.8 %collective-permute-start.44 = (bf16[512,256]{1,0:T(8,128)(2,1)S(1)}, bf16[512,256]{1,0:T(8,128)(2,1)S(1)}, u32[]{:S(2)}, u32[]{:S(2)}) collective-permute-start(bf16[512,256]{1,0:T(8,128)(2,1)S(1)} %get-tuple-element.5), channel_id=1, source_target_pairs={{8,0},{9,1},{10,2},{11,3},{12,4},{13,5},{14,6},{15,7},{16,8},{17,9... | collective-permute-start | bytes 786440 | tf_op jit(solution)/shard_map/ppermute | solution.py:104
  139.8 14.5 %collective-permute-start.42 = (bf16[512,256]{1,0:T(8,128)(2,1)S(1)}, bf16[512,256]{1,0:T(8,128)(2,1)S(1)}, u32[]{:S(2)}, u32[]{:S(2)}) collective-permute-start(bf16[512,256]{1,0:T(8,128)(2,1)S(1)} %get-tuple-element.4), channel_id=1, source_target_pairs={{0,8},{1,9},{2,10},{3,11},{4,12},{5,13},{6,14},{7,15},{8,16},{9,17... | collective-permute-start | bytes 786440 | tf_op jit(solution)/shard_map/ppermute | solution.py:104
  (24 other events, 148.1 us)

commit v2 on v1

--- a/solution.py
+++ b/solution.py
@@ -106,28 +106,33 @@
 
 ACROSS_Y = routes(lambda z, y, x, c: (z, 1 - y, x, c))
 ACROSS_X = routes(lambda z, y, x, c: (z, y, 1 - x, c))
+ACROSS_XY = routes(lambda z, y, x, c: (z, 1 - y, 1 - x, c))
 ACROSS_C = routes(lambda z, y, x, c: (z, y, x, 1 - c))
-UP = along_line({0: 1, 1: 2, 2: 3})
-DOWN = along_line({1: 0, 2: 1, 3: 2})
+PAIRS = along_line({0: 1, 1: 0, 2: 3, 3: 2})
+MIDDLE = along_line({1: 2, 2: 1})
+OUTWARD = along_line({1: 0, 2: 3})
+INWARD = along_line({0: 1, 3: 2})
+TWO_OUT = along_line({1: 3, 2: 0})
+TWO_IN = along_line({3: 1, 0: 2})
 MIX = [routes(lambda z, y, x, c, k=k: (z, y, x ^ (k >> 1), c ^ (k & 1))) for k in range(4)]
 
 
 def line_gather(block):
-    below = send(block, UP)
-    above = send(block, DOWN)
-    second = send(below, along_line({1: 2, 2: 3})) + send(above, along_line({1: 0, 2: 1}))
-    third = send(second, along_line({1: 0, 2: 3}))
-    return below, above, second, third
-
-
-def line_reduce(first, second, third_up, third_down, own):
-    far = send(first.astype(jnp.bfloat16), along_line({0: 1, 3: 2})).astype(jnp.float32)
-    middle = (second + far).astype(jnp.bfloat16)
-    climbed = send(middle, along_line({0: 1, 1: 2})).astype(jnp.float32)
-    sunk = send(middle, along_line({3: 2, 2: 1})).astype(jnp.float32)
-    from_below = send((third_up + climbed).astype(jnp.bfloat16), UP)
-    from_above = send((third_down + sunk).astype(jnp.bfloat16), DOWN)
-    return own + from_below.astype(jnp.float32) + from_above.astype(jnp.float32)
+    first = send(block, PAIRS)
+    middle = send(block, MIDDLE)
+    second = send(first, MIDDLE) + send(middle, OUTWARD)
+    third = middle + send(first, TWO_OUT)
+    return first, second, third
+
+
+def line_reduce(own, first, second, third):
+    third_b, second_b = third.astype(jnp.bfloat16), second.astype(jnp.bfloat16)
+    jumped = send(third_b, TWO_IN).astype(jnp.float32)
+    inward = send(second_b, INWARD).astype(jnp.float32)
+    across = send(second_b, MIDDLE).astype(jnp.float32)
+    last = send((third + inward).astype(jnp.bfloat16), MIDDLE).astype(jnp.float32)
+    paired = send((first + across + jumped).astype(jnp.bfloat16), PAIRS).astype(jnp.float32)
+    return own + last + paired
 
 
 def full_window(prompts, responses, head_projection_matrix, positive):
@@ -140,17 +145,13 @@
     both = jnp.concatenate([prompts, responses], axis=0)
 
     def features(line, pair):
-        line = line % LINE
         return lax.dynamic_slice_in_dim(both, (line * PAIR + pair) * depth, depth, axis=1)
 
-    below, above, second, third = line_gather(head_projection_matrix)
+    first, second, third = line_gather(head_projection_matrix)
     emb = jnp.zeros((2 * row_count, width), jnp.float32)
-    for block, hop in ((head_projection_matrix, 0), (below, -1), (above, 1), (second, 2)):
-        emb = emb + matmul(features(z + hop, y), block)
-        emb = emb + matmul(features(z + hop, 1 - y), send(block, ACROSS_Y))
-    emb = emb + matmul(features(LINE - 1 - z, y), third)
-    third_table = routes(lambda z, y, x, c: (z, 1 - y, x, c) if z in (0, LINE - 1) else None)
-    emb = emb + matmul(features(LINE - 1 - z, 1 - y), send(third, third_table))
+    for k, block in enumerate((head_projection_matrix, first, second, third)):
+        emb = emb + matmul(features(z ^ k, y), block)
+        emb = emb + matmul(features(z ^ k, 1 - y), send(block, ACROSS_Y))
     emb = emb.astype(jnp.bfloat16)
     prompt_emb, response_emb = emb[:row_count], emb[row_count:]
 
@@ -159,20 +160,18 @@
         piece = lax.dynamic_slice_in_dim(response_emb, (mp ^ k) * quarter, quarter, axis=0)
         pieces.append(piece if k == 0 else send(piece, MIX[k]))
     response_rows = jnp.concatenate(pieces, axis=1)
-    below, above, second, third = line_gather(response_rows)
-    below = jnp.where(z == 0, third, below)
-    above = jnp.where(z == LINE - 1, third, above)
-    held = jnp.concatenate([response_rows, below, above, second], axis=0)
-
-    plane = jnp.concatenate([prompt_emb, send(prompt_emb, ACROSS_Y)], axis=0)
-    beside = send(plane, ACROSS_X)
-    half = jnp.concatenate([plane, beside], axis=1)
+    held = jnp.concatenate([response_rows, *line_gather(response_rows)], axis=0)
+
+    near = jnp.concatenate([prompt_emb, send(prompt_emb, ACROSS_X)], axis=1)
+    across = jnp.concatenate([send(prompt_emb, ACROSS_Y), send(prompt_emb, ACROSS_XY)], axis=1)
+    half = jnp.concatenate([near, across], axis=0)
     other = send(half, ACROSS_C)
-    plane = jnp.concatenate([plane, other[:, :width], beside, other[:, width:]], axis=1)
+    plane = [half[:, :width], other[:, :width], half[:, width:], other[:, width:]]
+    plane = jnp.concatenate(plane, axis=1)
     wanted = jnp.concatenate([positive, send(positive, ACROSS_Y)], axis=0)
 
     pair_scores = cross_cols(plane, held) * factor + LOGIT_BIAS
-    lines = jnp.stack([z, (z + LINE - 1) % LINE, (z + 1) % LINE, (z + 2) % LINE])
+    lines = jnp.stack([z ^ k for k in range(LINE)])
     column_ids = ((lines * PAIR + y) * row_count + mp * quarter)[:, None] + lax.iota(
         jnp.int32, quarter
     )[None, :]
@@ -183,8 +182,7 @@
     weight = (-labels * jax.nn.sigmoid(margin) * (factor / row_count)).astype(jnp.bfloat16)
 
     parts = cross_rows(weight, plane)
-    own, lower, upper, far = [parts[k * quarter : (k + 1) * quarter] for k in range(4)]
-    grad = line_reduce(jnp.where(z == 0, lower, upper), far, upper, lower, own)
+    grad = line_reduce(*[parts[k * quarter : (k + 1) * quarter] for k in range(LINE)])
     grad = grad.astype(jnp.bfloat16)
     grad_response = jnp.zeros((row_count, width), jnp.bfloat16)
     for k in range(SIDE * CORES):
@@ -198,30 +196,21 @@
     mine = jnp.concatenate([parts[:, :width], parts[:, 2 * width : 3 * width]], axis=1)
     away = jnp.concatenate([parts[:, width : 2 * width], parts[:, 3 * width :]], axis=1)
     mine = mine + send(away.astype(jnp.bfloat16), ACROSS_C).astype(jnp.float32)
-    mine = mine[:, :width] + send(mine[:, width:].astype(jnp.bfloat16), ACROSS_X).astype(
-        jnp.float32
-    )
-    grad_prompt = mine[:row_count] + send(
-        mine[row_count:].astype(jnp.bfloat16), ACROSS_Y
-    ).astype(jnp.float32)
+    away = mine.astype(jnp.bfloat16)
+    grad_prompt = (
+        mine[:row_count, :width]
+        + send(away[:row_count, width:], ACROSS_X).astype(jnp.float32)
+        + send(away[row_count:, :width], ACROSS_Y).astype(jnp.float32)
+        + send(away[row_count:, width:], ACROSS_XY).astype(jnp.float32)
+    )
     grads = jnp.concatenate([grad_prompt.astype(jnp.bfloat16), grad_response], axis=0)
 
     def head(line):
         away = cross_rows(features(line, 1 - y), grads).astype(jnp.bfloat16)
         return cross_rows(features(line, y), grads) + send(away, ACROSS_Y).astype(jnp.float32)
 
-    lower_half = z < LINE // 2
-    end_block = head(jnp.where(lower_half, z - 1, z + 1))
-    far_block = head(z + 2)
-    near_block = head(jnp.where(lower_half, z + 1, z - 1))
-    own_block = head(z)
-    head_grad = line_reduce(
-        end_block,
-        far_block,
-        jnp.where(z == 2, end_block, near_block),
-        jnp.where(z == 1, end_block, near_block),
-        own_block,
-    )
+    third, second, first, own = [head(z ^ k) for k in (3, 2, 1, 0)]
+    head_grad = line_reduce(own, first, second, third)
 
     losses = losses[:row_count] + send(losses[row_count:], ACROSS_Y)
     losses = losses + send(losses, ACROSS_X)

time: 158 us -> 147 us (0.930)
  starting transfers between devices: 76.9 us -> 67.5 us
  matrix products: 27.2 us -> 24.6 us
    ppermute x45 -> x46, starting transfers between devices: 76.9 us -> 67.5 us  [send(): return lax.ppermute(block, ('dp', 'mp'), table)]
    dot_general x11 -> x9, matrix products: 14 us -> 11.3 us  [matmul(): jnp.dot(left_side, righthand_term, preferred_element_type=jnp.float32)]
    ppermute x45 -> x46, waiting for transfers between devices: 44.4 us -> 45.9 us  [send(): return lax.ppermute(block, ('dp', 'mp'), table)]
  transfers between devices with their start and end apart: 45 -> 46, of which waited for: 19 -> 15; matrix products, arithmetic and copies ran while one was open for 17% -> 16% of each run, Pallas kernels for 0% -> 0%
where the time goes in v2:
time: 147 us; the launch traced here: 146 us
  starting transfers between devices  67.5 us (46%)
  waiting for transfers between devices  45.9 us (31%)
  matrix products  24.6 us (17%)
  local copies, waits for them, and re-layouts  5.13 us (3%)
    ppermute x46, starting transfers between devices, send(): return lax.ppermute(block, ('dp', 'mp'), table)  67.5 us
    ppermute x46, waiting for transfers between devices, send(): return lax.ppermute(block, ('dp', 'mp'), table)  45.9 us
    dot_general x9, matrix products, cross_rows(): lax.dot_general(left_side, righthand_term, (((0,), (0,)), ((), ())), pref...  12.5 us
    dot_general x9, matrix products, matmul(): jnp.dot(left_side, righthand_term, preferred_element_type=jnp.float32)  11.3 us
    unnamed x7, local copies, waits for them, and re-layouts  3.17 us
  transfers between devices with their start and end apart: 46, of which 15 were waited for; matrix products, arithmetic and copies ran while one was open for 16% of the time, Pallas kernels for 0%

profile of v2, /device:TPU:0, one launch (start us, length us, event | category | flops | bytes accessed | tf_op | source)
XLA Modules:
  0.0 145.8 jit_solution(7876972999411985862)
XLA Ops:
  1.5 5.9 %collective-permute-start.2 = (bf16[512,256]{1,0:T(8,128)(2,1)}, bf16[512,256]{1,0:T(8,128)(2,1)S(1)}, u32[]{:S(2)}, u32[]{:S(2)}) collective-permute-start(bf16[512,256]{1,0:T(8,128)(2,1)} %param.6), channel_id=1, source_target_pairs={{0,8},{1,9},{2,10},{3,11},{4,12},{5,13},{6,14},{7,15},{8,0},{9,1},... | collective-permute-start | bytes 786440 | tf_op jit(solution)/shard_map/ppermute | solution.py:104
  8.9 3.2 %constant_dynamic-update-slice_fusion.1 = bf16[512,4096]{1,0:T(8,128)(2,1)} fusion(bf16[256,4096]{1,0:T(8,128)(2,1)} %param.4), kind=kLoop, calls=%fused_computation.73 | loop fusion | bytes 4194304
  21.2 4.4 %collective-permute-done.8 = bf16[512,256]{1,0:T(8,128)(2,1)S(1)} collective-permute-done((bf16[512,256]{1,0:T(8,128)(2,1)S(1)}, bf16[512,256]{1,0:T(8,128)(2,1)S(1)}, u32[]{:S(2)}, u32[]{:S(2)}) %collective-permute-start.8) | collective-permute-done | bytes 262176 | tf_op jit(solution)/shard_map/ppermute | solution.py:104
  28.6 1.9 %collective-permute-done.6 = bf16[512,256]{1,0:T(8,128)(2,1)S(1)} collective-permute-done((bf16[512,256]{1,0:T(8,128)(2,1)S(1)}, bf16[512,256]{1,0:T(8,128)(2,1)S(1)}, u32[]{:S(2)}, u32[]{:S(2)}) %collective-permute-start.6) | collective-permute-done | bytes 262176 | tf_op jit(solution)/shard_map/ppermute | solution.py:104
  34.4 3.4 %collective-permute-done.7 = bf16[512,256]{1,0:T(8,128)(2,1)S(1)} collective-permute-done((bf16[512,256]{1,0:T(8,128)(2,1)S(1)}, bf16[512,256]{1,0:T(8,128)(2,1)S(1)}, u32[]{:S(2)}, u32[]{:S(2)}) %collective-permute-start.7) | collective-permute-done | bytes 262176 | tf_op jit(solution)/shard_map/ppermute | solution.py:104
  41.9 2.5 %collective-permute-start.12 = (bf16[256,256]{1,0:T(8,128)(2,1)S(1)}, bf16[256,256]{1,0:T(8,128)(2,1)S(1)}, u32[]{:S(2)}, u32[]{:S(2)}) collective-permute-start(bf16[256,256]{1,0:T(8,128)(2,1)S(1)} %get-tuple-element.22), channel_id=1, source_target_pairs={{0,6},{1,7},{2,4},{3,5},{4,2},{5,3},{6,0},{7,1},{8,14},{9,15},{10,... | collective-permute-start | bytes 393224 | tf_op jit(solution)/shard_map/ppermute | solution.py:104
  47.1 5.3 %collective-permute-done.15 = bf16[64,256]{1,0:T(8,128)(2,1)S(1)} collective-permute-done((bf16[64,256]{1,0:T(8,128)(2,1)S(1)}, bf16[64,256]{1,0:T(8,128)(2,1)S(1)}, u32[]{:S(2)}, u32[]{:S(2)}) %collective-permute-start.15) | collective-permute-done | bytes 32800 | tf_op jit(solution)/shard_map/ppermute | solution.py:104
  54.2 4.3 %collective-permute-start.17 = (bf16[64,1024]{1,0:T(8,128)(2,1)S(1)}, bf16[64,1024]{1,0:T(8,128)(2,1)S(1)}, u32[]{:S(2)}, u32[]{:S(2)}) collective-permute-start(bf16[64,1024]{1,0:T(8,128)(2,1)S(1)} %pad_maximum_fusion.6), channel_id=1, source_target_pairs={{0,8},{1,9},{2,10},{3,11},{4,12},{5,13},{6,14},{7,15},{8,0},{9,1},... | collective-permute-start | bytes 393224 | tf_op jit(solution)/shard_map/ppermute | solution.py:104
  58.8 2.8 %collective-permute-done.17 = bf16[64,1024]{1,0:T(8,128)(2,1)S(1)} collective-permute-done((bf16[64,1024]{1,0:T(8,128)(2,1)S(1)}, bf16[64,1024]{1,0:T(8,128)(2,1)S(1)}, u32[]{:S(2)}, u32[]{:S(2)}) %collective-permute-start.17) | collective-permute-done | bytes 131104 | tf_op jit(solution)/shard_map/ppermute | solution.py:104
  64.9 4.7 %collective-permute-done.21 = bf16[64,1024]{1,0:T(8,128)(2,1)S(1)} collective-permute-done((bf16[64,1024]{1,0:T(8,128)(2,1)S(1)}, bf16[64,1024]{1,0:T(8,128)(2,1)S(1)}, u32[]{:S(2)}, u32[]{:S(2)}) %collective-permute-start.21) | collective-permute-done | bytes 131104 | tf_op jit(solution)/shard_map/ppermute | solution.py:104
  69.7 3.4 %collective-permute-done.20 = bf16[64,1024]{1,0:T(8,128)(2,1)S(1)} collective-permute-done((bf16[64,1024]{1,0:T(8,128)(2,1)S(1)}, bf16[64,1024]{1,0:T(8,128)(2,1)S(1)}, u32[]{:S(2)}, u32[]{:S(2)}) %collective-permute-start.20) | collective-permute-done | bytes 131104 | tf_op jit(solution)/shard_map/ppermute | solution.py:104
  74.6 2.2 %collective-permute-start.29 = (bf16[64,1024]{1,0:T(8,128)(2,1)S(1)}, bf16[64,1024]{1,0:T(8,128)(2,1)S(1)}, u32[]{:S(2)}, u32[]{:S(2)}) collective-permute-start(bf16[64,1024]{1,0:T(8,128)(2,1)S(1)} %get-tuple-element.10), channel_id=1, source_target_pairs={{0,8},{1,9},{2,10},{3,11},{4,12},{5,13},{6,14},{7,15},{24,16},{25,... | collective-permute-start | bytes 393224 | tf_op jit(solution)/shard_map/ppermute | solution.py:104
  77.5 4.0 %collective-permute-start.32 = (bf16[64,1024]{1,0:T(8,128)(2,1)S(1)}, bf16[64,1024]{1,0:T(8,128)(2,1)S(1)}, u32[]{:S(2)}, u32[]{:S(2)}) collective-permute-start(bf16[64,1024]{1,0:T(8,128)(2,1)S(1)} %get-tuple-element.11), channel_id=1, source_target_pairs={{0,16},{1,17},{2,18},{3,19},{4,20},{5,21},{6,22},{7,23},{24,8},{25... | collective-permute-start | bytes 393224 | tf_op jit(solution)/shard_map/ppermute | solution.py:104
  82.1 1.9 %collective-permute-done.32 = bf16[64,1024]{1,0:T(8,128)(2,1)S(1)} collective-permute-done((bf16[64,1024]{1,0:T(8,128)(2,1)S(1)}, bf16[64,1024]{1,0:T(8,128)(2,1)S(1)}, u32[]{:S(2)}, u32[]{:S(2)}) %collective-permute-start.32) | collective-permute-done | bytes 131104 | tf_op jit(solution)/shard_map/ppermute | solution.py:104
  84.1 2.8 %collective-permute-start.33 = (bf16[64,1024]{1,0:T(8,128)(2,1)S(1)}, bf16[64,1024]{1,0:T(8,128)(2,1)S(1)}, u32[]{:S(2)}, u32[]{:S(2)}) collective-permute-start(bf16[64,1024]{1,0:T(8,128)(2,1)S(1)} %get-tuple-element.9), channel_id=1, source_target_pairs={{0,8},{1,9},{2,10},{3,11},{4,12},{5,13},{6,14},{7,15},{8,0},{9,1},... | collective-permute-start | bytes 393224 | tf_op jit(solution)/shard_map/ppermute | solution.py:104
  87.8 2.1 %collective-permute-done.33 = bf16[64,1024]{1,0:T(8,128)(2,1)S(1)} collective-permute-done((bf16[64,1024]{1,0:T(8,128)(2,1)S(1)}, bf16[64,1024]{1,0:T(8,128)(2,1)S(1)}, u32[]{:S(2)}, u32[]{:S(2)}) %collective-permute-start.33) | collective-permute-done | bytes 131104 | tf_op jit(solution)/shard_map/ppermute | solution.py:104
  95.9 3.7 %collective-permute-done.28 = bf16[256,256]{1,0:T(8,128)(2,1)S(1)} collective-permute-done((bf16[256,256]{1,0:T(8,128)(2,1)S(1)}, bf16[256,256]{1,0:T(8,128)(2,1)S(1)}, u32[]{:S(2)}, u32[]{:S(2)}) %collective-permute-start.28) | collective-permute-done | bytes 131104 | tf_op jit(solution)/shard_map/ppermute | solution.py:104
  99.6 2.2 %collective-permute-done.27 = bf16[256,256]{1,0:T(8,128)(2,1)S(1)} collective-permute-done((bf16[256,256]{1,0:T(8,128)(2,1)S(1)}, bf16[256,256]{1,0:T(8,128)(2,1)S(1)}, u32[]{:S(2)}, u32[]{:S(2)}) %collective-permute-start.27) | collective-permute-done | bytes 131104 | tf_op jit(solution)/shard_map/ppermute | solution.py:104
  106.8 5.7 %collective-permute-done.39 = bf16[512,256]{1,0:T(8,128)(2,1)S(1)} collective-permute-done((bf16[512,256]{1,0:T(8,128)(2,1)S(1)}, bf16[512,256]{1,0:T(8,128)(2,1)S(1)}, u32[]{:S(2)}, u32[]{:S(2)}) %collective-permute-start.39) | collective-permute-done | bytes 262176 | tf_op jit(solution)/shard_map/ppermute | solution.py:104
  113.9 5.8 %collective-permute-start.40 = (bf16[512,256]{1,0:T(8,128)(2,1)S(1)}, bf16[512,256]{1,0:T(8,128)(2,1)S(1)}, u32[]{:S(2)}, u32[]{:S(2)}) collective-permute-start(bf16[512,256]{1,0:T(8,128)(2,1)S(1)} %fusion.10), channel_id=1, source_target_pairs={{0,8},{1,9},{2,10},{3,11},{4,12},{5,13},{6,14},{7,15},{24,16},{25,... | collective-permute-start | bytes 786440 | tf_op jit(solution)/shard_map/ppermute | solution.py:104
  125.1 5.0 %collective-permute-start.44 = (bf16[512,256]{1,0:T(8,128)(2,1)S(1)}, bf16[512,256]{1,0:T(8,128)(2,1)S(1)}, u32[]{:S(2)}, u32[]{:S(2)}) collective-permute-start(bf16[512,256]{1,0:T(8,128)(2,1)S(1)} %get-tuple-element.13), channel_id=1, source_target_pairs={{0,16},{1,17},{2,18},{3,19},{4,20},{5,21},{6,22},{7,23},{24,8},{25... | collective-permute-start | bytes 786440 | tf_op jit(solution)/shard_map/ppermute | solution.py:104
  135.7 2.6 %collective-permute-start.45 = (bf16[512,256]{1,0:T(8,128)(2,1)S(1)}, bf16[512,256]{1,0:T(8,128)(2,1)S(1)}, u32[]{:S(2)}, u32[]{:S(2)}) collective-permute-start(bf16[512,256]{1,0:T(8,128)(2,1)S(1)} %fusion.11), channel_id=1, source_target_pairs={{0,8},{1,9},{2,10},{3,11},{4,12},{5,13},{6,14},{7,15},{8,0},{9,1},... | collective-permute-start | bytes 786440 | tf_op jit(solution)/shard_map/ppermute | solution.py:104
  139.3 2.5 %collective-permute-done.23 = f32[256]{0:T(256)S(1)} collective-permute-done((f32[256]{0:T(256)S(1)}, f32[256]{0:T(256)S(1)}, u32[]{:S(2)}, u32[]{:S(2)}) %collective-permute-start.23) | collective-permute-done | bytes 1056 | tf_op jit(solution)/shard_map/ppermute | solution.py:104
  143.6 2.2 %fusion.5 = f32[512,256]{1,0:T(8,128)} fusion(bf16[512,256]{1,0:T(8,128)(2,1)S(1)} %collective-permute-done.45, bf16[512,256]{1,0:T(8,128)(2,1)S(1)} %collective-permute-done.41, bf16[512,256]{1,0:T(8,128)(2,1)S(1)} %collective-permute-done.37, bf16[512,4096]{1,0:T(8,128)(2,1)} %constant_dynamic-update-slice_fusion, s32[]{:T(128)S(6)} %select_n.70, ...), kind=kOutput, calls=%fused_computation.11 | convolution fusion | flops 135528448 | bytes 2097156 | tf_op jit(solution)/shard_map/dot_general | solution.py:23
  (127 shorter events, 60.0 us)
Async XLA Ops:
  0.6 17.9 %collective-permute-start.5 = (bf16[512,256]{1,0:T(8,128)(2,1)}, bf16[512,256]{1,0:T(8,128)(2,1)S(1)}, u32[]{:S(2)}, u32[]{:S(2)}) collective-permute-start(bf16[512,256]{1,0:T(8,128)(2,1)} %param.6), channel_id=1, source_target_pairs={{8,16},{9,17},{10,18},{11,19},{12,20},{13,21},{14,22},{15,23},{16,... | collective-permute-start | bytes 786440 | tf_op jit(solution)/shard_map/ppermute | solution.py:104
  1.5 12.1 %collective-permute-start.2 = (bf16[512,256]{1,0:T(8,128)(2,1)}, bf16[512,256]{1,0:T(8,128)(2,1)S(1)}, u32[]{:S(2)}, u32[]{:S(2)}) collective-permute-start(bf16[512,256]{1,0:T(8,128)(2,1)} %param.6), channel_id=1, source_target_pairs={{0,8},{1,9},{2,10},{3,11},{4,12},{5,13},{6,14},{7,15},{8,0},{9,1},... | collective-permute-start | bytes 786440 | tf_op jit(solution)/shard_map/ppermute | solution.py:104
  7.4 12.5 %collective-permute-start.1 = (bf16[512,256]{1,0:T(8,128)(2,1)}, bf16[512,256]{1,0:T(8,128)(2,1)S(1)}, u32[]{:S(2)}, u32[]{:S(2)}) collective-permute-start(bf16[512,256]{1,0:T(8,128)(2,1)} %param.6), channel_id=1, source_target_pairs={{0,4},{1,5},{2,6},{3,7},{4,0},{5,1},{6,2},{7,3},{8,12},{9,13},{10,... | collective-permute-start | bytes 786440 | tf_op jit(solution)/shard_map/ppermute | solution.py:104
  13.6 12.0 %collective-permute-start.8 = (bf16[512,256]{1,0:T(8,128)(2,1)S(1)}, bf16[512,256]{1,0:T(8,128)(2,1)S(1)}, u32[]{:S(2)}, u32[]{:S(2)}) collective-permute-start(bf16[512,256]{1,0:T(8,128)(2,1)S(1)} %collective-permute-done.2), channel_id=1, source_target_pairs={{8,24},{9,25},{10,26},{11,27},{12,28},{13,29},{14,30},{15,31},{16,... | collective-permute-start | bytes 786440 | tf_op jit(solution)/shard_map/ppermute | solution.py:104
  16.3 12.3 %collective-permute-start.4 = (bf16[512,256]{1,0:T(8,128)(2,1)S(1)}, bf16[512,256]{1,0:T(8,128)(2,1)S(1)}, u32[]{:S(2)}, u32[]{:S(2)}) collective-permute-start(bf16[512,256]{1,0:T(8,128)(2,1)S(1)} %collective-permute-done.2), channel_id=1, source_target_pairs={{8,16},{9,17},{10,18},{11,19},{12,20},{13,21},{14,22},{15,23},{16,... | collective-permute-start | bytes 786440 | tf_op jit(solution)/shard_map/ppermute | solution.py:104
  17.0 22.1 %collective-permute-start.3 = (bf16[512,256]{1,0:T(8,128)(2,1)S(1)}, bf16[512,256]{1,0:T(8,128)(2,1)S(1)}, u32[]{:S(2)}, u32[]{:S(2)}) collective-permute-start(bf16[512,256]{1,0:T(8,128)(2,1)S(1)} %collective-permute-done.2), channel_id=1, source_target_pairs={{0,4},{1,5},{2,6},{3,7},{4,0},{5,1},{6,2},{7,3},{8,12},{9,13},{10,... | collective-permute-start | bytes 786440 | tf_op jit(solution)/shard_map/ppermute | solution.py:104
  18.6 11.9 %collective-permute-start.6 = (bf16[512,256]{1,0:T(8,128)(2,1)S(1)}, bf16[512,256]{1,0:T(8,128)(2,1)S(1)}, u32[]{:S(2)}, u32[]{:S(2)}) collective-permute-start(bf16[512,256]{1,0:T(8,128)(2,1)S(1)} %collective-permute-done.5), channel_id=1, source_target_pairs={{8,0},{9,1},{10,2},{11,3},{12,4},{13,5},{14,6},{15,7},{16,24},{17,... | collective-permute-start | bytes 786440 | tf_op jit(solution)/shard_map/ppermute | solution.py:104
  41.9 12.3 %collective-permute-start.12 = (bf16[256,256]{1,0:T(8,128)(2,1)S(1)}, bf16[256,256]{1,0:T(8,128)(2,1)S(1)}, u32[]{:S(2)}, u32[]{:S(2)}) collective-permute-start(bf16[256,256]{1,0:T(8,128)(2,1)S(1)} %get-tuple-element.22), channel_id=1, source_target_pairs={{0,6},{1,7},{2,4},{3,5},{4,2},{5,3},{6,0},{7,1},{8,14},{9,15},{10,... | collective-permute-start | bytes 393224 | tf_op jit(solution)/shard_map/ppermute | solution.py:104
  44.5 14.0 %collective-permute-start.11 = (bf16[256,256]{1,0:T(8,128)(2,1)S(1)}, bf16[256,256]{1,0:T(8,128)(2,1)S(1)}, u32[]{:S(2)}, u32[]{:S(2)}) collective-permute-start(bf16[256,256]{1,0:T(8,128)(2,1)S(1)} %get-tuple-element.22), channel_id=1, source_target_pairs={{0,4},{1,5},{2,6},{3,7},{4,0},{5,1},{6,2},{7,3},{8,12},{9,13},{10,... | collective-permute-start | bytes 393224 | tf_op jit(solution)/shard_map/ppermute | solution.py:104
  45.0 13.5 %collective-permute-start.10 = (bf16[256,256]{1,0:T(8,128)(2,1)S(1)}, bf16[256,256]{1,0:T(8,128)(2,1)S(1)}, u32[]{:S(2)}, u32[]{:S(2)}) collective-permute-start(bf16[256,256]{1,0:T(8,128)(2,1)S(1)} %get-tuple-element.22), channel_id=1, source_target_pairs={{0,2},{1,3},{2,0},{3,1},{4,6},{5,7},{6,4},{7,5},{8,10},{9,11},{10,... | collective-permute-start | bytes 393224 | tf_op jit(solution)/shard_map/ppermute | solution.py:104
  53.5 10.0 %collective-permute-start.19 = (bf16[64,1024]{1,0:T(8,128)(2,1)S(1)}, bf16[64,1024]{1,0:T(8,128)(2,1)S(1)}, u32[]{:S(2)}, u32[]{:S(2)}) collective-permute-start(bf16[64,1024]{1,0:T(8,128)(2,1)S(1)} %pad_maximum_fusion.6), channel_id=1, source_target_pairs={{8,16},{9,17},{10,18},{11,19},{12,20},{13,21},{14,22},{15,23},{16,... | collective-permute-start | bytes 393224 | tf_op jit(solution)/shard_map/ppermute | solution.py:104
  58.5 14.6 %collective-permute-start.13 = (bf16[512,512]{1,0:T(8,128)(2,1)S(1)}, bf16[512,512]{1,0:T(8,128)(2,1)S(1)}, u32[]{:S(2)}, u32[]{:S(2)}) collective-permute-start(bf16[512,512]{1,0:T(8,128)(2,1)S(1)} %maximum_maximum_fusion), channel_id=1, source_target_pairs={{0,1},{1,0},{2,3},{3,2},{4,5},{5,4},{6,7},{7,6},{8,9},{9,8},{10,11... | collective-permute-start | bytes 1572872 | tf_op jit(solution)/shard_map/ppermute | solution.py:104
  61.6 8.0 %collective-permute-start.21 = (bf16[64,1024]{1,0:T(8,128)(2,1)S(1)}, bf16[64,1024]{1,0:T(8,128)(2,1)S(1)}, u32[]{:S(2)}, u32[]{:S(2)}) collective-permute-start(bf16[64,1024]{1,0:T(8,128)(2,1)S(1)} %collective-permute-done.17), channel_id=1, source_target_pairs={{8,24},{9,25},{10,26},{11,27},{12,28},{13,29},{14,30},{15,31},{16,... | collective-permute-start | bytes 393224 | tf_op jit(solution)/shard_map/ppermute | solution.py:104
  63.6 9.6 %collective-permute-start.20 = (bf16[64,1024]{1,0:T(8,128)(2,1)S(1)}, bf16[64,1024]{1,0:T(8,128)(2,1)S(1)}, u32[]{:S(2)}, u32[]{:S(2)}) collective-permute-start(bf16[64,1024]{1,0:T(8,128)(2,1)S(1)} %collective-permute-done.19), channel_id=1, source_target_pairs={{8,0},{9,1},{10,2},{11,3},{12,4},{13,5},{14,6},{15,7},{16,24},{17,... | collective-permute-start | bytes 393224 | tf_op jit(solution)/shard_map/ppermute | solution.py:104
  103.2 9.2 %collective-permute-start.39 = (bf16[512,256]{1,0:T(8,128)(2,1)S(1)}, bf16[512,256]{1,0:T(8,128)(2,1)S(1)}, u32[]{:S(2)}, u32[]{:S(2)}) collective-permute-start(bf16[512,256]{1,0:T(8,128)(2,1)S(1)} %convolution_convert_fusion.1), channel_id=1, source_target_pairs={{0,4},{1,5},{2,6},{3,7},{4,0},{5,1},{6,2},{7,3},{8,12},{9,13},{10,... | collective-permute-start | bytes 786440 | tf_op jit(solution)/shard_map/ppermute | solution.py:104
  105.9 17.2 %collective-permute-start.38 = (bf16[512,256]{1,0:T(8,128)(2,1)S(1)}, bf16[512,256]{1,0:T(8,128)(2,1)S(1)}, u32[]{:S(2)}, u32[]{:S(2)}) collective-permute-start(bf16[512,256]{1,0:T(8,128)(2,1)S(1)} %convolution_convert_fusion.2), channel_id=1, source_target_pairs={{0,4},{1,5},{2,6},{3,7},{4,0},{5,1},{6,2},{7,3},{8,12},{9,13},{10,... | collective-permute-start | bytes 786440 | tf_op jit(solution)/shard_map/ppermute | solution.py:104
  113.9 9.8 %collective-permute-start.40 = (bf16[512,256]{1,0:T(8,128)(2,1)S(1)}, bf16[512,256]{1,0:T(8,128)(2,1)S(1)}, u32[]{:S(2)}, u32[]{:S(2)}) collective-permute-start(bf16[512,256]{1,0:T(8,128)(2,1)S(1)} %fusion.10), channel_id=1, source_target_pairs={{0,8},{1,9},{2,10},{3,11},{4,12},{5,13},{6,14},{7,15},{24,16},{25,... | collective-permute-start | bytes 786440 | tf_op jit(solution)/shard_map/ppermute | solution.py:104
  121.1 12.5 %collective-permute-start.42 = (bf16[512,256]{1,0:T(8,128)(2,1)S(1)}, bf16[512,256]{1,0:T(8,128)(2,1)S(1)}, u32[]{:S(2)}, u32[]{:S(2)}) collective-permute-start(bf16[512,256]{1,0:T(8,128)(2,1)S(1)} %convolution_convert_fusion), channel_id=1, source_target_pairs={{0,4},{1,5},{2,6},{3,7},{4,0},{5,1},{6,2},{7,3},{8,12},{9,13},{10,... | collective-permute-start | bytes 786440 | tf_op jit(solution)/shard_map/ppermute | solution.py:104
  122.4 11.9 %collective-permute-start.43 = (bf16[512,256]{1,0:T(8,128)(2,1)S(1)}, bf16[512,256]{1,0:T(8,128)(2,1)S(1)}, u32[]{:S(2)}, u32[]{:S(2)}) collective-permute-start(bf16[512,256]{1,0:T(8,128)(2,1)S(1)} %fusion.10), channel_id=1, source_target_pairs={{8,16},{9,17},{10,18},{11,19},{12,20},{13,21},{14,22},{15,23},{16,... | collective-permute-start | bytes 786440 | tf_op jit(solution)/shard_map/ppermute | solution.py:104
  125.1 9.2 %collective-permute-start.44 = (bf16[512,256]{1,0:T(8,128)(2,1)S(1)}, bf16[512,256]{1,0:T(8,128)(2,1)S(1)}, u32[]{:S(2)}, u32[]{:S(2)}) collective-permute-start(bf16[512,256]{1,0:T(8,128)(2,1)S(1)} %get-tuple-element.13), channel_id=1, source_target_pairs={{0,16},{1,17},{2,18},{3,19},{4,20},{5,21},{6,22},{7,23},{24,8},{25... | collective-permute-start | bytes 786440 | tf_op jit(solution)/shard_map/ppermute | solution.py:104
  130.1 8.2 %collective-permute-start.22 = (f32[256]{0:T(256)S(1)}, f32[256]{0:T(256)S(1)}, u32[]{:S(2)}, u32[]{:S(2)}) collective-permute-start(f32[256]{0:T(256)S(1)} %slice.82), channel_id=1, source_target_pairs={{0,4},{1,5},{2,6},{3,7},{4,0},{5,1},{6,2},{7,3},{8,12},{9,13},{10,... | collective-permute-start | bytes 3080 | tf_op jit(solution)/shard_map/ppermute | solution.py:104
  132.7 10.8 %collective-permute-start.37 = (bf16[512,256]{1,0:T(8,128)(2,1)S(1)}, bf16[512,256]{1,0:T(8,128)(2,1)S(1)}, u32[]{:S(2)}, u32[]{:S(2)}) collective-permute-start(bf16[512,256]{1,0:T(8,128)(2,1)S(1)} %convolution_convert_fusion.3), channel_id=1, source_target_pairs={{0,4},{1,5},{2,6},{3,7},{4,0},{5,1},{6,2},{7,3},{8,12},{9,13},{10,... | collective-permute-start | bytes 786440 | tf_op jit(solution)/shard_map/ppermute | solution.py:104
  133.6 10.0 %collective-permute-start.41 = (bf16[512,256]{1,0:T(8,128)(2,1)S(1)}, bf16[512,256]{1,0:T(8,128)(2,1)S(1)}, u32[]{:S(2)}, u32[]{:S(2)}) collective-permute-start(bf16[512,256]{1,0:T(8,128)(2,1)S(1)} %get-tuple-element.12), channel_id=1, source_target_pairs={{8,16},{9,17},{10,18},{11,19},{12,20},{13,21},{14,22},{15,23},{16,... | collective-permute-start | bytes 786440 | tf_op jit(solution)/shard_map/ppermute | solution.py:104
  135.7 7.9 %collective-permute-start.45 = (bf16[512,256]{1,0:T(8,128)(2,1)S(1)}, bf16[512,256]{1,0:T(8,128)(2,1)S(1)}, u32[]{:S(2)}, u32[]{:S(2)}) collective-permute-start(bf16[512,256]{1,0:T(8,128)(2,1)S(1)} %fusion.11), channel_id=1, source_target_pairs={{0,8},{1,9},{2,10},{3,11},{4,12},{5,13},{6,14},{7,15},{8,0},{9,1},... | collective-permute-start | bytes 786440 | tf_op jit(solution)/shard_map/ppermute | solution.py:104
  (25 other events, 171.9 us)

commit v3 on v2

--- a/solution.py
+++ b/solution.py
@@ -3,6 +3,8 @@
 import jax
 import jax.numpy as jnp
 from jax import lax
+from jax.experimental import pallas as pl
+from jax.experimental.pallas import tpu as pltpu
 from jax.sharding import PartitionSpec as P
 
 E = 1024
@@ -135,24 +137,81 @@
     return own + last + paired
 
 
+def project(prompts, responses, blocks, weights, total, kind):
+    row_count = prompts.shape[0]
+    depth, width = weights[0].shape
+    count = len(weights)
+
+    def kernel(block_ref, prompt_ref, response_ref, *refs):
+        weight_refs, total_ref, out_ref, sum_ref = refs[:count], refs[count], refs[-2], refs[-1]
+        step = pl.program_id(0)
+
+        @pl.when(step == 0)
+        def _():
+            sum_ref[...] = total_ref[...] if total is not None else jnp.zeros_like(sum_ref)
+
+        for k in range(count):
+
+            @pl.when(step == k)
+            def _(k=k):
+                sum_ref[:row_count] += matmul(prompt_ref[...], weight_refs[k][...])
+                sum_ref[row_count:] += matmul(response_ref[...], weight_refs[k][...])
+
+        @pl.when(step == count - 1)
+        def _():
+            out_ref[...] = sum_ref[...].astype(out_ref.dtype)
+
+    whole = pl.BlockSpec((2 * row_count, width), lambda i, block: (0, 0))
+    piece = pl.BlockSpec((row_count, depth), lambda i, block: (0, block[i]))
+    weight = pl.BlockSpec((depth, width), lambda i, block: (0, 0))
+    operands = [prompts, responses, *weights] + ([total] if total is not None else [])
+    return pl.pallas_call(
+        kernel,
+        grid_spec=pltpu.PrefetchScalarGridSpec(
+            num_scalar_prefetch=1,
+            grid=(count,),
+            in_specs=[piece, piece] + [weight] * count + [whole] * (total is not None),
+            out_specs=whole,
+            scratch_shapes=[pltpu.VMEM((2 * row_count, width), jnp.float32)],
+        ),
+        out_shape=jax.ShapeDtypeStruct((2 * row_count, width), kind),
+        compiler_params=pltpu.CompilerParams(vmem_limit_bytes=32 * 1024 * 1024),
+        cost_estimate=pl.CostEstimate(
+            flops=4 * count * row_count * depth * width,
+            bytes_accessed=4 * count * row_count * depth + 2 * count * depth * width,
+            transcendentals=0,
+        ),
+    )(jnp.stack(blocks).astype(jnp.int32), *operands)
+
+
 def full_window(prompts, responses, head_projection_matrix, positive):
     row_count = prompts.shape[0]
     depth, width = head_projection_matrix.shape
     factor = LOGIT_SCALE / math.sqrt(E)
     dp, mp = lax.axis_index("dp"), lax.axis_index("mp")
-    z, y = dp // PAIR, dp % PAIR
+    z, y, c = dp // PAIR, dp % PAIR, mp % CORES
     quarter = row_count // (SIDE * CORES)
-    both = jnp.concatenate([prompts, responses], axis=0)
-
-    def features(line, pair):
-        return lax.dynamic_slice_in_dim(both, (line * PAIR + pair) * depth, depth, axis=1)
-
-    first, second, third = line_gather(head_projection_matrix)
-    emb = jnp.zeros((2 * row_count, width), jnp.float32)
-    for k, block in enumerate((head_projection_matrix, first, second, third)):
-        emb = emb + matmul(features(z ^ k, y), block)
-        emb = emb + matmul(features(z ^ k, 1 - y), send(block, ACROSS_Y))
-    emb = emb.astype(jnp.bfloat16)
+
+    def features(array, line, pair):
+        return lax.dynamic_slice_in_dim(array, (line * PAIR + pair) * depth, depth, axis=1)
+
+    lines = [z ^ k for k in range(LINE)]
+    own = head_projection_matrix
+    own_y = send(own, ACROSS_Y)
+    first, second, third = line_gather(own)
+    first_y, second_y, third_y = [send(block, ACROSS_Y) for block in (first, second, third)]
+    here = [line * PAIR + y for line in lines]
+    there = [line * PAIR + 1 - y for line in lines]
+    emb = project(
+        prompts,
+        responses,
+        [here[0], there[0], here[1], there[1]],
+        [own, own_y, first, first_y],
+        None,
+        jnp.float32,
+    )
+    emb = project(prompts, responses, [here[2], here[3]], [second, third], emb, jnp.float32)
+    emb = project(prompts, responses, [there[2], there[3]], [second_y, third_y], emb, jnp.bfloat16)
     prompt_emb, response_emb = emb[:row_count], emb[row_count:]
 
     pieces = []
@@ -162,6 +221,7 @@
     response_rows = jnp.concatenate(pieces, axis=1)
     held = jnp.concatenate([response_rows, *line_gather(response_rows)], axis=0)
 
+    prompt_emb, response_rows = lax.optimization_barrier((prompt_emb, response_rows))
     near = jnp.concatenate([prompt_emb, send(prompt_emb, ACROSS_X)], axis=1)
     across = jnp.concatenate([send(prompt_emb, ACROSS_Y), send(prompt_emb, ACROSS_XY)], axis=1)
     half = jnp.concatenate([near, across], axis=0)
@@ -170,9 +230,22 @@
     plane = jnp.concatenate(plane, axis=1)
     wanted = jnp.concatenate([positive, send(positive, ACROSS_Y)], axis=0)
 
+    mine = jnp.where(c == 0, prompts, responses)
+    mine = jnp.concatenate([features(mine, line, 1 - y) for line in lines], axis=1)
+    mine, half = lax.optimization_barrier((mine, half))
+    fetched = send(mine, ACROSS_Y)
+    sibling = send(fetched, ACROSS_C)
+
+    def turned(array):
+        return [array[:, k * depth : (k + 1) * depth].T for k in range(LINE)]
+
+    arrays = [[features(array, line, y).T for line in lines] for array in (prompts, responses)]
+    arrays = arrays + [turned(fetched), turned(sibling)]
+    columns = [jnp.concatenate([array[k] for array in arrays], axis=1) for k in range(LINE)]
+    columns = lax.optimization_barrier(columns)
+
     pair_scores = cross_cols(plane, held) * factor + LOGIT_BIAS
-    lines = jnp.stack([z ^ k for k in range(LINE)])
-    column_ids = ((lines * PAIR + y) * row_count + mp * quarter)[:, None] + lax.iota(
+    column_ids = ((jnp.stack(lines) * PAIR + y) * row_count + mp * quarter)[:, None] + lax.iota(
         jnp.int32, quarter
     )[None, :]
     column_ids = column_ids.reshape(-1)
@@ -191,30 +264,33 @@
         grad_response = lax.dynamic_update_slice_in_dim(
             grad_response, piece, (mp ^ k) * quarter, axis=0
         )
+    grad_response_y = send(grad_response, ACROSS_Y)
 
     parts = matmul(weight, held)
     mine = jnp.concatenate([parts[:, :width], parts[:, 2 * width : 3 * width]], axis=1)
     away = jnp.concatenate([parts[:, width : 2 * width], parts[:, 3 * width :]], axis=1)
     mine = mine + send(away.astype(jnp.bfloat16), ACROSS_C).astype(jnp.float32)
-    away = mine.astype(jnp.bfloat16)
-    grad_prompt = (
-        mine[:row_count, :width]
-        + send(away[:row_count, width:], ACROSS_X).astype(jnp.float32)
-        + send(away[row_count:, :width], ACROSS_Y).astype(jnp.float32)
-        + send(away[row_count:, width:], ACROSS_XY).astype(jnp.float32)
-    )
-    grads = jnp.concatenate([grad_prompt.astype(jnp.bfloat16), grad_response], axis=0)
-
-    def head(line):
-        away = cross_rows(features(line, 1 - y), grads).astype(jnp.bfloat16)
-        return cross_rows(features(line, y), grads) + send(away, ACROSS_Y).astype(jnp.float32)
-
-    third, second, first, own = [head(z ^ k) for k in (3, 2, 1, 0)]
-    head_grad = line_reduce(own, first, second, third)
+    mine = mine[:, :width] + send(mine[:, width:].astype(jnp.bfloat16), ACROSS_X).astype(
+        jnp.float32
+    )
+    mine_y = send(mine.astype(jnp.bfloat16), ACROSS_Y).astype(jnp.float32)
+    grad_prompt = (mine[:row_count] + mine_y[row_count:]).astype(jnp.bfloat16)
+    grad_prompt_y = (mine[row_count:] + mine_y[:row_count]).astype(jnp.bfloat16)
 
     losses = losses[:row_count] + send(losses[row_count:], ACROSS_Y)
     losses = losses + send(losses, ACROSS_X)
     losses = losses + send(losses, ACROSS_C)
+    losses, grad_response_y = lax.optimization_barrier((losses, grad_response_y))
+
+    grads = [
+        grad_prompt,
+        grad_response,
+        jnp.where(c == 0, grad_prompt_y, grad_response_y),
+        jnp.where(c == 0, grad_response_y, grad_prompt_y),
+    ]
+    grads = jnp.concatenate(grads, axis=0)
+    third, second, first, own = [matmul(columns[k], grads) for k in (3, 2, 1, 0)]
+    head_grad = line_reduce(own, first, second, third)
     return (losses / row_count, head_grad)
 
 

time: 147 us -> 148 us (level)
  waiting for transfers between devices: 45.9 us -> 69 us
  matrix products: 24.6 us -> 5.65 us
  starting transfers between devices: 67.5 us -> 55.3 us
  other arithmetic: 1.37 us -> 9.36 us
  Pallas kernels: 0 us -> 4.68 us
  local copies, waits for them, and re-layouts: 5.13 us -> 2.58 us
    ppermute x46 -> x44, waiting for transfers between devices: 45.9 us -> 69 us  [send(): return lax.ppermute(block, ('dp', 'mp'), table)]
    ppermute x46 -> x44, starting transfers between devices: 67.5 us -> 55.3 us  [send(): return lax.ppermute(block, ('dp', 'mp'), table)]
    dot_general x9 -> x1, matrix products: 12.5 us -> 0.54 us  [cross_rows(): lax.dot_general(left_side, righthand_term, (((0,), (0,)), ((), ())), pref...]
    dot_general x9 -> x5, matrix products: 11.3 us -> 3.4 us  [matmul(): jnp.dot(left_side, righthand_term, preferred_element_type=jnp.float32)]
    pallas_call x0 -> x3, Pallas kernels: none -> 4.68 us  [project(): pl.pallas_call(kernel, grid_spec=pltpu.PrefetchScalarGridSpec(num_scalar_...]
    select_n x0 -> x3, other arithmetic: none -> 3.39 us  [the longest x1 3.3 us: full_window(): mine = jnp.where(c == 0, prompts, responses)]
    unnamed x7 -> x12, local copies, waits for them, and re-layouts: 3.17 us -> 1.61 us
    concatenate x1 -> x0, local copies, waits for them, and re-layouts: 1.51 us -> none  [full_window(): both = jnp.concatenate([prompts, responses], axis=0)]
  transfers between devices with their start and end apart: 46 -> 44, of which waited for: 15 -> 20; matrix products, arithmetic and copies ran while one was open for 16% -> 10% of each run, Pallas kernels for 0% -> 3%
where the time goes in v3:
time: 148 us
  waiting for transfers between devices  69 us (47%)
  starting transfers between devices  55.3 us (37%)
  other arithmetic  9.36 us (6%)
  matrix products  5.65 us (4%)
  Pallas kernels  4.68 us (3%)
  local copies, waits for them, and re-layouts  2.58 us (2%)
    ppermute x44, waiting for transfers between devices, send(): return lax.ppermute(block, ('dp', 'mp'), table)  69 us
    ppermute x44, starting transfers between devices, send(): return lax.ppermute(block, ('dp', 'mp'), table)  55.3 us
    pallas_call x3, Pallas kernels, project(): pl.pallas_call(kernel, grid_spec=pltpu.PrefetchScalarGridSpec(num_scalar_...  4.68 us
    dot_general x5, matrix products, matmul(): jnp.dot(left_side, righthand_term, preferred_element_type=jnp.float32)  3.4 us
    select_n x1, other arithmetic, full_window(): mine = jnp.where(c == 0, prompts, responses)  3.3 us
  transfers between devices with their start and end apart: 44, of which 20 were waited for; matrix products, arithmetic and copies ran while one was open for 10% of the time, Pallas kernels for 3%

profile of v3, /device:TPU:0, one launch (start us, length us, event | category | flops | bytes accessed | tf_op | source)
XLA Modules:
  0.0 147.9 jit_solution(15312955846024412583)
XLA Ops:
  0.6 3.1 %collective-permute-start.1 = (bf16[512,256]{1,0:T(8,128)(2,1)}, bf16[512,256]{1,0:T(8,128)(2,1)S(1)}, u32[]{:S(2)}, u32[]{:S(2)}) collective-permute-start(bf16[512,256]{1,0:T(8,128)(2,1)} %refs_0_.1), channel_id=1, source_target_pairs={{0,8},{1,9},{2,10},{3,11},{4,12},{5,13},{6,14},{7,15},{8,0},{9,1},... | collective-permute-start | bytes 786440 | tf_op jit(solution)/shard_map/ppermute | solution.py:106
  6.0 4.3 %collective-permute-done.1.refs_2_ = bf16[512,256]{1,0:T(8,128)(2,1)S(1)} collective-permute-done((bf16[512,256]{1,0:T(8,128)(2,1)}, bf16[512,256]{1,0:T(8,128)(2,1)S(1)}, u32[]{:S(2)}, u32[]{:S(2)}) %collective-permute-start.1) | collective-permute-done | bytes 262176 | tf_op jit(solution)/shard_map/ppermute | solution.py:106
  15.9 3.3 %broadcast_select_fusion = bf16[256,4096]{1,0:T(8,128)(2,1)} fusion(bf16[256,4096]{1,0:T(8,128)(2,1)} %prompt_ref.5, bf16[256,4096]{1,0:T(8,128)(2,1)} %response_ref.5, pred[]{:T(512)S(6)} %eq.24), kind=kLoop, calls=%fused_computation | loop fusion | flops 1048576 | bytes 6291457 | tf_op jit(solution)/shard_map/jit(_where)/select_n | solution.py:233
  19.6 11.8 %collective-permute-done.4 = bf16[512,256]{1,0:T(8,128)(2,1)} collective-permute-done((bf16[512,256]{1,0:T(8,128)(2,1)S(1)}, bf16[512,256]{1,0:T(8,128)(2,1)}, u32[]{:S(2)}, u32[]{:S(2)}) %collective-permute-start.4) | collective-permute-done | bytes 262176 | tf_op jit(solution)/shard_map/ppermute | solution.py:106
  37.4 2.1 %shard_map.59.refs_2_ = f32[512,256]{1,0:T(8,128)S(1)} custom-call(s32[4]{0:T(128)S(1)} %pad_add_fusion.3.block_ref, bf16[256,4096]{1,0:T(8,128)(2,1)S(1)} %copy-done, bf16[256,4096]{1,0:T(8,128)(2,1)S(1)} %copy-done.1, bf16[512,256]{1,0:T(8,128)(2,1)S(1)} %copy-done.3, bf16[512,256]{1,0:T(8,128)(2,1)S(1)} %collective-permute-done.8.refs_1_, ...), custom_call_target="tpu_custom_call" | custom-call | flops 536870912 | bytes 3145728 | tf_op jit(solution)/shard_map/pallas_call | solution.py:168
  41.7 3.5 %collective-permute-done.7.refs_1_ = bf16[512,256]{1,0:T(8,128)(2,1)S(1)} collective-permute-done((bf16[512,256]{1,0:T(8,128)(2,1)S(1)}, bf16[512,256]{1,0:T(8,128)(2,1)S(1)}, u32[]{:S(2)}, u32[]{:S(2)}) %collective-permute-start.7) | collective-permute-done | bytes 262176 | tf_op jit(solution)/shard_map/ppermute | solution.py:106
  48.6 2.0 %collective-permute-done.11 = bf16[64,256]{1,0:T(8,128)(2,1)S(1)} collective-permute-done((bf16[64,256]{1,0:T(8,128)(2,1)S(1)}, bf16[64,256]{1,0:T(8,128)(2,1)S(1)}, u32[]{:S(2)}, u32[]{:S(2)}) %collective-permute-start.11) | collective-permute-done | bytes 32800 | tf_op jit(solution)/shard_map/ppermute | solution.py:106
  53.0 2.1 %collective-permute-start.15 = (bf16[256,256]{1,0:T(8,128)(2,1)S(1)}, bf16[256,256]{1,0:T(8,128)(2,1)S(1)}, u32[]{:S(2)}, u32[]{:S(2)}) collective-permute-start(bf16[256,256]{1,0:T(8,128)(2,1)S(1)} %get-tuple-element.10), channel_id=1, source_target_pairs={{0,6},{1,7},{2,4},{3,5},{4,2},{5,3},{6,0},{7,1},{8,14},{9,15},{10,... | collective-permute-start | bytes 393224 | tf_op jit(solution)/shard_map/ppermute | solution.py:106
  58.6 2.0 %collective-permute-done.14 = bf16[256,256]{1,0:T(8,128)(2,1)S(1)} collective-permute-done((bf16[256,256]{1,0:T(8,128)(2,1)S(1)}, bf16[256,256]{1,0:T(8,128)(2,1)S(1)}, u32[]{:S(2)}, u32[]{:S(2)}) %collective-permute-start.14) | collective-permute-done | bytes 131104 | tf_op jit(solution)/shard_map/ppermute | solution.py:106
  65.2 6.4 %collective-permute-done.21 = bf16[64,1024]{1,0:T(8,128)(2,1)S(1)} collective-permute-done((bf16[64,1024]{1,0:T(8,128)(2,1)}, bf16[64,1024]{1,0:T(8,128)(2,1)S(1)}, u32[]{:S(2)}, u32[]{:S(2)}) %collective-permute-start.21) | collective-permute-done | bytes 131104 | tf_op jit(solution)/shard_map/ppermute | solution.py:106
  71.6 2.5 %collective-permute-done.20 = bf16[64,1024]{1,0:T(8,128)(2,1)S(1)} collective-permute-done((bf16[64,1024]{1,0:T(8,128)(2,1)S(1)}, bf16[64,1024]{1,0:T(8,128)(2,1)S(1)}, u32[]{:S(2)}, u32[]{:S(2)}) %collective-permute-start.20) | collective-permute-done | bytes 131104 | tf_op jit(solution)/shard_map/ppermute | solution.py:106
  74.2 1.7 %fusion.2 = (f32[512]{0:T(512)S(1)}, f32[512,256]{0,1:T(8,128)S(1)}) fusion(bf16[64,1024]{1,0:T(8,128)(2,1)S(1)} %add.236, bf16[64,1024]{1,0:T(8,128)(2,1)S(1)} %add.235, bf16[64,1024]{1,0:T(8,128)(2,1)} %collective-permute-done.17, bf16[64,256]{1,0:T(8,128)(2,1)S(1)} %collective-permute-done.12, bf16[64,256]{1,0:T(8,128)(2,1)S(1)} %collective-permute-done.11, ...), kind=kOutput, calls=%fused_computation.13 | convolution fusion | flops 278003200 | bytes 2102272 | tf_op jit(solution)/shard_map/dot_general | solution.py:31
  81.7 5.1 %collective-permute-done.22 = f32[256]{0:T(256)S(1)} collective-permute-done((f32[256]{0:T(256)S(1)}, f32[256]{0:T(256)S(1)}, u32[]{:S(2)}, u32[]{:S(2)}) %collective-permute-start.22) | collective-permute-done | bytes 1056 | tf_op jit(solution)/shard_map/ppermute | solution.py:106
  86.8 3.0 %collective-permute-start.28 = (bf16[64,1024]{1,0:T(8,128)(2,1)S(1)}, bf16[64,1024]{1,0:T(8,128)(2,1)S(1)}, u32[]{:S(2)}, u32[]{:S(2)}) collective-permute-start(bf16[64,1024]{1,0:T(8,128)(2,1)S(1)} %get-tuple-element.49), channel_id=1, source_target_pairs={{0,16},{1,17},{2,18},{3,19},{4,20},{5,21},{6,22},{7,23},{24,8},{25... | collective-permute-start | bytes 393224 | tf_op jit(solution)/shard_map/ppermute | solution.py:106
  93.2 5.2 %collective-permute-start.29 = (bf16[64,1024]{1,0:T(8,128)(2,1)S(1)}, bf16[64,1024]{1,0:T(8,128)(2,1)S(1)}, u32[]{:S(2)}, u32[]{:S(2)}) collective-permute-start(bf16[64,1024]{1,0:T(8,128)(2,1)S(1)} %get-tuple-element.47), channel_id=1, source_target_pairs={{0,8},{1,9},{2,10},{3,11},{4,12},{5,13},{6,14},{7,15},{8,0},{9,1},... | collective-permute-start | bytes 393224 | tf_op jit(solution)/shard_map/ppermute | solution.py:106
  98.7 2.7 %collective-permute-done.29 = bf16[64,1024]{1,0:T(8,128)(2,1)S(1)} collective-permute-done((bf16[64,1024]{1,0:T(8,128)(2,1)S(1)}, bf16[64,1024]{1,0:T(8,128)(2,1)S(1)}, u32[]{:S(2)}, u32[]{:S(2)}) %collective-permute-start.29) | collective-permute-done | bytes 131104 | tf_op jit(solution)/shard_map/ppermute | solution.py:106
  106.4 5.8 %collective-permute-done.37 = bf16[512,256]{1,0:T(8,128)(2,1)S(1)} collective-permute-done((bf16[512,256]{1,0:T(8,128)(2,1)S(1)}, bf16[512,256]{1,0:T(8,128)(2,1)S(1)}, u32[]{:S(2)}, u32[]{:S(2)}) %collective-permute-start.37) | collective-permute-done | bytes 262176 | tf_op jit(solution)/shard_map/ppermute | solution.py:106
  113.3 6.9 %collective-permute-done.38 = bf16[512,256]{1,0:T(8,128)(2,1)S(1)} collective-permute-done((bf16[512,256]{1,0:T(8,128)(2,1)S(1)}, bf16[512,256]{1,0:T(8,128)(2,1)S(1)}, u32[]{:S(2)}, u32[]{:S(2)}) %collective-permute-start.38) | collective-permute-done | bytes 262176 | tf_op jit(solution)/shard_map/ppermute | solution.py:106
  121.3 3.9 %collective-permute-start.39 = (bf16[512,256]{1,0:T(8,128)(2,1)S(1)}, bf16[512,256]{1,0:T(8,128)(2,1)S(1)}, u32[]{:S(2)}, u32[]{:S(2)}) collective-permute-start(bf16[512,256]{1,0:T(8,128)(2,1)S(1)} %convolution_convert_fusion), channel_id=1, source_target_pairs={{0,8},{1,9},{2,10},{3,11},{4,12},{5,13},{6,14},{7,15},{24,16},{25,... | collective-permute-start | bytes 786440 | tf_op jit(solution)/shard_map/ppermute | solution.py:106
  126.5 3.1 %collective-permute-done.39 = bf16[512,256]{1,0:T(8,128)(2,1)S(1)} collective-permute-done((bf16[512,256]{1,0:T(8,128)(2,1)S(1)}, bf16[512,256]{1,0:T(8,128)(2,1)S(1)}, u32[]{:S(2)}, u32[]{:S(2)}) %collective-permute-start.39) | collective-permute-done | bytes 262176 | tf_op jit(solution)/shard_map/ppermute | solution.py:106
  130.0 4.1 %collective-permute-start.42 = (bf16[512,256]{1,0:T(8,128)(2,1)S(1)}, bf16[512,256]{1,0:T(8,128)(2,1)S(1)}, u32[]{:S(2)}, u32[]{:S(2)}) collective-permute-start(bf16[512,256]{1,0:T(8,128)(2,1)S(1)} %get-tuple-element.51), channel_id=1, source_target_pairs={{0,16},{1,17},{2,18},{3,19},{4,20},{5,21},{6,22},{7,23},{24,8},{25... | collective-permute-start | bytes 786440 | tf_op jit(solution)/shard_map/ppermute | solution.py:106
  135.3 2.7 %collective-permute-done.42 = bf16[512,256]{1,0:T(8,128)(2,1)S(1)} collective-permute-done((bf16[512,256]{1,0:T(8,128)(2,1)S(1)}, bf16[512,256]{1,0:T(8,128)(2,1)S(1)}, u32[]{:S(2)}, u32[]{:S(2)}) %collective-permute-start.42) | collective-permute-done | bytes 262176 | tf_op jit(solution)/shard_map/ppermute | solution.py:106
  138.1 4.5 %collective-permute-start.43 = (bf16[512,256]{1,0:T(8,128)(2,1)S(1)}, bf16[512,256]{1,0:T(8,128)(2,1)S(1)}, u32[]{:S(2)}, u32[]{:S(2)}) collective-permute-start(bf16[512,256]{1,0:T(8,128)(2,1)S(1)} %add_convert_fusion), channel_id=1, source_target_pairs={{0,8},{1,9},{2,10},{3,11},{4,12},{5,13},{6,14},{7,15},{8,0},{9,1},... | collective-permute-start | bytes 786440 | tf_op jit(solution)/shard_map/ppermute | solution.py:106
  143.1 3.9 %collective-permute-done.43 = bf16[512,256]{1,0:T(8,128)(2,1)S(1)} collective-permute-done((bf16[512,256]{1,0:T(8,128)(2,1)S(1)}, bf16[512,256]{1,0:T(8,128)(2,1)S(1)}, u32[]{:S(2)}, u32[]{:S(2)}) %collective-permute-start.43) | collective-permute-done | bytes 262176 | tf_op jit(solution)/shard_map/ppermute | solution.py:106
  (137 shorter events, 50.9 us)
Async XLA Ops:
  0.6 9.6 %collective-permute-start.1 = (bf16[512,256]{1,0:T(8,128)(2,1)}, bf16[512,256]{1,0:T(8,128)(2,1)S(1)}, u32[]{:S(2)}, u32[]{:S(2)}) collective-permute-start(bf16[512,256]{1,0:T(8,128)(2,1)} %refs_0_.1), channel_id=1, source_target_pairs={{0,8},{1,9},{2,10},{3,11},{4,12},{5,13},{6,14},{7,15},{8,0},{9,1},... | collective-permute-start | bytes 786440 | tf_op jit(solution)/shard_map/ppermute | solution.py:106
  3.7 10.9 %collective-permute-start.3 = (bf16[512,256]{1,0:T(8,128)(2,1)}, bf16[512,256]{1,0:T(8,128)(2,1)S(1)}, u32[]{:S(2)}, u32[]{:S(2)}) collective-permute-start(bf16[512,256]{1,0:T(8,128)(2,1)} %refs_0_.1), channel_id=1, source_target_pairs={{8,16},{9,17},{10,18},{11,19},{12,20},{13,21},{14,22},{15,23},{16,... | collective-permute-start | bytes 786440 | tf_op jit(solution)/shard_map/ppermute | solution.py:106
  4.4 31.3 %collective-permute-start.8 = (bf16[512,256]{1,0:T(8,128)(2,1)}, bf16[512,256]{1,0:T(8,128)(2,1)S(1)}, u32[]{:S(2)}, u32[]{:S(2)}) collective-permute-start(bf16[512,256]{1,0:T(8,128)(2,1)} %refs_0_.1), channel_id=1, source_target_pairs={{0,4},{1,5},{2,6},{3,7},{4,0},{5,1},{6,2},{7,3},{8,12},{9,13},{10,... | collective-permute-start | bytes 786440 | tf_op jit(solution)/shard_map/ppermute | solution.py:106
  10.2 25.5 %collective-permute-start.9 = (bf16[512,256]{1,0:T(8,128)(2,1)S(1)}, bf16[512,256]{1,0:T(8,128)(2,1)S(1)}, u32[]{:S(2)}, u32[]{:S(2)}) collective-permute-start(bf16[512,256]{1,0:T(8,128)(2,1)S(1)} %collective-permute-done.1.refs_2_), channel_id=1, source_target_pairs={{0,4},{1,5},{2,6},{3,7},{4,0},{5,1},{6,2},{7,3},{8,12},{9,13},{10,... | collective-permute-start | bytes 786440 | tf_op jit(solution)/shard_map/ppermute | solution.py:106
  13.3 19.7 %collective-permute-start.6 = (bf16[512,256]{1,0:T(8,128)(2,1)S(1)}, bf16[512,256]{1,0:T(8,128)(2,1)}, u32[]{:S(2)}, u32[]{:S(2)}) collective-permute-start(bf16[512,256]{1,0:T(8,128)(2,1)S(1)} %collective-permute-done.1.refs_2_), channel_id=1, source_target_pairs={{8,24},{9,25},{10,26},{11,27},{12,28},{13,29},{14,30},{15,31},{16,... | collective-permute-start | bytes 786440 | tf_op jit(solution)/shard_map/ppermute | solution.py:106
  14.6 16.7 %collective-permute-start.4 = (bf16[512,256]{1,0:T(8,128)(2,1)S(1)}, bf16[512,256]{1,0:T(8,128)(2,1)}, u32[]{:S(2)}, u32[]{:S(2)}) collective-permute-start(bf16[512,256]{1,0:T(8,128)(2,1)S(1)} %collective-permute-done.3), channel_id=1, source_target_pairs={{8,0},{9,1},{10,2},{11,3},{12,4},{13,5},{14,6},{15,7},{16,24},{17,... | collective-permute-start | bytes 786440 | tf_op jit(solution)/shard_map/ppermute | solution.py:106
  19.2 41.7 %collective-permute-start = (s32[256]{0:T(256)S(1)}, s32[256]{0:T(256)S(1)}, u32[]{:S(2)}, u32[]{:S(2)}) collective-permute-start(s32[256]{0:T(256)S(1)} %copy-done.5), channel_id=1, source_target_pairs={{0,4},{1,5},{2,6},{3,7},{4,0},{5,1},{6,2},{7,3},{8,12},{9,13},{10,... | collective-permute-start | bytes 3080 | tf_op jit(solution)/shard_map/ppermute | solution.py:106
  32.4 9.3 %collective-permute-start.5 = (bf16[512,256]{1,0:T(8,128)(2,1)S(1)}, bf16[512,256]{1,0:T(8,128)(2,1)S(1)}, u32[]{:S(2)}, u32[]{:S(2)}) collective-permute-start(bf16[512,256]{1,0:T(8,128)(2,1)S(1)} %add.223.refs_0_), channel_id=1, source_target_pairs={{0,4},{1,5},{2,6},{3,7},{4,0},{5,1},{6,2},{7,3},{8,12},{9,13},{10,... | collective-permute-start | bytes 786440 | tf_op jit(solution)/shard_map/ppermute | solution.py:106
  34.0 11.2 %collective-permute-start.7 = (bf16[512,256]{1,0:T(8,128)(2,1)S(1)}, bf16[512,256]{1,0:T(8,128)(2,1)S(1)}, u32[]{:S(2)}, u32[]{:S(2)}) collective-permute-start(bf16[512,256]{1,0:T(8,128)(2,1)S(1)} %add.224.refs_1_), channel_id=1, source_target_pairs={{0,4},{1,5},{2,6},{3,7},{4,0},{5,1},{6,2},{7,3},{8,12},{9,13},{10,... | collective-permute-start | bytes 786440 | tf_op jit(solution)/shard_map/ppermute | solution.py:106
  60.7 13.4 %collective-permute-start.16 = (bf16[512,512]{1,0:T(8,128)(2,1)S(1)}, bf16[512,512]{1,0:T(8,128)(2,1)S(1)}, u32[]{:S(2)}, u32[]{:S(2)}) collective-permute-start(bf16[512,512]{1,0:T(8,128)(2,1)S(1)} %maximum_maximum_fusion), channel_id=1, source_target_pairs={{0,1},{1,0},{2,3},{3,2},{4,5},{5,4},{6,7},{7,6},{8,9},{9,8},{10,11... | collective-permute-start | bytes 1572872 | tf_op jit(solution)/shard_map/ppermute | solution.py:106
  60.9 45.5 %collective-permute-start.34 = (bf16[256,2048]{1,0:T(8,128)(2,1)}, bf16[256,2048]{1,0:T(8,128)(2,1)S(1)}, u32[]{:S(2)}, u32[]{:S(2)}) collective-permute-start(bf16[256,2048]{1,0:T(8,128)(2,1)} %pad_maximum_fusion.1), channel_id=1, source_target_pairs={{0,4},{1,5},{2,6},{3,7},{4,0},{5,1},{6,2},{7,3},{8,12},{9,13},{10,... | collective-permute-start | bytes 3145736 | tf_op jit(solution)/shard_map/ppermute | solution.py:106
  61.8 9.7 %collective-permute-start.18 = (bf16[64,1024]{1,0:T(8,128)(2,1)}, bf16[64,1024]{1,0:T(8,128)(2,1)S(1)}, u32[]{:S(2)}, u32[]{:S(2)}) collective-permute-start(bf16[64,1024]{1,0:T(8,128)(2,1)} %collective-permute-done.17), channel_id=1, source_target_pairs={{8,16},{9,17},{10,18},{11,19},{12,20},{13,21},{14,22},{15,23},{16,... | collective-permute-start | bytes 393224 | tf_op jit(solution)/shard_map/ppermute | solution.py:106
  62.5 9.0 %collective-permute-start.21 = (bf16[64,1024]{1,0:T(8,128)(2,1)}, bf16[64,1024]{1,0:T(8,128)(2,1)S(1)}, u32[]{:S(2)}, u32[]{:S(2)}) collective-permute-start(bf16[64,1024]{1,0:T(8,128)(2,1)} %collective-permute-done.17), channel_id=1, source_target_pairs={{8,24},{9,25},{10,26},{11,27},{12,28},{13,29},{14,30},{15,31},{16,... | collective-permute-start | bytes 393224 | tf_op jit(solution)/shard_map/ppermute | solution.py:106
  63.8 10.3 %collective-permute-start.20 = (bf16[64,1024]{1,0:T(8,128)(2,1)S(1)}, bf16[64,1024]{1,0:T(8,128)(2,1)S(1)}, u32[]{:S(2)}, u32[]{:S(2)}) collective-permute-start(bf16[64,1024]{1,0:T(8,128)(2,1)S(1)} %collective-permute-done.19), channel_id=1, source_target_pairs={{8,0},{9,1},{10,2},{11,3},{12,4},{13,5},{14,6},{15,7},{16,24},{17,... | collective-permute-start | bytes 393224 | tf_op jit(solution)/shard_map/ppermute | solution.py:106
  76.5 13.4 %collective-permute-start.25 = (bf16[64,1024]{1,0:T(8,128)(2,1)S(1)}, bf16[64,1024]{1,0:T(8,128)(2,1)S(1)}, u32[]{:S(2)}, u32[]{:S(2)}) collective-permute-start(bf16[64,1024]{1,0:T(8,128)(2,1)S(1)} %get-tuple-element.48), channel_id=1, source_target_pairs={{0,8},{1,9},{2,10},{3,11},{4,12},{5,13},{6,14},{7,15},{24,16},{25,... | collective-permute-start | bytes 393224 | tf_op jit(solution)/shard_map/ppermute | solution.py:106
  77.9 12.9 %collective-permute-start.27 = (bf16[64,1024]{1,0:T(8,128)(2,1)S(1)}, bf16[64,1024]{1,0:T(8,128)(2,1)S(1)}, u32[]{:S(2)}, u32[]{:S(2)}) collective-permute-start(bf16[64,1024]{1,0:T(8,128)(2,1)S(1)} %get-tuple-element.48), channel_id=1, source_target_pairs={{8,16},{9,17},{10,18},{11,19},{12,20},{13,21},{14,22},{15,23},{16,... | collective-permute-start | bytes 393224 | tf_op jit(solution)/shard_map/ppermute | solution.py:106
  81.6 20.9 %collective-permute-start.36 = (bf16[512,512]{1,0:T(8,128)(2,1)S(1)}, bf16[512,512]{1,0:T(8,128)(2,1)S(1)}, u32[]{:S(2)}, u32[]{:S(2)}) collective-permute-start(bf16[512,512]{1,0:T(8,128)(2,1)S(1)} %pad_maximum_fusion.7), channel_id=1, source_target_pairs={{0,1},{1,0},{2,3},{3,2},{4,5},{5,4},{6,7},{7,6},{8,9},{9,8},{10,11... | collective-permute-start | bytes 1572872 | tf_op jit(solution)/shard_map/ppermute | solution.py:106
  89.9 8.7 %collective-permute-start.23 = (f32[256]{0:T(256)S(1)}, f32[256]{0:T(256)S(1)}, u32[]{:S(2)}, u32[]{:S(2)}) collective-permute-start(f32[256]{0:T(256)S(1)} %slice_add_fusion.5), channel_id=1, source_target_pairs={{0,2},{1,3},{2,0},{3,1},{4,6},{5,7},{6,4},{7,5},{8,10},{9,11},{10,... | collective-permute-start | bytes 3080 | tf_op jit(solution)/shard_map/ppermute | solution.py:106
  98.6 14.6 %collective-permute-start.24 = (f32[256]{0:T(256)S(1)}, f32[256]{0:T(256)S(1)}, u32[]{:S(2)}, u32[]{:S(2)}) collective-permute-start(f32[256]{0:T(256)S(1)} %add.241), channel_id=1, source_target_pairs={{0,1},{1,0},{2,3},{3,2},{4,5},{5,4},{6,7},{7,6},{8,9},{9,8},{10,11... | collective-permute-start | bytes 3080 | tf_op jit(solution)/shard_map/ppermute | solution.py:106
  103.6 8.6 %collective-permute-start.37 = (bf16[512,256]{1,0:T(8,128)(2,1)S(1)}, bf16[512,256]{1,0:T(8,128)(2,1)S(1)}, u32[]{:S(2)}, u32[]{:S(2)}) collective-permute-start(bf16[512,256]{1,0:T(8,128)(2,1)S(1)} %slice.205), channel_id=1, source_target_pairs={{0,2},{1,3},{2,0},{3,1},{4,6},{5,7},{6,4},{7,5},{8,10},{9,11},{10,... | collective-permute-start | bytes 786440 | tf_op jit(solution)/shard_map/ppermute | solution.py:106
  106.4 13.9 %collective-permute-start.35 = (bf16[256,2048]{1,0:T(8,128)(2,1)S(1)}, bf16[256,2048]{1,0:T(8,128)(2,1)S(1)}, u32[]{:S(2)}, u32[]{:S(2)}) collective-permute-start(bf16[256,2048]{1,0:T(8,128)(2,1)S(1)} %collective-permute-done.34), channel_id=1, source_target_pairs={{0,1},{1,0},{2,3},{3,2},{4,5},{5,4},{6,7},{7,6},{8,9},{9,8},{10,11... | collective-permute-start | bytes 3145736 | tf_op jit(solution)/shard_map/ppermute | solution.py:106
  125.8 9.5 %collective-permute-start.41 = (bf16[512,256]{1,0:T(8,128)(2,1)S(1)}, bf16[512,256]{1,0:T(8,128)(2,1)S(1)}, u32[]{:S(2)}, u32[]{:S(2)}) collective-permute-start(bf16[512,256]{1,0:T(8,128)(2,1)S(1)} %convolution_convert_fusion), channel_id=1, source_target_pairs={{8,16},{9,17},{10,18},{11,19},{12,20},{13,21},{14,22},{15,23},{16,... | collective-permute-start | bytes 786440 | tf_op jit(solution)/shard_map/ppermute | solution.py:106
  134.6 8.5 %collective-permute-start.40 = (bf16[512,256]{1,0:T(8,128)(2,1)S(1)}, bf16[512,256]{1,0:T(8,128)(2,1)S(1)}, u32[]{:S(2)}, u32[]{:S(2)}) collective-permute-start(bf16[512,256]{1,0:T(8,128)(2,1)S(1)} %get-tuple-element.50), channel_id=1, source_target_pairs={{8,16},{9,17},{10,18},{11,19},{12,20},{13,21},{14,22},{15,23},{16,... | collective-permute-start | bytes 786440 | tf_op jit(solution)/shard_map/ppermute | solution.py:106
  138.1 8.9 %collective-permute-start.43 = (bf16[512,256]{1,0:T(8,128)(2,1)S(1)}, bf16[512,256]{1,0:T(8,128)(2,1)S(1)}, u32[]{:S(2)}, u32[]{:S(2)}) collective-permute-start(bf16[512,256]{1,0:T(8,128)(2,1)S(1)} %add_convert_fusion), channel_id=1, source_target_pairs={{0,8},{1,9},{2,10},{3,11},{4,12},{5,13},{6,14},{7,15},{8,0},{9,1},... | collective-permute-start | bytes 786440 | tf_op jit(solution)/shard_map/ppermute | solution.py:106
  (26 other events, 194.9 us)

commit v4 on v3

--- a/solution.py
+++ b/solution.py
@@ -129,12 +129,29 @@
 
 def line_reduce(own, first, second, third):
     third_b, second_b = third.astype(jnp.bfloat16), second.astype(jnp.bfloat16)
-    jumped = send(third_b, TWO_IN).astype(jnp.float32)
-    inward = send(second_b, INWARD).astype(jnp.float32)
-    across = send(second_b, MIDDLE).astype(jnp.float32)
+    jumped, inward, across = lax.optimization_barrier(
+        (send(third_b, TWO_IN), send(second_b, INWARD), send(second_b, MIDDLE))
+    )
+    jumped, inward, across = [block.astype(jnp.float32) for block in (jumped, inward, across)]
     last = send((third + inward).astype(jnp.bfloat16), MIDDLE).astype(jnp.float32)
     paired = send((first + across + jumped).astype(jnp.bfloat16), PAIRS).astype(jnp.float32)
     return own + last + paired
+
+
+TAIL = 16
+
+
+def with_tail(block, values):
+    high = lax.reduce_precision(values, 8, 7)
+    middle = lax.reduce_precision(values - high, 8, 7)
+    terms = jnp.concatenate([high, middle, values - high - middle])
+    rows = jnp.pad(terms, (0, TAIL * block.shape[1] - terms.size)).reshape(TAIL, -1)
+    return jnp.concatenate([block.astype(jnp.bfloat16), rows.astype(jnp.bfloat16)], axis=0)
+
+
+def tail_of(message, values):
+    terms = message[-TAIL:].astype(jnp.float32).reshape(-1)[: 3 * values.size].reshape(3, -1)
+    return terms[0] + terms[1] + terms[2]
 
 
 def project(prompts, responses, blocks, weights, total, kind):
@@ -221,10 +238,8 @@
     response_rows = jnp.concatenate(pieces, axis=1)
     held = jnp.concatenate([response_rows, *line_gather(response_rows)], axis=0)
 
-    prompt_emb, response_rows = lax.optimization_barrier((prompt_emb, response_rows))
     near = jnp.concatenate([prompt_emb, send(prompt_emb, ACROSS_X)], axis=1)
-    across = jnp.concatenate([send(prompt_emb, ACROSS_Y), send(prompt_emb, ACROSS_XY)], axis=1)
-    half = jnp.concatenate([near, across], axis=0)
+    half = jnp.concatenate([near, send(near, ACROSS_Y)], axis=0)
     other = send(half, ACROSS_C)
     plane = [half[:, :width], other[:, :width], half[:, width:], other[:, width:]]
     plane = jnp.concatenate(plane, axis=1)
@@ -257,6 +272,23 @@
     parts = cross_rows(weight, plane)
     grad = line_reduce(*[parts[k * quarter : (k + 1) * quarter] for k in range(LINE)])
     grad = grad.astype(jnp.bfloat16)
+
+    parts = matmul(weight, held)
+    mine = jnp.concatenate([parts[:, :width], parts[:, 2 * width : 3 * width]], axis=1)
+    away = jnp.concatenate([parts[:, width : 2 * width], parts[:, 3 * width :]], axis=1)
+    message = send(with_tail(away, losses), ACROSS_C)
+    losses = losses + tail_of(message, losses)
+    mine = mine + message[: 2 * row_count].astype(jnp.float32)
+    message = send(with_tail(mine[:, width:], losses), ACROSS_X)
+    losses = losses + tail_of(message, losses)
+    mine = mine[:, :width] + message[: 2 * row_count].astype(jnp.float32)
+    grad, mine, losses = lax.optimization_barrier((grad, mine, losses))
+    message = send(with_tail(mine, losses), ACROSS_Y)
+    losses = losses[:row_count] + tail_of(message, losses)[row_count:]
+    mine_y = message[: 2 * row_count].astype(jnp.float32)
+    grad_prompt = (mine[:row_count] + mine_y[row_count:]).astype(jnp.bfloat16)
+    grad_prompt_y = (mine[row_count:] + mine_y[:row_count]).astype(jnp.bfloat16)
+
     grad_response = jnp.zeros((row_count, width), jnp.bfloat16)
     for k in range(SIDE * CORES):
         piece = grad[:, k * width : (k + 1) * width]
@@ -265,23 +297,6 @@
             grad_response, piece, (mp ^ k) * quarter, axis=0
         )
     grad_response_y = send(grad_response, ACROSS_Y)
-
-    parts = matmul(weight, held)
-    mine = jnp.concatenate([parts[:, :width], parts[:, 2 * width : 3 * width]], axis=1)
-    away = jnp.concatenate([parts[:, width : 2 * width], parts[:, 3 * width :]], axis=1)
-    mine = mine + send(away.astype(jnp.bfloat16), ACROSS_C).astype(jnp.float32)
-    mine = mine[:, :width] + send(mine[:, width:].astype(jnp.bfloat16), ACROSS_X).astype(
-        jnp.float32
-    )
-    mine_y = send(mine.astype(jnp.bfloat16), ACROSS_Y).astype(jnp.float32)
-    grad_prompt = (mine[:row_count] + mine_y[row_count:]).astype(jnp.bfloat16)
-    grad_prompt_y = (mine[row_count:] + mine_y[:row_count]).astype(jnp.bfloat16)
-
-    losses = losses[:row_count] + send(losses[row_count:], ACROSS_Y)
-    losses = losses + send(losses, ACROSS_X)
-    losses = losses + send(losses, ACROSS_C)
-    losses, grad_response_y = lax.optimization_barrier((losses, grad_response_y))
-
     grads = [
         grad_prompt,
         grad_response,

time: 148 us -> 147 us (level)
  waiting for transfers between devices: 69 us -> 55.5 us
  local copies, waits for them, and re-layouts: 2.58 us -> 10.7 us
  other arithmetic: 9.36 us -> 11.8 us
  Pallas kernels: 4.68 us -> 6.59 us
    ppermute x44 -> x40, waiting for transfers between devices: 69 us -> 55.5 us  [send(): return lax.ppermute(block, ('dp', 'mp'), table)]
    unnamed x12 -> x55, local copies, waits for them, and re-layouts: 1.61 us -> 4.26 us
    transpose x1, local copies, waits for them, and re-layouts: 0.24 us -> 2.59 us  [full_window(): features(array, line, y)]
    pallas_call x3, Pallas kernels: 4.68 us -> 6.59 us  [project(): pl.pallas_call(kernel, grid_spec=pltpu.PrefetchScalarGridSpec(num_scalar_...]
    transpose x2, local copies, waits for them, and re-layouts: 0.18 us -> 2.08 us  [turned(): return [array[:, k * depth:(k + 1) * depth].T for k in range(LINE)]]
    ppermute x44 -> x40, starting transfers between devices: 55.3 us -> 54 us  [send(): return lax.ppermute(block, ('dp', 'mp'), table)]
  transfers between devices with their start and end apart: 44 -> 40, of which waited for: 20 -> 19; matrix products, arithmetic and copies ran while one was open for 10% -> 15% of each run, Pallas kernels for 3% -> 4%
where the time goes in v4:
time: 147 us
  waiting for transfers between devices  55.5 us (38%)
  starting transfers between devices  54 us (37%)
  other arithmetic  11.8 us (8%)
  local copies, waits for them, and re-layouts  10.7 us (7%)
  Pallas kernels  6.59 us (4%)
  matrix products  6.5 us (4%)
  between operations  1.48 us (1%)
    ppermute x40, waiting for transfers between devices, send(): return lax.ppermute(block, ('dp', 'mp'), table)  55.5 us
    ppermute x40, starting transfers between devices, send(): return lax.ppermute(block, ('dp', 'mp'), table)  54 us
    pallas_call x3, Pallas kernels, project(): pl.pallas_call(kernel, grid_spec=pltpu.PrefetchScalarGridSpec(num_scalar_...  6.59 us
    unnamed x55, local copies, waits for them, and re-layouts  4.26 us
    dot_general x5, matrix products, matmul(): jnp.dot(left_side, righthand_term, preferred_element_type=jnp.float32)  4.24 us
    select_n x1, other arithmetic, full_window(): mine = jnp.where(c == 0, prompts, responses)  3.12 us
  transfers between devices with their start and end apart: 40, of which 19 were waited for; matrix products, arithmetic and copies ran while one was open for 15% of the time, Pallas kernels for 4%

profile of v4, /device:TPU:0, one launch (start us, length us, event | category | flops | bytes accessed | tf_op | source)
XLA Modules:
  0.0 146.6 jit_solution(7548641475857102198)
XLA Ops:
  0.6 3.1 %collective-permute-start.1 = (bf16[512,256]{1,0:T(8,128)(2,1)}, bf16[512,256]{1,0:T(8,128)(2,1)S(1)}, u32[]{:S(2)}, u32[]{:S(2)}) collective-permute-start(bf16[512,256]{1,0:T(8,128)(2,1)} %refs_0_.1), channel_id=1, source_target_pairs={{0,8},{1,9},{2,10},{3,11},{4,12},{5,13},{6,14},{7,15},{8,0},{9,1},... | collective-permute-start | bytes 786440 | tf_op jit(solution)/shard_map/ppermute | solution.py:106
  6.0 4.3 %collective-permute-done.1.refs_2_ = bf16[512,256]{1,0:T(8,128)(2,1)S(1)} collective-permute-done((bf16[512,256]{1,0:T(8,128)(2,1)}, bf16[512,256]{1,0:T(8,128)(2,1)S(1)}, u32[]{:S(2)}, u32[]{:S(2)}) %collective-permute-start.1) | collective-permute-done | bytes 262176 | tf_op jit(solution)/shard_map/ppermute | solution.py:106
  13.5 3.1 %broadcast_select_fusion = bf16[256,4096]{1,0:T(8,128)(2,1)} fusion(bf16[256,4096]{1,0:T(8,128)(2,1)} %prompt_ref.5, bf16[256,4096]{1,0:T(8,128)(2,1)} %response_ref.5, pred[]{:T(512)S(6)} %eq.24), kind=kLoop, calls=%fused_computation | loop fusion | flops 1048576 | bytes 6291457 | tf_op jit(solution)/shard_map/jit(_where)/select_n | solution.py:248
  18.9 11.0 %collective-permute-done.4 = bf16[512,256]{1,0:T(8,128)(2,1)} collective-permute-done((bf16[512,256]{1,0:T(8,128)(2,1)S(1)}, bf16[512,256]{1,0:T(8,128)(2,1)}, u32[]{:S(2)}, u32[]{:S(2)}) %collective-permute-start.4) | collective-permute-done | bytes 262176 | tf_op jit(solution)/shard_map/ppermute | solution.py:106
  37.1 3.0 %shard_map.59.refs_2_ = f32[512,256]{1,0:T(8,128)S(1)} custom-call(s32[4]{0:T(128)S(1)} %pad_add_fusion.3.block_ref, bf16[256,4096]{1,0:T(8,128)(2,1)S(1)} %copy-done, bf16[256,4096]{1,0:T(8,128)(2,1)S(1)} %copy-done.1, bf16[512,256]{1,0:T(8,128)(2,1)S(1)} %copy-done.2, bf16[512,256]{1,0:T(8,128)(2,1)S(1)} %collective-permute-done.8.refs_1_, ...), custom_call_target="tpu_custom_call" | custom-call | flops 536870912 | bytes 3145728 | tf_op jit(solution)/shard_map/pallas_call | solution.py:185
  41.4 2.5 %collective-permute-done.7.refs_1_ = bf16[512,256]{1,0:T(8,128)(2,1)} collective-permute-done((bf16[512,256]{1,0:T(8,128)(2,1)S(1)}, bf16[512,256]{1,0:T(8,128)(2,1)}, u32[]{:S(2)}, u32[]{:S(2)}) %collective-permute-start.7) | collective-permute-done | bytes 262176 | tf_op jit(solution)/shard_map/ppermute | solution.py:106
  43.9 2.3 %shard_map.61 = bf16[512,256]{1,0:T(8,128)(2,1)S(1)} custom-call(s32[2]{0:T(128)S(1)} %get-tuple-element.93.block_ref, bf16[256,4096]{1,0:T(8,128)(2,1)S(1)} %copy-done, bf16[256,4096]{1,0:T(8,128)(2,1)S(1)} %copy-done.1, bf16[512,256]{1,0:T(8,128)(2,1)} %collective-permute-done.5.refs_0_, bf16[512,256]{1,0:T(8,128)(2,1)} %collective-permute-done.7.refs_1_, ...), custom_call_target="tpu_custom_call" | custom-call | flops 268435456 | bytes 1572864 | tf_op jit(solution)/shard_map/pallas_call | solution.py:185
  48.9 2.4 %collective-permute-done.10 = bf16[256,256]{1,0:T(8,128)(2,1)S(1)} collective-permute-done((bf16[256,256]{1,0:T(8,128)(2,1)S(1)}, bf16[256,256]{1,0:T(8,128)(2,1)S(1)}, u32[]{:S(2)}, u32[]{:S(2)}) %collective-permute-start.10) | collective-permute-done | bytes 131104 | tf_op jit(solution)/shard_map/ppermute | solution.py:106
  55.0 2.0 %collective-permute-done.14 = bf16[64,256]{1,0:T(8,128)(2,1)S(1)} collective-permute-done((bf16[64,256]{1,0:T(8,128)(2,1)S(1)}, bf16[64,256]{1,0:T(8,128)(2,1)S(1)}, u32[]{:S(2)}, u32[]{:S(2)}) %collective-permute-start.14) | collective-permute-done | bytes 32800 | tf_op jit(solution)/shard_map/ppermute | solution.py:106
  59.1 4.6 %collective-permute-done.16 = bf16[64,1024]{1,0:T(8,128)(2,1)} collective-permute-done((bf16[64,1024]{1,0:T(8,128)(2,1)S(1)}, bf16[64,1024]{1,0:T(8,128)(2,1)}, u32[]{:S(2)}, u32[]{:S(2)}) %collective-permute-start.16) | collective-permute-done | bytes 131104 | tf_op jit(solution)/shard_map/ppermute | solution.py:106
  66.9 2.6 %dynamic-slice_bitcast_fusion = (bf16[512,256]{0,1:T(8,128)(2,1)}, bf16[512,256]{0,1:T(8,128)(2,1)}, bf16[512,256]{0,1:T(8,128)(2,1)}, bf16[512,256]{0,1:T(8,128...) fusion(bf16[256,4096]{1,0:T(8,128)(2,1)} %response_ref.5, ...), kind=kLoop, calls=%fused_computation.51 | loop fusion | bytes 4194320 | tf_op jit(solution)/shard_map/transpose | solution.py:257
  69.6 3.9 %collective-permute-done.20 = bf16[64,1024]{1,0:T(8,128)(2,1)} collective-permute-done((bf16[64,1024]{1,0:T(8,128)(2,1)}, bf16[64,1024]{1,0:T(8,128)(2,1)}, u32[]{:S(2)}, u32[]{:S(2)}) %collective-permute-start.20) | collective-permute-done | bytes 131104 | tf_op jit(solution)/shard_map/ppermute | solution.py:106
  83.9 4.0 %collective-permute-start.21 = (bf16[64,1024]{1,0:T(8,128)(2,1)S(1)}, bf16[64,1024]{1,0:T(8,128)(2,1)S(1)}, u32[]{:S(2)}, u32[]{:S(2)}) collective-permute-start(bf16[64,1024]{1,0:T(8,128)(2,1)S(1)} %get-tuple-element.61), channel_id=1, source_target_pairs={{0,16},{1,17},{2,18},{3,19},{4,20},{5,21},{6,22},{7,23},{24,8},{25... | collective-permute-start | bytes 393224 | tf_op jit(solution)/shard_map/ppermute | solution.py:106
  88.0 3.0 %collective-permute-done.21 = bf16[64,1024]{1,0:T(8,128)(2,1)S(1)} collective-permute-done((bf16[64,1024]{1,0:T(8,128)(2,1)S(1)}, bf16[64,1024]{1,0:T(8,128)(2,1)S(1)}, u32[]{:S(2)}, u32[]{:S(2)}) %collective-permute-start.21) | collective-permute-done | bytes 131104 | tf_op jit(solution)/shard_map/ppermute | solution.py:106
  92.4 5.2 %collective-permute-start.25 = (bf16[64,1024]{1,0:T(8,128)(2,1)S(1)}, bf16[64,1024]{1,0:T(8,128)(2,1)}, u32[]{:S(2)}, u32[]{:S(2)}) collective-permute-start(bf16[64,1024]{1,0:T(8,128)(2,1)S(1)} %get-tuple-element.59), channel_id=1, source_target_pairs={{0,8},{1,9},{2,10},{3,11},{4,12},{5,13},{6,14},{7,15},{8,0},{9,1},... | collective-permute-start | bytes 393224 | tf_op jit(solution)/shard_map/ppermute | solution.py:106
  101.8 2.0 %slice_bitcast_fusion.1 = (bf16[512,256]{0,1:T(8,128)(2,1)}, bf16[512,256]{0,1:T(8,128)(2,1)S(1)}, bf16[512,256]{0,1:T(8,128)(2,1)S(1)}, bf16[512,256]{0,1:T(8,128)(2,1)S(1)}) fusion(bf16[256,2048]{1,0:T(8,128)(2,1)} %collective-permute-done.29), kind=kLoop, calls=%fused_computation.36 | loop fusion | bytes 2097152 | tf_op jit(solution)/shard_map/transpose | solution.py:255
  108.4 2.3 %collective-permute-done.32 = bf16[64,256]{1,0:T(8,128)(2,1)S(1)} collective-permute-done((bf16[64,256]{1,0:T(8,128)(2,1)S(1)}, bf16[64,256]{1,0:T(8,128)(2,1)S(1)}, u32[]{:S(2)}, u32[]{:S(2)}) %collective-permute-start.32) | collective-permute-done | bytes 32800 | tf_op jit(solution)/shard_map/ppermute | solution.py:106
  112.3 2.3 %collective-permute-done.28 = bf16[528,256]{1,0:T(8,128)(2,1)S(1)} collective-permute-done((bf16[528,256]{1,0:T(8,128)(2,1)S(1)}, bf16[528,256]{1,0:T(8,128)(2,1)S(1)}, u32[]{:S(2)}, u32[]{:S(2)}) %collective-permute-start.28) | collective-permute-done | bytes 270368 | tf_op jit(solution)/shard_map/ppermute | solution.py:106
  114.6 2.7 %collective-permute-done.34 = bf16[256,256]{1,0:T(8,128)(2,1)S(1)} collective-permute-done((bf16[256,256]{1,0:T(8,128)(2,1)S(1)}, bf16[256,256]{1,0:T(8,128)(2,1)S(1)}, u32[]{:S(2)}, u32[]{:S(2)}) %collective-permute-start.34) | collective-permute-done | bytes 131104 | tf_op jit(solution)/shard_map/ppermute | solution.py:106
  120.2 2.7 %collective-permute-start.36 = (bf16[512,256]{1,0:T(8,128)(2,1)S(1)}, bf16[512,256]{1,0:T(8,128)(2,1)S(1)}, u32[]{:S(2)}, u32[]{:S(2)}) collective-permute-start(bf16[512,256]{1,0:T(8,128)(2,1)S(1)} %convolution_convert_fusion), channel_id=1, source_target_pairs={{0,8},{1,9},{2,10},{3,11},{4,12},{5,13},{6,14},{7,15},{24,16},{25,... | collective-permute-start | bytes 786440 | tf_op jit(solution)/shard_map/ppermute | solution.py:106
  124.0 4.0 %collective-permute-start.35 = (bf16[512,256]{1,0:T(8,128)(2,1)S(1)}, bf16[512,256]{1,0:T(8,128)(2,1)S(1)}, u32[]{:S(2)}, u32[]{:S(2)}) collective-permute-start(bf16[512,256]{1,0:T(8,128)(2,1)S(1)} %get-tuple-element.91), channel_id=1, source_target_pairs={{0,16},{1,17},{2,18},{3,19},{4,20},{5,21},{6,22},{7,23},{24,8},{25... | collective-permute-start | bytes 786440 | tf_op jit(solution)/shard_map/ppermute | solution.py:106
  128.3 5.0 %collective-permute-done.35 = bf16[512,256]{1,0:T(8,128)(2,1)S(1)} collective-permute-done((bf16[512,256]{1,0:T(8,128)(2,1)S(1)}, bf16[512,256]{1,0:T(8,128)(2,1)S(1)}, u32[]{:S(2)}, u32[]{:S(2)}) %collective-permute-start.35) | collective-permute-done | bytes 262176 | tf_op jit(solution)/shard_map/ppermute | solution.py:106
  134.5 6.4 %collective-permute-start.39 = (bf16[512,256]{1,0:T(8,128)(2,1)S(1)}, bf16[512,256]{1,0:T(8,128)(2,1)S(1)}, u32[]{:S(2)}, u32[]{:S(2)}) collective-permute-start(bf16[512,256]{1,0:T(8,128)(2,1)S(1)} %fusion.4), channel_id=1, source_target_pairs={{0,8},{1,9},{2,10},{3,11},{4,12},{5,13},{6,14},{7,15},{8,0},{9,1},... | collective-permute-start | bytes 786440 | tf_op jit(solution)/shard_map/ppermute | solution.py:106
  141.5 3.8 %collective-permute-done.39 = bf16[512,256]{1,0:T(8,128)(2,1)S(1)} collective-permute-done((bf16[512,256]{1,0:T(8,128)(2,1)S(1)}, bf16[512,256]{1,0:T(8,128)(2,1)S(1)}, u32[]{:S(2)}, u32[]{:S(2)}) %collective-permute-start.39) | collective-permute-done | bytes 262176 | tf_op jit(solution)/shard_map/ppermute | solution.py:106
  (189 shorter events, 56.9 us)
Async XLA Ops:
  0.6 9.6 %collective-permute-start.1 = (bf16[512,256]{1,0:T(8,128)(2,1)}, bf16[512,256]{1,0:T(8,128)(2,1)S(1)}, u32[]{:S(2)}, u32[]{:S(2)}) collective-permute-start(bf16[512,256]{1,0:T(8,128)(2,1)} %refs_0_.1), channel_id=1, source_target_pairs={{0,8},{1,9},{2,10},{3,11},{4,12},{5,13},{6,14},{7,15},{8,0},{9,1},... | collective-permute-start | bytes 786440 | tf_op jit(solution)/shard_map/ppermute | solution.py:106
  3.7 8.5 %collective-permute-start.3 = (bf16[512,256]{1,0:T(8,128)(2,1)}, bf16[512,256]{1,0:T(8,128)(2,1)S(1)}, u32[]{:S(2)}, u32[]{:S(2)}) collective-permute-start(bf16[512,256]{1,0:T(8,128)(2,1)} %refs_0_.1), channel_id=1, source_target_pairs={{8,16},{9,17},{10,18},{11,19},{12,20},{13,21},{14,22},{15,23},{16,... | collective-permute-start | bytes 786440 | tf_op jit(solution)/shard_map/ppermute | solution.py:106
  4.4 31.1 %collective-permute-start.8 = (bf16[512,256]{1,0:T(8,128)(2,1)}, bf16[512,256]{1,0:T(8,128)(2,1)S(1)}, u32[]{:S(2)}, u32[]{:S(2)}) collective-permute-start(bf16[512,256]{1,0:T(8,128)(2,1)} %refs_0_.1), channel_id=1, source_target_pairs={{0,4},{1,5},{2,6},{3,7},{4,0},{5,1},{6,2},{7,3},{8,12},{9,13},{10,... | collective-permute-start | bytes 786440 | tf_op jit(solution)/shard_map/ppermute | solution.py:106
  10.2 8.2 %collective-permute-start.2 = (bf16[512,256]{1,0:T(8,128)(2,1)S(1)}, bf16[512,256]{1,0:T(8,128)(2,1)S(1)}, u32[]{:S(2)}, u32[]{:S(2)}) collective-permute-start(bf16[512,256]{1,0:T(8,128)(2,1)S(1)} %collective-permute-done.1.refs_2_), channel_id=1, source_target_pairs={{8,16},{9,17},{10,18},{11,19},{12,20},{13,21},{14,22},{15,23},{16,... | collective-permute-start | bytes 786440 | tf_op jit(solution)/shard_map/ppermute | solution.py:106
  10.9 21.6 %collective-permute-start.6 = (bf16[512,256]{1,0:T(8,128)(2,1)S(1)}, bf16[512,256]{1,0:T(8,128)(2,1)}, u32[]{:S(2)}, u32[]{:S(2)}) collective-permute-start(bf16[512,256]{1,0:T(8,128)(2,1)S(1)} %collective-permute-done.1.refs_2_), channel_id=1, source_target_pairs={{8,24},{9,25},{10,26},{11,27},{12,28},{13,29},{14,30},{15,31},{16,... | collective-permute-start | bytes 786440 | tf_op jit(solution)/shard_map/ppermute | solution.py:106
  12.2 17.6 %collective-permute-start.4 = (bf16[512,256]{1,0:T(8,128)(2,1)S(1)}, bf16[512,256]{1,0:T(8,128)(2,1)}, u32[]{:S(2)}, u32[]{:S(2)}) collective-permute-start(bf16[512,256]{1,0:T(8,128)(2,1)S(1)} %collective-permute-done.3), channel_id=1, source_target_pairs={{8,0},{9,1},{10,2},{11,3},{12,4},{13,5},{14,6},{15,7},{16,24},{17,... | collective-permute-start | bytes 786440 | tf_op jit(solution)/shard_map/ppermute | solution.py:106
  16.7 18.8 %collective-permute-start.9 = (bf16[512,256]{1,0:T(8,128)(2,1)S(1)}, bf16[512,256]{1,0:T(8,128)(2,1)}, u32[]{:S(2)}, u32[]{:S(2)}) collective-permute-start(bf16[512,256]{1,0:T(8,128)(2,1)S(1)} %collective-permute-done.1.refs_2_), channel_id=1, source_target_pairs={{0,4},{1,5},{2,6},{3,7},{4,0},{5,1},{6,2},{7,3},{8,12},{9,13},{10,... | collective-permute-start | bytes 786440 | tf_op jit(solution)/shard_map/ppermute | solution.py:106
  18.5 51.2 %collective-permute-start = (s32[256]{0:T(256)S(1)}, s32[256]{0:T(256)S(1)}, u32[]{:S(2)}, u32[]{:S(2)}) collective-permute-start(s32[256]{0:T(256)S(1)} %copy-done.26), channel_id=1, source_target_pairs={{0,4},{1,5},{2,6},{3,7},{4,0},{5,1},{6,2},{7,3},{8,12},{9,13},{10,... | collective-permute-start | bytes 3080 | tf_op jit(solution)/shard_map/ppermute | solution.py:106
  30.9 10.5 %collective-permute-start.5 = (bf16[512,256]{1,0:T(8,128)(2,1)S(1)}, bf16[512,256]{1,0:T(8,128)(2,1)}, u32[]{:S(2)}, u32[]{:S(2)}) collective-permute-start(bf16[512,256]{1,0:T(8,128)(2,1)S(1)} %add.257.refs_0_), channel_id=1, source_target_pairs={{0,4},{1,5},{2,6},{3,7},{4,0},{5,1},{6,2},{7,3},{8,12},{9,13},{10,... | collective-permute-start | bytes 786440 | tf_op jit(solution)/shard_map/ppermute | solution.py:106
  33.6 10.4 %collective-permute-start.7 = (bf16[512,256]{1,0:T(8,128)(2,1)S(1)}, bf16[512,256]{1,0:T(8,128)(2,1)}, u32[]{:S(2)}, u32[]{:S(2)}) collective-permute-start(bf16[512,256]{1,0:T(8,128)(2,1)S(1)} %add.258.refs_1_), channel_id=1, source_target_pairs={{0,4},{1,5},{2,6},{3,7},{4,0},{5,1},{6,2},{7,3},{8,12},{9,13},{10,... | collective-permute-start | bytes 786440 | tf_op jit(solution)/shard_map/ppermute | solution.py:106
  58.8 18.7 %collective-permute-start.12 = (bf16[512,512]{1,0:T(8,128)(2,1)S(1)}, bf16[512,512]{1,0:T(8,128)(2,1)S(1)}, u32[]{:S(2)}, u32[]{:S(2)}) collective-permute-start(bf16[512,512]{1,0:T(8,128)(2,1)S(1)} %pad_maximum_fusion.7), channel_id=1, source_target_pairs={{0,1},{1,0},{2,3},{3,2},{4,5},{5,4},{6,7},{7,6},{8,9},{9,8},{10,11... | collective-permute-start | bytes 1572872 | tf_op jit(solution)/shard_map/ppermute | solution.py:106
  63.7 10.8 %collective-permute-start.17 = (bf16[64,1024]{1,0:T(8,128)(2,1)}, bf16[64,1024]{1,0:T(8,128)(2,1)S(1)}, u32[]{:S(2)}, u32[]{:S(2)}) collective-permute-start(bf16[64,1024]{1,0:T(8,128)(2,1)} %collective-permute-done.16), channel_id=1, source_target_pairs={{8,16},{9,17},{10,18},{11,19},{12,20},{13,21},{14,22},{15,23},{16,... | collective-permute-start | bytes 393224 | tf_op jit(solution)/shard_map/ppermute | solution.py:106
  64.3 9.2 %collective-permute-start.20 = (bf16[64,1024]{1,0:T(8,128)(2,1)}, bf16[64,1024]{1,0:T(8,128)(2,1)}, u32[]{:S(2)}, u32[]{:S(2)}) collective-permute-start(bf16[64,1024]{1,0:T(8,128)(2,1)} %collective-permute-done.16), channel_id=1, source_target_pairs={{8,24},{9,25},{10,26},{11,27},{12,28},{13,29},{14,30},{15,31},{16,... | collective-permute-start | bytes 393224 | tf_op jit(solution)/shard_map/ppermute | solution.py:106
  65.6 9.9 %collective-permute-start.19 = (bf16[64,1024]{1,0:T(8,128)(2,1)S(1)}, bf16[64,1024]{1,0:T(8,128)(2,1)}, u32[]{:S(2)}, u32[]{:S(2)}) collective-permute-start(bf16[64,1024]{1,0:T(8,128)(2,1)S(1)} %collective-permute-done.18), channel_id=1, source_target_pairs={{8,0},{9,1},{10,2},{11,3},{12,4},{13,5},{14,6},{15,7},{16,24},{17,... | collective-permute-start | bytes 393224 | tf_op jit(solution)/shard_map/ppermute | solution.py:106
  76.5 25.2 %collective-permute-start.29 = (bf16[256,2048]{1,0:T(8,128)(2,1)}, bf16[256,2048]{1,0:T(8,128)(2,1)}, u32[]{:S(2)}, u32[]{:S(2)}) collective-permute-start(bf16[256,2048]{1,0:T(8,128)(2,1)} %pad_maximum_fusion.1), channel_id=1, source_target_pairs={{0,4},{1,5},{2,6},{3,7},{4,0},{5,1},{6,2},{7,3},{8,12},{9,13},{10,... | collective-permute-start | bytes 3145736 | tf_op jit(solution)/shard_map/ppermute | solution.py:106
  81.8 15.9 %collective-permute-start.26 = (bf16[528,512]{1,0:T(8,128)(2,1)S(1)}, bf16[528,512]{1,0:T(8,128)(2,1)S(1)}, u32[]{:S(2)}, u32[]{:S(2)}) collective-permute-start(bf16[528,512]{1,0:T(8,128)(2,1)S(1)} %pad_maximum_fusion.6), channel_id=1, source_target_pairs={{0,1},{1,0},{2,3},{3,2},{4,5},{5,4},{6,7},{7,6},{8,9},{9,8},{10,11... | collective-permute-start | bytes 1622024 | tf_op jit(solution)/shard_map/ppermute | solution.py:106
  81.9 9.1 %collective-permute-start.22 = (bf16[64,1024]{1,0:T(8,128)(2,1)S(1)}, bf16[64,1024]{1,0:T(8,128)(2,1)S(1)}, u32[]{:S(2)}, u32[]{:S(2)}) collective-permute-start(bf16[64,1024]{1,0:T(8,128)(2,1)S(1)} %get-tuple-element.60), channel_id=1, source_target_pairs={{0,8},{1,9},{2,10},{3,11},{4,12},{5,13},{6,14},{7,15},{24,16},{25,... | collective-permute-start | bytes 393224 | tf_op jit(solution)/shard_map/ppermute | solution.py:106
  92.4 8.3 %collective-permute-start.25 = (bf16[64,1024]{1,0:T(8,128)(2,1)S(1)}, bf16[64,1024]{1,0:T(8,128)(2,1)}, u32[]{:S(2)}, u32[]{:S(2)}) collective-permute-start(bf16[64,1024]{1,0:T(8,128)(2,1)S(1)} %get-tuple-element.59), channel_id=1, source_target_pairs={{0,8},{1,9},{2,10},{3,11},{4,12},{5,13},{6,14},{7,15},{8,0},{9,1},... | collective-permute-start | bytes 393224 | tf_op jit(solution)/shard_map/ppermute | solution.py:106
  101.7 15.8 %collective-permute-start.30 = (bf16[256,2048]{1,0:T(8,128)(2,1)}, bf16[256,2048]{1,0:T(8,128)(2,1)S(1)}, u32[]{:S(2)}, u32[]{:S(2)}) collective-permute-start(bf16[256,2048]{1,0:T(8,128)(2,1)} %collective-permute-done.29), channel_id=1, source_target_pairs={{0,1},{1,0},{2,3},{3,2},{4,5},{5,4},{6,7},{7,6},{8,9},{9,8},{10,11... | collective-permute-start | bytes 3145736 | tf_op jit(solution)/shard_map/ppermute | solution.py:106
  105.6 8.9 %collective-permute-start.28 = (bf16[528,256]{1,0:T(8,128)(2,1)S(1)}, bf16[528,256]{1,0:T(8,128)(2,1)S(1)}, u32[]{:S(2)}, u32[]{:S(2)}) collective-permute-start(bf16[528,256]{1,0:T(8,128)(2,1)S(1)} %pad_maximum_fusion.11), channel_id=1, source_target_pairs={{0,4},{1,5},{2,6},{3,7},{4,0},{5,1},{6,2},{7,3},{8,12},{9,13},{10,... | collective-permute-start | bytes 811016 | tf_op jit(solution)/shard_map/ppermute | solution.py:106
  120.2 8.2 %collective-permute-start.36 = (bf16[512,256]{1,0:T(8,128)(2,1)S(1)}, bf16[512,256]{1,0:T(8,128)(2,1)S(1)}, u32[]{:S(2)}, u32[]{:S(2)}) collective-permute-start(bf16[512,256]{1,0:T(8,128)(2,1)S(1)} %convolution_convert_fusion), channel_id=1, source_target_pairs={{0,8},{1,9},{2,10},{3,11},{4,12},{5,13},{6,14},{7,15},{24,16},{25,... | collective-permute-start | bytes 786440 | tf_op jit(solution)/shard_map/ppermute | solution.py:106
  124.0 9.3 %collective-permute-start.35 = (bf16[512,256]{1,0:T(8,128)(2,1)S(1)}, bf16[512,256]{1,0:T(8,128)(2,1)S(1)}, u32[]{:S(2)}, u32[]{:S(2)}) collective-permute-start(bf16[512,256]{1,0:T(8,128)(2,1)S(1)} %get-tuple-element.91), channel_id=1, source_target_pairs={{0,16},{1,17},{2,18},{3,19},{4,20},{5,21},{6,22},{7,23},{24,8},{25... | collective-permute-start | bytes 786440 | tf_op jit(solution)/shard_map/ppermute | solution.py:106
  133.4 8.1 %collective-permute-start.38 = (bf16[512,256]{1,0:T(8,128)(2,1)S(1)}, bf16[512,256]{1,0:T(8,128)(2,1)S(1)}, u32[]{:S(2)}, u32[]{:S(2)}) collective-permute-start(bf16[512,256]{1,0:T(8,128)(2,1)S(1)} %add_convert_fusion), channel_id=1, source_target_pairs={{8,16},{9,17},{10,18},{11,19},{12,20},{13,21},{14,22},{15,23},{16,... | collective-permute-start | bytes 786440 | tf_op jit(solution)/shard_map/ppermute | solution.py:106
  134.5 10.7 %collective-permute-start.39 = (bf16[512,256]{1,0:T(8,128)(2,1)S(1)}, bf16[512,256]{1,0:T(8,128)(2,1)S(1)}, u32[]{:S(2)}, u32[]{:S(2)}) collective-permute-start(bf16[512,256]{1,0:T(8,128)(2,1)S(1)} %fusion.4), channel_id=1, source_target_pairs={{0,8},{1,9},{2,10},{3,11},{4,12},{5,13},{6,14},{7,15},{8,0},{9,1},... | collective-permute-start | bytes 786440 | tf_op jit(solution)/shard_map/ppermute | solution.py:106
  (43 other events, 205.2 us)

commit v5 on v3

--- a/solution.py
+++ b/solution.py
@@ -116,46 +116,54 @@
 INWARD = along_line({0: 1, 3: 2})
 TWO_OUT = along_line({1: 3, 2: 0})
 TWO_IN = along_line({3: 1, 0: 2})
-MIX = [routes(lambda z, y, x, c, k=k: (z, y, x ^ (k >> 1), c ^ (k & 1))) for k in range(4)]
+PLANE = [
+    routes(lambda z, y, x, c, k=k: (z, y ^ (k >> 2), x ^ (k >> 1 & 1), c ^ (k & 1)))
+    for k in range(PAIR * SIDE * CORES)
+]
 
 
 def line_gather(block):
     first = send(block, PAIRS)
     middle = send(block, MIDDLE)
-    second = send(first, MIDDLE) + send(middle, OUTWARD)
-    third = middle + send(first, TWO_OUT)
-    return first, second, third
-
-
-def line_reduce(own, first, second, third):
-    third_b, second_b = third.astype(jnp.bfloat16), second.astype(jnp.bfloat16)
-    jumped = send(third_b, TWO_IN).astype(jnp.float32)
-    inward = send(second_b, INWARD).astype(jnp.float32)
-    across = send(second_b, MIDDLE).astype(jnp.float32)
-    last = send((third + inward).astype(jnp.bfloat16), MIDDLE).astype(jnp.float32)
-    paired = send((first + across + jumped).astype(jnp.bfloat16), PAIRS).astype(jnp.float32)
-    return own + last + paired
+    return first, (send(first, MIDDLE), send(middle, OUTWARD)), (middle, send(first, TWO_OUT))
+
+
+def line_reduce(own, first, second, third, second_b, third_b, beside=(), later=()):
+    jumped, inward, across = send(third_b, TWO_IN), send(second_b, INWARD), send(second_b, MIDDLE)
+    jumped, inward, across, *beside = lax.optimization_barrier((jumped, inward, across, *beside))
+    jumped, inward, across = [block.astype(jnp.float32) for block in (jumped, inward, across)]
+    paired = send((first + across + jumped).astype(jnp.bfloat16), PAIRS)
+    last = send((third + inward).astype(jnp.bfloat16), MIDDLE)
+    later = later(*beside) if later else ()
+    last, paired, *later = lax.optimization_barrier((last, paired, *later))
+    return own + last.astype(jnp.float32) + paired.astype(jnp.float32), beside, later
 
 
 def project(prompts, responses, blocks, weights, total, kind):
     row_count = prompts.shape[0]
-    depth, width = weights[0].shape
+    depth, width = weights[0][0].shape
     count = len(weights)
+    terms = [term for weight in weights for term in weight]
 
     def kernel(block_ref, prompt_ref, response_ref, *refs):
-        weight_refs, total_ref, out_ref, sum_ref = refs[:count], refs[count], refs[-2], refs[-1]
+        term_refs = list(refs[: len(terms)])
+        total_ref, out_ref, sum_ref = refs[len(terms)], refs[-2], refs[-1]
         step = pl.program_id(0)
 
         @pl.when(step == 0)
         def _():
             sum_ref[...] = total_ref[...] if total is not None else jnp.zeros_like(sum_ref)
 
-        for k in range(count):
+        for k, weight in enumerate(weights):
+            mine = [term_refs.pop(0) for _ in weight]
 
             @pl.when(step == k)
-            def _(k=k):
-                sum_ref[:row_count] += matmul(prompt_ref[...], weight_refs[k][...])
-                sum_ref[row_count:] += matmul(response_ref[...], weight_refs[k][...])
+            def _(mine=mine):
+                block = mine[0][...]
+                for ref in mine[1:]:
+                    block = block + ref[...]
+                sum_ref[:row_count] += matmul(prompt_ref[...], block)
+                sum_ref[row_count:] += matmul(response_ref[...], block)
 
         @pl.when(step == count - 1)
         def _():
@@ -163,14 +171,14 @@
 
     whole = pl.BlockSpec((2 * row_count, width), lambda i, block: (0, 0))
     piece = pl.BlockSpec((row_count, depth), lambda i, block: (0, block[i]))
-    weight = pl.BlockSpec((depth, width), lambda i, block: (0, 0))
-    operands = [prompts, responses, *weights] + ([total] if total is not None else [])
+    term = pl.BlockSpec((depth, width), lambda i, block: (0, 0))
+    operands = [prompts, responses, *terms] + ([total] if total is not None else [])
     return pl.pallas_call(
         kernel,
         grid_spec=pltpu.PrefetchScalarGridSpec(
             num_scalar_prefetch=1,
             grid=(count,),
-            in_specs=[piece, piece] + [weight] * count + [whole] * (total is not None),
+            in_specs=[piece, piece] + [term] * len(terms) + [whole] * (total is not None),
             out_specs=whole,
             scratch_shapes=[pltpu.VMEM((2 * row_count, width), jnp.float32)],
         ),
@@ -178,16 +186,80 @@
         compiler_params=pltpu.CompilerParams(vmem_limit_bytes=32 * 1024 * 1024),
         cost_estimate=pl.CostEstimate(
             flops=4 * count * row_count * depth * width,
-            bytes_accessed=4 * count * row_count * depth + 2 * count * depth * width,
+            bytes_accessed=4 * count * row_count * depth + 2 * len(terms) * depth * width,
             transcendentals=0,
         ),
     )(jnp.stack(blocks).astype(jnp.int32), *operands)
 
 
+def compare(half, other, held, wanted, ids, row_count):
+    prompt_rows, width = half.shape[0], half.shape[1] // 2
+    quarter = held[0][0].shape[0]
+    count = len(held) * quarter
+    factor = LOGIT_SCALE / math.sqrt(E)
+    terms = [term for block in held for term in block]
+
+    def kernel(half_ref, other_ref, wanted_ref, ids_ref, *refs):
+        term_refs, refs = list(refs[: len(terms)]), refs[len(terms) :]
+        loss_ref, mine_ref, away_ref, parts_ref, second_ref, third_ref, rows_ref = refs
+        for k, block in enumerate(held):
+            mine = [term_refs.pop(0)[...] for _ in block]
+            rows_ref[k * quarter : (k + 1) * quarter] = sum(mine[1:], mine[0])
+        sources = [
+            (half_ref, 0, mine_ref, 0),
+            (other_ref, 0, away_ref, 0),
+            (half_ref, 1, mine_ref, 1),
+            (other_ref, 1, away_ref, 1),
+        ]
+        scores = jnp.zeros((prompt_rows, count), jnp.float32)
+        for k, (ref, place, _, _) in enumerate(sources):
+            scores += cross_cols(
+                ref[:, place * width : (place + 1) * width],
+                rows_ref[:, k * width : (k + 1) * width],
+            )
+        scores = scores * factor + LOGIT_BIAS
+        match = wanted_ref[...] == ids_ref[...]
+        margin = jnp.where(match, -scores, scores)
+        small = jnp.exp(-jnp.abs(margin))
+        loss_ref[...] = jnp.sum(
+            jnp.maximum(margin, 0.0) + jnp.log1p(small), axis=1, keepdims=True
+        )
+        share = jnp.where(margin >= 0.0, 1.0, small) / (1.0 + small)
+        share = share * (factor / row_count)
+        weight = jnp.where(match, -share, share).astype(jnp.bfloat16)
+        for k, (ref, place, out, goal) in enumerate(sources):
+            columns = slice(k * width, (k + 1) * width)
+            part = cross_rows(weight, ref[:, place * width : (place + 1) * width])
+            parts_ref[:, columns] = part
+            second_ref[:, columns] = part[2 * quarter : 3 * quarter].astype(jnp.bfloat16)
+            third_ref[:, columns] = part[3 * quarter :].astype(jnp.bfloat16)
+            part = matmul(weight, rows_ref[:, columns])
+            out[:, goal * width : (goal + 1) * width] = part.astype(out.dtype)
+
+    full = half.shape[1] * 2
+    return pl.pallas_call(
+        kernel,
+        out_shape=[
+            jax.ShapeDtypeStruct((prompt_rows, 1), jnp.float32),
+            jax.ShapeDtypeStruct((prompt_rows, 2 * width), jnp.float32),
+            jax.ShapeDtypeStruct((prompt_rows, 2 * width), jnp.bfloat16),
+            jax.ShapeDtypeStruct((count, full), jnp.float32),
+            jax.ShapeDtypeStruct((quarter, full), jnp.bfloat16),
+            jax.ShapeDtypeStruct((quarter, full), jnp.bfloat16),
+        ],
+        scratch_shapes=[pltpu.VMEM((count, full), jnp.bfloat16)],
+        compiler_params=pltpu.CompilerParams(vmem_limit_bytes=32 * 1024 * 1024),
+        cost_estimate=pl.CostEstimate(
+            flops=6 * prompt_rows * count * full,
+            bytes_accessed=6 * prompt_rows * full + 6 * count * full,
+            transcendentals=2 * prompt_rows * count,
+        ),
+    )(half, other, wanted, ids, *terms)
+
+
 def full_window(prompts, responses, head_projection_matrix, positive):
     row_count = prompts.shape[0]
     depth, width = head_projection_matrix.shape
-    factor = LOGIT_SCALE / math.sqrt(E)
     dp, mp = lax.axis_index("dp"), lax.axis_index("mp")
     z, y, c = dp // PAIR, dp % PAIR, mp % CORES
     quarter = row_count // (SIDE * CORES)
@@ -196,39 +268,50 @@
         return lax.dynamic_slice_in_dim(array, (line * PAIR + pair) * depth, depth, axis=1)
 
     lines = [z ^ k for k in range(LINE)]
-    own = head_projection_matrix
-    own_y = send(own, ACROSS_Y)
-    first, second, third = line_gather(own)
-    first_y, second_y, third_y = [send(block, ACROSS_Y) for block in (first, second, third)]
     here = [line * PAIR + y for line in lines]
     there = [line * PAIR + 1 - y for line in lines]
+    own = head_projection_matrix
+    first, middle = send(own, PAIRS), send(own, MIDDLE)
+    inner, outer = send(first, MIDDLE), send(middle, OUTWARD)
+    last = send(inner, OUTWARD)
+    own_y, first_y, middle_y, inner_y, outer_y, last_y = [
+        send(block, ACROSS_Y) for block in (own, first, middle, inner, outer, last)
+    ]
     emb = project(
         prompts,
         responses,
         [here[0], there[0], here[1], there[1]],
-        [own, own_y, first, first_y],
+        [(own,), (own_y,), (first,), (first_y,)],
         None,
         jnp.float32,
     )
-    emb = project(prompts, responses, [here[2], here[3]], [second, third], emb, jnp.float32)
-    emb = project(prompts, responses, [there[2], there[3]], [second_y, third_y], emb, jnp.bfloat16)
+    emb = project(
+        prompts,
+        responses,
+        [here[2], there[2], here[3]],
+        [(inner, outer), (inner_y, outer_y), (middle, last)],
+        emb,
+        jnp.float32,
+    )
+    emb = project(prompts, responses, [there[3]], [(middle_y, last_y)], emb, jnp.bfloat16)
     prompt_emb, response_emb = emb[:row_count], emb[row_count:]
 
     pieces = []
     for k in range(SIDE * CORES):
         piece = lax.dynamic_slice_in_dim(response_emb, (mp ^ k) * quarter, quarter, axis=0)
-        pieces.append(piece if k == 0 else send(piece, MIX[k]))
+        pieces.append(piece if k == 0 else send(piece, PLANE[k]))
+    prompt_emb, pieces[1] = lax.optimization_barrier((prompt_emb, pieces[1]))
     response_rows = jnp.concatenate(pieces, axis=1)
-    held = jnp.concatenate([response_rows, *line_gather(response_rows)], axis=0)
-
-    prompt_emb, response_rows = lax.optimization_barrier((prompt_emb, response_rows))
+    first, second, third = line_gather(response_rows)
+    held = [(response_rows,), (first,), second, third]
+
     near = jnp.concatenate([prompt_emb, send(prompt_emb, ACROSS_X)], axis=1)
-    across = jnp.concatenate([send(prompt_emb, ACROSS_Y), send(prompt_emb, ACROSS_XY)], axis=1)
-    half = jnp.concatenate([near, across], axis=0)
+    half = jnp.concatenate([near, send(near, ACROSS_Y)], axis=0)
     other = send(half, ACROSS_C)
-    plane = [half[:, :width], other[:, :width], half[:, width:], other[:, width:]]
-    plane = jnp.concatenate(plane, axis=1)
     wanted = jnp.concatenate([positive, send(positive, ACROSS_Y)], axis=0)
+    ids = ((jnp.stack(lines) * PAIR + y) * row_count + mp * quarter)[:, None] + lax.iota(
+        jnp.int32, quarter
+    )[None, :]
 
     mine = jnp.where(c == 0, prompts, responses)
     mine = jnp.concatenate([features(mine, line, 1 - y) for line in lines], axis=1)
@@ -244,43 +327,42 @@
     columns = [jnp.concatenate([array[k] for array in arrays], axis=1) for k in range(LINE)]
     columns = lax.optimization_barrier(columns)
 
-    pair_scores = cross_cols(plane, held) * factor + LOGIT_BIAS
-    column_ids = ((jnp.stack(lines) * PAIR + y) * row_count + mp * quarter)[:, None] + lax.iota(
-        jnp.int32, quarter
-    )[None, :]
-    column_ids = column_ids.reshape(-1)
-    labels = jnp.where(wanted[:, None] == column_ids[None, :], 1.0, -1.0).astype(jnp.float32)
-    margin = -labels * pair_scores
-    losses = jnp.sum(jax.nn.softplus(margin), axis=1)
-    weight = (-labels * jax.nn.sigmoid(margin) * (factor / row_count)).astype(jnp.bfloat16)
-
-    parts = cross_rows(weight, plane)
-    grad = line_reduce(*[parts[k * quarter : (k + 1) * quarter] for k in range(LINE)])
-    grad = grad.astype(jnp.bfloat16)
-    grad_response = jnp.zeros((row_count, width), jnp.bfloat16)
-    for k in range(SIDE * CORES):
-        piece = grad[:, k * width : (k + 1) * width]
-        piece = piece if k == 0 else send(piece, MIX[k])
-        grad_response = lax.dynamic_update_slice_in_dim(
-            grad_response, piece, (mp ^ k) * quarter, axis=0
-        )
-    grad_response_y = send(grad_response, ACROSS_Y)
-
-    parts = matmul(weight, held)
-    mine = jnp.concatenate([parts[:, :width], parts[:, 2 * width : 3 * width]], axis=1)
-    away = jnp.concatenate([parts[:, width : 2 * width], parts[:, 3 * width :]], axis=1)
-    mine = mine + send(away.astype(jnp.bfloat16), ACROSS_C).astype(jnp.float32)
-    mine = mine[:, :width] + send(mine[:, width:].astype(jnp.bfloat16), ACROSS_X).astype(
-        jnp.float32
-    )
+    losses, mine, away, parts, second_b, third_b = compare(
+        half, other, held, wanted[:, None], ids.reshape(1, -1), row_count
+    )
+    losses = losses[:, 0]
+    losses = losses[:row_count], send(losses[row_count:], ACROSS_Y)
+
+    mine = mine + send(away, ACROSS_C).astype(jnp.float32)
+    aside = send(mine[:, width:].astype(jnp.bfloat16), ACROSS_X)
+
+    def after(aside, loss):
+        loss = losses[0] + loss
+        return loss, send(loss, ACROSS_X)
+
+    grad, (aside, _), losses = line_reduce(
+        *[parts[k * quarter : (k + 1) * quarter] for k in range(LINE)],
+        second_b,
+        third_b,
+        (aside, losses[1]),
+        after,
+    )
+    mine = mine[:, :width] + aside.astype(jnp.float32)
     mine_y = send(mine.astype(jnp.bfloat16), ACROSS_Y).astype(jnp.float32)
     grad_prompt = (mine[:row_count] + mine_y[row_count:]).astype(jnp.bfloat16)
     grad_prompt_y = (mine[row_count:] + mine_y[:row_count]).astype(jnp.bfloat16)
-
-    losses = losses[:row_count] + send(losses[row_count:], ACROSS_Y)
-    losses = losses + send(losses, ACROSS_X)
+    grad = grad.astype(jnp.bfloat16)
+    gathered = [jnp.zeros((row_count, width), jnp.bfloat16)] * PAIR
+    for k in range(PAIR * SIDE * CORES):
+        pair, away = divmod(k, SIDE * CORES)
+        piece = grad[:, away * width : (away + 1) * width]
+        piece = piece if k == 0 else send(piece, PLANE[k])
+        gathered[pair] = lax.dynamic_update_slice_in_dim(
+            gathered[pair], piece, (mp ^ away) * quarter, axis=0
+        )
+    grad_response, grad_response_y = gathered
+    losses = losses[0] + losses[1]
     losses = losses + send(losses, ACROSS_C)
-    losses, grad_response_y = lax.optimization_barrier((losses, grad_response_y))
 
     grads = [
         grad_prompt,
@@ -289,8 +371,10 @@
         jnp.where(c == 0, grad_response_y, grad_prompt_y),
     ]
     grads = jnp.concatenate(grads, axis=0)
-    third, second, first, own = [matmul(columns[k], grads) for k in (3, 2, 1, 0)]
-    head_grad = line_reduce(own, first, second, third)
+    third = matmul(columns[3], grads)
+    third_b, grads = lax.optimization_barrier((third.astype(jnp.bfloat16), grads))
+    second, first, own = [matmul(columns[k], grads) for k in (2, 1, 0)]
+    head_grad, _, _ = line_reduce(own, first, second, third, second.astype(jnp.bfloat16), third_b)
     return (losses / row_count, head_grad)
 
 

time: 148 us -> 163 us (1.10); the launches traced: 148 us -> 161 us
  local copies, waits for them, and re-layouts: 2.58 us -> 21 us
  waiting for transfers between devices: 69 us -> 64 us
  matrix products: 5.65 us -> 1.91 us
  starting transfers between devices: 55.3 us -> 58.7 us
  Pallas kernels: 4.68 us -> 7.8 us
  other arithmetic: 9.36 us -> 6.42 us
    unnamed x12 -> x53, local copies, waits for them, and re-layouts: 1.61 us -> 16.9 us
    ppermute x44 -> x48, waiting for transfers between devices: 69 us -> 64 us  [send(): return lax.ppermute(block, ('dp', 'mp'), table)]
    pallas_call x0 -> x1, Pallas kernels: none -> 3.71 us  [compare(): pl.pallas_call(kernel, out_shape=[jax.ShapeDtypeStruct((prompt_rows, 1),...]
    ppermute x44 -> x48, starting transfers between devices: 55.3 us -> 58.7 us  [send(): return lax.ppermute(block, ('dp', 'mp'), table)]
    dot_general x2 -> x0, matrix products: 2.26 us -> none  [the longest x1 1.71 us: cross_cols(): lax.dot_general(left_side, righthand_term, (((1,), (1,)), ((), ())), pref...]
    select_n x1, other arithmetic: 3.3 us -> 1.53 us  [full_window(): mine = jnp.where(c == 0, prompts, responses)]
    dot_general x5 -> x4, matrix products: 3.4 us -> 1.91 us  [matmul(): jnp.dot(left_side, righthand_term, preferred_element_type=jnp.float32)]
  transfers between devices with their start and end apart: 44 -> 48, of which waited for: 20 -> 22; matrix products, arithmetic and copies ran while one was open for 10% -> 6% of each run, Pallas kernels for 3% -> 5%
where the time goes in v5:
time: 163 us; the launch traced here: 161 us
  waiting for transfers between devices  64 us (39%)
  starting transfers between devices  58.7 us (36%)
  local copies, waits for them, and re-layouts  21 us (13%)
  Pallas kernels  7.8 us (5%)
  other arithmetic  6.42 us (4%)
  matrix products  1.91 us (1%)
    ppermute x48, waiting for transfers between devices, send(): return lax.ppermute(block, ('dp', 'mp'), table)  64 us
    ppermute x48, starting transfers between devices, send(): return lax.ppermute(block, ('dp', 'mp'), table)  58.7 us
    unnamed x53, local copies, waits for them, and re-layouts  16.9 us
    pallas_call x3, Pallas kernels, project(): pl.pallas_call(kernel, grid_spec=pltpu.PrefetchScalarGridSpec(num_scalar_...  4.09 us
    pallas_call x1, Pallas kernels, compare(): pl.pallas_call(kernel, out_shape=[jax.ShapeDtypeStruct((prompt_rows, 1),...  3.71 us
  transfers between devices with their start and end apart: 48, of which 22 were waited for; matrix products, arithmetic and copies ran while one was open for 6% of the time, Pallas kernels for 5%

profile of v5, /device:TPU:0, one launch (start us, length us, event | category | flops | bytes accessed | tf_op | source)
XLA Modules:
  0.0 161.0 jit_solution(15663735074122682719)
XLA Ops:
  0.6 3.1 %collective-permute-start.2 = (bf16[512,256]{1,0:T(8,128)(2,1)}, bf16[512,256]{1,0:T(8,128)(2,1)S(1)}, u32[]{:S(2)}, u32[]{:S(2)}) collective-permute-start(bf16[512,256]{1,0:T(8,128)(2,1)} %refs_0_.1), channel_id=1, source_target_pairs={{0,8},{1,9},{2,10},{3,11},{4,12},{5,13},{6,14},{7,15},{8,0},{9,1},... | collective-permute-start | bytes 786440 | tf_op jit(solution)/shard_map/ppermute | solution.py:106
  4.4 5.8 %collective-permute-done.2.refs_2_ = bf16[512,256]{1,0:T(8,128)(2,1)S(1)} collective-permute-done((bf16[512,256]{1,0:T(8,128)(2,1)}, bf16[512,256]{1,0:T(8,128)(2,1)S(1)}, u32[]{:S(2)}, u32[]{:S(2)}) %collective-permute-start.2) | collective-permute-done | bytes 262176 | tf_op jit(solution)/shard_map/ppermute | solution.py:106
  17.4 3.1 %collective-permute-done.9.refs_1_ = bf16[512,256]{1,0:T(8,128)(2,1)S(1)} collective-permute-done((bf16[512,256]{1,0:T(8,128)(2,1)}, bf16[512,256]{1,0:T(8,128)(2,1)S(1)}, u32[]{:S(2)}, u32[]{:S(2)}) %collective-permute-start.9) | collective-permute-done | bytes 262176 | tf_op jit(solution)/shard_map/ppermute | solution.py:106
  22.8 2.3 %collective-permute-done.6.refs_1_ = bf16[512,256]{1,0:T(8,128)(2,1)S(1)} collective-permute-done((bf16[512,256]{1,0:T(8,128)(2,1)S(1)}, bf16[512,256]{1,0:T(8,128)(2,1)S(1)}, u32[]{:S(2)}, u32[]{:S(2)}) %collective-permute-start.6) | collective-permute-done | bytes 262176 | tf_op jit(solution)/shard_map/ppermute | solution.py:106
  25.1 3.7 %collective-permute-done.4.refs_5_ = bf16[512,256]{1,0:T(8,128)(2,1)S(1)} collective-permute-done((bf16[512,256]{1,0:T(8,128)(2,1)S(1)}, bf16[512,256]{1,0:T(8,128)(2,1)S(1)}, u32[]{:S(2)}, u32[]{:S(2)}) %collective-permute-start.4) | collective-permute-done | bytes 262176 | tf_op jit(solution)/shard_map/ppermute | solution.py:106
  36.2 2.1 %shard_map.59.refs_6_ = f32[512,256]{1,0:T(8,128)S(1)} custom-call(s32[4]{0:T(128)S(1)} %pad_add_fusion.2.block_ref, bf16[256,4096]{1,0:T(8,128)(2,1)S(1)} %copy-done, bf16[256,4096]{1,0:T(8,128)(2,1)S(1)} %copy-done.2, bf16[512,256]{1,0:T(8,128)(2,1)S(1)} %copy-done.9, bf16[512,256]{1,0:T(8,128)(2,1)S(1)} %copy-done.11, ...), custom_call_target="tpu_custom_call" | custom-call | flops 536870912 | bytes 3145728 | tf_op jit(solution)/shard_map/pallas_call | solution.py:176
  38.3 4.6 %collective-permute-done.8.refs_3_ = bf16[512,256]{1,0:T(8,128)(2,1)S(1)} collective-permute-done((bf16[512,256]{1,0:T(8,128)(2,1)S(1)}, bf16[512,256]{1,0:T(8,128)(2,1)S(1)}, u32[]{:S(2)}, u32[]{:S(2)}) %collective-permute-start.8) | collective-permute-done | bytes 262176 | tf_op jit(solution)/shard_map/ppermute | solution.py:106
  44.6 2.1 %collective-permute-done.5.refs_1_ = bf16[512,256]{1,0:T(8,128)(2,1)S(1)} collective-permute-done((bf16[512,256]{1,0:T(8,128)(2,1)S(1)}, bf16[512,256]{1,0:T(8,128)(2,1)S(1)}, u32[]{:S(2)}, u32[]{:S(2)}) %collective-permute-start.5) | collective-permute-done | bytes 262176 | tf_op jit(solution)/shard_map/ppermute | solution.py:106
  51.3 2.7 %collective-permute-done.12 = bf16[256,256]{1,0:T(8,128)(2,1)S(1)} collective-permute-done((bf16[256,256]{1,0:T(8,128)(2,1)S(1)}, bf16[256,256]{1,0:T(8,128)(2,1)S(1)}, u32[]{:S(2)}, u32[]{:S(2)}) %collective-permute-start.12) | collective-permute-done | bytes 131104 | tf_op jit(solution)/shard_map/ppermute | solution.py:106
  61.8 4.6 %collective-permute-start.18 = (bf16[64,1024]{1,0:T(8,128)(2,1)S(1)}, bf16[64,1024]{1,0:T(8,128)(2,1)S(1)}, u32[]{:S(2)}, u32[]{:S(2)}) collective-permute-start(bf16[64,1024]{1,0:T(8,128)(2,1)S(1)} %pad_maximum_fusion.7.refs_0_), channel_id=1, source_target_pairs={{0,8},{1,9},{2,10},{3,11},{4,12},{5,13},{6,14},{7,15},{8,0},{9,1},... | collective-permute-start | bytes 393224 | tf_op jit(solution)/shard_map/ppermute | solution.py:106
  68.4 2.0 %collective-permute-done.18.refs_1_ = bf16[64,1024]{1,0:T(8,128)(2,1)S(1)} collective-permute-done((bf16[64,1024]{1,0:T(8,128)(2,1)S(1)}, bf16[64,1024]{1,0:T(8,128)(2,1)S(1)}, u32[]{:S(2)}, u32[]{:S(2)}) %collective-permute-start.18) | collective-permute-done | bytes 131104 | tf_op jit(solution)/shard_map/ppermute | solution.py:106
  76.1 7.6 %collective-permute-done.21.refs_3_ = bf16[64,1024]{1,0:T(8,128)(2,1)} collective-permute-done((bf16[64,1024]{1,0:T(8,128)(2,1)S(1)}, bf16[64,1024]{1,0:T(8,128)(2,1)}, u32[]{:S(2)}, u32[]{:S(2)}) %collective-permute-start.21) | collective-permute-done | bytes 131104 | tf_op jit(solution)/shard_map/ppermute | solution.py:106
  89.4 3.7 %shard_map.62 = (f32[512,1]{1,0:T(8,128)S(1)}, f32[512,512]{1,0:T(8,128)S(1)}, bf16[512,512]{1,0:T(8,128)(2,1)}, f32[256,1024]{1,0:T(8,128)S(1)}, bf16[64,1024]{...) custom-call(bf16[512,512]{1,0:T(8,128)(2,1)S(1)} %copy-done.8, bf16[512,512]{1,0:T(8,128)(2,1)S(1)} %copy-done.16, ...), custom_call_target="tpu_custom_call" | custom-call | flops 805306368 | bytes 4718592 | tf_op jit(solution)/shard_map/pallas_call | solution.py:240
  99.2 4.0 %collective-permute-start.23 = (bf16[64,1024]{1,0:T(8,128)(2,1)S(1)}, bf16[64,1024]{1,0:T(8,128)(2,1)S(1)}, u32[]{:S(2)}, u32[]{:S(2)}) collective-permute-start(bf16[64,1024]{1,0:T(8,128)(2,1)S(1)} %copy-done.20), channel_id=1, source_target_pairs={{0,16},{1,17},{2,18},{3,19},{4,20},{5,21},{6,22},{7,23},{24,8},{25... | collective-permute-start | bytes 393224 | tf_op jit(solution)/shard_map/ppermute | solution.py:106
  109.3 3.4 %collective-permute-done.27 = bf16[512,256]{1,0:T(8,128)(2,1)S(1)} collective-permute-done((bf16[512,256]{1,0:T(8,128)(2,1)S(1)}, bf16[512,256]{1,0:T(8,128)(2,1)S(1)}, u32[]{:S(2)}, u32[]{:S(2)}) %collective-permute-start.27) | collective-permute-done | bytes 262176 | tf_op jit(solution)/shard_map/ppermute | solution.py:106
  116.8 2.6 %collective-permute-done.30 = bf16[64,1024]{1,0:T(8,128)(2,1)S(1)} collective-permute-done((bf16[64,1024]{1,0:T(8,128)(2,1)S(1)}, bf16[64,1024]{1,0:T(8,128)(2,1)S(1)}, u32[]{:S(2)}, u32[]{:S(2)}) %collective-permute-start.30) | collective-permute-done | bytes 131104 | tf_op jit(solution)/shard_map/ppermute | solution.py:106
  124.8 3.3 %collective-permute-done.38 = bf16[64,256]{1,0:T(8,128)(2,1)S(1)} collective-permute-done((bf16[64,256]{1,0:T(8,128)(2,1)S(1)}, bf16[64,256]{1,0:T(8,128)(2,1)S(1)}, u32[]{:S(2)}, u32[]{:S(2)}) %collective-permute-start.38) | collective-permute-done | bytes 32800 | tf_op jit(solution)/shard_map/ppermute | solution.py:106
  129.1 3.0 %collective-permute-done.39 = bf16[64,256]{1,0:T(8,128)(2,1)S(1)} collective-permute-done((bf16[64,256]{1,0:T(8,128)(2,1)S(1)}, bf16[64,256]{1,0:T(8,128)(2,1)S(1)}, u32[]{:S(2)}, u32[]{:S(2)}) %collective-permute-start.39) | collective-permute-done | bytes 32800 | tf_op jit(solution)/shard_map/ppermute | solution.py:106
  132.2 4.1 %collective-permute-done.42 = bf16[64,256]{1,0:T(8,128)(2,1)S(1)} collective-permute-done((bf16[64,256]{1,0:T(8,128)(2,1)S(1)}, bf16[64,256]{1,0:T(8,128)(2,1)S(1)}, u32[]{:S(2)}, u32[]{:S(2)}) %collective-permute-start.42) | collective-permute-done | bytes 32800 | tf_op jit(solution)/shard_map/ppermute | solution.py:106
  137.9 3.4 %collective-permute-start.44 = (bf16[512,256]{1,0:T(8,128)(2,1)S(1)}, bf16[512,256]{1,0:T(8,128)(2,1)S(1)}, u32[]{:S(2)}, u32[]{:S(2)}) collective-permute-start(bf16[512,256]{1,0:T(8,128)(2,1)S(1)} %convolution_convert_fusion), channel_id=1, source_target_pairs={{0,8},{1,9},{2,10},{3,11},{4,12},{5,13},{6,14},{7,15},{24,16},{25,... | collective-permute-start | bytes 786440 | tf_op jit(solution)/shard_map/ppermute | solution.py:106
  142.0 4.0 %collective-permute-start.43 = (bf16[512,256]{1,0:T(8,128)(2,1)S(1)}, bf16[512,256]{1,0:T(8,128)(2,1)S(1)}, u32[]{:S(2)}, u32[]{:S(2)}) collective-permute-start(bf16[512,256]{1,0:T(8,128)(2,1)S(1)} %get-tuple-element.54), channel_id=1, source_target_pairs={{0,16},{1,17},{2,18},{3,19},{4,20},{5,21},{6,22},{7,23},{24,8},{25... | collective-permute-start | bytes 786440 | tf_op jit(solution)/shard_map/ppermute | solution.py:106
  147.1 4.5 %collective-permute-done.43 = bf16[512,256]{1,0:T(8,128)(2,1)S(1)} collective-permute-done((bf16[512,256]{1,0:T(8,128)(2,1)S(1)}, bf16[512,256]{1,0:T(8,128)(2,1)S(1)}, u32[]{:S(2)}, u32[]{:S(2)}) %collective-permute-start.43) | collective-permute-done | bytes 262176 | tf_op jit(solution)/shard_map/ppermute | solution.py:106
  151.7 3.8 %collective-permute-start.47 = (bf16[512,256]{1,0:T(8,128)(2,1)S(1)}, bf16[512,256]{1,0:T(8,128)(2,1)S(1)}, u32[]{:S(2)}, u32[]{:S(2)}) collective-permute-start(bf16[512,256]{1,0:T(8,128)(2,1)S(1)} %add_convert_fusion), channel_id=1, source_target_pairs={{0,8},{1,9},{2,10},{3,11},{4,12},{5,13},{6,14},{7,15},{8,0},{9,1},... | collective-permute-start | bytes 786440 | tf_op jit(solution)/shard_map/ppermute | solution.py:106
  156.7 3.4 %collective-permute-done.47 = bf16[512,256]{1,0:T(8,128)(2,1)S(1)} collective-permute-done((bf16[512,256]{1,0:T(8,128)(2,1)S(1)}, bf16[512,256]{1,0:T(8,128)(2,1)S(1)}, u32[]{:S(2)}, u32[]{:S(2)}) %collective-permute-start.47) | collective-permute-done | bytes 262176 | tf_op jit(solution)/shard_map/ppermute | solution.py:106
  (181 shorter events, 72.9 us)
Async XLA Ops:
  0.6 9.6 %collective-permute-start.2 = (bf16[512,256]{1,0:T(8,128)(2,1)}, bf16[512,256]{1,0:T(8,128)(2,1)S(1)}, u32[]{:S(2)}, u32[]{:S(2)}) collective-permute-start(bf16[512,256]{1,0:T(8,128)(2,1)} %refs_0_.1), channel_id=1, source_target_pairs={{0,8},{1,9},{2,10},{3,11},{4,12},{5,13},{6,14},{7,15},{8,0},{9,1},... | collective-permute-start | bytes 786440 | tf_op jit(solution)/shard_map/ppermute | solution.py:106
  10.9 9.5 %collective-permute-start.9 = (bf16[512,256]{1,0:T(8,128)(2,1)}, bf16[512,256]{1,0:T(8,128)(2,1)S(1)}, u32[]{:S(2)}, u32[]{:S(2)}) collective-permute-start(bf16[512,256]{1,0:T(8,128)(2,1)} %refs_0_.1), channel_id=1, source_target_pairs={{0,4},{1,5},{2,6},{3,7},{4,0},{5,1},{6,2},{7,3},{8,12},{9,13},{10,... | collective-permute-start | bytes 786440 | tf_op jit(solution)/shard_map/ppermute | solution.py:106
  12.7 12.5 %collective-permute-start.6 = (bf16[512,256]{1,0:T(8,128)(2,1)S(1)}, bf16[512,256]{1,0:T(8,128)(2,1)S(1)}, u32[]{:S(2)}, u32[]{:S(2)}) collective-permute-start(bf16[512,256]{1,0:T(8,128)(2,1)S(1)} %collective-permute-done.refs_4_), channel_id=1, source_target_pairs={{8,0},{9,1},{10,2},{11,3},{12,4},{13,5},{14,6},{15,7},{16,24},{17,... | collective-permute-start | bytes 786440 | tf_op jit(solution)/shard_map/ppermute | solution.py:106
  14.0 14.8 %collective-permute-start.4 = (bf16[512,256]{1,0:T(8,128)(2,1)S(1)}, bf16[512,256]{1,0:T(8,128)(2,1)S(1)}, u32[]{:S(2)}, u32[]{:S(2)}) collective-permute-start(bf16[512,256]{1,0:T(8,128)(2,1)S(1)} %collective-permute-done.3.refs_0_), channel_id=1, source_target_pairs={{8,0},{9,1},{10,2},{11,3},{12,4},{13,5},{14,6},{15,7},{16,24},{17,... | collective-permute-start | bytes 786440 | tf_op jit(solution)/shard_map/ppermute | solution.py:106
  15.3 14.2 %collective-permute-start.10 = (bf16[512,256]{1,0:T(8,128)(2,1)S(1)}, bf16[512,256]{1,0:T(8,128)(2,1)S(1)}, u32[]{:S(2)}, u32[]{:S(2)}) collective-permute-start(bf16[512,256]{1,0:T(8,128)(2,1)S(1)} %collective-permute-done.2.refs_2_), channel_id=1, source_target_pairs={{0,4},{1,5},{2,6},{3,7},{4,0},{5,1},{6,2},{7,3},{8,12},{9,13},{10,... | collective-permute-start | bytes 786440 | tf_op jit(solution)/shard_map/ppermute | solution.py:106
  15.7 29.0 %collective-permute-start.1 = (bf16[512,256]{1,0:T(8,128)(2,1)S(1)}, bf16[512,256]{1,0:T(8,128)(2,1)S(1)}, u32[]{:S(2)}, u32[]{:S(2)}) collective-permute-start(bf16[512,256]{1,0:T(8,128)(2,1)S(1)} %collective-permute-done.refs_4_), channel_id=1, source_target_pairs={{0,4},{1,5},{2,6},{3,7},{4,0},{5,1},{6,2},{7,3},{8,12},{9,13},{10,... | collective-permute-start | bytes 786440 | tf_op jit(solution)/shard_map/ppermute | solution.py:106
  21.1 17.2 %collective-permute-start.7 = (bf16[512,256]{1,0:T(8,128)(2,1)S(1)}, bf16[512,256]{1,0:T(8,128)(2,1)S(1)}, u32[]{:S(2)}, u32[]{:S(2)}) collective-permute-start(bf16[512,256]{1,0:T(8,128)(2,1)S(1)} %collective-permute-done.3.refs_0_), channel_id=1, source_target_pairs={{0,4},{1,5},{2,6},{3,7},{4,0},{5,1},{6,2},{7,3},{8,12},{9,13},{10,... | collective-permute-start | bytes 786440 | tf_op jit(solution)/shard_map/ppermute | solution.py:106
  25.1 17.8 %collective-permute-start.8 = (bf16[512,256]{1,0:T(8,128)(2,1)S(1)}, bf16[512,256]{1,0:T(8,128)(2,1)S(1)}, u32[]{:S(2)}, u32[]{:S(2)}) collective-permute-start(bf16[512,256]{1,0:T(8,128)(2,1)S(1)} %collective-permute-done.6.refs_1_), channel_id=1, source_target_pairs={{0,4},{1,5},{2,6},{3,7},{4,0},{5,1},{6,2},{7,3},{8,12},{9,13},{10,... | collective-permute-start | bytes 786440 | tf_op jit(solution)/shard_map/ppermute | solution.py:106
  28.8 18.0 %collective-permute-start.5 = (bf16[512,256]{1,0:T(8,128)(2,1)S(1)}, bf16[512,256]{1,0:T(8,128)(2,1)S(1)}, u32[]{:S(2)}, u32[]{:S(2)}) collective-permute-start(bf16[512,256]{1,0:T(8,128)(2,1)S(1)} %collective-permute-done.4.refs_5_), channel_id=1, source_target_pairs={{0,4},{1,5},{2,6},{3,7},{4,0},{5,1},{6,2},{7,3},{8,12},{9,13},{10,... | collective-permute-start | bytes 786440 | tf_op jit(solution)/shard_map/ppermute | solution.py:106
  49.8 24.7 %collective-permute-start.15 = (s32[256]{0:T(256)S(1)}, s32[256]{0:T(256)S(1)}, u32[]{:S(2)}, u32[]{:S(2)}) collective-permute-start(s32[256]{0:T(256)S(1)} %copy-done.25), channel_id=1, source_target_pairs={{0,4},{1,5},{2,6},{3,7},{4,0},{5,1},{6,2},{7,3},{8,12},{9,13},{10,... | collective-permute-start | bytes 3080 | tf_op jit(solution)/shard_map/ppermute | solution.py:106
  54.0 13.1 %collective-permute-start.13 = (bf16[256,512]{1,0:T(8,128)(2,1)S(1)}, bf16[256,512]{1,0:T(8,128)(2,1)S(1)}, u32[]{:S(2)}, u32[]{:S(2)}) collective-permute-start(bf16[256,512]{1,0:T(8,128)(2,1)S(1)} %constant_dynamic-update-slice_fusion), channel_id=1, source_target_pairs={{0,4},{1,5},{2,6},{3,7},{4,0},{5,1},{6,2},{7,3},{8,12},{9,13},{10,... | collective-permute-start | bytes 786440 | tf_op jit(solution)/shard_map/ppermute | solution.py:106
  67.1 16.6 %collective-permute-start.14 = (bf16[512,512]{1,0:T(8,128)(2,1)S(1)}, bf16[512,512]{1,0:T(8,128)(2,1)S(1)}, u32[]{:S(2)}, u32[]{:S(2)}) collective-permute-start(bf16[512,512]{1,0:T(8,128)(2,1)S(1)} %pad_maximum_fusion.5.half_ref), channel_id=1, source_target_pairs={{0,1},{1,0},{2,3},{3,2},{4,5},{5,4},{6,7},{7,6},{8,9},{9,8},{10,11... | collective-permute-start | bytes 1572872 | tf_op jit(solution)/shard_map/ppermute | solution.py:106
  71.7 12.0 %collective-permute-start.22 = (bf16[64,1024]{1,0:T(8,128)(2,1)S(1)}, bf16[64,1024]{1,0:T(8,128)(2,1)}, u32[]{:S(2)}, u32[]{:S(2)}) collective-permute-start(bf16[64,1024]{1,0:T(8,128)(2,1)S(1)} %collective-permute-done.18.refs_1_), channel_id=1, source_target_pairs={{8,24},{9,25},{10,26},{11,27},{12,28},{13,29},{14,30},{15,31},{16,... | collective-permute-start | bytes 393224 | tf_op jit(solution)/shard_map/ppermute | solution.py:106
  73.0 10.7 %collective-permute-start.21 = (bf16[64,1024]{1,0:T(8,128)(2,1)S(1)}, bf16[64,1024]{1,0:T(8,128)(2,1)}, u32[]{:S(2)}, u32[]{:S(2)}) collective-permute-start(bf16[64,1024]{1,0:T(8,128)(2,1)S(1)} %collective-permute-done.20.refs_4_), channel_id=1, source_target_pairs={{8,0},{9,1},{10,2},{11,3},{12,4},{13,5},{14,6},{15,7},{16,24},{17,... | collective-permute-start | bytes 393224 | tf_op jit(solution)/shard_map/ppermute | solution.py:106
  74.5 31.2 %collective-permute-start.33 = (bf16[256,2048]{1,0:T(8,128)(2,1)}, bf16[256,2048]{1,0:T(8,128)(2,1)}, u32[]{:S(2)}, u32[]{:S(2)}) collective-permute-start(bf16[256,2048]{1,0:T(8,128)(2,1)} %pad_maximum_fusion), channel_id=1, source_target_pairs={{0,4},{1,5},{2,6},{3,7},{4,0},{5,1},{6,2},{7,3},{8,12},{9,13},{10,... | collective-permute-start | bytes 3145736 | tf_op jit(solution)/shard_map/ppermute | solution.py:106
  97.2 12.1 %collective-permute-start.24 = (bf16[64,1024]{1,0:T(8,128)(2,1)S(1)}, bf16[64,1024]{1,0:T(8,128)(2,1)S(1)}, u32[]{:S(2)}, u32[]{:S(2)}) collective-permute-start(bf16[64,1024]{1,0:T(8,128)(2,1)S(1)} %copy-done.18), channel_id=1, source_target_pairs={{0,8},{1,9},{2,10},{3,11},{4,12},{5,13},{6,14},{7,15},{24,16},{25,... | collective-permute-start | bytes 393224 | tf_op jit(solution)/shard_map/ppermute | solution.py:106
  98.5 10.8 %collective-permute-start.25 = (bf16[64,1024]{1,0:T(8,128)(2,1)S(1)}, bf16[64,1024]{1,0:T(8,128)(2,1)S(1)}, u32[]{:S(2)}, u32[]{:S(2)}) collective-permute-start(bf16[64,1024]{1,0:T(8,128)(2,1)S(1)} %copy-done.18), channel_id=1, source_target_pairs={{8,16},{9,17},{10,18},{11,19},{12,20},{13,21},{14,22},{15,23},{16,... | collective-permute-start | bytes 393224 | tf_op jit(solution)/shard_map/ppermute | solution.py:106
  99.2 10.1 %collective-permute-start.23 = (bf16[64,1024]{1,0:T(8,128)(2,1)S(1)}, bf16[64,1024]{1,0:T(8,128)(2,1)S(1)}, u32[]{:S(2)}, u32[]{:S(2)}) collective-permute-start(bf16[64,1024]{1,0:T(8,128)(2,1)S(1)} %copy-done.20), channel_id=1, source_target_pairs={{0,16},{1,17},{2,18},{3,19},{4,20},{5,21},{6,22},{7,23},{24,8},{25... | collective-permute-start | bytes 393224 | tf_op jit(solution)/shard_map/ppermute | solution.py:106
  109.3 27.3 %collective-permute-start.34 = (bf16[256,2048]{1,0:T(8,128)(2,1)}, bf16[256,2048]{1,0:T(8,128)(2,1)S(1)}, u32[]{:S(2)}, u32[]{:S(2)}) collective-permute-start(bf16[256,2048]{1,0:T(8,128)(2,1)} %collective-permute-done.33), channel_id=1, source_target_pairs={{0,1},{1,0},{2,3},{3,2},{4,5},{5,4},{6,7},{7,6},{8,9},{9,8},{10,11... | collective-permute-start | bytes 3145736 | tf_op jit(solution)/shard_map/ppermute | solution.py:106
  116.0 20.3 %collective-permute-start.35 = (bf16[512,256]{1,0:T(8,128)(2,1)S(1)}, bf16[512,256]{1,0:T(8,128)(2,1)S(1)}, u32[]{:S(2)}, u32[]{:S(2)}) collective-permute-start(bf16[512,256]{1,0:T(8,128)(2,1)S(1)} %get-tuple-element.66), channel_id=1, source_target_pairs={{0,4},{1,5},{2,6},{3,7},{4,0},{5,1},{6,2},{7,3},{8,12},{9,13},{10,... | collective-permute-start | bytes 786440 | tf_op jit(solution)/shard_map/ppermute | solution.py:106
  120.1 12.0 %collective-permute-start.40 = (bf16[64,256]{1,0:T(8,128)(2,1)S(1)}, bf16[64,256]{1,0:T(8,128)(2,1)S(1)}, u32[]{:S(2)}, u32[]{:S(2)}) collective-permute-start(bf16[64,256]{1,0:T(8,128)(2,1)S(1)} %get-tuple-element.95), channel_id=1, source_target_pairs={{0,5},{1,4},{2,7},{3,6},{4,1},{5,0},{6,3},{7,2},{8,13},{9,12},{10,... | collective-permute-start | bytes 98312 | tf_op jit(solution)/shard_map/ppermute | solution.py:106
  122.6 9.6 %collective-permute-start.41 = (bf16[64,256]{1,0:T(8,128)(2,1)S(1)}, bf16[64,256]{1,0:T(8,128)(2,1)S(1)}, u32[]{:S(2)}, u32[]{:S(2)}) collective-permute-start(bf16[64,256]{1,0:T(8,128)(2,1)S(1)} %get-tuple-element.94), channel_id=1, source_target_pairs={{0,6},{1,7},{2,4},{3,5},{4,2},{5,3},{6,0},{7,1},{8,14},{9,15},{10,... | collective-permute-start | bytes 98312 | tf_op jit(solution)/shard_map/ppermute | solution.py:106
  137.9 9.2 %collective-permute-start.44 = (bf16[512,256]{1,0:T(8,128)(2,1)S(1)}, bf16[512,256]{1,0:T(8,128)(2,1)S(1)}, u32[]{:S(2)}, u32[]{:S(2)}) collective-permute-start(bf16[512,256]{1,0:T(8,128)(2,1)S(1)} %convolution_convert_fusion), channel_id=1, source_target_pairs={{0,8},{1,9},{2,10},{3,11},{4,12},{5,13},{6,14},{7,15},{24,16},{25,... | collective-permute-start | bytes 786440 | tf_op jit(solution)/shard_map/ppermute | solution.py:106
  142.0 9.6 %collective-permute-start.43 = (bf16[512,256]{1,0:T(8,128)(2,1)S(1)}, bf16[512,256]{1,0:T(8,128)(2,1)S(1)}, u32[]{:S(2)}, u32[]{:S(2)}) collective-permute-start(bf16[512,256]{1,0:T(8,128)(2,1)S(1)} %get-tuple-element.54), channel_id=1, source_target_pairs={{0,16},{1,17},{2,18},{3,19},{4,20},{5,21},{6,22},{7,23},{24,8},{25... | collective-permute-start | bytes 786440 | tf_op jit(solution)/shard_map/ppermute | solution.py:106
  (50 other events, 207.1 us)

commit v6 on v5

--- a/solution.py
+++ b/solution.py
@@ -108,7 +108,8 @@
 
 ACROSS_Y = routes(lambda z, y, x, c: (z, 1 - y, x, c))
 ACROSS_X = routes(lambda z, y, x, c: (z, y, 1 - x, c))
-ACROSS_XY = routes(lambda z, y, x, c: (z, 1 - y, 1 - x, c))
+Y_ENDS = routes(lambda z, y, x, c: (z, 1 - y, x, c) if z in (0, 3) else None)
+Y_MIDDLE = routes(lambda z, y, x, c: (z, 1 - y, x, c) if z in (1, 2) else None)
 ACROSS_C = routes(lambda z, y, x, c: (z, y, x, 1 - c))
 PAIRS = along_line({0: 1, 1: 0, 2: 3, 3: 2})
 MIDDLE = along_line({1: 2, 2: 1})
@@ -116,10 +117,7 @@
 INWARD = along_line({0: 1, 3: 2})
 TWO_OUT = along_line({1: 3, 2: 0})
 TWO_IN = along_line({3: 1, 0: 2})
-PLANE = [
-    routes(lambda z, y, x, c, k=k: (z, y ^ (k >> 2), x ^ (k >> 1 & 1), c ^ (k & 1)))
-    for k in range(PAIR * SIDE * CORES)
-]
+MIX = [routes(lambda z, y, x, c, k=k: (z, y, x ^ (k >> 1), c ^ (k & 1))) for k in range(4)]
 
 
 def line_gather(block):
@@ -139,51 +137,79 @@
     return own + last.astype(jnp.float32) + paired.astype(jnp.float32), beside, later
 
 
+def place(buffer):
+    return pltpu.VMEM(buffer.shape, buffer.dtype)
+
+
 def project(prompts, responses, blocks, weights, total, kind):
     row_count = prompts.shape[0]
     depth, width = weights[0][0].shape
     count = len(weights)
     terms = [term for weight in weights for term in weight]
 
-    def kernel(block_ref, prompt_ref, response_ref, *refs):
-        term_refs = list(refs[: len(terms)])
-        total_ref, out_ref, sum_ref = refs[len(terms)], refs[-2], refs[-1]
-        step = pl.program_id(0)
-
-        @pl.when(step == 0)
-        def _():
-            sum_ref[...] = total_ref[...] if total is not None else jnp.zeros_like(sum_ref)
-
+    def kernel(block_ref, *refs):
+        arrays, term_refs, refs = refs[:2], refs[2 : 2 + len(terms)], refs[2 + len(terms) :]
+        if total is not None:
+            total_ref, *refs = refs
+        out_ref, feature_buf, term_buf, sum_buf, out_buf, term_sem, feature_sem, sem = refs
+        loads, weight_loads = [], []
+        at = 0
+        if total is not None:
+            total_load = pltpu.make_async_copy(total_ref, sum_buf, sem.at[0])
+            total_load.start()
         for k, weight in enumerate(weights):
-            mine = [term_refs.pop(0) for _ in weight]
-
-            @pl.when(step == k)
-            def _(mine=mine):
-                block = mine[0][...]
-                for ref in mine[1:]:
-                    block = block + ref[...]
-                sum_ref[:row_count] += matmul(prompt_ref[...], block)
-                sum_ref[row_count:] += matmul(response_ref[...], block)
-
-        @pl.when(step == count - 1)
-        def _():
-            out_ref[...] = sum_ref[...].astype(out_ref.dtype)
-
-    whole = pl.BlockSpec((2 * row_count, width), lambda i, block: (0, 0))
-    piece = pl.BlockSpec((row_count, depth), lambda i, block: (0, block[i]))
-    term = pl.BlockSpec((depth, width), lambda i, block: (0, 0))
+            start = pl.multiple_of(block_ref[k] * depth, depth)
+            for array in range(2):
+                load = pltpu.make_async_copy(
+                    arrays[array].at[:, pl.ds(start, depth)],
+                    feature_buf.at[k, array],
+                    feature_sem.at[k, array],
+                )
+                load.start()
+                loads.append(load)
+            weight_loads.append([])
+            for _ in weight:
+                load = pltpu.make_async_copy(term_refs[at], term_buf.at[at], term_sem.at[at])
+                load.start()
+                weight_loads[-1].append((load, at))
+                at += 1
+        if total is not None:
+            total_load.wait()
+        for k in range(count):
+            block = None
+            for load, at in weight_loads[k]:
+                load.wait()
+                block = term_buf[at] if block is None else block + term_buf[at]
+            for array in range(2):
+                loads[2 * k + array].wait()
+                rows = slice(array * row_count, (array + 1) * row_count)
+                part = matmul(feature_buf[k, array], block)
+                if k == 0 and total is None:
+                    sum_buf[rows] = part
+                else:
+                    sum_buf[rows] += part
+        out_buf[...] = sum_buf[...].astype(out_buf.dtype)
+        store = pltpu.make_async_copy(out_buf, out_ref, sem.at[1])
+        store.start()
+        store.wait()
+
+    anywhere = pl.BlockSpec(memory_space=pl.ANY)
     operands = [prompts, responses, *terms] + ([total] if total is not None else [])
     return pl.pallas_call(
         kernel,
-        grid_spec=pltpu.PrefetchScalarGridSpec(
-            num_scalar_prefetch=1,
-            grid=(count,),
-            in_specs=[piece, piece] + [term] * len(terms) + [whole] * (total is not None),
-            out_specs=whole,
-            scratch_shapes=[pltpu.VMEM((2 * row_count, width), jnp.float32)],
-        ),
+        in_specs=[pl.BlockSpec(memory_space=pltpu.SMEM)] + [anywhere] * len(operands),
+        out_specs=anywhere,
+        scratch_shapes=[
+            pltpu.VMEM((count, 2, row_count, depth), jnp.bfloat16),
+            pltpu.VMEM((len(terms), depth, width), jnp.bfloat16),
+            pltpu.VMEM((2 * row_count, width), jnp.float32),
+            pltpu.VMEM((2 * row_count, width), kind),
+            pltpu.SemaphoreType.DMA((len(terms),)),
+            pltpu.SemaphoreType.DMA((count, 2)),
+            pltpu.SemaphoreType.DMA((2,)),
+        ],
         out_shape=jax.ShapeDtypeStruct((2 * row_count, width), kind),
-        compiler_params=pltpu.CompilerParams(vmem_limit_bytes=32 * 1024 * 1024),
+        compiler_params=pltpu.CompilerParams(vmem_limit_bytes=16 * 1024 * 1024),
         cost_estimate=pl.CostEstimate(
             flops=4 * count * row_count * depth * width,
             bytes_accessed=4 * count * row_count * depth + 2 * len(terms) * depth * width,
@@ -195,66 +221,97 @@
 def compare(half, other, held, wanted, ids, row_count):
     prompt_rows, width = half.shape[0], half.shape[1] // 2
     quarter = held[0][0].shape[0]
-    count = len(held) * quarter
+    count, full = len(held) * quarter, 4 * width
     factor = LOGIT_SCALE / math.sqrt(E)
-    terms = [term for block in held for term in block]
-
-    def kernel(half_ref, other_ref, wanted_ref, ids_ref, *refs):
-        term_refs, refs = list(refs[: len(terms)]), refs[len(terms) :]
-        loss_ref, mine_ref, away_ref, parts_ref, second_ref, third_ref, rows_ref = refs
+    operands = [wanted, ids, half, other] + [term for block in held for term in block]
+    results = [
+        jax.ShapeDtypeStruct((prompt_rows, 1), jnp.float32),
+        jax.ShapeDtypeStruct((prompt_rows, 2 * width), jnp.float32),
+        jax.ShapeDtypeStruct((prompt_rows, 2 * width), jnp.bfloat16),
+        jax.ShapeDtypeStruct((count, full), jnp.float32),
+        jax.ShapeDtypeStruct((quarter, full), jnp.bfloat16),
+        jax.ShapeDtypeStruct((quarter, full), jnp.bfloat16),
+    ]
+
+    def kernel(*refs):
+        sources, refs = refs[: len(operands)], refs[len(operands) :]
+        goals, refs = refs[: len(results)], refs[len(results) :]
+        buffers, refs = refs[: len(operands)], refs[len(operands) :]
+        outs, (rows_buf, load_sem, store_sem) = refs[: len(results)], refs[len(results) :]
+        loads = [
+            pltpu.make_async_copy(source, buffer, load_sem.at[k])
+            for k, (source, buffer) in enumerate(zip(sources, buffers))
+        ]
+        stores = [
+            pltpu.make_async_copy(out, goal, store_sem.at[k])
+            for k, (out, goal) in enumerate(zip(outs, goals))
+        ]
+        for load in loads:
+            load.start()
+        for load in loads:
+            load.wait()
+        wanted_buf, ids_buf, half_buf, other_buf, *term_bufs = buffers
+        loss_buf, mine_buf, away_buf, parts_buf, second_buf, third_buf = outs
         for k, block in enumerate(held):
-            mine = [term_refs.pop(0)[...] for _ in block]
-            rows_ref[k * quarter : (k + 1) * quarter] = sum(mine[1:], mine[0])
-        sources = [
-            (half_ref, 0, mine_ref, 0),
-            (other_ref, 0, away_ref, 0),
-            (half_ref, 1, mine_ref, 1),
-            (other_ref, 1, away_ref, 1),
+            mine = [term_bufs.pop(0)[...] for _ in block]
+            rows_buf[k * quarter : (k + 1) * quarter] = sum(mine[1:], mine[0])
+        places = [
+            (half_buf, 0, mine_buf),
+            (other_buf, 0, away_buf),
+            (half_buf, 1, mine_buf),
+            (other_buf, 1, away_buf),
         ]
         scores = jnp.zeros((prompt_rows, count), jnp.float32)
-        for k, (ref, place, _, _) in enumerate(sources):
+        for k, (buffer, at, _) in enumerate(places):
             scores += cross_cols(
-                ref[:, place * width : (place + 1) * width],
-                rows_ref[:, k * width : (k + 1) * width],
+                buffer[:, at * width : (at + 1) * width], rows_buf[:, k * width : (k + 1) * width]
             )
         scores = scores * factor + LOGIT_BIAS
-        match = wanted_ref[...] == ids_ref[...]
+        match = wanted_buf[...] == ids_buf[...]
         margin = jnp.where(match, -scores, scores)
         small = jnp.exp(-jnp.abs(margin))
-        loss_ref[...] = jnp.sum(
-            jnp.maximum(margin, 0.0) + jnp.log1p(small), axis=1, keepdims=True
-        )
         share = jnp.where(margin >= 0.0, 1.0, small) / (1.0 + small)
         share = share * (factor / row_count)
         weight = jnp.where(match, -share, share).astype(jnp.bfloat16)
-        for k, (ref, place, out, goal) in enumerate(sources):
+        for k, (buffer, at, _) in enumerate(places):
             columns = slice(k * width, (k + 1) * width)
-            part = cross_rows(weight, ref[:, place * width : (place + 1) * width])
-            parts_ref[:, columns] = part
-            second_ref[:, columns] = part[2 * quarter : 3 * quarter].astype(jnp.bfloat16)
-            third_ref[:, columns] = part[3 * quarter :].astype(jnp.bfloat16)
-            part = matmul(weight, rows_ref[:, columns])
-            out[:, goal * width : (goal + 1) * width] = part.astype(out.dtype)
-
-    full = half.shape[1] * 2
+            part = cross_rows(weight, buffer[:, at * width : (at + 1) * width])
+            parts_buf[:, columns] = part
+            second_buf[:, columns] = part[2 * quarter : 3 * quarter].astype(jnp.bfloat16)
+            third_buf[:, columns] = part[3 * quarter :].astype(jnp.bfloat16)
+        for store in stores[3:]:
+            store.start()
+        for k, (_, at, out) in enumerate(places):
+            part = matmul(weight, rows_buf[:, k * width : (k + 1) * width])
+            out[:, at * width : (at + 1) * width] = part.astype(out.dtype)
+        for store in stores[1:3]:
+            store.start()
+        loss_buf[...] = jnp.sum(
+            jnp.maximum(margin, 0.0) + jnp.log1p(small), axis=1, keepdims=True
+        )
+        stores[0].start()
+        for store in stores:
+            store.wait()
+
+    anywhere = pl.BlockSpec(memory_space=pl.ANY)
     return pl.pallas_call(
         kernel,
-        out_shape=[
-            jax.ShapeDtypeStruct((prompt_rows, 1), jnp.float32),
-            jax.ShapeDtypeStruct((prompt_rows, 2 * width), jnp.float32),
-            jax.ShapeDtypeStruct((prompt_rows, 2 * width), jnp.bfloat16),
-            jax.ShapeDtypeStruct((count, full), jnp.float32),
-            jax.ShapeDtypeStruct((quarter, full), jnp.bfloat16),
-            jax.ShapeDtypeStruct((quarter, full), jnp.bfloat16),
+        in_specs=[anywhere] * len(operands),
+        out_specs=[anywhere] * len(results),
+        out_shape=results,
+        scratch_shapes=[place(array) for array in operands + results]
+        + [
+            pltpu.VMEM((count, full), jnp.bfloat16),
+            pltpu.SemaphoreType.DMA((len(operands),)),
+            pltpu.SemaphoreType.DMA((len(results),)),
         ],
-        scratch_shapes=[pltpu.VMEM((count, full), jnp.bfloat16)],
-        compiler_params=pltpu.CompilerParams(vmem_limit_bytes=32 * 1024 * 1024),
+        compiler_params=pltpu.CompilerParams(vmem_limit_bytes=24 * 1024 * 1024),
         cost_estimate=pl.CostEstimate(
             flops=6 * prompt_rows * count * full,
             bytes_accessed=6 * prompt_rows * full + 6 * count * full,
             transcendentals=2 * prompt_rows * count,
         ),
-    )(half, other, wanted, ids, *terms)
+    )(*operands)
 
 
 def full_window(prompts, responses, head_projection_matrix, positive):
@@ -271,12 +328,26 @@
     here = [line * PAIR + y for line in lines]
     there = [line * PAIR + 1 - y for line in lines]
     own = head_projection_matrix
-    first, middle = send(own, PAIRS), send(own, MIDDLE)
-    inner, outer = send(first, MIDDLE), send(middle, OUTWARD)
-    last = send(inner, OUTWARD)
-    own_y, first_y, middle_y, inner_y, outer_y, last_y = [
-        send(block, ACROSS_Y) for block in (own, first, middle, inner, outer, last)
-    ]
+    first, middle, own_y, wanted = lax.optimization_barrier(
+        (
+            send(own, PAIRS),
+            send(own, MIDDLE),
+            send(own, ACROSS_Y),
+            jnp.concatenate([positive, send(positive, ACROSS_Y)], axis=0)[:, None],
+        )
+    )
+    inner, outer, first_y = lax.optimization_barrier(
+        (send(first, MIDDLE), send(middle, OUTWARD), send(first, ACROSS_Y))
+    )
+    last, middle_y, inner_y, outer_y = lax.optimization_barrier(
+        (
+            send(inner, OUTWARD),
+            send(middle, Y_MIDDLE),
+            send(inner, Y_MIDDLE),
+            send(outer, Y_ENDS),
+        )
+    )
+    last_y = send(last, Y_ENDS)
     emb = project(
         prompts,
         responses,
@@ -299,16 +370,15 @@
     pieces = []
     for k in range(SIDE * CORES):
         piece = lax.dynamic_slice_in_dim(response_emb, (mp ^ k) * quarter, quarter, axis=0)
-        pieces.append(piece if k == 0 else send(piece, PLANE[k]))
-    prompt_emb, pieces[1] = lax.optimization_barrier((prompt_emb, pieces[1]))
+        pieces.append(piece if k == 0 else send(piece, MIX[k]))
     response_rows = jnp.concatenate(pieces, axis=1)
+    prompt_emb, response_rows = lax.optimization_barrier((prompt_emb, response_rows))
     first, second, third = line_gather(response_rows)
     held = [(response_rows,), (first,), second, third]
 
     near = jnp.concatenate([prompt_emb, send(prompt_emb, ACROSS_X)], axis=1)
     half = jnp.concatenate([near, send(near, ACROSS_Y)], axis=0)
     other = send(half, ACROSS_C)
-    wanted = jnp.concatenate([positive, send(positive, ACROSS_Y)], axis=0)
     ids = ((jnp.stack(lines) * PAIR + y) * row_count + mp * quarter)[:, None] + lax.iota(
         jnp.int32, quarter
     )[None, :]
@@ -328,7 +398,7 @@
     columns = lax.optimization_barrier(columns)
 
     losses, mine, away, parts, second_b, third_b = compare(
-        half, other, held, wanted[:, None], ids.reshape(1, -1), row_count
+        half, other, held, wanted, ids.reshape(1, -1), row_count
     )
     losses = losses[:, 0]
     losses = losses[:row_count], send(losses[row_count:], ACROSS_Y)
@@ -352,15 +422,14 @@
     grad_prompt = (mine[:row_count] + mine_y[row_count:]).astype(jnp.bfloat16)
     grad_prompt_y = (mine[row_count:] + mine_y[:row_count]).astype(jnp.bfloat16)
     grad = grad.astype(jnp.bfloat16)
-    gathered = [jnp.zeros((row_count, width), jnp.bfloat16)] * PAIR
-    for k in range(PAIR * SIDE * CORES):
-        pair, away = divmod(k, SIDE * CORES)
-        piece = grad[:, away * width : (away + 1) * width]
-        piece = piece if k == 0 else send(piece, PLANE[k])
-        gathered[pair] = lax.dynamic_update_slice_in_dim(
-            gathered[pair], piece, (mp ^ away) * quarter, axis=0
+    grad_response = jnp.zeros((row_count, width), jnp.bfloat16)
+    for k in range(SIDE * CORES):
+        piece = grad[:, k * width : (k + 1) * width]
+        piece = piece if k == 0 else send(piece, MIX[k])
+        grad_response = lax.dynamic_update_slice_in_dim(
+            grad_response, piece, (mp ^ k) * quarter, axis=0
         )
-    grad_response, grad_response_y = gathered
+    grad_response_y = send(grad_response, ACROSS_Y)
     losses = losses[0] + losses[1]
     losses = losses + send(losses, ACROSS_C)
 

time: 163 us -> 162 us (level)
  waiting for transfers between devices: 64 us -> 59.8 us
  Pallas kernels: 7.8 us -> 10.9 us
    ppermute x48 -> x45, waiting for transfers between devices: 64 us -> 59.8 us  [send(): return lax.ppermute(block, ('dp', 'mp'), table)]
    pallas_call x4, Pallas kernels: 7.8 us -> 10.9 us  [the longest x3 5.9 us: project(): pl.pallas_call(kernel, in_specs=[pl.BlockSpec(memory_space=pltpu.SMEM)] +...]
    ppermute x48 -> x45, starting transfers between devices: 58.7 us -> 57.9 us  [send(): return lax.ppermute(block, ('dp', 'mp'), table)]
    unnamed x53 -> x59, local copies, waits for them, and re-layouts: 16.9 us -> 17.4 us
  transfers between devices with their start and end apart: 48 -> 45, of which waited for: 22 -> 18; matrix products, arithmetic and copies ran while one was open for 6% -> 7% of each run, Pallas kernels for 5% -> 6%
where the time goes in v6:
time: 162 us; the launch traced here: 160 us
  waiting for transfers between devices  59.8 us (37%)
  starting transfers between devices  57.9 us (36%)
  local copies, waits for them, and re-layouts  21.4 us (13%)
  Pallas kernels  10.9 us (7%)
  other arithmetic  7.14 us (4%)
  matrix products  1.91 us (1%)
    ppermute x45, waiting for transfers between devices, send(): return lax.ppermute(block, ('dp', 'mp'), table)  59.8 us
    ppermute x45, starting transfers between devices, send(): return lax.ppermute(block, ('dp', 'mp'), table)  57.9 us
    unnamed x59, local copies, waits for them, and re-layouts  17.4 us
    pallas_call x3, Pallas kernels, project(): pl.pallas_call(kernel, in_specs=[pl.BlockSpec(memory_space=pltpu.SMEM)] +...  5.9 us
    pallas_call x1, Pallas kernels, compare(): pl.pallas_call(kernel, in_specs=[anywhere] * len(operands), out_specs=[an...  4.99 us
  transfers between devices with their start and end apart: 45, of which 18 were waited for; matrix products, arithmetic and copies ran while one was open for 7% of the time, Pallas kernels for 6%

profile of v6, /device:TPU:0, one launch (start us, length us, event | category | flops | bytes accessed | tf_op | source)
XLA Modules:
  0.0 160.3 jit_solution(17678525841226304759)
XLA Ops:
  0.6 3.1 %collective-permute-start = (bf16[512,256]{1,0:T(8,128)(2,1)}, bf16[512,256]{1,0:T(8,128)(2,1)S(1)}, u32[]{:S(2)}, u32[]{:S(2)}) collective-permute-start(bf16[512,256]{1,0:T(8,128)(2,1)} %refs_2_.1), channel_id=1, source_target_pairs={{0,8},{1,9},{2,10},{3,11},{4,12},{5,13},{6,14},{7,15},{8,0},{9,1},... | collective-permute-start | bytes 786440 | tf_op jit(solution)/shard_map/ppermute | solution.py:106
  6.5 6.0 %collective-permute-done.3 = s32[256]{0:T(256)S(1)} collective-permute-done((s32[256]{0:T(256)}, s32[256]{0:T(256)S(1)}, u32[]{:S(2)}, u32[]{:S(2)}) %collective-permute-start.3) | collective-permute-done | bytes 1056 | tf_op jit(solution)/shard_map/ppermute | solution.py:106
  17.5 8.1 %collective-permute-done.5.refs_3_ = bf16[512,256]{1,0:T(8,128)(2,1)S(1)} collective-permute-done((bf16[512,256]{1,0:T(8,128)(2,1)S(1)}, bf16[512,256]{1,0:T(8,128)(2,1)S(1)}, u32[]{:S(2)}, u32[]{:S(2)}) %collective-permute-start.5) | collective-permute-done | bytes 262176 | tf_op jit(solution)/shard_map/ppermute | solution.py:106
  28.3 3.4 %collective-permute-start.10 = (bf16[512,256]{1,0:T(8,128)(2,1)S(1)}, bf16[512,256]{1,0:T(8,128)(2,1)S(1)}, u32[]{:S(2)}, u32[]{:S(2)}) collective-permute-start(bf16[512,256]{1,0:T(8,128)(2,1)S(1)} %collective-permute-done.5.refs_3_), channel_id=1, source_target_pairs={{0,4},{1,5},{2,6},{3,7},{4,0},{5,1},{6,2},{7,3},{24,28},{25,29},{2... | collective-permute-start | bytes 786440 | tf_op jit(solution)/shard_map/ppermute | solution.py:106
  32.4 3.9 %collective-permute-done.7.refs_7_ = bf16[512,256]{1,0:T(8,128)(2,1)} collective-permute-done((bf16[512,256]{1,0:T(8,128)(2,1)S(1)}, bf16[512,256]{1,0:T(8,128)(2,1)}, u32[]{:S(2)}, u32[]{:S(2)}) %collective-permute-start.7) | collective-permute-done | bytes 262176 | tf_op jit(solution)/shard_map/ppermute | solution.py:106
  37.8 3.6 %collective-permute-start.11 = (bf16[512,256]{1,0:T(8,128)(2,1)}, bf16[512,256]{1,0:T(8,128)(2,1)S(1)}, u32[]{:S(2)}, u32[]{:S(2)}) collective-permute-start(bf16[512,256]{1,0:T(8,128)(2,1)} %collective-permute-done.7.refs_7_), channel_id=1, source_target_pairs={{0,4},{1,5},{2,6},{3,7},{4,0},{5,1},{6,2},{7,3},{24,28},{25,29},{2... | collective-permute-start | bytes 786440 | tf_op jit(solution)/shard_map/ppermute | solution.py:106
  41.6 1.6 copy-done
  46.7 2.6 %shard_map.59.refs_8_ = f32[512,256]{1,0:T(8,128)S(1)} custom-call(s32[4]{0:T(128)S(1)} %pad_add_fusion.2.block_ref, bf16[256,4096]{1,0:T(8,128)(2,1)S(1)} %copy-done, bf16[256,4096]{1,0:T(8,128)(2,1)S(1)} %copy-done.2, bf16[512,256]{1,0:T(8,128)(2,1)S(1)} %copy-done.9, bf16[512,256]{1,0:T(8,128)(2,1)S(1)} %collective-permute-done.2.refs_3_, ...), custom_call_target="tpu_custom_call" | custom-call | flops 536870912 | bytes 3145728 | tf_op jit(solution)/shard_map/pallas_call | solution.py:198
  49.3 2.5 %shard_map.60.refs_4_ = f32[512,256]{1,0:T(8,128)S(1)} custom-call(s32[3]{0:T(128)S(1)} %pad_add_fusion.1.block_ref, bf16[256,4096]{1,0:T(8,128)(2,1)S(1)} %copy-done.1, bf16[256,4096]{1,0:T(8,128)(2,1)S(1)} %copy-done.3, bf16[512,256]{1,0:T(8,128)(2,1)S(1)} %collective-permute-done.4.refs_2_, bf16[512,256]{1,0:T(8,128)(2,1)S(1)} %copy-done.11, ...), custom_call_target="tpu_custom_call" | custom-call | flops 402653184 | bytes 3145728 | tf_op jit(solution)/shard_map/pallas_call | solution.py:198
  54.6 2.1 %collective-permute-done.13 = bf16[64,256]{1,0:T(8,128)(2,1)S(1)} collective-permute-done((bf16[64,256]{1,0:T(8,128)(2,1)S(1)}, bf16[64,256]{1,0:T(8,128)(2,1)S(1)}, u32[]{:S(2)}, u32[]{:S(2)}) %collective-permute-start.13) | collective-permute-done | bytes 32800 | tf_op jit(solution)/shard_map/ppermute | solution.py:106
  58.7 4.7 %collective-permute-done.15 = bf16[256,256]{1,0:T(8,128)(2,1)S(1)} collective-permute-done((bf16[256,256]{1,0:T(8,128)(2,1)S(1)}, bf16[256,256]{1,0:T(8,128)(2,1)S(1)}, u32[]{:S(2)}, u32[]{:S(2)}) %collective-permute-start.15) | collective-permute-done | bytes 131104 | tf_op jit(solution)/shard_map/ppermute | solution.py:106
  66.5 3.1 %collective-permute-start.18 = (bf16[64,1024]{1,0:T(8,128)(2,1)S(1)}, bf16[64,1024]{1,0:T(8,128)(2,1)S(1)}, u32[]{:S(2)}, u32[]{:S(2)}) collective-permute-start(bf16[64,1024]{1,0:T(8,128)(2,1)S(1)} %pad_maximum_fusion.7.refs_4_), channel_id=1, source_target_pairs={{0,8},{1,9},{2,10},{3,11},{4,12},{5,13},{6,14},{7,15},{8,0},{9,1},... | collective-permute-start | bytes 393224 | tf_op jit(solution)/shard_map/ppermute | solution.py:106
  79.3 8.2 %collective-permute-done.21.refs_7_ = bf16[64,1024]{1,0:T(8,128)(2,1)} collective-permute-done((bf16[64,1024]{1,0:T(8,128)(2,1)S(1)}, bf16[64,1024]{1,0:T(8,128)(2,1)}, u32[]{:S(2)}, u32[]{:S(2)}) %collective-permute-start.21) | collective-permute-done | bytes 131104 | tf_op jit(solution)/shard_map/ppermute | solution.py:106
  93.2 5.0 %shard_map.62 = (f32[512,1]{1,0:T(8,128)S(1)}, f32[512,512]{1,0:T(8,128)S(1)}, bf16[512,512]{1,0:T(8,128)(2,1)}, f32[256,1024]{1,0:T(8,128)S(1)}, bf16[64,1024]{...) custom-call(s32[512,1]{1,0:T(8,128)S(1)} %copy-done.18, s32[1,256]{1,0:T(1,128)S(1)} %add.198.refs_1_, ...), custom_call_target="tpu_custom_call" | custom-call | flops 805306368 | bytes 4718592 | tf_op jit(solution)/shard_map/pallas_call | solution.py:297
  104.3 4.0 %collective-permute-start.23 = (bf16[64,1024]{1,0:T(8,128)(2,1)S(1)}, bf16[64,1024]{1,0:T(8,128)(2,1)S(1)}, u32[]{:S(2)}, u32[]{:S(2)}) collective-permute-start(bf16[64,1024]{1,0:T(8,128)(2,1)S(1)} %copy-done.24), channel_id=1, source_target_pairs={{0,16},{1,17},{2,18},{3,19},{4,20},{5,21},{6,22},{7,23},{24,8},{25... | collective-permute-start | bytes 393224 | tf_op jit(solution)/shard_map/ppermute | solution.py:106
  114.3 3.5 %collective-permute-done.27 = bf16[512,256]{1,0:T(8,128)(2,1)S(1)} collective-permute-done((bf16[512,256]{1,0:T(8,128)(2,1)S(1)}, bf16[512,256]{1,0:T(8,128)(2,1)S(1)}, u32[]{:S(2)}, u32[]{:S(2)}) %collective-permute-start.27) | collective-permute-done | bytes 262176 | tf_op jit(solution)/shard_map/ppermute | solution.py:106
  122.0 2.5 %collective-permute-done.30 = bf16[64,1024]{1,0:T(8,128)(2,1)S(1)} collective-permute-done((bf16[64,1024]{1,0:T(8,128)(2,1)S(1)}, bf16[64,1024]{1,0:T(8,128)(2,1)S(1)}, u32[]{:S(2)}, u32[]{:S(2)}) %collective-permute-start.30) | collective-permute-done | bytes 131104 | tf_op jit(solution)/shard_map/ppermute | solution.py:106
  127.1 1.9 %collective-permute-done.37 = bf16[64,256]{1,0:T(8,128)(2,1)S(1)} collective-permute-done((bf16[64,256]{1,0:T(8,128)(2,1)S(1)}, bf16[64,256]{1,0:T(8,128)(2,1)S(1)}, u32[]{:S(2)}, u32[]{:S(2)}) %collective-permute-start.37) | collective-permute-done | bytes 32800 | tf_op jit(solution)/shard_map/ppermute | solution.py:106
  130.9 4.5 %collective-permute-done.39 = bf16[256,256]{1,0:T(8,128)(2,1)S(1)} collective-permute-done((bf16[256,256]{1,0:T(8,128)(2,1)S(1)}, bf16[256,256]{1,0:T(8,128)(2,1)S(1)}, u32[]{:S(2)}, u32[]{:S(2)}) %collective-permute-start.39) | collective-permute-done | bytes 131104 | tf_op jit(solution)/shard_map/ppermute | solution.py:106
  136.9 3.4 %collective-permute-start.41 = (bf16[512,256]{1,0:T(8,128)(2,1)S(1)}, bf16[512,256]{1,0:T(8,128)(2,1)S(1)}, u32[]{:S(2)}, u32[]{:S(2)}) collective-permute-start(bf16[512,256]{1,0:T(8,128)(2,1)S(1)} %convolution_convert_fusion), channel_id=1, source_target_pairs={{0,8},{1,9},{2,10},{3,11},{4,12},{5,13},{6,14},{7,15},{24,16},{25,... | collective-permute-start | bytes 786440 | tf_op jit(solution)/shard_map/ppermute | solution.py:106
  141.0 4.0 %collective-permute-start.40 = (bf16[512,256]{1,0:T(8,128)(2,1)S(1)}, bf16[512,256]{1,0:T(8,128)(2,1)S(1)}, u32[]{:S(2)}, u32[]{:S(2)}) collective-permute-start(bf16[512,256]{1,0:T(8,128)(2,1)S(1)} %get-tuple-element.76), channel_id=1, source_target_pairs={{0,16},{1,17},{2,18},{3,19},{4,20},{5,21},{6,22},{7,23},{24,8},{25... | collective-permute-start | bytes 786440 | tf_op jit(solution)/shard_map/ppermute | solution.py:106
  146.4 4.5 %collective-permute-done.40 = bf16[512,256]{1,0:T(8,128)(2,1)S(1)} collective-permute-done((bf16[512,256]{1,0:T(8,128)(2,1)S(1)}, bf16[512,256]{1,0:T(8,128)(2,1)S(1)}, u32[]{:S(2)}, u32[]{:S(2)}) %collective-permute-start.40) | collective-permute-done | bytes 262176 | tf_op jit(solution)/shard_map/ppermute | solution.py:106
  151.0 3.8 %collective-permute-start.44 = (bf16[512,256]{1,0:T(8,128)(2,1)S(1)}, bf16[512,256]{1,0:T(8,128)(2,1)S(1)}, u32[]{:S(2)}, u32[]{:S(2)}) collective-permute-start(bf16[512,256]{1,0:T(8,128)(2,1)S(1)} %add_convert_fusion), channel_id=1, source_target_pairs={{0,8},{1,9},{2,10},{3,11},{4,12},{5,13},{6,14},{7,15},{8,0},{9,1},... | collective-permute-start | bytes 786440 | tf_op jit(solution)/shard_map/ppermute | solution.py:106
  156.0 3.4 %collective-permute-done.44 = bf16[512,256]{1,0:T(8,128)(2,1)S(1)} collective-permute-done((bf16[512,256]{1,0:T(8,128)(2,1)S(1)}, bf16[512,256]{1,0:T(8,128)(2,1)S(1)}, u32[]{:S(2)}, u32[]{:S(2)}) %collective-permute-start.44) | collective-permute-done | bytes 262176 | tf_op jit(solution)/shard_map/ppermute | solution.py:106
  (176 shorter events, 65.7 us)
Async XLA Ops:
  0.6 12.6 %collective-permute-start = (bf16[512,256]{1,0:T(8,128)(2,1)}, bf16[512,256]{1,0:T(8,128)(2,1)S(1)}, u32[]{:S(2)}, u32[]{:S(2)}) collective-permute-start(bf16[512,256]{1,0:T(8,128)(2,1)} %refs_2_.1), channel_id=1, source_target_pairs={{0,8},{1,9},{2,10},{3,11},{4,12},{5,13},{6,14},{7,15},{8,0},{9,1},... | collective-permute-start | bytes 786440 | tf_op jit(solution)/shard_map/ppermute | solution.py:106
  3.7 9.5 %collective-permute-start.1 = (bf16[512,256]{1,0:T(8,128)(2,1)}, bf16[512,256]{1,0:T(8,128)(2,1)S(1)}, u32[]{:S(2)}, u32[]{:S(2)}) collective-permute-start(bf16[512,256]{1,0:T(8,128)(2,1)} %refs_2_.1), channel_id=1, source_target_pairs={{8,16},{9,17},{10,18},{11,19},{12,20},{13,21},{14,22},{15,23},{16,... | collective-permute-start | bytes 786440 | tf_op jit(solution)/shard_map/ppermute | solution.py:106
  4.4 8.8 %collective-permute-start.2 = (bf16[512,256]{1,0:T(8,128)(2,1)}, bf16[512,256]{1,0:T(8,128)(2,1)S(1)}, u32[]{:S(2)}, u32[]{:S(2)}) collective-permute-start(bf16[512,256]{1,0:T(8,128)(2,1)} %refs_2_.1), channel_id=1, source_target_pairs={{0,4},{1,5},{2,6},{3,7},{4,0},{5,1},{6,2},{7,3},{8,12},{9,13},{10,... | collective-permute-start | bytes 786440 | tf_op jit(solution)/shard_map/ppermute | solution.py:106
  13.9 11.7 %collective-permute-start.5 = (bf16[512,256]{1,0:T(8,128)(2,1)S(1)}, bf16[512,256]{1,0:T(8,128)(2,1)S(1)}, u32[]{:S(2)}, u32[]{:S(2)}) collective-permute-start(bf16[512,256]{1,0:T(8,128)(2,1)S(1)} %collective-permute-done.1.refs_6_), channel_id=1, source_target_pairs={{8,0},{9,1},{10,2},{11,3},{12,4},{13,5},{14,6},{15,7},{16,24},{17,... | collective-permute-start | bytes 786440 | tf_op jit(solution)/shard_map/ppermute | solution.py:106
  15.2 10.4 %collective-permute-start.6 = (bf16[512,256]{1,0:T(8,128)(2,1)S(1)}, bf16[512,256]{1,0:T(8,128)(2,1)S(1)}, u32[]{:S(2)}, u32[]{:S(2)}) collective-permute-start(bf16[512,256]{1,0:T(8,128)(2,1)S(1)} %collective-permute-done.refs_4_), channel_id=1, source_target_pairs={{0,4},{1,5},{2,6},{3,7},{4,0},{5,1},{6,2},{7,3},{8,12},{9,13},{10,... | collective-permute-start | bytes 786440 | tf_op jit(solution)/shard_map/ppermute | solution.py:106
  16.8 15.6 %collective-permute-start.8 = (bf16[512,256]{1,0:T(8,128)(2,1)S(1)}, bf16[512,256]{1,0:T(8,128)(2,1)S(1)}, u32[]{:S(2)}, u32[]{:S(2)}) collective-permute-start(bf16[512,256]{1,0:T(8,128)(2,1)S(1)} %collective-permute-done.1.refs_6_), channel_id=1, source_target_pairs={{8,12},{9,13},{10,14},{11,15},{12,8},{13,9},{14,10},{15,11},{16,20... | collective-permute-start | bytes 786440 | tf_op jit(solution)/shard_map/ppermute | solution.py:106
  26.3 10.1 %collective-permute-start.7 = (bf16[512,256]{1,0:T(8,128)(2,1)S(1)}, bf16[512,256]{1,0:T(8,128)(2,1)}, u32[]{:S(2)}, u32[]{:S(2)}) collective-permute-start(bf16[512,256]{1,0:T(8,128)(2,1)S(1)} %collective-permute-done.4.refs_2_), channel_id=1, source_target_pairs={{8,0},{9,1},{10,2},{11,3},{12,4},{13,5},{14,6},{15,7},{16,24},{17,... | collective-permute-start | bytes 786440 | tf_op jit(solution)/shard_map/ppermute | solution.py:106
  27.6 8.8 %collective-permute-start.9 = (bf16[512,256]{1,0:T(8,128)(2,1)S(1)}, bf16[512,256]{1,0:T(8,128)(2,1)S(1)}, u32[]{:S(2)}, u32[]{:S(2)}) collective-permute-start(bf16[512,256]{1,0:T(8,128)(2,1)S(1)} %collective-permute-done.4.refs_2_), channel_id=1, source_target_pairs={{8,12},{9,13},{10,14},{11,15},{12,8},{13,9},{14,10},{15,11},{16,20... | collective-permute-start | bytes 786440 | tf_op jit(solution)/shard_map/ppermute | solution.py:106
  28.3 8.8 %collective-permute-start.10 = (bf16[512,256]{1,0:T(8,128)(2,1)S(1)}, bf16[512,256]{1,0:T(8,128)(2,1)S(1)}, u32[]{:S(2)}, u32[]{:S(2)}) collective-permute-start(bf16[512,256]{1,0:T(8,128)(2,1)S(1)} %collective-permute-done.5.refs_3_), channel_id=1, source_target_pairs={{0,4},{1,5},{2,6},{3,7},{4,0},{5,1},{6,2},{7,3},{24,28},{25,29},{2... | collective-permute-start | bytes 786440 | tf_op jit(solution)/shard_map/ppermute | solution.py:106
  37.8 14.1 %collective-permute-start.11 = (bf16[512,256]{1,0:T(8,128)(2,1)}, bf16[512,256]{1,0:T(8,128)(2,1)S(1)}, u32[]{:S(2)}, u32[]{:S(2)}) collective-permute-start(bf16[512,256]{1,0:T(8,128)(2,1)} %collective-permute-done.7.refs_7_), channel_id=1, source_target_pairs={{0,4},{1,5},{2,6},{3,7},{4,0},{5,1},{6,2},{7,3},{24,28},{25,29},{2... | collective-permute-start | bytes 786440 | tf_op jit(solution)/shard_map/ppermute | solution.py:106
  71.0 16.5 %collective-permute-start.17 = (bf16[512,512]{1,0:T(8,128)(2,1)S(1)}, bf16[512,512]{1,0:T(8,128)(2,1)S(1)}, u32[]{:S(2)}, u32[]{:S(2)}) collective-permute-start(bf16[512,512]{1,0:T(8,128)(2,1)S(1)} %pad_maximum_fusion.5.refs_2_), channel_id=1, source_target_pairs={{0,1},{1,0},{2,3},{3,2},{4,5},{5,4},{6,7},{7,6},{8,9},{9,8},{10,11... | collective-permute-start | bytes 1572872 | tf_op jit(solution)/shard_map/ppermute | solution.py:106
  75.2 12.3 %collective-permute-start.22 = (bf16[64,1024]{1,0:T(8,128)(2,1)S(1)}, bf16[64,1024]{1,0:T(8,128)(2,1)}, u32[]{:S(2)}, u32[]{:S(2)}) collective-permute-start(bf16[64,1024]{1,0:T(8,128)(2,1)S(1)} %collective-permute-done.18.refs_5_), channel_id=1, source_target_pairs={{8,24},{9,25},{10,26},{11,27},{12,28},{13,29},{14,30},{15,31},{16,... | collective-permute-start | bytes 393224 | tf_op jit(solution)/shard_map/ppermute | solution.py:106
  76.5 11.0 %collective-permute-start.21 = (bf16[64,1024]{1,0:T(8,128)(2,1)S(1)}, bf16[64,1024]{1,0:T(8,128)(2,1)}, u32[]{:S(2)}, u32[]{:S(2)}) collective-permute-start(bf16[64,1024]{1,0:T(8,128)(2,1)S(1)} %collective-permute-done.20.refs_8_), channel_id=1, source_target_pairs={{8,0},{9,1},{10,2},{11,3},{12,4},{13,5},{14,6},{15,7},{16,24},{17,... | collective-permute-start | bytes 393224 | tf_op jit(solution)/shard_map/ppermute | solution.py:106
  77.8 32.8 %collective-permute-start.33 = (bf16[256,2048]{1,0:T(8,128)(2,1)}, bf16[256,2048]{1,0:T(8,128)(2,1)}, u32[]{:S(2)}, u32[]{:S(2)}) collective-permute-start(bf16[256,2048]{1,0:T(8,128)(2,1)} %pad_maximum_fusion), channel_id=1, source_target_pairs={{0,4},{1,5},{2,6},{3,7},{4,0},{5,1},{6,2},{7,3},{8,12},{9,13},{10,... | collective-permute-start | bytes 3145736 | tf_op jit(solution)/shard_map/ppermute | solution.py:106
  100.5 7.8 %collective-permute-start.26 = (bf16[512,512]{1,0:T(8,128)(2,1)}, bf16[512,512]{1,0:T(8,128)(2,1)}, u32[]{:S(2)}, u32[]{:S(2)}) collective-permute-start(bf16[512,512]{1,0:T(8,128)(2,1)} %get-tuple-element.61), channel_id=1, source_target_pairs={{0,1},{1,0},{2,3},{3,2},{4,5},{5,4},{6,7},{7,6},{8,9},{9,8},{10,11... | collective-permute-start | bytes 1572872 | tf_op jit(solution)/shard_map/ppermute | solution.py:106
  102.2 12.1 %collective-permute-start.24 = (bf16[64,1024]{1,0:T(8,128)(2,1)S(1)}, bf16[64,1024]{1,0:T(8,128)(2,1)S(1)}, u32[]{:S(2)}, u32[]{:S(2)}) collective-permute-start(bf16[64,1024]{1,0:T(8,128)(2,1)S(1)} %copy-done.22), channel_id=1, source_target_pairs={{0,8},{1,9},{2,10},{3,11},{4,12},{5,13},{6,14},{7,15},{24,16},{25,... | collective-permute-start | bytes 393224 | tf_op jit(solution)/shard_map/ppermute | solution.py:106
  103.6 10.7 %collective-permute-start.25 = (bf16[64,1024]{1,0:T(8,128)(2,1)S(1)}, bf16[64,1024]{1,0:T(8,128)(2,1)S(1)}, u32[]{:S(2)}, u32[]{:S(2)}) collective-permute-start(bf16[64,1024]{1,0:T(8,128)(2,1)S(1)} %copy-done.22), channel_id=1, source_target_pairs={{8,16},{9,17},{10,18},{11,19},{12,20},{13,21},{14,22},{15,23},{16,... | collective-permute-start | bytes 393224 | tf_op jit(solution)/shard_map/ppermute | solution.py:106
  104.3 10.0 %collective-permute-start.23 = (bf16[64,1024]{1,0:T(8,128)(2,1)S(1)}, bf16[64,1024]{1,0:T(8,128)(2,1)S(1)}, u32[]{:S(2)}, u32[]{:S(2)}) collective-permute-start(bf16[64,1024]{1,0:T(8,128)(2,1)S(1)} %copy-done.24), channel_id=1, source_target_pairs={{0,16},{1,17},{2,18},{3,19},{4,20},{5,21},{6,22},{7,23},{24,8},{25... | collective-permute-start | bytes 393224 | tf_op jit(solution)/shard_map/ppermute | solution.py:106
  109.5 8.2 %collective-permute-start.27 = (bf16[512,256]{1,0:T(8,128)(2,1)S(1)}, bf16[512,256]{1,0:T(8,128)(2,1)S(1)}, u32[]{:S(2)}, u32[]{:S(2)}) collective-permute-start(bf16[512,256]{1,0:T(8,128)(2,1)S(1)} %slice.153), channel_id=1, source_target_pairs={{0,2},{1,3},{2,0},{3,1},{4,6},{5,7},{6,4},{7,5},{8,10},{9,11},{10,... | collective-permute-start | bytes 786440 | tf_op jit(solution)/shard_map/ppermute | solution.py:106
  114.3 21.3 %collective-permute-start.34 = (bf16[256,2048]{1,0:T(8,128)(2,1)}, bf16[256,2048]{1,0:T(8,128)(2,1)S(1)}, u32[]{:S(2)}, u32[]{:S(2)}) collective-permute-start(bf16[256,2048]{1,0:T(8,128)(2,1)} %collective-permute-done.33), channel_id=1, source_target_pairs={{0,1},{1,0},{2,3},{3,2},{4,5},{5,4},{6,7},{7,6},{8,9},{9,8},{10,11... | collective-permute-start | bytes 3145736 | tf_op jit(solution)/shard_map/ppermute | solution.py:106
  121.0 9.8 %collective-permute-start.35 = (bf16[512,256]{1,0:T(8,128)(2,1)S(1)}, bf16[512,256]{1,0:T(8,128)(2,1)S(1)}, u32[]{:S(2)}, u32[]{:S(2)}) collective-permute-start(bf16[512,256]{1,0:T(8,128)(2,1)S(1)} %get-tuple-element.88), channel_id=1, source_target_pairs={{0,4},{1,5},{2,6},{3,7},{4,0},{5,1},{6,2},{7,3},{8,12},{9,13},{10,... | collective-permute-start | bytes 786440 | tf_op jit(solution)/shard_map/ppermute | solution.py:106
  136.9 9.5 %collective-permute-start.41 = (bf16[512,256]{1,0:T(8,128)(2,1)S(1)}, bf16[512,256]{1,0:T(8,128)(2,1)S(1)}, u32[]{:S(2)}, u32[]{:S(2)}) collective-permute-start(bf16[512,256]{1,0:T(8,128)(2,1)S(1)} %convolution_convert_fusion), channel_id=1, source_target_pairs={{0,8},{1,9},{2,10},{3,11},{4,12},{5,13},{6,14},{7,15},{24,16},{25,... | collective-permute-start | bytes 786440 | tf_op jit(solution)/shard_map/ppermute | solution.py:106
  141.0 9.9 %collective-permute-start.40 = (bf16[512,256]{1,0:T(8,128)(2,1)S(1)}, bf16[512,256]{1,0:T(8,128)(2,1)S(1)}, u32[]{:S(2)}, u32[]{:S(2)}) collective-permute-start(bf16[512,256]{1,0:T(8,128)(2,1)S(1)} %get-tuple-element.76), channel_id=1, source_target_pairs={{0,16},{1,17},{2,18},{3,19},{4,20},{5,21},{6,22},{7,23},{24,8},{25... | collective-permute-start | bytes 786440 | tf_op jit(solution)/shard_map/ppermute | solution.py:106
  151.0 8.4 %collective-permute-start.44 = (bf16[512,256]{1,0:T(8,128)(2,1)S(1)}, bf16[512,256]{1,0:T(8,128)(2,1)S(1)}, u32[]{:S(2)}, u32[]{:S(2)}) collective-permute-start(bf16[512,256]{1,0:T(8,128)(2,1)S(1)} %add_convert_fusion), channel_id=1, source_target_pairs={{0,8},{1,9},{2,10},{3,11},{4,12},{5,13},{6,14},{7,15},{8,0},{9,1},... | collective-permute-start | bytes 786440 | tf_op jit(solution)/shard_map/ppermute | solution.py:106
  (50 other events, 183.8 us)

commit v7 on v0

--- a/solution.py
+++ b/solution.py
@@ -3,6 +3,8 @@
 import jax
 import jax.numpy as jnp
 from jax import lax
+from jax.experimental import pallas as pl
+from jax.experimental.pallas import tpu as pltpu
 from jax.sharding import PartitionSpec as P
 
 E = 1024
@@ -31,19 +33,19 @@
     )
 
 
-def per_device(prompts, responses, head_projection_matrix, positive):
+def matmul(left_side, righthand_term):
+    return jnp.dot(left_side, righthand_term, preferred_element_type=jnp.float32)
+
+
+def general(prompts, responses, head_projection_matrix, positive):
     row_count = prompts.shape[0]
     col_count = head_projection_matrix.shape[1]
     factor = LOGIT_SCALE / math.sqrt(E)
     cycle_size = lax.axis_size("dp")
     position = lax.axis_index("dp")
     segment = lax.all_gather(head_projection_matrix, "dp", axis=0, tiled=True)
-    prompt_cols = prompts
-    response_cols = responses
-    prompt_proj = jnp.dot(prompt_cols, segment, preferred_element_type=jnp.float32)
-    response_proj = jnp.dot(response_cols, segment, preferred_element_type=jnp.float32)
-    prompt_emb = prompt_proj.astype(jnp.bfloat16)
-    visiting = response_proj.astype(jnp.bfloat16)
+    prompt_emb = matmul(prompts, segment).astype(jnp.bfloat16)
+    visiting = matmul(responses, segment).astype(jnp.bfloat16)
     local_ids = lax.iota(jnp.int32, row_count)
     prompt_gradient_total = jnp.zeros((row_count, col_count), jnp.float32)
     grad_response = jnp.zeros((row_count, col_count), jnp.float32)
@@ -59,9 +61,7 @@
         pairwise_weight = (-labels * jax.nn.sigmoid(margin) * (factor / row_count)).astype(
             jnp.bfloat16
         )
-        prompt_gradient_total = prompt_gradient_total + jnp.dot(
-            pairwise_weight, visiting, preferred_element_type=jnp.float32
-        )
+        prompt_gradient_total = prompt_gradient_total + matmul(pairwise_weight, visiting)
         contribution = cross_rows(pairwise_weight, prompt_emb)
         if offset == 0:
             grad_response = contribution
@@ -71,15 +71,347 @@
             visiting = passed_along(visiting, "dp", 1)
     grad_prompt_b = prompt_gradient_total.astype(jnp.bfloat16)
     grad_response_b = grad_response.astype(jnp.bfloat16)
-    prompt_cols = prompts
-    response_cols = responses
     head_grad = lax.psum_scatter(
-        cross_rows(prompt_cols, grad_prompt_b) + cross_rows(response_cols, grad_response_b),
+        cross_rows(prompts, grad_prompt_b) + cross_rows(responses, grad_response_b),
         "dp",
         scatter_dimension=0,
         tiled=True,
     )
     return (row_losses / row_count, head_grad)
+
+
+LINE, PAIR, SIDE, CORES = 4, 2, 2, 2
+
+
+def routes(move):
+    table = []
+    for z in range(LINE):
+        for y in range(PAIR):
+            for x in range(SIDE):
+                for c in range(CORES):
+                    goal = move(z, y, x, c)
+                    if goal is not None:
+                        gz, gy, gx, gc = goal
+                        source = (z * PAIR + y) * SIDE * CORES + x * CORES + c
+                        target = (gz * PAIR + gy) * SIDE * CORES + gx * CORES + gc
+                        table.append((source, target))
+    return table
+
+
+def along_line(moves):
+    return routes(lambda z, y, x, c: (moves[z], y, x, c) if z in moves else None)
+
+
+def send(block, table):
+    return lax.ppermute(block, ("dp", "mp"), table)
+
+
+ACROSS_Y = routes(lambda z, y, x, c: (z, 1 - y, x, c))
+ACROSS_X = routes(lambda z, y, x, c: (z, y, 1 - x, c))
+Y_ENDS = routes(lambda z, y, x, c: (z, 1 - y, x, c) if z in (0, 3) else None)
+Y_MIDDLE = routes(lambda z, y, x, c: (z, 1 - y, x, c) if z in (1, 2) else None)
+ACROSS_C = routes(lambda z, y, x, c: (z, y, x, 1 - c))
+PAIRS = along_line({0: 1, 1: 0, 2: 3, 3: 2})
+MIDDLE = along_line({1: 2, 2: 1})
+OUTWARD = along_line({1: 0, 2: 3})
+INWARD = along_line({0: 1, 3: 2})
+TWO_OUT = along_line({1: 3, 2: 0})
+TWO_IN = along_line({3: 1, 0: 2})
+FAR = along_line({0: 2, 1: 3, 2: 0, 3: 1})
+FAR_Y = routes(lambda z, y, x, c: (z ^ 2, 1 - y, x, c))
+PAIRS_X = routes(lambda z, y, x, c: (z ^ 1, y, 1 - x, c))
+MIX = [routes(lambda z, y, x, c, k=k: (z, y, x ^ (k >> 1), c ^ (k & 1))) for k in range(4)]
+
+
+def line_reduce(own, first, second, third, second_b, third_b, own_y, first_y):
+    jumped, inward, across, first_y = lax.optimization_barrier(
+        (
+            send(third_b, TWO_IN),
+            send(second_b, INWARD),
+            send(second_b, MIDDLE),
+            send(first_y, ACROSS_Y),
+        )
+    )
+    jumped, inward, across, first_y = [
+        block.astype(jnp.float32) for block in (jumped, inward, across, first_y)
+    ]
+    paired = send((first + first_y + across + jumped).astype(jnp.bfloat16), PAIRS)
+    last = send((third + inward).astype(jnp.bfloat16), MIDDLE)
+    own = own + send(own_y, ACROSS_Y).astype(jnp.float32)
+    return own + last.astype(jnp.float32) + paired.astype(jnp.float32)
+
+
+def project(prompts, responses, blocks, weights, total, kind):
+    row_count = prompts.shape[0]
+    depth, width = weights[0][0].shape
+    count = len(weights)
+    terms = [term for weight in weights for term in weight]
+
+    def kernel(block_ref, *refs):
+        arrays, term_refs, refs = refs[:2], list(refs[2 : 2 + len(terms)]), refs[2 + len(terms) :]
+        if total is not None:
+            total_ref, *refs = refs
+        out_ref, feature_buf, sum_buf, sem = refs
+        loads = []
+        for k in range(count):
+            start = pl.multiple_of(block_ref[k] * depth, depth)
+            for array in range(2):
+                load = pltpu.make_async_copy(
+                    arrays[array].at[:, pl.ds(start, depth)],
+                    feature_buf.at[k, array],
+                    sem.at[k, array],
+                )
+                load.start()
+                loads.append(load)
+        for k, weight in enumerate(weights):
+            block = term_refs.pop(0)[...]
+            for _ in weight[1:]:
+                block = block + term_refs.pop(0)[...]
+            for array in range(2):
+                loads[2 * k + array].wait()
+                rows = slice(array * row_count, (array + 1) * row_count)
+                part = matmul(feature_buf[k, array], block)
+                if k > 0:
+                    part += sum_buf[rows]
+                elif total is not None:
+                    part += total_ref[rows]
+                if k < count - 1:
+                    sum_buf[rows] = part
+                else:
+                    out_ref[rows] = part.astype(out_ref.dtype)
+
+    inside = pl.BlockSpec(memory_space=pltpu.VMEM)
+    operands = terms + ([total] if total is not None else [])
+    return pl.pallas_call(
+        kernel,
+        in_specs=[pl.BlockSpec(memory_space=pltpu.SMEM)]
+        + [pl.BlockSpec(memory_space=pltpu.HBM)] * 2
+        + [inside] * len(operands),
+        out_specs=inside,
+        scratch_shapes=[
+            pltpu.VMEM((count, 2, row_count, depth), jnp.bfloat16),
+            pltpu.VMEM((2 * row_count, width), jnp.float32),
+            pltpu.SemaphoreType.DMA((count, 2)),
+        ],
+        out_shape=jax.ShapeDtypeStruct((2 * row_count, width), kind),
+        compiler_params=pltpu.CompilerParams(vmem_limit_bytes=12 * 1024 * 1024),
+        cost_estimate=pl.CostEstimate(
+            flops=4 * count * row_count * depth * width,
+            bytes_accessed=4 * count * row_count * depth + 2 * len(terms) * depth * width,
+            transcendentals=0,
+        ),
+    )(blocks, prompts, responses, *operands)
+
+
+def compare(half, other, held, wanted, ids, row_count):
+    prompt_rows, width = half.shape[0], half.shape[1] // 2
+    quarter = held[0].shape[0]
+    count, full = len(held) * quarter, 4 * width
+    factor = LOGIT_SCALE / math.sqrt(E)
+
+    def kernel(wanted_ref, ids_ref, half_ref, other_ref, *refs):
+        held_refs, refs = refs[: len(held)], refs[len(held) :]
+        loss_ref, mine_ref, away_ref, *part_refs, rows_ref = refs
+        for k, ref in enumerate(held_refs):
+            rows_ref[k * quarter : (k + 1) * quarter] = ref[...]
+        places = [
+            (half_ref, 0, mine_ref),
+            (other_ref, 0, away_ref),
+            (half_ref, 1, mine_ref),
+            (other_ref, 1, away_ref),
+        ]
+        scores = jnp.zeros((count, prompt_rows), jnp.float32)
+        for k, (ref, at, _) in enumerate(places):
+            scores += cross_cols(
+                rows_ref[:, k * width : (k + 1) * width], ref[:, at * width : (at + 1) * width]
+            )
+        scores = scores * factor + LOGIT_BIAS
+        match = wanted_ref[...] == ids_ref[...]
+        margin = jnp.where(match, -scores, scores)
+        small = jnp.exp(-jnp.abs(margin))
+        loss_ref[...] = jnp.sum(
+            jnp.maximum(margin, 0.0) + jnp.log1p(small), axis=0, keepdims=True
+        )
+        share = jnp.where(margin >= 0.0, 1.0, small) / (1.0 + small)
+        share = share * (factor / row_count)
+        weight = jnp.where(match, -share, share).astype(jnp.bfloat16)
+        for k, (ref, at, out) in enumerate(places):
+            columns, goal = slice(k * width, (k + 1) * width), slice(at * width, (at + 1) * width)
+            part = matmul(weight, ref[:, goal])
+            for block, part_ref in enumerate(part_refs):
+                rows = part[block * quarter : (block + 1) * quarter]
+                part_ref[:, columns] = rows.astype(part_ref.dtype)
+            out[:, goal] = cross_rows(weight, rows_ref[:, columns]).astype(out.dtype)
+
+    return pl.pallas_call(
+        kernel,
+        in_specs=[pl.BlockSpec(memory_space=pltpu.VMEM)] * (4 + len(held)),
+        out_specs=[pl.BlockSpec(memory_space=pltpu.VMEM)] * (3 + len(held)),
+        out_shape=[
+            jax.ShapeDtypeStruct((1, prompt_rows), jnp.float32),
+            jax.ShapeDtypeStruct((prompt_rows, 2 * width), jnp.float32),
+            jax.ShapeDtypeStruct((prompt_rows, 2 * width), jnp.bfloat16),
+            jax.ShapeDtypeStruct((quarter, full), jnp.float32),
+        ]
+        + [jax.ShapeDtypeStruct((quarter, full), jnp.bfloat16)] * (len(held) - 1),
+        scratch_shapes=[pltpu.VMEM((count, full), jnp.bfloat16)],
+        compiler_params=pltpu.CompilerParams(vmem_limit_bytes=16 * 1024 * 1024),
+        cost_estimate=pl.CostEstimate(
+            flops=6 * prompt_rows * count * full,
+            bytes_accessed=6 * prompt_rows * full + 6 * count * full,
+            transcendentals=2 * prompt_rows * count,
+        ),
+    )(wanted, ids, half, other, *held)
+
+
+def full_window(prompts, responses, head_projection_matrix, positive):
+    row_count = prompts.shape[0]
+    depth, width = head_projection_matrix.shape
+    dp, mp = lax.axis_index("dp"), lax.axis_index("mp")
+    z, y = dp // PAIR, dp % PAIR
+    quarter = row_count // (SIDE * CORES)
+    tie = lax.optimization_barrier
+
+    here = [(z ^ k) * PAIR + y for k in range(LINE)]
+    there = [(z ^ k) * PAIR + 1 - y for k in range(LINE)]
+    orders = [here[0], there[0], here[1], there[1]], [here[2], there[2], here[3]], [there[3]]
+    ids = jnp.stack([here[0], here[2], there[0], there[2]]) * row_count + mp * quarter
+    ids = (ids[:, None] + lax.iota(jnp.int32, quarter)).reshape(-1, 1)
+    own, orders, here, there, places, even, left, ids = tie(
+        (
+            head_projection_matrix,
+            [jnp.stack(order).astype(jnp.int32) for order in orders],
+            [(index * depth).astype(jnp.uint32) for index in here],
+            [(index * depth).astype(jnp.uint32) for index in there],
+            [((mp ^ k) * quarter).astype(jnp.uint32) for k in range(SIDE * CORES)],
+            mp % CORES == 0,
+            mp < CORES,
+            ids,
+        )
+    )
+    zero = jnp.uint32(0)
+
+    def features(array, start):
+        return lax.dynamic_slice(array, (zero, start), (row_count, depth))
+
+    first, middle, own_y, positive_z = tie(
+        (
+            send(own, PAIRS),
+            send(own, MIDDLE),
+            send(own, ACROSS_Y),
+            send(positive, PAIRS),
+        )
+    )
+    wanted = jnp.concatenate([positive, positive_z], axis=0)[None, :]
+    columns = [
+        jnp.concatenate([features(prompts, start).T, features(responses, start).T], axis=1)
+        for start in here + there[:2]
+    ]
+    mine = jnp.concatenate(
+        [jnp.where(even, features(prompts, f), features(responses, f)) for f in there[2:]], axis=1
+    )
+    inner, outer, first_y, wanted, columns, mine = tie(
+        (send(first, MIDDLE), send(middle, OUTWARD), send(first, ACROSS_Y), wanted, columns, mine)
+    )
+    emb = project(
+        prompts,
+        responses,
+        orders[0],
+        [(own,), (own_y,), (first,), (first_y,)],
+        None,
+        jnp.float32,
+    )
+    last, inner_y, outer_y, emb = tie(
+        (send(inner, OUTWARD), send(inner, Y_MIDDLE), send(outer, Y_ENDS), emb)
+    )
+    emb = project(
+        prompts,
+        responses,
+        orders[1],
+        [(inner, outer), (inner_y, outer_y), (middle, last)],
+        emb,
+        jnp.float32,
+    )
+    middle_y, last_y, emb = tie((send(middle, Y_MIDDLE), send(last, Y_ENDS), emb))
+    emb = project(prompts, responses, orders[2], [(middle_y, last_y)], emb, jnp.bfloat16)
+    prompt_emb, response_emb = emb[:row_count], emb[row_count:]
+
+    pieces = []
+    for k in range(SIDE * CORES):
+        piece = lax.dynamic_slice(response_emb, (places[k], zero), (quarter, width))
+        pieces.append(piece if k == 0 else send(piece, MIX[k]))
+    response_rows = jnp.concatenate(pieces, axis=1)
+
+    response_rows, mine = tie((response_rows, mine))
+    held = [send(response_rows, table) for table in (FAR, ACROSS_Y, FAR_Y)]
+    near = jnp.concatenate([prompt_emb, send(prompt_emb, PAIRS)], axis=0)
+    near_c = send(near, ACROSS_C)
+    held, beside = tie((held, send(near, ACROSS_X)))
+    half = jnp.concatenate([near, beside], axis=1)
+    other = jnp.concatenate([near_c, send(beside, ACROSS_C)], axis=1)
+    fetched = send(mine, ACROSS_Y)
+    losses, mine, away, *parts = compare(
+        half, other, [response_rows, *held], wanted, ids, row_count
+    )
+
+    back = [send(part, table) for part, table in zip(parts[1:], (FAR, ACROSS_Y, FAR_Y))]
+    losses = losses[0]
+    losses = losses + send(losses, ACROSS_C)
+    mine = mine + send(away, ACROSS_C).astype(jnp.float32)
+    aside = send(mine[:, width:].astype(jnp.bfloat16), ACROSS_X)
+    back, aside, fetched = tie((back, aside, fetched))
+    grad = parts[0] + sum(part.astype(jnp.float32) for part in back)
+    grad = grad.astype(jnp.bfloat16)
+    mine = mine[:, :width] + aside.astype(jnp.float32)
+    far = send(mine[row_count:].astype(jnp.bfloat16), PAIRS)
+    sibling = send(fetched, ACROSS_C)
+
+    pieces = [grad[:, k * width : (k + 1) * width] for k in range(SIDE * CORES)]
+    pieces = [pieces[0]] + [send(pieces[k], MIX[k]) for k in range(1, SIDE * CORES)]
+    pieces, far, sibling = tie((pieces, far, sibling))
+    swapped = [jnp.where(even, pieces[k], pieces[k ^ 1]) for k in range(SIDE * CORES)]
+    swapped = [jnp.where(left, swapped[k], swapped[k ^ 2]) for k in range(SIDE * CORES)]
+    grad_response = jnp.concatenate(swapped, axis=0)
+    grad_response_y = send(grad_response, ACROSS_Y)
+    grad_prompt = (mine[:row_count] + far.astype(jnp.float32)).astype(jnp.bfloat16)
+    grad_prompt_y = send(grad_prompt, ACROSS_Y)
+    losses_x = send(losses[:row_count], ACROSS_X)
+    losses_z = send(losses[row_count:], PAIRS)
+    losses_xz = send(losses[row_count:], PAIRS_X)
+    columns_y = [
+        jnp.concatenate(
+            [array[:, k * depth : (k + 1) * depth].T for array in (fetched, sibling)], axis=1
+        )
+        for k in range(2)
+    ]
+    grad_response_y, grad_prompt_y, losses_x, losses_z, losses_xz, columns_y = tie(
+        (grad_response_y, grad_prompt_y, losses_x, losses_z, losses_xz, columns_y)
+    )
+    losses = (losses[:row_count] + losses_x) + (losses_z + losses_xz)
+
+    grads = jnp.concatenate([grad_prompt, grad_response], axis=0)
+    grads_y = jnp.concatenate(
+        [
+            jnp.where(even, grad_prompt_y, grad_response_y),
+            jnp.where(even, grad_response_y, grad_prompt_y),
+        ],
+        axis=0,
+    )
+    third = matmul(columns[3], grads) + matmul(columns_y[1], grads_y)
+    third_b, grads = tie((third.astype(jnp.bfloat16), grads))
+    second = matmul(columns[2], grads) + matmul(columns_y[0], grads_y)
+    second_b, grads = tie((second.astype(jnp.bfloat16), grads))
+    first_y, own_y = [matmul(columns[k], grads).astype(jnp.bfloat16) for k in (5, 4)]
+    first, own = [matmul(columns[k], grads) for k in (1, 0)]
+    head_grad = line_reduce(own, first, second, third, second_b, third_b, own_y, first_y)
+    return (losses / row_count, head_grad)
+
+
+def per_device(prompts, responses, head_projection_matrix, positive):
+    whole = lax.axis_size("dp") == STEPS == LINE * PAIR
+    whole = whole and lax.axis_size("mp") == SIDE * CORES
+    step = full_window if whole else general
+    return step(prompts, responses, head_projection_matrix, positive)
 
 
 def solution(mesh):

time: 331 us -> 139 us (0.42)
  waiting for transfers between devices: 265 us -> 58.3 us
  starting transfers between devices: 13 us -> 57.2 us
  matrix products: 29.4 us -> 3.55 us
  between operations: 14.3 us -> 1.28 us
  Pallas kernels: 0 us -> 6.67 us
  other arithmetic: 5.69 us -> 11 us
    reduce_scatter x1 -> x0, waiting for transfers between devices: 100 us -> none  [per_device(): lax.psum_scatter(cross_rows(prompt_cols, grad_prompt_b) + cross_rows(resp...]
    all_gather x1 -> x0, waiting for transfers between devices: 54.2 us -> none  [per_device(): segment = lax.all_gather(head_projection_matrix, 'dp', axis=0, tiled=True)]
    psum x1 -> x0, waiting for transfers between devices: 48.1 us -> none  [per_device(): pair_scores = lax.psum(partial_logits, 'mp') * factor + LOGIT_BIAS]
    ppermute x14 -> x46, starting transfers between devices: 12.9 us -> 57.2 us  [send(): return lax.ppermute(block, ('dp', 'mp'), table)]
    dot_general x26 -> x8, matrix products: 29.4 us -> 3.55 us  [matmul(): jnp.dot(left_side, righthand_term, preferred_element_type=jnp.float32)]
    pallas_call x0 -> x4, Pallas kernels: none -> 6.67 us  [the longest x3 5.05 us: project(): pl.pallas_call(kernel, in_specs=[pl.BlockSpec(memory_space=pltpu.SMEM)] +...]
    select_n x0 -> x2, other arithmetic: none -> 4.98 us  [the longest x1 4.96 us: full_window(): jnp.where(even, features(prompts, f), features(responses, f))]
    concatenate x0 -> x16, other arithmetic: none -> 4.79 us  [the longest x1 1.06 us: full_window(): other = jnp.concatenate([near_c, send(beside, ACROSS_C)], axis=1)]
  transfers between devices with their start and end apart: 17 -> 46, of which waited for: 13 -> 21; matrix products, arithmetic and copies ran while one was open for 7% -> 8% of each run, Pallas kernels for 0% -> 3%
where the time goes in v7:
time: 139 us; the launch traced here: 138 us
  waiting for transfers between devices  58.3 us (42%)
  starting transfers between devices  57.2 us (41%)
  other arithmetic  11 us (8%)
  Pallas kernels  6.67 us (5%)
  matrix products  3.55 us (3%)
    ppermute x46, waiting for transfers between devices, send(): return lax.ppermute(block, ('dp', 'mp'), table)  58.3 us
    ppermute x46, starting transfers between devices, send(): return lax.ppermute(block, ('dp', 'mp'), table)  57.2 us
    pallas_call x3, Pallas kernels, project(): pl.pallas_call(kernel, in_specs=[pl.BlockSpec(memory_space=pltpu.SMEM)] +...  5.05 us
    select_n x1, other arithmetic, full_window(): jnp.where(even, features(prompts, f), features(responses, f))  4.96 us
    dot_general x8, matrix products, matmul(): jnp.dot(left_side, righthand_term, preferred_element_type=jnp.float32)  3.55 us
  transfers between devices with their start and end apart: 46, of which 21 were waited for; matrix products, arithmetic and copies ran while one was open for 8% of the time, Pallas kernels for 3%

profile of v7, /device:TPU:0, one launch (start us, length us, event | category | flops | bytes accessed | tf_op | source)
XLA Modules:
  0.0 138.5 jit_solution(18326901359053079083)
XLA Ops:
  1.0 3.0 %collective-permute-start.2 = (bf16[512,256]{1,0:T(8,128)(2,1)}, bf16[512,256]{1,0:T(8,128)(2,1)S(1)}, u32[]{:S(2)}, u32[]{:S(2)}) collective-permute-start(bf16[512,256]{1,0:T(8,128)(2,1)} %refs_2_), channel_id=1, source_target_pairs={{0,4},{1,5},{2,6},{3,7},{4,0},{5,1},{6,2},{7,3},{8,12},{9,13},{10,... | collective-permute-start | bytes 786440 | tf_op jit(solution)/shard_map/ppermute | solution.py:106
  4.6 4.5 %collective-permute-start = (bf16[512,256]{1,0:T(8,128)(2,1)}, bf16[512,256]{1,0:T(8,128)(2,1)S(1)}, u32[]{:S(2)}, u32[]{:S(2)}) collective-permute-start(bf16[512,256]{1,0:T(8,128)(2,1)} %refs_2_), channel_id=1, source_target_pairs={{0,8},{1,9},{2,10},{3,11},{4,12},{5,13},{6,14},{7,15},{8,0},{9,1},... | collective-permute-start | bytes 786440 | tf_op jit(solution)/shard_map/ppermute | solution.py:106
  9.2 5.0 %dynamic-slice_select_fusion.1 = (bf16[256,512]{1,0:T(8,128)(2,1)S(1)}, bf16[256,512]{1,0:T(8,128)(2,1)S(1)}, bf16[512,256]{0,1:T(8,128)(2,1)S(1)}, bf16[512,256...) fusion(bf16[256,4096]{1,0:T(8,128)(2,1)} %refs_1_.5, ...), kind=kLoop, calls=%fused_computation.38 | loop fusion | flops 262144 | bytes 7864353 | tf_op jit(solution)/shard_map/jit(_where)/select_n | solution.py:311
  18.9 4.5 %collective-permute-done.6.refs_5_ = bf16[512,256]{1,0:T(8,128)(2,1)S(1)} collective-permute-done((bf16[512,256]{1,0:T(8,128)(2,1)S(1)}, bf16[512,256]{1,0:T(8,128)(2,1)S(1)}, u32[]{:S(2)}, u32[]{:S(2)}) %collective-permute-start.6) | collective-permute-done | bytes 262176 | tf_op jit(solution)/shard_map/ppermute | solution.py:106
  23.3 3.8 %collective-permute-done.5.refs_3_ = bf16[512,256]{1,0:T(8,128)(2,1)S(1)} collective-permute-done((bf16[512,256]{1,0:T(8,128)(2,1)S(1)}, bf16[512,256]{1,0:T(8,128)(2,1)S(1)}, u32[]{:S(2)}, u32[]{:S(2)}) %collective-permute-start.5) | collective-permute-done | bytes 262176 | tf_op jit(solution)/shard_map/ppermute | solution.py:106
  27.1 3.1 %collective-permute-start.10 = (bf16[512,256]{1,0:T(8,128)(2,1)S(1)}, bf16[512,256]{1,0:T(8,128)(2,1)S(1)}, u32[]{:S(2)}, u32[]{:S(2)}) collective-permute-start(bf16[512,256]{1,0:T(8,128)(2,1)S(1)} %collective-permute-done.5.refs_3_), channel_id=1, source_target_pairs={{0,4},{1,5},{2,6},{3,7},{4,0},{5,1},{6,2},{7,3},{24,28},{25,29},{2... | collective-permute-start | bytes 786440 | tf_op jit(solution)/shard_map/ppermute | solution.py:106
  33.0 2.4 %shard_map.59.refs_8_ = f32[512,256]{1,0:T(8,128)S(1)} custom-call(s32[4]{0:T(128)S(1)} %get-tuple-element.100.block_ref, bf16[256,4096]{1,0:T(8,128)(2,1)S(1)} %copy-done, bf16[256,4096]{1,0:T(8,128)(2,1)S(1)} %copy-done.1, bf16[512,256]{1,0:T(8,128)(2,1)S(1)} %copy-done.2, bf16[512,256]{1,0:T(8,128)(2,1)S(1)} %collective-permute-done.2.refs_3_, ...), custom_call_target="tpu_custom_call" | custom-call | flops 536870912 | bytes 3145728 | tf_op jit(solution)/shard_map/pallas_call | solution.py:185
  35.4 3.8 %collective-permute-done.8.refs_7_ = bf16[512,256]{1,0:T(8,128)(2,1)S(1)} collective-permute-done((bf16[512,256]{1,0:T(8,128)(2,1)S(1)}, bf16[512,256]{1,0:T(8,128)(2,1)S(1)}, u32[]{:S(2)}, u32[]{:S(2)}) %collective-permute-start.8) | collective-permute-done | bytes 262176 | tf_op jit(solution)/shard_map/ppermute | solution.py:106
  39.2 2.9 %collective-permute-start.11 = (bf16[512,256]{1,0:T(8,128)(2,1)S(1)}, bf16[512,256]{1,0:T(8,128)(2,1)S(1)}, u32[]{:S(2)}, u32[]{:S(2)}) collective-permute-start(bf16[512,256]{1,0:T(8,128)(2,1)S(1)} %collective-permute-done.8.refs_7_), channel_id=1, source_target_pairs={{0,4},{1,5},{2,6},{3,7},{4,0},{5,1},{6,2},{7,3},{24,28},{25,29},{2... | collective-permute-start | bytes 786440 | tf_op jit(solution)/shard_map/ppermute | solution.py:106
  42.1 2.0 %shard_map.60.refs_4_ = f32[512,256]{1,0:T(8,128)S(1)} custom-call(s32[3]{0:T(128)S(1)} %pad_add_fusion.2.block_ref, bf16[256,4096]{1,0:T(8,128)(2,1)S(1)} %copy-done, bf16[256,4096]{1,0:T(8,128)(2,1)S(1)} %copy-done.1, bf16[512,256]{1,0:T(8,128)(2,1)S(1)} %collective-permute-done.4.refs_2_, bf16[512,256]{1,0:T(8,128)(2,1)S(1)} %collective-permute-done.5.refs_3_, ...), custom_call_target="tpu_custom_call" | custom-call | flops 402653184 | bytes 3145728 | tf_op jit(solution)/shard_map/pallas_call | solution.py:185
  44.1 3.3 %collective-permute-done.11.refs_3_ = bf16[512,256]{1,0:T(8,128)(2,1)S(1)} collective-permute-done((bf16[512,256]{1,0:T(8,128)(2,1)S(1)}, bf16[512,256]{1,0:T(8,128)(2,1)S(1)}, u32[]{:S(2)}, u32[]{:S(2)}) %collective-permute-start.11) | collective-permute-done | bytes 262176 | tf_op jit(solution)/shard_map/ppermute | solution.py:106
  50.2 3.0 %collective-permute-done.12 = bf16[256,256]{1,0:T(8,128)(2,1)S(1)} collective-permute-done((bf16[256,256]{1,0:T(8,128)(2,1)S(1)}, bf16[256,256]{1,0:T(8,128)(2,1)S(1)}, u32[]{:S(2)}, u32[]{:S(2)}) %collective-permute-start.12) | collective-permute-done | bytes 131104 | tf_op jit(solution)/shard_map/ppermute | solution.py:106
  58.0 1.9 %collective-permute-start.16 = (bf16[64,1024]{1,0:T(8,128)(2,1)S(1)}, bf16[64,1024]{1,0:T(8,128)(2,1)S(1)}, u32[]{:S(2)}, u32[]{:S(2)}) collective-permute-start(bf16[64,1024]{1,0:T(8,128)(2,1)S(1)} %pad_maximum_fusion.15.refs_0_), channel_id=1, source_target_pairs={{0,16},{1,17},{2,18},{3,19},{4,20},{5,21},{6,22},{7,23},{8,24},{9,... | collective-permute-start | bytes 393224 | tf_op jit(solution)/shard_map/ppermute | solution.py:106
  59.9 7.4 %collective-permute-done.18.refs_3_ = bf16[64,1024]{1,0:T(8,128)(2,1)S(1)} collective-permute-done((bf16[64,1024]{1,0:T(8,128)(2,1)S(1)}, bf16[64,1024]{1,0:T(8,128)(2,1)S(1)}, u32[]{:S(2)}, u32[]{:S(2)}) %collective-permute-start.18) | collective-permute-done | bytes 131104 | tf_op jit(solution)/shard_map/ppermute | solution.py:106
  71.0 1.6 %shard_map.62 = (f32[1,512]{1,0:T(1,128)S(1)}, f32[512,512]{1,0:T(8,128)S(1)}, bf16[512,512]{1,0:T(8,128)(2,1)S(1)}, f32[64,1024]{1,0:T(8,128)S(1)}, bf16[64,102...) custom-call(s32[1,512]{1,0:T(1,128)S(1)} %bitcast.58, s32[256,1]{1,0:T(8,128)S(1)} %copy.6.ids_ref, ...), custom_call_target="tpu_custom_call" | custom-call | flops 805306368 | bytes 4718592 | tf_op jit(solution)/shard_map/pallas_call | solution.py:246
  76.9 3.2 %collective-permute-start.25 = (bf16[64,1024]{1,0:T(8,128)(2,1)S(1)}, bf16[64,1024]{1,0:T(8,128)(2,1)S(1)}, u32[]{:S(2)}, u32[]{:S(2)}) collective-permute-start(bf16[64,1024]{1,0:T(8,128)(2,1)S(1)} %get-tuple-element.126), channel_id=1, source_target_pairs={{0,20},{1,21},{2,22},{3,23},{4,16},{5,17},{6,18},{7,19},{8,28},{9,... | collective-permute-start | bytes 393224 | tf_op jit(solution)/shard_map/ppermute | solution.py:106
  80.2 7.4 %collective-permute-done.28 = bf16[256,1024]{1,0:T(8,128)(2,1)S(1)} collective-permute-done((bf16[256,1024]{1,0:T(8,128)(2,1)S(1)}, bf16[256,1024]{1,0:T(8,128)(2,1)S(1)}, u32[]{:S(2)}, u32[]{:S(2)}) %collective-permute-start.28) | collective-permute-done | bytes 524320 | tf_op jit(solution)/shard_map/ppermute | solution.py:106
  87.9 4.7 %collective-permute-done.24 = bf16[64,1024]{1,0:T(8,128)(2,1)S(1)} collective-permute-done((bf16[64,1024]{1,0:T(8,128)(2,1)S(1)}, bf16[64,1024]{1,0:T(8,128)(2,1)S(1)}, u32[]{:S(2)}, u32[]{:S(2)}) %collective-permute-start.24) | collective-permute-done | bytes 131104 | tf_op jit(solution)/shard_map/ppermute | solution.py:106
  103.5 4.2 %collective-permute-done.34 = bf16[256,256]{1,0:T(8,128)(2,1)S(1)} collective-permute-done((bf16[256,256]{1,0:T(8,128)(2,1)S(1)}, bf16[256,256]{1,0:T(8,128)(2,1)S(1)}, u32[]{:S(2)}, u32[]{:S(2)}) %collective-permute-start.34) | collective-permute-done | bytes 131104 | tf_op jit(solution)/shard_map/ppermute | solution.py:106
  111.4 5.2 %collective-permute-start.41 = (bf16[512,256]{1,0:T(8,128)(2,1)S(1)}, bf16[512,256]{1,0:T(8,128)(2,1)S(1)}, u32[]{:S(2)}, u32[]{:S(2)}) collective-permute-start(bf16[512,256]{1,0:T(8,128)(2,1)S(1)} %fusion.4), channel_id=1, source_target_pairs={{0,8},{1,9},{2,10},{3,11},{4,12},{5,13},{6,14},{7,15},{24,16},{25,... | collective-permute-start | bytes 786440 | tf_op jit(solution)/shard_map/ppermute | solution.py:106
  120.8 2.5 %collective-permute-done.41 = bf16[512,256]{1,0:T(8,128)(2,1)S(1)} collective-permute-done((bf16[512,256]{1,0:T(8,128)(2,1)S(1)}, bf16[512,256]{1,0:T(8,128)(2,1)S(1)}, u32[]{:S(2)}, u32[]{:S(2)}) %collective-permute-start.41) | collective-permute-done | bytes 262176 | tf_op jit(solution)/shard_map/ppermute | solution.py:106
  123.3 2.9 %collective-permute-done.43 = bf16[512,256]{1,0:T(8,128)(2,1)S(1)} collective-permute-done((bf16[512,256]{1,0:T(8,128)(2,1)S(1)}, bf16[512,256]{1,0:T(8,128)(2,1)S(1)}, u32[]{:S(2)}, u32[]{:S(2)}) %collective-permute-start.43) | collective-permute-done | bytes 262176 | tf_op jit(solution)/shard_map/ppermute | solution.py:106
  127.8 5.2 %collective-permute-start.45 = (bf16[512,256]{1,0:T(8,128)(2,1)S(1)}, bf16[512,256]{1,0:T(8,128)(2,1)S(1)}, u32[]{:S(2)}, u32[]{:S(2)}) collective-permute-start(bf16[512,256]{1,0:T(8,128)(2,1)S(1)} %fusion.5), channel_id=1, source_target_pairs={{0,8},{1,9},{2,10},{3,11},{4,12},{5,13},{6,14},{7,15},{8,0},{9,1},... | collective-permute-start | bytes 786440 | tf_op jit(solution)/shard_map/ppermute | solution.py:106
  133.6 3.8 %collective-permute-done.45 = bf16[512,256]{1,0:T(8,128)(2,1)S(1)} collective-permute-done((bf16[512,256]{1,0:T(8,128)(2,1)S(1)}, bf16[512,256]{1,0:T(8,128)(2,1)S(1)}, u32[]{:S(2)}, u32[]{:S(2)}) %collective-permute-start.45) | collective-permute-done | bytes 262176 | tf_op jit(solution)/shard_map/ppermute | solution.py:106
  (133 shorter events, 45.8 us)
Async XLA Ops:
  1.0 15.0 %collective-permute-start.2 = (bf16[512,256]{1,0:T(8,128)(2,1)}, bf16[512,256]{1,0:T(8,128)(2,1)S(1)}, u32[]{:S(2)}, u32[]{:S(2)}) collective-permute-start(bf16[512,256]{1,0:T(8,128)(2,1)} %refs_2_), channel_id=1, source_target_pairs={{0,4},{1,5},{2,6},{3,7},{4,0},{5,1},{6,2},{7,3},{8,12},{9,13},{10,... | collective-permute-start | bytes 786440 | tf_op jit(solution)/shard_map/ppermute | solution.py:106
  4.0 12.1 %collective-permute-start.1 = (bf16[512,256]{1,0:T(8,128)(2,1)}, bf16[512,256]{1,0:T(8,128)(2,1)S(1)}, u32[]{:S(2)}, u32[]{:S(2)}) collective-permute-start(bf16[512,256]{1,0:T(8,128)(2,1)} %refs_2_), channel_id=1, source_target_pairs={{8,16},{9,17},{10,18},{11,19},{12,20},{13,21},{14,22},{15,23},{16,... | collective-permute-start | bytes 786440 | tf_op jit(solution)/shard_map/ppermute | solution.py:106
  4.6 11.4 %collective-permute-start = (bf16[512,256]{1,0:T(8,128)(2,1)}, bf16[512,256]{1,0:T(8,128)(2,1)S(1)}, u32[]{:S(2)}, u32[]{:S(2)}) collective-permute-start(bf16[512,256]{1,0:T(8,128)(2,1)} %refs_2_), channel_id=1, source_target_pairs={{0,8},{1,9},{2,10},{3,11},{4,12},{5,13},{6,14},{7,15},{8,0},{9,1},... | collective-permute-start | bytes 786440 | tf_op jit(solution)/shard_map/ppermute | solution.py:106
  17.5 9.7 %collective-permute-start.5 = (bf16[512,256]{1,0:T(8,128)(2,1)S(1)}, bf16[512,256]{1,0:T(8,128)(2,1)S(1)}, u32[]{:S(2)}, u32[]{:S(2)}) collective-permute-start(bf16[512,256]{1,0:T(8,128)(2,1)S(1)} %collective-permute-done.1.refs_6_), channel_id=1, source_target_pairs={{8,0},{9,1},{10,2},{11,3},{12,4},{13,5},{14,6},{15,7},{16,24},{17,... | collective-permute-start | bytes 786440 | tf_op jit(solution)/shard_map/ppermute | solution.py:106
  27.1 8.3 %collective-permute-start.10 = (bf16[512,256]{1,0:T(8,128)(2,1)S(1)}, bf16[512,256]{1,0:T(8,128)(2,1)S(1)}, u32[]{:S(2)}, u32[]{:S(2)}) collective-permute-start(bf16[512,256]{1,0:T(8,128)(2,1)S(1)} %collective-permute-done.5.refs_3_), channel_id=1, source_target_pairs={{0,4},{1,5},{2,6},{3,7},{4,0},{5,1},{6,2},{7,3},{24,28},{25,29},{2... | collective-permute-start | bytes 786440 | tf_op jit(solution)/shard_map/ppermute | solution.py:106
  31.0 8.3 %collective-permute-start.8 = (bf16[512,256]{1,0:T(8,128)(2,1)S(1)}, bf16[512,256]{1,0:T(8,128)(2,1)S(1)}, u32[]{:S(2)}, u32[]{:S(2)}) collective-permute-start(bf16[512,256]{1,0:T(8,128)(2,1)S(1)} %collective-permute-done.4.refs_2_), channel_id=1, source_target_pairs={{8,0},{9,1},{10,2},{11,3},{12,4},{13,5},{14,6},{15,7},{16,24},{17,... | collective-permute-start | bytes 786440 | tf_op jit(solution)/shard_map/ppermute | solution.py:106
  32.3 11.9 %collective-permute-start.7 = (bf16[512,256]{1,0:T(8,128)(2,1)S(1)}, bf16[512,256]{1,0:T(8,128)(2,1)S(1)}, u32[]{:S(2)}, u32[]{:S(2)}) collective-permute-start(bf16[512,256]{1,0:T(8,128)(2,1)S(1)} %collective-permute-done.1.refs_6_), channel_id=1, source_target_pairs={{8,12},{9,13},{10,14},{11,15},{12,8},{13,9},{14,10},{15,11},{16,20... | collective-permute-start | bytes 786440 | tf_op jit(solution)/shard_map/ppermute | solution.py:106
  53.9 14.1 %collective-permute-start.19 = (bf16[512,256]{1,0:T(8,128)(2,1)}, bf16[512,256]{1,0:T(8,128)(2,1)}, u32[]{:S(2)}, u32[]{:S(2)}) collective-permute-start(bf16[512,256]{1,0:T(8,128)(2,1)} %pad_maximum_fusion.11), channel_id=1, source_target_pairs={{0,2},{1,3},{2,0},{3,1},{4,6},{5,7},{6,4},{7,5},{8,10},{9,11},{10,... | collective-permute-start | bytes 786440 | tf_op jit(solution)/shard_map/ppermute | solution.py:106
  55.4 11.8 %collective-permute-start.18 = (bf16[64,1024]{1,0:T(8,128)(2,1)S(1)}, bf16[64,1024]{1,0:T(8,128)(2,1)S(1)}, u32[]{:S(2)}, u32[]{:S(2)}) collective-permute-start(bf16[64,1024]{1,0:T(8,128)(2,1)S(1)} %pad_maximum_fusion.15.refs_0_), channel_id=1, source_target_pairs={{0,20},{1,21},{2,22},{3,23},{4,16},{5,17},{6,18},{7,19},{8,28},{9,... | collective-permute-start | bytes 393224 | tf_op jit(solution)/shard_map/ppermute | solution.py:106
  56.8 10.5 %collective-permute-start.17 = (bf16[64,1024]{1,0:T(8,128)(2,1)S(1)}, bf16[64,1024]{1,0:T(8,128)(2,1)S(1)}, u32[]{:S(2)}, u32[]{:S(2)}) collective-permute-start(bf16[64,1024]{1,0:T(8,128)(2,1)S(1)} %pad_maximum_fusion.15.refs_0_), channel_id=1, source_target_pairs={{0,4},{1,5},{2,6},{3,7},{4,0},{5,1},{6,2},{7,3},{8,12},{9,13},{10,... | collective-permute-start | bytes 393224 | tf_op jit(solution)/shard_map/ppermute | solution.py:106
  58.0 10.1 %collective-permute-start.16 = (bf16[64,1024]{1,0:T(8,128)(2,1)S(1)}, bf16[64,1024]{1,0:T(8,128)(2,1)S(1)}, u32[]{:S(2)}, u32[]{:S(2)}) collective-permute-start(bf16[64,1024]{1,0:T(8,128)(2,1)S(1)} %pad_maximum_fusion.15.refs_0_), channel_id=1, source_target_pairs={{0,16},{1,17},{2,18},{3,19},{4,20},{5,21},{6,22},{7,23},{8,24},{9,... | collective-permute-start | bytes 393224 | tf_op jit(solution)/shard_map/ppermute | solution.py:106
  59.9 9.3 %collective-permute-start.20 = (bf16[512,256]{1,0:T(8,128)(2,1)}, bf16[512,256]{1,0:T(8,128)(2,1)}, u32[]{:S(2)}, u32[]{:S(2)}) collective-permute-start(bf16[512,256]{1,0:T(8,128)(2,1)} %pad_maximum_fusion.11), channel_id=1, source_target_pairs={{0,1},{1,0},{2,3},{3,2},{4,5},{5,4},{6,7},{7,6},{8,9},{9,8},{10,11... | collective-permute-start | bytes 786440 | tf_op jit(solution)/shard_map/ppermute | solution.py:106
  72.8 14.8 %collective-permute-start.28 = (bf16[256,1024]{1,0:T(8,128)(2,1)S(1)}, bf16[256,1024]{1,0:T(8,128)(2,1)S(1)}, u32[]{:S(2)}, u32[]{:S(2)}) collective-permute-start(bf16[256,1024]{1,0:T(8,128)(2,1)S(1)} %copy-done.4), channel_id=1, source_target_pairs={{0,4},{1,5},{2,6},{3,7},{4,0},{5,1},{6,2},{7,3},{8,12},{9,13},{10,... | collective-permute-start | bytes 1572872 | tf_op jit(solution)/shard_map/ppermute | solution.py:106
  74.8 17.9 %collective-permute-start.27 = (bf16[512,256]{1,0:T(8,128)(2,1)S(1)}, bf16[512,256]{1,0:T(8,128)(2,1)S(1)}, u32[]{:S(2)}, u32[]{:S(2)}) collective-permute-start(bf16[512,256]{1,0:T(8,128)(2,1)S(1)} %slice.89), channel_id=1, source_target_pairs={{0,2},{1,3},{2,0},{3,1},{4,6},{5,7},{6,4},{7,5},{8,10},{9,11},{10,... | collective-permute-start | bytes 786440 | tf_op jit(solution)/shard_map/ppermute | solution.py:106
  75.8 12.2 %collective-permute-start.23 = (bf16[64,1024]{1,0:T(8,128)(2,1)S(1)}, bf16[64,1024]{1,0:T(8,128)(2,1)S(1)}, u32[]{:S(2)}, u32[]{:S(2)}) collective-permute-start(bf16[64,1024]{1,0:T(8,128)(2,1)S(1)} %get-tuple-element.124), channel_id=1, source_target_pairs={{0,16},{1,17},{2,18},{3,19},{4,20},{5,21},{6,22},{7,23},{8,24},{9,... | collective-permute-start | bytes 393224 | tf_op jit(solution)/shard_map/ppermute | solution.py:106
  75.8 16.9 %collective-permute-start.24 = (bf16[64,1024]{1,0:T(8,128)(2,1)S(1)}, bf16[64,1024]{1,0:T(8,128)(2,1)S(1)}, u32[]{:S(2)}, u32[]{:S(2)}) collective-permute-start(bf16[64,1024]{1,0:T(8,128)(2,1)S(1)} %get-tuple-element.125), channel_id=1, source_target_pairs={{0,4},{1,5},{2,6},{3,7},{4,0},{5,1},{6,2},{7,3},{8,12},{9,13},{10,... | collective-permute-start | bytes 393224 | tf_op jit(solution)/shard_map/ppermute | solution.py:106
  76.9 15.7 %collective-permute-start.25 = (bf16[64,1024]{1,0:T(8,128)(2,1)S(1)}, bf16[64,1024]{1,0:T(8,128)(2,1)S(1)}, u32[]{:S(2)}, u32[]{:S(2)}) collective-permute-start(bf16[64,1024]{1,0:T(8,128)(2,1)S(1)} %get-tuple-element.126), channel_id=1, source_target_pairs={{0,20},{1,21},{2,22},{3,23},{4,16},{5,17},{6,18},{7,19},{8,28},{9,... | collective-permute-start | bytes 393224 | tf_op jit(solution)/shard_map/ppermute | solution.py:106
  92.7 8.4 %collective-permute-start.33 = (bf16[256,1024]{1,0:T(8,128)(2,1)S(1)}, bf16[256,1024]{1,0:T(8,128)(2,1)S(1)}, u32[]{:S(2)}, u32[]{:S(2)}) collective-permute-start(bf16[256,1024]{1,0:T(8,128)(2,1)S(1)} %collective-permute-done.28), channel_id=1, source_target_pairs={{0,1},{1,0},{2,3},{3,2},{4,5},{5,4},{6,7},{7,6},{8,9},{9,8},{10,11... | collective-permute-start | bytes 1572872 | tf_op jit(solution)/shard_map/ppermute | solution.py:106
  110.7 10.1 %collective-permute-start.42 = (bf16[512,256]{1,0:T(8,128)(2,1)S(1)}, bf16[512,256]{1,0:T(8,128)(2,1)S(1)}, u32[]{:S(2)}, u32[]{:S(2)}) collective-permute-start(bf16[512,256]{1,0:T(8,128)(2,1)S(1)} %fusion.4), channel_id=1, source_target_pairs={{8,16},{9,17},{10,18},{11,19},{12,20},{13,21},{14,22},{15,23},{16,... | collective-permute-start | bytes 786440 | tf_op jit(solution)/shard_map/ppermute | solution.py:106
  111.4 11.9 %collective-permute-start.41 = (bf16[512,256]{1,0:T(8,128)(2,1)S(1)}, bf16[512,256]{1,0:T(8,128)(2,1)S(1)}, u32[]{:S(2)}, u32[]{:S(2)}) collective-permute-start(bf16[512,256]{1,0:T(8,128)(2,1)S(1)} %fusion.4), channel_id=1, source_target_pairs={{0,8},{1,9},{2,10},{3,11},{4,12},{5,13},{6,14},{7,15},{24,16},{25,... | collective-permute-start | bytes 786440 | tf_op jit(solution)/shard_map/ppermute | solution.py:106
  116.9 9.3 %collective-permute-start.43 = (bf16[512,256]{1,0:T(8,128)(2,1)S(1)}, bf16[512,256]{1,0:T(8,128)(2,1)S(1)}, u32[]{:S(2)}, u32[]{:S(2)}) collective-permute-start(bf16[512,256]{1,0:T(8,128)(2,1)S(1)} %convolution_convert_fusion), channel_id=1, source_target_pairs={{0,4},{1,5},{2,6},{3,7},{4,0},{5,1},{6,2},{7,3},{8,12},{9,13},{10,... | collective-permute-start | bytes 786440 | tf_op jit(solution)/shard_map/ppermute | solution.py:106
  118.2 8.4 %collective-permute-start.40 = (bf16[512,256]{1,0:T(8,128)(2,1)S(1)}, bf16[512,256]{1,0:T(8,128)(2,1)S(1)}, u32[]{:S(2)}, u32[]{:S(2)}) collective-permute-start(bf16[512,256]{1,0:T(8,128)(2,1)S(1)} %get-tuple-element.154), channel_id=1, source_target_pairs={{0,16},{1,17},{2,18},{3,19},{4,20},{5,21},{6,22},{7,23},{24,8},{25... | collective-permute-start | bytes 786440 | tf_op jit(solution)/shard_map/ppermute | solution.py:106
  119.9 13.7 %collective-permute-start.39 = (bf16[512,256]{1,0:T(8,128)(2,1)S(1)}, bf16[512,256]{1,0:T(8,128)(2,1)S(1)}, u32[]{:S(2)}, u32[]{:S(2)}) collective-permute-start(bf16[512,256]{1,0:T(8,128)(2,1)S(1)} %convolution_convert_fusion.1), channel_id=1, source_target_pairs={{0,4},{1,5},{2,6},{3,7},{4,0},{5,1},{6,2},{7,3},{8,12},{9,13},{10,... | collective-permute-start | bytes 786440 | tf_op jit(solution)/shard_map/ppermute | solution.py:106
  127.8 9.6 %collective-permute-start.45 = (bf16[512,256]{1,0:T(8,128)(2,1)S(1)}, bf16[512,256]{1,0:T(8,128)(2,1)S(1)}, u32[]{:S(2)}, u32[]{:S(2)}) collective-permute-start(bf16[512,256]{1,0:T(8,128)(2,1)S(1)} %fusion.5), channel_id=1, source_target_pairs={{0,8},{1,9},{2,10},{3,11},{4,12},{5,13},{6,14},{7,15},{8,0},{9,1},... | collective-permute-start | bytes 786440 | tf_op jit(solution)/shard_map/ppermute | solution.py:106
  (28 other events, 183.3 us)

commit v8 on v7

--- a/solution.py
+++ b/solution.py
@@ -119,7 +119,6 @@
 TWO_IN = along_line({3: 1, 0: 2})
 FAR = along_line({0: 2, 1: 3, 2: 0, 3: 1})
 FAR_Y = routes(lambda z, y, x, c: (z ^ 2, 1 - y, x, c))
-PAIRS_X = routes(lambda z, y, x, c: (z ^ 1, y, 1 - x, c))
 MIX = [routes(lambda z, y, x, c, k=k: (z, y, x ^ (k >> 1), c ^ (k & 1))) for k in range(4)]
 
 
@@ -139,6 +138,91 @@
     last = send((third + inward).astype(jnp.bfloat16), MIDDLE)
     own = own + send(own_y, ACROSS_Y).astype(jnp.float32)
     return own + last.astype(jnp.float32) + paired.astype(jnp.float32)
+
+
+TAIL = 16
+
+
+def tail_rows(rows):
+    terms = []
+    for row in rows:
+        for _ in range(3):
+            term = row.astype(jnp.bfloat16).astype(jnp.float32)
+            terms.append(term)
+            row = row - term
+    terms.append(jnp.zeros((TAIL - len(terms), rows[0].shape[1]), jnp.float32))
+    return jnp.concatenate(terms, axis=0).astype(jnp.bfloat16)
+
+
+def tail_of(message, row):
+    terms = message[-TAIL:].astype(jnp.float32)[3 * row : 3 * row + 3]
+    return terms[0:1] + terms[1:2] + terms[2:3]
+
+
+def in_vmem(kernel, results, *operands):
+    inside = pl.BlockSpec(memory_space=pltpu.VMEM)
+    size = sum(array.size * array.dtype.itemsize for array in (*operands, *results))
+    return pl.pallas_call(
+        kernel,
+        in_specs=[inside] * len(operands),
+        out_specs=[inside] * len(results),
+        out_shape=results,
+        compiler_params=pltpu.CompilerParams(vmem_limit_bytes=12 * 1024 * 1024),
+        cost_estimate=pl.CostEstimate(flops=size, bytes_accessed=size, transcendentals=0),
+    )(*operands)
+
+
+def after_cores(mine, message, loss):
+    rows, width = mine.shape[0], mine.shape[1] // 2
+    half = rows // 2
+
+    def kernel(mine_ref, message_ref, loss_ref, kept_ref, out_ref, total_ref):
+        kept_ref[...] = mine_ref[:, :width] + message_ref[:rows, :width].astype(jnp.float32)
+        sent = mine_ref[:, width:] + message_ref[:rows, width:].astype(jnp.float32)
+        out_ref[:rows] = sent.astype(jnp.bfloat16)
+        total = loss_ref[...] + tail_of(message_ref, 0)
+        total_ref[...] = total
+        out_ref[rows:] = tail_rows([total[:, :half], total[:, half:]])
+
+    results = [
+        jax.ShapeDtypeStruct((rows, width), jnp.float32),
+        jax.ShapeDtypeStruct((rows + TAIL, width), jnp.bfloat16),
+        jax.ShapeDtypeStruct((1, rows), jnp.float32),
+    ]
+    return in_vmem(kernel, results, mine, message, loss)
+
+
+def after_sides(kept, message, loss):
+    rows, width = kept.shape[0] // 2, kept.shape[1]
+
+    def kernel(kept_ref, message_ref, loss_ref, own_ref, out_ref, total_ref):
+        own_ref[...] = kept_ref[:rows] + message_ref[:rows].astype(jnp.float32)
+        sent = kept_ref[rows:] + message_ref[rows : 2 * rows].astype(jnp.float32)
+        out_ref[:rows] = sent.astype(jnp.bfloat16)
+        total_ref[...] = loss_ref[:, :rows] + tail_of(message_ref, 0)
+        out_ref[rows:] = tail_rows([loss_ref[:, rows:] + tail_of(message_ref, 1)])
+
+    results = [
+        jax.ShapeDtypeStruct((rows, width), jnp.float32),
+        jax.ShapeDtypeStruct((rows + TAIL, width), jnp.bfloat16),
+        jax.ShapeDtypeStruct((1, rows), jnp.float32),
+    ]
+    return in_vmem(kernel, results, kept, message, loss)
+
+
+def after_line(own, message, loss):
+    rows, width = own.shape
+
+    def kernel(own_ref, message_ref, loss_ref, out_ref, total_ref):
+        total = own_ref[...] + message_ref[:rows].astype(jnp.float32)
+        out_ref[...] = total.astype(jnp.bfloat16)
+        total_ref[...] = loss_ref[...] + tail_of(message_ref, 0)
+
+    results = [
+        jax.ShapeDtypeStruct((rows, width), jnp.bfloat16),
+        jax.ShapeDtypeStruct((1, rows), jnp.float32),
+    ]
+    return in_vmem(kernel, results, own, message, loss)
 
 
 def project(prompts, responses, blocks, weights, total, kind):
@@ -203,54 +287,58 @@
     )(blocks, prompts, responses, *operands)
 
 
-def compare(half, other, held, wanted, ids, row_count):
-    prompt_rows, width = half.shape[0], half.shape[1] // 2
+def compare(groups, held, wanted, ids, row_count):
+    rows, width = groups[0][0].shape
+    prompt_rows, across = rows * len(groups), len(groups[0])
     quarter = held[0].shape[0]
-    count, full = len(held) * quarter, 4 * width
+    count, full = len(held) * quarter, across * width
     factor = LOGIT_SCALE / math.sqrt(E)
-
-    def kernel(wanted_ref, ids_ref, half_ref, other_ref, *refs):
+    operands = [wanted, ids, *[piece for group in groups for piece in group], *held]
+
+    def kernel(wanted_ref, ids_ref, *refs):
+        group_refs = [refs[g * across : (g + 1) * across] for g in range(len(groups))]
+        refs = refs[len(groups) * across :]
         held_refs, refs = refs[: len(held)], refs[len(held) :]
         loss_ref, mine_ref, away_ref, *part_refs, rows_ref = refs
         for k, ref in enumerate(held_refs):
             rows_ref[k * quarter : (k + 1) * quarter] = ref[...]
-        places = [
-            (half_ref, 0, mine_ref),
-            (other_ref, 0, away_ref),
-            (half_ref, 1, mine_ref),
-            (other_ref, 1, away_ref),
-        ]
-        scores = jnp.zeros((count, prompt_rows), jnp.float32)
-        for k, (ref, at, _) in enumerate(places):
-            scores += cross_cols(
-                rows_ref[:, k * width : (k + 1) * width], ref[:, at * width : (at + 1) * width]
-            )
-        scores = scores * factor + LOGIT_BIAS
-        match = wanted_ref[...] == ids_ref[...]
-        margin = jnp.where(match, -scores, scores)
-        small = jnp.exp(-jnp.abs(margin))
-        loss_ref[...] = jnp.sum(
-            jnp.maximum(margin, 0.0) + jnp.log1p(small), axis=0, keepdims=True
-        )
-        share = jnp.where(margin >= 0.0, 1.0, small) / (1.0 + small)
-        share = share * (factor / row_count)
-        weight = jnp.where(match, -share, share).astype(jnp.bfloat16)
-        for k, (ref, at, out) in enumerate(places):
-            columns, goal = slice(k * width, (k + 1) * width), slice(at * width, (at + 1) * width)
-            part = matmul(weight, ref[:, goal])
+        weights, losses = [], []
+        for g, pieces in enumerate(group_refs):
+            scores = jnp.zeros((count, rows), jnp.float32)
+            for k, ref in enumerate(pieces):
+                scores += cross_cols(rows_ref[:, k * width : (k + 1) * width], ref[...])
+            scores = scores * factor + LOGIT_BIAS
+            match = wanted_ref[:, g * rows : (g + 1) * rows] == ids_ref[...]
+            margin = jnp.where(match, -scores, scores)
+            small = jnp.exp(-jnp.abs(margin))
+            soft = jnp.maximum(margin, 0.0) + jnp.log1p(small)
+            losses.append(jnp.sum(soft, axis=0, keepdims=True))
+            share = jnp.where(margin >= 0.0, 1.0, small) / (1.0 + small)
+            share = share * (factor / row_count)
+            weights.append(jnp.where(match, -share, share).astype(jnp.bfloat16))
+        for k in range(across):
+            columns = slice(k * width, (k + 1) * width)
+            part = sum(matmul(weight, pieces[k][...]) for weight, pieces in zip(weights, group_refs))
             for block, part_ref in enumerate(part_refs):
-                rows = part[block * quarter : (block + 1) * quarter]
-                part_ref[:, columns] = rows.astype(part_ref.dtype)
-            out[:, goal] = cross_rows(weight, rows_ref[:, columns]).astype(out.dtype)
+                part_rows = part[block * quarter : (block + 1) * quarter]
+                part_ref[:, columns] = part_rows.astype(part_ref.dtype)
+        for k in range(across):
+            out, goal = (mine_ref, away_ref)[k % 2], slice(k // 2 * width, (k // 2 + 1) * width)
+            for g, weight in enumerate(weights):
+                part = cross_rows(weight, rows_ref[:, k * width : (k + 1) * width])
+                out[g * rows : (g + 1) * rows, goal] = part.astype(out.dtype)
+        loss = jnp.concatenate(losses, axis=1)
+        loss_ref[...] = loss
+        away_ref[prompt_rows:] = tail_rows([loss])
 
     return pl.pallas_call(
         kernel,
-        in_specs=[pl.BlockSpec(memory_space=pltpu.VMEM)] * (4 + len(held)),
+        in_specs=[pl.BlockSpec(memory_space=pltpu.VMEM)] * len(operands),
         out_specs=[pl.BlockSpec(memory_space=pltpu.VMEM)] * (3 + len(held)),
         out_shape=[
             jax.ShapeDtypeStruct((1, prompt_rows), jnp.float32),
-            jax.ShapeDtypeStruct((prompt_rows, 2 * width), jnp.float32),
-            jax.ShapeDtypeStruct((prompt_rows, 2 * width), jnp.bfloat16),
+            jax.ShapeDtypeStruct((prompt_rows, full // 2), jnp.float32),
+            jax.ShapeDtypeStruct((prompt_rows + TAIL, full // 2), jnp.bfloat16),
             jax.ShapeDtypeStruct((quarter, full), jnp.float32),
         ]
         + [jax.ShapeDtypeStruct((quarter, full), jnp.bfloat16)] * (len(held) - 1),
@@ -261,7 +349,7 @@
             bytes_accessed=6 * prompt_rows * full + 6 * count * full,
             transcendentals=2 * prompt_rows * count,
         ),
-    )(wanted, ids, half, other, *held)
+    )(*operands)
 
 
 def full_window(prompts, responses, head_projection_matrix, positive):
@@ -274,7 +362,7 @@
 
     here = [(z ^ k) * PAIR + y for k in range(LINE)]
     there = [(z ^ k) * PAIR + 1 - y for k in range(LINE)]
-    orders = [here[0], there[0], here[1], there[1]], [here[2], there[2], here[3]], [there[3]]
+    orders = here[:1] + there[:1] + here[1:2], [there[1], here[2], there[2], here[3]], [there[3]]
     ids = jnp.stack([here[0], here[2], there[0], there[2]]) * row_count + mp * quarter
     ids = (ids[:, None] + lax.iota(jnp.int32, quarter)).reshape(-1, 1)
     own, orders, here, there, places, even, left, ids = tie(
@@ -294,15 +382,16 @@
     def features(array, start):
         return lax.dynamic_slice(array, (zero, start), (row_count, depth))
 
-    first, middle, own_y, positive_z = tie(
-        (
-            send(own, PAIRS),
-            send(own, MIDDLE),
-            send(own, ACROSS_Y),
-            send(positive, PAIRS),
-        )
-    )
-    wanted = jnp.concatenate([positive, positive_z], axis=0)[None, :]
+    own_y = send(own, ACROSS_Y)
+    first, middle = send(own, PAIRS), send(own, MIDDLE)
+    wanted = jnp.concatenate([positive, send(positive, PAIRS)], axis=0)[None, :]
+    inner, outer, first_y = send(first, MIDDLE), send(middle, OUTWARD), send(first, ACROSS_Y)
+    last = send(inner, OUTWARD)
+    emb = project(
+        prompts, responses, orders[0], [(own,), (own_y,), (first,)], None, jnp.float32
+    )
+    inner_late, middle_late, emb = tie((inner, middle, emb))
+    inner_y, outer_y = send(inner_late, Y_MIDDLE), send(outer, Y_ENDS)
     columns = [
         jnp.concatenate([features(prompts, start).T, features(responses, start).T], axis=1)
         for start in here + there[:2]
@@ -310,29 +399,16 @@
     mine = jnp.concatenate(
         [jnp.where(even, features(prompts, f), features(responses, f)) for f in there[2:]], axis=1
     )
-    inner, outer, first_y, wanted, columns, mine = tie(
-        (send(first, MIDDLE), send(middle, OUTWARD), send(first, ACROSS_Y), wanted, columns, mine)
-    )
-    emb = project(
-        prompts,
-        responses,
-        orders[0],
-        [(own,), (own_y,), (first,), (first_y,)],
-        None,
-        jnp.float32,
-    )
-    last, inner_y, outer_y, emb = tie(
-        (send(inner, OUTWARD), send(inner, Y_MIDDLE), send(outer, Y_ENDS), emb)
-    )
+    emb, columns, wanted, mine = tie((emb, columns, wanted, mine))
     emb = project(
         prompts,
         responses,
         orders[1],
-        [(inner, outer), (inner_y, outer_y), (middle, last)],
+        [(first_y,), (inner, outer), (inner_y, outer_y), (middle, last)],
         emb,
         jnp.float32,
     )
-    middle_y, last_y, emb = tie((send(middle, Y_MIDDLE), send(last, Y_ENDS), emb))
+    middle_y, last_y, emb = tie((send(middle_late, Y_MIDDLE), send(last, Y_ENDS), emb))
     emb = project(prompts, responses, orders[2], [(middle_y, last_y)], emb, jnp.bfloat16)
     prompt_emb, response_emb = emb[:row_count], emb[row_count:]
 
@@ -340,54 +416,43 @@
     for k in range(SIDE * CORES):
         piece = lax.dynamic_slice(response_emb, (places[k], zero), (quarter, width))
         pieces.append(piece if k == 0 else send(piece, MIX[k]))
+    pieces[1], mine, prompt_emb = tie((pieces[1], mine, prompt_emb))
+    fetched = send(mine, ACROSS_Y)
+    prompt_pair = send(prompt_emb, PAIRS)
     response_rows = jnp.concatenate(pieces, axis=1)
-
-    response_rows, mine = tie((response_rows, mine))
+    response_rows, prompt_emb = tie((response_rows, prompt_emb))
+
     held = [send(response_rows, table) for table in (FAR, ACROSS_Y, FAR_Y)]
-    near = jnp.concatenate([prompt_emb, send(prompt_emb, PAIRS)], axis=0)
-    near_c = send(near, ACROSS_C)
-    held, beside = tie((held, send(near, ACROSS_X)))
-    half = jnp.concatenate([near, beside], axis=1)
-    other = jnp.concatenate([near_c, send(beside, ACROSS_C)], axis=1)
-    fetched = send(mine, ACROSS_Y)
-    losses, mine, away, *parts = compare(
-        half, other, [response_rows, *held], wanted, ids, row_count
-    )
+    groups = [prompt_emb, prompt_pair]
+    groups = [[block, send(block, ACROSS_C), send(block, ACROSS_X)] for block in groups]
+    held, fetched, *beside = tie((held, fetched, *[group[2] for group in groups]))
+    groups = [[*group[:2], x, send(x, ACROSS_C)] for group, x in zip(groups, beside)]
+    sibling = send(fetched, ACROSS_C)
+    losses, mine, away, *parts = compare(groups, [response_rows, *held], wanted, ids, row_count)
 
     back = [send(part, table) for part, table in zip(parts[1:], (FAR, ACROSS_Y, FAR_Y))]
-    losses = losses[0]
-    losses = losses + send(losses, ACROSS_C)
-    mine = mine + send(away, ACROSS_C).astype(jnp.float32)
-    aside = send(mine[:, width:].astype(jnp.bfloat16), ACROSS_X)
-    back, aside, fetched = tie((back, aside, fetched))
-    grad = parts[0] + sum(part.astype(jnp.float32) for part in back)
-    grad = grad.astype(jnp.bfloat16)
-    mine = mine[:, :width] + aside.astype(jnp.float32)
-    far = send(mine[row_count:].astype(jnp.bfloat16), PAIRS)
-    sibling = send(fetched, ACROSS_C)
-
-    pieces = [grad[:, k * width : (k + 1) * width] for k in range(SIDE * CORES)]
-    pieces = [pieces[0]] + [send(pieces[k], MIX[k]) for k in range(1, SIDE * CORES)]
-    pieces, far, sibling = tie((pieces, far, sibling))
-    swapped = [jnp.where(even, pieces[k], pieces[k ^ 1]) for k in range(SIDE * CORES)]
-    swapped = [jnp.where(left, swapped[k], swapped[k ^ 2]) for k in range(SIDE * CORES)]
-    grad_response = jnp.concatenate(swapped, axis=0)
-    grad_response_y = send(grad_response, ACROSS_Y)
-    grad_prompt = (mine[:row_count] + far.astype(jnp.float32)).astype(jnp.bfloat16)
-    grad_prompt_y = send(grad_prompt, ACROSS_Y)
-    losses_x = send(losses[:row_count], ACROSS_X)
-    losses_z = send(losses[row_count:], PAIRS)
-    losses_xz = send(losses[row_count:], PAIRS_X)
+    mine, aside, losses = after_cores(mine, send(away, ACROSS_C), losses)
     columns_y = [
         jnp.concatenate(
             [array[:, k * depth : (k + 1) * depth].T for array in (fetched, sibling)], axis=1
         )
         for k in range(2)
     ]
-    grad_response_y, grad_prompt_y, losses_x, losses_z, losses_xz, columns_y = tie(
-        (grad_response_y, grad_prompt_y, losses_x, losses_z, losses_xz, columns_y)
-    )
-    losses = (losses[:row_count] + losses_x) + (losses_z + losses_xz)
+    back, aside, columns_y = tie((back, send(aside, ACROSS_X), columns_y))
+    grad = parts[0] + sum(part.astype(jnp.float32) for part in back)
+    grad = grad.astype(jnp.bfloat16)
+    mine, far, losses = after_sides(mine, aside, losses)
+
+    pieces = [grad[:, k * width : (k + 1) * width] for k in range(SIDE * CORES)]
+    pieces = [pieces[0]] + [send(pieces[k], MIX[k]) for k in range(1, SIDE * CORES)]
+    pieces, far = tie((pieces, send(far, PAIRS)))
+    swapped = [jnp.where(even, pieces[k], pieces[k ^ 1]) for k in range(SIDE * CORES)]
+    swapped = [jnp.where(left, swapped[k], swapped[k ^ 2]) for k in range(SIDE * CORES)]
+    grad_response = jnp.concatenate(swapped, axis=0)
+    grad_response_y = send(grad_response, ACROSS_Y)
+    grad_prompt, losses = after_line(mine, far, losses)
+    grad_prompt_y = send(grad_prompt, ACROSS_Y)
+    grad_response_y, grad_prompt_y = tie((grad_response_y, grad_prompt_y))
 
     grads = jnp.concatenate([grad_prompt, grad_response], axis=0)
     grads_y = jnp.concatenate(
@@ -404,7 +469,7 @@
     first_y, own_y = [matmul(columns[k], grads).astype(jnp.bfloat16) for k in (5, 4)]
     first, own = [matmul(columns[k], grads) for k in (1, 0)]
     head_grad = line_reduce(own, first, second, third, second_b, third_b, own_y, first_y)
-    return (losses / row_count, head_grad)
+    return (losses[0] / row_count, head_grad)
 
 
 def per_device(prompts, responses, head_projection_matrix, positive):

time: 139 us -> 127 us (0.914)
  waiting for transfers between devices: 58.3 us -> 48.3 us
    ppermute x46 -> x45, waiting for transfers between devices: 58.3 us -> 48.3 us  [send(): return lax.ppermute(block, ('dp', 'mp'), table)]
    concatenate x4 -> x1, other arithmetic: 2.79 us -> 0.01 us  [full_window(): wanted = jnp.concatenate([positive, send(positive, PAIRS)], axis=0)[None, :]]
    concatenate x6, other arithmetic: 1.02 us -> 2.61 us  [full_window(): jnp.concatenate([features(prompts, start).T, features(responses, start).T...]
    ppermute x46 -> x45, starting transfers between devices: 57.2 us -> 56.1 us  [send(): return lax.ppermute(block, ('dp', 'mp'), table)]
  transfers between devices with their start and end apart: 46 -> 45, of which waited for: 21 -> 22; matrix products, arithmetic and copies ran while one was open for 8% -> 8% of each run, Pallas kernels for 3% -> 4%
where the time goes in v8:
time: 127 us; the launch traced here: 126 us
  starting transfers between devices  56.1 us (44%)
  waiting for transfers between devices  48.3 us (38%)
  other arithmetic  9.8 us (8%)
  Pallas kernels  6.83 us (5%)
  matrix products  2.73 us (2%)
    ppermute x45, starting transfers between devices, send(): return lax.ppermute(block, ('dp', 'mp'), table)  56.1 us
    ppermute x45, waiting for transfers between devices, send(): return lax.ppermute(block, ('dp', 'mp'), table)  48.3 us
    pallas_call x3, Pallas kernels, project(): pl.pallas_call(kernel, in_specs=[pl.BlockSpec(memory_space=pltpu.SMEM)] +...  5.04 us
    select_n x1, other arithmetic, full_window(): jnp.where(even, features(prompts, f), features(responses, f))  4.96 us
    dot_general x8, matrix products, matmul(): jnp.dot(left_side, righthand_term, preferred_element_type=jnp.float32)  2.73 us
    concatenate x6, other arithmetic, full_window(): jnp.concatenate([features(prompts, start).T, features(responses, start).T...  2.61 us
  transfers between devices with their start and end apart: 45, of which 22 were waited for; matrix products, arithmetic and copies ran while one was open for 8% of the time, Pallas kernels for 4%

profile of v8, /device:TPU:0, one launch (start us, length us, event | category | flops | bytes accessed | tf_op | source)
XLA Modules:
  0.0 125.8 jit_solution(13512907590442245173)
XLA Ops:
  1.0 3.0 %collective-permute-start = (bf16[512,256]{1,0:T(8,128)(2,1)}, bf16[512,256]{1,0:T(8,128)(2,1)S(1)}, u32[]{:S(2)}, u32[]{:S(2)}) collective-permute-start(bf16[512,256]{1,0:T(8,128)(2,1)} %refs_2_), channel_id=1, source_target_pairs={{0,8},{1,9},{2,10},{3,11},{4,12},{5,13},{6,14},{7,15},{8,0},{9,1},... | collective-permute-start | bytes 786440 | tf_op jit(solution)/shard_map/ppermute | solution.py:106
  6.3 4.4 %collective-permute-start.4 = (s32[256]{0:T(256)}, s32[256]{0:T(256)S(1)}, u32[]{:S(2)}, u32[]{:S(2)}) collective-permute-start(s32[256]{0:T(256)} %param.7), channel_id=1, source_target_pairs={{0,8},{1,9},{2,10},{3,11},{4,12},{5,13},{6,14},{7,15},{8,0},{9,1},... | collective-permute-start | bytes 3080 | tf_op jit(solution)/shard_map/ppermute | solution.py:106
  10.7 5.0 %dynamic-slice_select_fusion.1 = (bf16[256,512]{1,0:T(8,128)(2,1)S(1)}, bf16[256,512]{1,0:T(8,128)(2,1)S(1)}, bf16[512,256]{0,1:T(8,128)(2,1)S(1)}, bf16[512,256...) fusion(bf16[256,4096]{1,0:T(8,128)(2,1)} %refs_1_.5, ...), kind=kLoop, calls=%fused_computation.24 | loop fusion | flops 262144 | bytes 7864353 | tf_op jit(solution)/shard_map/jit(_where)/select_n | solution.py:400
  21.7 2.0 %shard_map.59.refs_9_ = f32[512,256]{1,0:T(8,128)S(1)} custom-call(s32[3]{0:T(128)S(1)} %pad_add_fusion.1.block_ref, bf16[256,4096]{1,0:T(8,128)(2,1)S(1)} %copy-done, bf16[256,4096]{1,0:T(8,128)(2,1)S(1)} %copy-done.1, bf16[512,256]{1,0:T(8,128)(2,1)S(1)} %copy-done.2, bf16[512,256]{1,0:T(8,128)(2,1)S(1)} %collective-permute-done.3.refs_3_, ...), custom_call_target="tpu_custom_call" | custom-call | flops 402653184 | bytes 2359296 | tf_op jit(solution)/shard_map/pallas_call | solution.py:269
  24.4 1.8 %collective-permute-done.9.refs_4_ = bf16[512,256]{1,0:T(8,128)(2,1)S(1)} collective-permute-done((bf16[512,256]{1,0:T(8,128)(2,1)S(1)}, bf16[512,256]{1,0:T(8,128)(2,1)S(1)}, u32[]{:S(2)}, u32[]{:S(2)}) %collective-permute-start.9) | collective-permute-done | bytes 262176 | tf_op jit(solution)/shard_map/ppermute | solution.py:106
  26.2 2.4 %collective-permute-start.11 = (bf16[512,256]{1,0:T(8,128)(2,1)S(1)}, bf16[512,256]{1,0:T(8,128)(2,1)S(1)}, u32[]{:S(2)}, u32[]{:S(2)}) collective-permute-start(bf16[512,256]{1,0:T(8,128)(2,1)S(1)} %collective-permute-done.9.refs_4_), channel_id=1, source_target_pairs={{0,4},{1,5},{2,6},{3,7},{4,0},{5,1},{6,2},{7,3},{24,28},{25,29},{2... | collective-permute-start | bytes 786440 | tf_op jit(solution)/shard_map/ppermute | solution.py:106
  31.3 2.4 %collective-permute-start.7 = (bf16[512,256]{1,0:T(8,128)(2,1)S(1)}, bf16[512,256]{1,0:T(8,128)(2,1)S(1)}, u32[]{:S(2)}, u32[]{:S(2)}) collective-permute-start(bf16[512,256]{1,0:T(8,128)(2,1)S(1)} %collective-permute-done.6.refs_8_), channel_id=1, source_target_pairs={{0,4},{1,5},{2,6},{3,7},{4,0},{5,1},{6,2},{7,3},{24,28},{25,29},{2... | collective-permute-start | bytes 786440 | tf_op jit(solution)/shard_map/ppermute | solution.py:106
  35.1 2.4 %shard_map.60.refs_4_ = f32[512,256]{1,0:T(8,128)S(1)} custom-call(s32[4]{0:T(128)S(1)} %get-tuple-element.99.block_ref, bf16[256,4096]{1,0:T(8,128)(2,1)S(1)} %copy-done, bf16[256,4096]{1,0:T(8,128)(2,1)S(1)} %copy-done.1, bf16[512,256]{1,0:T(8,128)(2,1)S(1)} %collective-permute-done.8.refs_2_, bf16[512,256]{1,0:T(8,128)(2,1)S(1)} %collective-permute-done.1.refs_3_, ...), custom_call_target="tpu_custom_call" | custom-call | flops 536870912 | bytes 3932160 | tf_op jit(solution)/shard_map/pallas_call | solution.py:269
  37.5 2.6 %collective-permute-done.7.refs_3_ = bf16[512,256]{1,0:T(8,128)(2,1)S(1)} collective-permute-done((bf16[512,256]{1,0:T(8,128)(2,1)S(1)}, bf16[512,256]{1,0:T(8,128)(2,1)S(1)}, u32[]{:S(2)}, u32[]{:S(2)}) %collective-permute-start.7) | collective-permute-done | bytes 262176 | tf_op jit(solution)/shard_map/ppermute | solution.py:106
  44.2 2.1 %collective-permute-done.14 = bf16[64,256]{1,0:T(8,128)(2,1)S(1)} collective-permute-done((bf16[64,256]{1,0:T(8,128)(2,1)S(1)}, bf16[64,256]{1,0:T(8,128)(2,1)S(1)}, u32[]{:S(2)}, u32[]{:S(2)}) %collective-permute-start.14) | collective-permute-done | bytes 32800 | tf_op jit(solution)/shard_map/ppermute | solution.py:106
  47.6 4.6 %collective-permute-start.16 = (bf16[64,1024]{1,0:T(8,128)(2,1)S(1)}, bf16[64,1024]{1,0:T(8,128)(2,1)S(1)}, u32[]{:S(2)}, u32[]{:S(2)}) collective-permute-start(bf16[64,1024]{1,0:T(8,128)(2,1)S(1)} %pad_maximum_fusion.12.refs_8_), channel_id=1, source_target_pairs={{0,16},{1,17},{2,18},{3,19},{4,20},{5,21},{6,22},{7,23},{8,24},{9,... | collective-permute-start | bytes 393224 | tf_op jit(solution)/shard_map/ppermute | solution.py:106
  53.8 2.8 %collective-permute-start.18 = (bf16[64,1024]{1,0:T(8,128)(2,1)S(1)}, bf16[64,1024]{1,0:T(8,128)(2,1)S(1)}, u32[]{:S(2)}, u32[]{:S(2)}) collective-permute-start(bf16[64,1024]{1,0:T(8,128)(2,1)S(1)} %pad_maximum_fusion.12.refs_8_), channel_id=1, source_target_pairs={{0,20},{1,21},{2,22},{3,23},{4,16},{5,17},{6,18},{7,19},{8,28},{9,... | collective-permute-start | bytes 393224 | tf_op jit(solution)/shard_map/ppermute | solution.py:106
  56.6 2.2 %collective-permute-done.16.refs_9_ = bf16[64,1024]{1,0:T(8,128)(2,1)S(1)} collective-permute-done((bf16[64,1024]{1,0:T(8,128)(2,1)S(1)}, bf16[64,1024]{1,0:T(8,128)(2,1)S(1)}, u32[]{:S(2)}, u32[]{:S(2)}) %collective-permute-start.16) | collective-permute-done | bytes 131104 | tf_op jit(solution)/shard_map/ppermute | solution.py:106
  60.8 4.1 %collective-permute-done.18.refs_11_ = bf16[64,1024]{1,0:T(8,128)(2,1)S(1)} collective-permute-done((bf16[64,1024]{1,0:T(8,128)(2,1)S(1)}, bf16[64,1024]{1,0:T(8,128)(2,1)S(1)}, u32[]{:S(2)}, u32[]{:S(2)}) %collective-permute-start.18) | collective-permute-done | bytes 131104 | tf_op jit(solution)/shard_map/ppermute | solution.py:106
  69.5 2.2 %collective-permute-start.27 = (bf16[64,1024]{1,0:T(8,128)(2,1)S(1)}, bf16[64,1024]{1,0:T(8,128)(2,1)S(1)}, u32[]{:S(2)}, u32[]{:S(2)}) collective-permute-start(bf16[64,1024]{1,0:T(8,128)(2,1)S(1)} %get-tuple-element.124), channel_id=1, source_target_pairs={{0,16},{1,17},{2,18},{3,19},{4,20},{5,21},{6,22},{7,23},{8,24},{9,... | collective-permute-start | bytes 393224 | tf_op jit(solution)/shard_map/ppermute | solution.py:106
  75.6 6.7 %collective-permute-done.27 = bf16[64,1024]{1,0:T(8,128)(2,1)S(1)} collective-permute-done((bf16[64,1024]{1,0:T(8,128)(2,1)S(1)}, bf16[64,1024]{1,0:T(8,128)(2,1)S(1)}, u32[]{:S(2)}, u32[]{:S(2)}) %collective-permute-start.27) | collective-permute-done | bytes 131104 | tf_op jit(solution)/shard_map/ppermute | solution.py:106
  82.4 3.0 %collective-permute-done.29 = bf16[64,1024]{1,0:T(8,128)(2,1)S(1)} collective-permute-done((bf16[64,1024]{1,0:T(8,128)(2,1)S(1)}, bf16[64,1024]{1,0:T(8,128)(2,1)S(1)}, u32[]{:S(2)}, u32[]{:S(2)}) %collective-permute-start.29) | collective-permute-done | bytes 131104 | tf_op jit(solution)/shard_map/ppermute | solution.py:106
  87.5 2.1 %collective-permute-done.33 = bf16[64,256]{1,0:T(8,128)(2,1)S(1)} collective-permute-done((bf16[64,256]{1,0:T(8,128)(2,1)S(1)}, bf16[64,256]{1,0:T(8,128)(2,1)S(1)}, u32[]{:S(2)}, u32[]{:S(2)}) %collective-permute-start.33) | collective-permute-done | bytes 32800 | tf_op jit(solution)/shard_map/ppermute | solution.py:106
  93.2 5.8 %collective-permute-done.36 = bf16[256,256]{1,0:T(8,128)(2,1)S(1)} collective-permute-done((bf16[256,256]{1,0:T(8,128)(2,1)S(1)}, bf16[256,256]{1,0:T(8,128)(2,1)S(1)}, u32[]{:S(2)}, u32[]{:S(2)}) %collective-permute-start.36) | collective-permute-done | bytes 131104 | tf_op jit(solution)/shard_map/ppermute | solution.py:106
  100.1 3.9 %collective-permute-start.40 = (bf16[512,256]{1,0:T(8,128)(2,1)S(1)}, bf16[512,256]{1,0:T(8,128)(2,1)S(1)}, u32[]{:S(2)}, u32[]{:S(2)}) collective-permute-start(bf16[512,256]{1,0:T(8,128)(2,1)S(1)} %fusion), channel_id=1, source_target_pairs={{0,8},{1,9},{2,10},{3,11},{4,12},{5,13},{6,14},{7,15},{24,16},{25,... | collective-permute-start | bytes 786440 | tf_op jit(solution)/shard_map/ppermute | solution.py:106
  104.7 4.0 %collective-permute-start.39 = (bf16[512,256]{1,0:T(8,128)(2,1)S(1)}, bf16[512,256]{1,0:T(8,128)(2,1)S(1)}, u32[]{:S(2)}, u32[]{:S(2)}) collective-permute-start(bf16[512,256]{1,0:T(8,128)(2,1)S(1)} %get-tuple-element.156), channel_id=1, source_target_pairs={{0,16},{1,17},{2,18},{3,19},{4,20},{5,21},{6,22},{7,23},{24,8},{25... | collective-permute-start | bytes 786440 | tf_op jit(solution)/shard_map/ppermute | solution.py:106
  111.9 2.8 %collective-permute-done.39 = bf16[512,256]{1,0:T(8,128)(2,1)S(1)} collective-permute-done((bf16[512,256]{1,0:T(8,128)(2,1)S(1)}, bf16[512,256]{1,0:T(8,128)(2,1)S(1)}, u32[]{:S(2)}, u32[]{:S(2)}) %collective-permute-start.39) | collective-permute-done | bytes 262176 | tf_op jit(solution)/shard_map/ppermute | solution.py:106
  114.7 3.6 %collective-permute-done.42 = bf16[512,256]{1,0:T(8,128)(2,1)S(1)} collective-permute-done((bf16[512,256]{1,0:T(8,128)(2,1)S(1)}, bf16[512,256]{1,0:T(8,128)(2,1)S(1)}, u32[]{:S(2)}, u32[]{:S(2)}) %collective-permute-start.42) | collective-permute-done | bytes 262176 | tf_op jit(solution)/shard_map/ppermute | solution.py:106
  121.7 3.2 %collective-permute-done.44 = bf16[512,256]{1,0:T(8,128)(2,1)S(1)} collective-permute-done((bf16[512,256]{1,0:T(8,128)(2,1)S(1)}, bf16[512,256]{1,0:T(8,128)(2,1)S(1)}, u32[]{:S(2)}, u32[]{:S(2)}) %collective-permute-start.44) | collective-permute-done | bytes 262176 | tf_op jit(solution)/shard_map/ppermute | solution.py:106
  (133 shorter events, 45.5 us)
Async XLA Ops:
  1.0 14.7 %collective-permute-start = (bf16[512,256]{1,0:T(8,128)(2,1)}, bf16[512,256]{1,0:T(8,128)(2,1)S(1)}, u32[]{:S(2)}, u32[]{:S(2)}) collective-permute-start(bf16[512,256]{1,0:T(8,128)(2,1)} %refs_2_), channel_id=1, source_target_pairs={{0,8},{1,9},{2,10},{3,11},{4,12},{5,13},{6,14},{7,15},{8,0},{9,1},... | collective-permute-start | bytes 786440 | tf_op jit(solution)/shard_map/ppermute | solution.py:106
  4.0 12.6 %collective-permute-start.2 = (bf16[512,256]{1,0:T(8,128)(2,1)}, bf16[512,256]{1,0:T(8,128)(2,1)S(1)}, u32[]{:S(2)}, u32[]{:S(2)}) collective-permute-start(bf16[512,256]{1,0:T(8,128)(2,1)} %refs_2_), channel_id=1, source_target_pairs={{8,16},{9,17},{10,18},{11,19},{12,20},{13,21},{14,22},{15,23},{16,... | collective-permute-start | bytes 786440 | tf_op jit(solution)/shard_map/ppermute | solution.py:106
  4.7 17.0 %collective-permute-start.3 = (bf16[512,256]{1,0:T(8,128)(2,1)}, bf16[512,256]{1,0:T(8,128)(2,1)S(1)}, u32[]{:S(2)}, u32[]{:S(2)}) collective-permute-start(bf16[512,256]{1,0:T(8,128)(2,1)} %refs_2_), channel_id=1, source_target_pairs={{0,4},{1,5},{2,6},{3,7},{4,0},{5,1},{6,2},{7,3},{8,12},{9,13},{10,... | collective-permute-start | bytes 786440 | tf_op jit(solution)/shard_map/ppermute | solution.py:106
  6.3 23.3 %collective-permute-start.4 = (s32[256]{0:T(256)}, s32[256]{0:T(256)S(1)}, u32[]{:S(2)}, u32[]{:S(2)}) collective-permute-start(s32[256]{0:T(256)} %param.7), channel_id=1, source_target_pairs={{0,8},{1,9},{2,10},{3,11},{4,12},{5,13},{6,14},{7,15},{8,0},{9,1},... | collective-permute-start | bytes 3080 | tf_op jit(solution)/shard_map/ppermute | solution.py:106
  16.6 9.6 %collective-permute-start.9 = (bf16[512,256]{1,0:T(8,128)(2,1)S(1)}, bf16[512,256]{1,0:T(8,128)(2,1)S(1)}, u32[]{:S(2)}, u32[]{:S(2)}) collective-permute-start(bf16[512,256]{1,0:T(8,128)(2,1)S(1)} %collective-permute-done.2.refs_7_), channel_id=1, source_target_pairs={{8,0},{9,1},{10,2},{11,3},{12,4},{13,5},{14,6},{15,7},{16,24},{17,... | collective-permute-start | bytes 786440 | tf_op jit(solution)/shard_map/ppermute | solution.py:106
  19.0 12.3 %collective-permute-start.6 = (bf16[512,256]{1,0:T(8,128)(2,1)S(1)}, bf16[512,256]{1,0:T(8,128)(2,1)S(1)}, u32[]{:S(2)}, u32[]{:S(2)}) collective-permute-start(bf16[512,256]{1,0:T(8,128)(2,1)S(1)} %collective-permute-done.1.refs_3_), channel_id=1, source_target_pairs={{8,0},{9,1},{10,2},{11,3},{12,4},{13,5},{14,6},{15,7},{16,24},{17,... | collective-permute-start | bytes 786440 | tf_op jit(solution)/shard_map/ppermute | solution.py:106
  21.2 12.7 %collective-permute-start.8 = (bf16[512,256]{1,0:T(8,128)(2,1)S(1)}, bf16[512,256]{1,0:T(8,128)(2,1)S(1)}, u32[]{:S(2)}, u32[]{:S(2)}) collective-permute-start(bf16[512,256]{1,0:T(8,128)(2,1)S(1)} %collective-permute-done.refs_4_), channel_id=1, source_target_pairs={{0,4},{1,5},{2,6},{3,7},{4,0},{5,1},{6,2},{7,3},{8,12},{9,13},{10,... | collective-permute-start | bytes 786440 | tf_op jit(solution)/shard_map/ppermute | solution.py:106
  23.7 10.2 %collective-permute-start.10 = (bf16[512,256]{1,0:T(8,128)(2,1)S(1)}, bf16[512,256]{1,0:T(8,128)(2,1)S(1)}, u32[]{:S(2)}, u32[]{:S(2)}) collective-permute-start(bf16[512,256]{1,0:T(8,128)(2,1)S(1)} %collective-permute-done.1.refs_3_), channel_id=1, source_target_pairs={{8,12},{9,13},{10,14},{11,15},{12,8},{13,9},{14,10},{15,11},{16,20... | collective-permute-start | bytes 786440 | tf_op jit(solution)/shard_map/ppermute | solution.py:106
  26.2 8.9 %collective-permute-start.11 = (bf16[512,256]{1,0:T(8,128)(2,1)S(1)}, bf16[512,256]{1,0:T(8,128)(2,1)S(1)}, u32[]{:S(2)}, u32[]{:S(2)}) collective-permute-start(bf16[512,256]{1,0:T(8,128)(2,1)S(1)} %collective-permute-done.9.refs_4_), channel_id=1, source_target_pairs={{0,4},{1,5},{2,6},{3,7},{4,0},{5,1},{6,2},{7,3},{24,28},{25,29},{2... | collective-permute-start | bytes 786440 | tf_op jit(solution)/shard_map/ppermute | solution.py:106
  31.3 8.8 %collective-permute-start.7 = (bf16[512,256]{1,0:T(8,128)(2,1)S(1)}, bf16[512,256]{1,0:T(8,128)(2,1)S(1)}, u32[]{:S(2)}, u32[]{:S(2)}) collective-permute-start(bf16[512,256]{1,0:T(8,128)(2,1)S(1)} %collective-permute-done.6.refs_8_), channel_id=1, source_target_pairs={{0,4},{1,5},{2,6},{3,7},{4,0},{5,1},{6,2},{7,3},{24,28},{25,29},{2... | collective-permute-start | bytes 786440 | tf_op jit(solution)/shard_map/ppermute | solution.py:106
  42.1 23.0 %collective-permute-start.19 = (bf16[256,1024]{1,0:T(8,128)(2,1)S(1)}, bf16[256,1024]{1,0:T(8,128)(2,1)S(1)}, u32[]{:S(2)}, u32[]{:S(2)}) collective-permute-start(bf16[256,1024]{1,0:T(8,128)(2,1)S(1)} %pad_maximum_fusion.6), channel_id=1, source_target_pairs={{0,4},{1,5},{2,6},{3,7},{4,0},{5,1},{6,2},{7,3},{8,12},{9,13},{10,... | collective-permute-start | bytes 1572872 | tf_op jit(solution)/shard_map/ppermute | solution.py:106
  47.6 11.2 %collective-permute-start.16 = (bf16[64,1024]{1,0:T(8,128)(2,1)S(1)}, bf16[64,1024]{1,0:T(8,128)(2,1)S(1)}, u32[]{:S(2)}, u32[]{:S(2)}) collective-permute-start(bf16[64,1024]{1,0:T(8,128)(2,1)S(1)} %pad_maximum_fusion.12.refs_8_), channel_id=1, source_target_pairs={{0,16},{1,17},{2,18},{3,19},{4,20},{5,21},{6,22},{7,23},{8,24},{9,... | collective-permute-start | bytes 393224 | tf_op jit(solution)/shard_map/ppermute | solution.py:106
  52.3 8.5 %collective-permute-start.17 = (bf16[64,1024]{1,0:T(8,128)(2,1)S(1)}, bf16[64,1024]{1,0:T(8,128)(2,1)S(1)}, u32[]{:S(2)}, u32[]{:S(2)}) collective-permute-start(bf16[64,1024]{1,0:T(8,128)(2,1)S(1)} %pad_maximum_fusion.12.refs_8_), channel_id=1, source_target_pairs={{0,4},{1,5},{2,6},{3,7},{4,0},{5,1},{6,2},{7,3},{8,12},{9,13},{10,... | collective-permute-start | bytes 393224 | tf_op jit(solution)/shard_map/ppermute | solution.py:106
  53.8 11.1 %collective-permute-start.18 = (bf16[64,1024]{1,0:T(8,128)(2,1)S(1)}, bf16[64,1024]{1,0:T(8,128)(2,1)S(1)}, u32[]{:S(2)}, u32[]{:S(2)}) collective-permute-start(bf16[64,1024]{1,0:T(8,128)(2,1)S(1)} %pad_maximum_fusion.12.refs_8_), channel_id=1, source_target_pairs={{0,20},{1,21},{2,22},{3,23},{4,16},{5,17},{6,18},{7,19},{8,28},{9,... | collective-permute-start | bytes 393224 | tf_op jit(solution)/shard_map/ppermute | solution.py:106
  69.5 12.9 %collective-permute-start.27 = (bf16[64,1024]{1,0:T(8,128)(2,1)S(1)}, bf16[64,1024]{1,0:T(8,128)(2,1)S(1)}, u32[]{:S(2)}, u32[]{:S(2)}) collective-permute-start(bf16[64,1024]{1,0:T(8,128)(2,1)S(1)} %get-tuple-element.124), channel_id=1, source_target_pairs={{0,16},{1,17},{2,18},{3,19},{4,20},{5,21},{6,22},{7,23},{8,24},{9,... | collective-permute-start | bytes 393224 | tf_op jit(solution)/shard_map/ppermute | solution.py:106
  71.7 10.7 %collective-permute-start.28 = (bf16[64,1024]{1,0:T(8,128)(2,1)S(1)}, bf16[64,1024]{1,0:T(8,128)(2,1)S(1)}, u32[]{:S(2)}, u32[]{:S(2)}) collective-permute-start(bf16[64,1024]{1,0:T(8,128)(2,1)S(1)} %get-tuple-element.125), channel_id=1, source_target_pairs={{0,4},{1,5},{2,6},{3,7},{4,0},{5,1},{6,2},{7,3},{8,12},{9,13},{10,... | collective-permute-start | bytes 393224 | tf_op jit(solution)/shard_map/ppermute | solution.py:106
  73.2 12.2 %collective-permute-start.29 = (bf16[64,1024]{1,0:T(8,128)(2,1)S(1)}, bf16[64,1024]{1,0:T(8,128)(2,1)S(1)}, u32[]{:S(2)}, u32[]{:S(2)}) collective-permute-start(bf16[64,1024]{1,0:T(8,128)(2,1)S(1)} %get-tuple-element.126), channel_id=1, source_target_pairs={{0,20},{1,21},{2,22},{3,23},{4,16},{5,17},{6,18},{7,19},{8,28},{9,... | collective-permute-start | bytes 393224 | tf_op jit(solution)/shard_map/ppermute | solution.py:106
  74.1 11.3 %collective-permute-start.30 = (bf16[528,256]{1,0:T(8,128)(2,1)S(1)}, bf16[528,256]{1,0:T(8,128)(2,1)S(1)}, u32[]{:S(2)}, u32[]{:S(2)}) collective-permute-start(bf16[528,256]{1,0:T(8,128)(2,1)S(1)} %get-tuple-element.127), channel_id=1, source_target_pairs={{0,2},{1,3},{2,0},{3,1},{4,6},{5,7},{6,4},{7,5},{8,10},{9,11},{10,... | collective-permute-start | bytes 811016 | tf_op jit(solution)/shard_map/ppermute | solution.py:106
  90.6 8.4 %collective-permute-start.37 = (bf16[256,256]{1,0:T(8,128)(2,1)S(1)}, bf16[256,256]{1,0:T(8,128)(2,1)S(1)}, u32[]{:S(2)}, u32[]{:S(2)}) collective-permute-start(bf16[256,256]{1,0:T(8,128)(2,1)S(1)} %get-tuple-element.143), channel_id=1, source_target_pairs={{0,4},{1,5},{2,6},{3,7},{4,0},{5,1},{6,2},{7,3},{8,12},{9,13},{10,... | collective-permute-start | bytes 393224 | tf_op jit(solution)/shard_map/ppermute | solution.py:106
  100.1 14.6 %collective-permute-start.40 = (bf16[512,256]{1,0:T(8,128)(2,1)S(1)}, bf16[512,256]{1,0:T(8,128)(2,1)S(1)}, u32[]{:S(2)}, u32[]{:S(2)}) collective-permute-start(bf16[512,256]{1,0:T(8,128)(2,1)S(1)} %fusion), channel_id=1, source_target_pairs={{0,8},{1,9},{2,10},{3,11},{4,12},{5,13},{6,14},{7,15},{24,16},{25,... | collective-permute-start | bytes 786440 | tf_op jit(solution)/shard_map/ppermute | solution.py:106
  104.0 10.7 %collective-permute-start.41 = (bf16[512,256]{1,0:T(8,128)(2,1)S(1)}, bf16[512,256]{1,0:T(8,128)(2,1)S(1)}, u32[]{:S(2)}, u32[]{:S(2)}) collective-permute-start(bf16[512,256]{1,0:T(8,128)(2,1)S(1)} %fusion), channel_id=1, source_target_pairs={{8,16},{9,17},{10,18},{11,19},{12,20},{13,21},{14,22},{15,23},{16,... | collective-permute-start | bytes 786440 | tf_op jit(solution)/shard_map/ppermute | solution.py:106
  104.7 10.0 %collective-permute-start.39 = (bf16[512,256]{1,0:T(8,128)(2,1)S(1)}, bf16[512,256]{1,0:T(8,128)(2,1)S(1)}, u32[]{:S(2)}, u32[]{:S(2)}) collective-permute-start(bf16[512,256]{1,0:T(8,128)(2,1)S(1)} %get-tuple-element.156), channel_id=1, source_target_pairs={{0,16},{1,17},{2,18},{3,19},{4,20},{5,21},{6,22},{7,23},{24,8},{25... | collective-permute-start | bytes 786440 | tf_op jit(solution)/shard_map/ppermute | solution.py:106
  109.0 9.3 %collective-permute-start.42 = (bf16[512,256]{1,0:T(8,128)(2,1)S(1)}, bf16[512,256]{1,0:T(8,128)(2,1)S(1)}, u32[]{:S(2)}, u32[]{:S(2)}) collective-permute-start(bf16[512,256]{1,0:T(8,128)(2,1)S(1)} %convolution_convert_fusion), channel_id=1, source_target_pairs={{0,4},{1,5},{2,6},{3,7},{4,0},{5,1},{6,2},{7,3},{8,12},{9,13},{10,... | collective-permute-start | bytes 786440 | tf_op jit(solution)/shard_map/ppermute | solution.py:106
  110.0 11.7 %collective-permute-start.38 = (bf16[512,256]{1,0:T(8,128)(2,1)S(1)}, bf16[512,256]{1,0:T(8,128)(2,1)S(1)}, u32[]{:S(2)}, u32[]{:S(2)}) collective-permute-start(bf16[512,256]{1,0:T(8,128)(2,1)S(1)} %convolution_convert_fusion.1), channel_id=1, source_target_pairs={{0,4},{1,5},{2,6},{3,7},{4,0},{5,1},{6,2},{7,3},{8,12},{9,13},{10,... | collective-permute-start | bytes 786440 | tf_op jit(solution)/shard_map/ppermute | solution.py:106
  (30 other events, 162.4 us)

commit v9 on v8

--- a/solution.py
+++ b/solution.py
@@ -128,19 +128,19 @@
             send(third_b, TWO_IN),
             send(second_b, INWARD),
             send(second_b, MIDDLE),
-            send(first_y, ACROSS_Y),
+            first_y,
         )
     )
-    jumped, inward, across, first_y = [
-        block.astype(jnp.float32) for block in (jumped, inward, across, first_y)
-    ]
-    paired = send((first + first_y + across + jumped).astype(jnp.bfloat16), PAIRS)
-    last = send((third + inward).astype(jnp.bfloat16), MIDDLE)
-    own = own + send(own_y, ACROSS_Y).astype(jnp.float32)
-    return own + last.astype(jnp.float32) + paired.astype(jnp.float32)
+    paired, last = second_round((first, first_y, across, jumped), (third, inward))
+    return own, own_y, send(paired, PAIRS), send(last, MIDDLE)
 
 
 TAIL = 16
+DIGIT_BITS = 8
+
+
+def cost(microseconds):
+    return pl.CostEstimate(flops=int(microseconds * 1e9), bytes_accessed=0, transcendentals=0)
 
 
 def tail_rows(rows):
@@ -159,16 +159,15 @@
     return terms[0:1] + terms[1:2] + terms[2:3]
 
 
-def in_vmem(kernel, results, *operands):
+def in_vmem(kernel, results, *operands, time):
     inside = pl.BlockSpec(memory_space=pltpu.VMEM)
-    size = sum(array.size * array.dtype.itemsize for array in (*operands, *results))
     return pl.pallas_call(
         kernel,
         in_specs=[inside] * len(operands),
         out_specs=[inside] * len(results),
         out_shape=results,
         compiler_params=pltpu.CompilerParams(vmem_limit_bytes=12 * 1024 * 1024),
-        cost_estimate=pl.CostEstimate(flops=size, bytes_accessed=size, transcendentals=0),
+        cost_estimate=cost(time),
     )(*operands)
 
 
@@ -189,7 +188,7 @@
         jax.ShapeDtypeStruct((rows + TAIL, width), jnp.bfloat16),
         jax.ShapeDtypeStruct((1, rows), jnp.float32),
     ]
-    return in_vmem(kernel, results, mine, message, loss)
+    return in_vmem(kernel, results, mine, message, loss, time=0.5)
 
 
 def after_sides(kept, message, loss):
@@ -207,7 +206,7 @@
         jax.ShapeDtypeStruct((rows + TAIL, width), jnp.bfloat16),
         jax.ShapeDtypeStruct((1, rows), jnp.float32),
     ]
-    return in_vmem(kernel, results, kept, message, loss)
+    return in_vmem(kernel, results, kept, message, loss, time=0.5)
 
 
 def after_line(own, message, loss):
@@ -222,28 +221,34 @@
         jax.ShapeDtypeStruct((rows, width), jnp.bfloat16),
         jax.ShapeDtypeStruct((1, rows), jnp.float32),
     ]
-    return in_vmem(kernel, results, own, message, loss)
-
-
-def project(prompts, responses, blocks, weights, total, kind):
+    return in_vmem(kernel, results, own, message, loss, time=0.5)
+
+
+def project(prompts, responses, blocks, weights, total, kind, time, digits=None):
     row_count = prompts.shape[0]
     depth, width = weights[0][0].shape
     count = len(weights)
     terms = [term for weight in weights for term in weight]
+    operands = terms + ([total] if total is not None else [])
+    operands += [digits] if digits is not None else []
 
     def kernel(block_ref, *refs):
         arrays, term_refs, refs = refs[:2], list(refs[2 : 2 + len(terms)]), refs[2 + len(terms) :]
         if total is not None:
             total_ref, *refs = refs
-        out_ref, feature_buf, sum_buf, sem = refs
+        if digits is not None:
+            digit_ref, *refs = refs
+        *out_refs, feature_buf, sum_buf, sem = refs
+
+        def columns(array, k):
+            start = pl.multiple_of(block_ref[k] * depth, depth)
+            return arrays[array].at[:, pl.ds(start, depth)]
+
         loads = []
         for k in range(count):
-            start = pl.multiple_of(block_ref[k] * depth, depth)
             for array in range(2):
                 load = pltpu.make_async_copy(
-                    arrays[array].at[:, pl.ds(start, depth)],
-                    feature_buf.at[k, array],
-                    sem.at[k, array],
+                    columns(array, k), feature_buf.at[k, array], sem.at[k, array]
                 )
                 load.start()
                 loads.append(load)
@@ -261,54 +266,235 @@
                     part += total_ref[rows]
                 if k < count - 1:
                     sum_buf[rows] = part
+                elif digits is not None:
+                    out_refs[array][:row_count] = part.astype(kind)
                 else:
-                    out_ref[rows] = part.astype(out_ref.dtype)
-
+                    out_refs[0][rows] = part.astype(kind)
+        if digits is not None:
+            wanted = digit_ref[...]
+            high = wanted >> DIGIT_BITS
+            low = wanted - (high << DIGIT_BITS)
+            rows = [high.astype(jnp.float32), low.astype(jnp.float32)]
+            rows.append(jnp.zeros((TAIL - 2, wanted.shape[1]), jnp.float32))
+            out_refs[0][row_count:] = jnp.concatenate(rows, axis=0).astype(kind)
+
+    results = [(2 * row_count, width)]
+    if digits is not None:
+        results = [(row_count + TAIL, width), (row_count, width)]
+    results = [jax.ShapeDtypeStruct(shape, kind) for shape in results]
     inside = pl.BlockSpec(memory_space=pltpu.VMEM)
-    operands = terms + ([total] if total is not None else [])
     return pl.pallas_call(
         kernel,
         in_specs=[pl.BlockSpec(memory_space=pltpu.SMEM)]
         + [pl.BlockSpec(memory_space=pltpu.HBM)] * 2
         + [inside] * len(operands),
-        out_specs=inside,
+        out_specs=[inside] * len(results),
         scratch_shapes=[
             pltpu.VMEM((count, 2, row_count, depth), jnp.bfloat16),
             pltpu.VMEM((2 * row_count, width), jnp.float32),
             pltpu.SemaphoreType.DMA((count, 2)),
         ],
-        out_shape=jax.ShapeDtypeStruct((2 * row_count, width), kind),
+        out_shape=results,
         compiler_params=pltpu.CompilerParams(vmem_limit_bytes=12 * 1024 * 1024),
-        cost_estimate=pl.CostEstimate(
-            flops=4 * count * row_count * depth * width,
-            bytes_accessed=4 * count * row_count * depth + 2 * len(terms) * depth * width,
-            transcendentals=0,
-        ),
+        cost_estimate=cost(time),
     )(blocks, prompts, responses, *operands)
 
 
-def compare(groups, held, wanted, ids, row_count):
-    rows, width = groups[0][0].shape
+def pick(prompts, responses, order, depth):
+    half = prompts.shape[0] // 2
+
+    def kernel(order_ref, prompt_ref, response_ref, out_ref, sem):
+        rows = pl.ds(pl.multiple_of(order_ref[3] * half, half), half)
+        for array, ref in enumerate((prompt_ref, response_ref)):
+
+            @pl.when(order_ref[2] == 1 - array)
+            def _(ref=ref):
+                copies = []
+                for k in range(2):
+                    start = pl.multiple_of(order_ref[k] * depth, depth)
+                    copy = pltpu.make_async_copy(
+                        ref.at[rows, pl.ds(start, depth)],
+                        out_ref.at[:, k * depth : (k + 1) * depth],
+                        sem.at[k],
+                    )
+                    copy.start()
+                    copies.append(copy)
+                for copy in copies:
+                    copy.wait()
+
+    return pl.pallas_call(
+        kernel,
+        in_specs=[pl.BlockSpec(memory_space=pltpu.SMEM)]
+        + [pl.BlockSpec(memory_space=pltpu.HBM)] * 2,
+        out_specs=pl.BlockSpec(memory_space=pltpu.VMEM),
+        out_shape=jax.ShapeDtypeStruct((half, 2 * depth), prompts.dtype),
+        scratch_shapes=[pltpu.SemaphoreType.DMA((2,))],
+        compiler_params=pltpu.CompilerParams(vmem_limit_bytes=4 * 1024 * 1024),
+        cost_estimate=cost(1),
+    )(order, prompts, responses)
+
+
+def slices(prompts, responses, blocks, depth):
+    count = blocks.shape[0]
+
+    def kernel(block_ref, prompt_ref, response_ref, *refs):
+        outs, sem = refs[:-1], refs[-1]
+        copies = []
+        for k in range(count):
+            start = pl.multiple_of(block_ref[k] * depth, depth)
+            for array, ref in enumerate((prompt_ref, response_ref)):
+                copy = pltpu.make_async_copy(
+                    ref.at[:, pl.ds(start, depth)], outs[array * count + k], sem.at[array, k]
+                )
+                copy.start()
+                copies.append(copy)
+        for copy in copies:
+            copy.wait()
+
+    shape = jax.ShapeDtypeStruct((prompts.shape[0], depth), prompts.dtype)
+    return pl.pallas_call(
+        kernel,
+        in_specs=[pl.BlockSpec(memory_space=pltpu.SMEM)]
+        + [pl.BlockSpec(memory_space=pltpu.HBM)] * 2,
+        out_specs=[pl.BlockSpec(memory_space=pltpu.VMEM)] * (2 * count),
+        out_shape=[shape] * (2 * count),
+        scratch_shapes=[pltpu.SemaphoreType.DMA((2, count))],
+        compiler_params=pltpu.CompilerParams(vmem_limit_bytes=8 * 1024 * 1024),
+        cost_estimate=cost(1),
+    )(blocks, prompts, responses)
+
+
+def own_products(features, grads):
+    rows, width = grads[0].shape
+    depth = features[0][0].shape[1]
+    kinds = [jnp.bfloat16] * 2 + [jnp.float32] * 4
+
+    def kernel(*refs):
+        grad_refs, refs = refs[:2], refs[2:]
+        for k, kind in enumerate(kinds):
+            total = cross_rows(grad_refs[0][...], refs[2 * k][...])
+            total += cross_rows(grad_refs[1][...], refs[2 * k + 1][...])
+            refs[2 * len(kinds) + k][...] = total.astype(kind)
+
+    results = [jax.ShapeDtypeStruct((width, depth), kind) for kind in kinds]
+    arrays = [array for block in features for array in block]
+    return in_vmem(kernel, results, *grads, *arrays, time=1)
+
+
+def in_order(order, fetched):
+    half, columns = fetched[0].shape
+
+    def kernel(order_ref, *refs):
+        place = order_ref[1] * half
+        start = (1 - order_ref[0]) * 2 * half
+        for part, ref in enumerate(refs[:-1]):
+            first = start if part < 2 else 2 * half - start
+            row = first + (place if part % 2 == 0 else half - place)
+            refs[-1][pl.ds(pl.multiple_of(row, half), half)] = ref[...]
+
+    inside = pl.BlockSpec(memory_space=pltpu.VMEM)
+    return pl.pallas_call(
+        kernel,
+        in_specs=[pl.BlockSpec(memory_space=pltpu.SMEM)] + [inside] * 4,
+        out_specs=inside,
+        out_shape=jax.ShapeDtypeStruct((4 * half, columns), fetched[0].dtype),
+        compiler_params=pltpu.CompilerParams(vmem_limit_bytes=8 * 1024 * 1024),
+        cost_estimate=cost(0.5),
+    )(order, *fetched)
+
+
+def far_products(totals, features, grads):
+    (width, depth), rows = totals[0].shape, grads[0].shape[0]
+
+    def kernel(first_ref, second_ref, prompt_ref, response_ref, feature_ref, *outs):
+        for k, ref in ((1, second_ref), (0, first_ref)):
+            columns = slice(k * depth, (k + 1) * depth)
+            total = ref[...] + cross_rows(prompt_ref[...], feature_ref[:rows, columns])
+            total += cross_rows(response_ref[...], feature_ref[rows:, columns])
+            outs[k][...] = total
+            outs[2 + k][...] = total.astype(jnp.bfloat16)
+
+    results = [jax.ShapeDtypeStruct((width, depth), jnp.float32)] * 2
+    results += [jax.ShapeDtypeStruct((width, depth), jnp.bfloat16)] * 2
+    return in_vmem(kernel, results, *totals, *grads, features, time=2)
+
+
+def second_round(*sums):
+    def kernel(*refs):
+        refs = list(refs)
+        for terms, out in zip(sums, refs[-len(sums) :]):
+            total = refs.pop(0)[...].astype(jnp.float32)
+            for _ in terms[1:]:
+                total += refs.pop(0)[...].astype(jnp.float32)
+            out[...] = total.astype(jnp.bfloat16)
+
+    shape = jax.ShapeDtypeStruct(sums[0][0].shape, jnp.bfloat16)
+    arrays = [term for terms in sums for term in terms]
+    return in_vmem(kernel, [shape] * len(sums), *arrays, time=0.5)
+
+
+def turned_sum(*terms):
+    def kernel(*refs):
+        total = refs[0][...].astype(jnp.float32)
+        for ref in refs[1:-1]:
+            total += ref[...].astype(jnp.float32)
+        refs[-1][...] = total.T
+
+    shape = terms[0].shape[::-1]
+    return in_vmem(kernel, [jax.ShapeDtypeStruct(shape, jnp.float32)], *terms, time=1)[0]
+
+
+def stacked(blocks):
+    rows, width = blocks[0].shape
+
+    def kernel(*refs):
+        for k, ref in enumerate(refs[:-1]):
+            refs[-1][k * rows : (k + 1) * rows] = ref[...]
+
+    result = jax.ShapeDtypeStruct((len(blocks) * rows, width), blocks[0].dtype)
+    return in_vmem(kernel, [result], *blocks, time=0.1)[0]
+
+
+def summed(terms, count):
+    rows, width = terms[0].shape[0], terms[0].shape[1] // count
+
+    def kernel(*refs):
+        for k, out in enumerate(refs[len(terms) :]):
+            columns = slice(k * width, (k + 1) * width)
+            total = refs[0][:, columns]
+            for ref in refs[1 : len(terms)]:
+                total += ref[:, columns].astype(jnp.float32)
+            out[...] = total.astype(jnp.bfloat16)
+
+    result = jax.ShapeDtypeStruct((rows, width), jnp.bfloat16)
+    return in_vmem(kernel, [result] * count, *terms, time=5)
+
+
+def compare(groups, held, wanted, starts, row_count, blocks):
+    rows, width = row_count, groups[0][0].shape[1]
     prompt_rows, across = rows * len(groups), len(groups[0])
-    quarter = held[0].shape[0]
-    count, full = len(held) * quarter, across * width
+    count, full = held.shape
+    quarter = count // blocks
     factor = LOGIT_SCALE / math.sqrt(E)
-    operands = [wanted, ids, *[piece for group in groups for piece in group], *held]
-
-    def kernel(wanted_ref, ids_ref, *refs):
+    operands = [wanted, *[piece for group in groups for piece in group], held]
+
+    def kernel(start_ref, wanted_ref, *refs):
         group_refs = [refs[g * across : (g + 1) * across] for g in range(len(groups))]
         refs = refs[len(groups) * across :]
-        held_refs, refs = refs[: len(held)], refs[len(held) :]
-        loss_ref, mine_ref, away_ref, *part_refs, rows_ref = refs
-        for k, ref in enumerate(held_refs):
-            rows_ref[k * quarter : (k + 1) * quarter] = ref[...]
+        rows_ref, loss_ref, mine_ref, away_ref, *part_refs = refs
+        count_up = lax.broadcasted_iota(jnp.int32, (quarter, 1), 0)
+        ids = jnp.concatenate([count_up + start_ref[k] for k in range(blocks)], axis=0)
         weights, losses = [], []
         for g, pieces in enumerate(group_refs):
             scores = jnp.zeros((count, rows), jnp.float32)
             for k, ref in enumerate(pieces):
-                scores += cross_cols(rows_ref[:, k * width : (k + 1) * width], ref[...])
+                scores += cross_cols(rows_ref[:, k * width : (k + 1) * width], ref[:rows])
             scores = scores * factor + LOGIT_BIAS
-            match = wanted_ref[:, g * rows : (g + 1) * rows] == ids_ref[...]
+            target = wanted_ref[...]
+            if g > 0:
+                tail = pieces[0][rows:].astype(jnp.float32)
+                target = (tail[0:1] * 2.0**DIGIT_BITS + tail[1:2]).astype(jnp.int32)
+            match = target == ids
             margin = jnp.where(match, -scores, scores)
             small = jnp.exp(-jnp.abs(margin))
             soft = jnp.maximum(margin, 0.0) + jnp.log1p(small)
@@ -318,7 +504,9 @@
             weights.append(jnp.where(match, -share, share).astype(jnp.bfloat16))
         for k in range(across):
             columns = slice(k * width, (k + 1) * width)
-            part = sum(matmul(weight, pieces[k][...]) for weight, pieces in zip(weights, group_refs))
+            part = sum(
+                matmul(weight, pieces[k][:rows]) for weight, pieces in zip(weights, group_refs)
+            )
             for block, part_ref in enumerate(part_refs):
                 part_rows = part[block * quarter : (block + 1) * quarter]
                 part_ref[:, columns] = part_rows.astype(part_ref.dtype)
@@ -333,23 +521,19 @@
 
     return pl.pallas_call(
         kernel,
-        in_specs=[pl.BlockSpec(memory_space=pltpu.VMEM)] * len(operands),
-        out_specs=[pl.BlockSpec(memory_space=pltpu.VMEM)] * (3 + len(held)),
+        in_specs=[pl.BlockSpec(memory_space=pltpu.SMEM)]
+        + [pl.BlockSpec(memory_space=pltpu.VMEM)] * len(operands),
+        out_specs=[pl.BlockSpec(memory_space=pltpu.VMEM)] * (3 + blocks),
         out_shape=[
             jax.ShapeDtypeStruct((1, prompt_rows), jnp.float32),
             jax.ShapeDtypeStruct((prompt_rows, full // 2), jnp.float32),
             jax.ShapeDtypeStruct((prompt_rows + TAIL, full // 2), jnp.bfloat16),
             jax.ShapeDtypeStruct((quarter, full), jnp.float32),
         ]
-        + [jax.ShapeDtypeStruct((quarter, full), jnp.bfloat16)] * (len(held) - 1),
-        scratch_shapes=[pltpu.VMEM((count, full), jnp.bfloat16)],
+        + [jax.ShapeDtypeStruct((quarter, full), jnp.bfloat16)] * (blocks - 1),
         compiler_params=pltpu.CompilerParams(vmem_limit_bytes=16 * 1024 * 1024),
-        cost_estimate=pl.CostEstimate(
-            flops=6 * prompt_rows * count * full,
-            bytes_accessed=6 * prompt_rows * full + 6 * count * full,
-            transcendentals=2 * prompt_rows * count,
-        ),
-    )(*operands)
+        cost_estimate=cost(2),
+    )(starts, *operands)
 
 
 def full_window(prompts, responses, head_projection_matrix, positive):
@@ -362,114 +546,111 @@
 
     here = [(z ^ k) * PAIR + y for k in range(LINE)]
     there = [(z ^ k) * PAIR + 1 - y for k in range(LINE)]
-    orders = here[:1] + there[:1] + here[1:2], [there[1], here[2], there[2], here[3]], [there[3]]
-    ids = jnp.stack([here[0], here[2], there[0], there[2]]) * row_count + mp * quarter
-    ids = (ids[:, None] + lax.iota(jnp.int32, quarter)).reshape(-1, 1)
-    own, orders, here, there, places, even, left, ids = tie(
+    even = (mp % CORES == 0).astype(jnp.int32)
+    orders = (
+        [there[2], there[3], even, mp // CORES],
+        [here[0], there[0], here[1]],
+        [there[1], here[2], there[2], here[3]],
+        [there[3]],
+        there[:2] + here,
+        [even, mp // CORES],
+    )
+    starts = jnp.stack([here[0], here[2], there[0], there[2]]) * row_count + mp * quarter
+    own, orders, places, swap, left, starts = tie(
         (
             head_projection_matrix,
             [jnp.stack(order).astype(jnp.int32) for order in orders],
-            [(index * depth).astype(jnp.uint32) for index in here],
-            [(index * depth).astype(jnp.uint32) for index in there],
             [((mp ^ k) * quarter).astype(jnp.uint32) for k in range(SIDE * CORES)],
-            mp % CORES == 0,
+            even == 1,
             mp < CORES,
-            ids,
+            starts.astype(jnp.int32),
         )
     )
-    zero = jnp.uint32(0)
-
-    def features(array, start):
-        return lax.dynamic_slice(array, (zero, start), (row_count, depth))
-
+
+    picked = pick(prompts, responses, orders[0], depth)
     own_y = send(own, ACROSS_Y)
-    first, middle = send(own, PAIRS), send(own, MIDDLE)
-    wanted = jnp.concatenate([positive, send(positive, PAIRS)], axis=0)[None, :]
+    first, middle, picked = tie(
+        (send(own, PAIRS), send(own, MIDDLE), picked)
+    )
     inner, outer, first_y = send(first, MIDDLE), send(middle, OUTWARD), send(first, ACROSS_Y)
+    inner, own_y = tie((inner, own_y))
     last = send(inner, OUTWARD)
-    emb = project(
-        prompts, responses, orders[0], [(own,), (own_y,), (first,)], None, jnp.float32
+    (emb,) = project(
+        prompts, responses, orders[1], [(own,), (own_y,), (first,)], None, jnp.float32, 2
     )
     inner_late, middle_late, emb = tie((inner, middle, emb))
     inner_y, outer_y = send(inner_late, Y_MIDDLE), send(outer, Y_ENDS)
-    columns = [
-        jnp.concatenate([features(prompts, start).T, features(responses, start).T], axis=1)
-        for start in here + there[:2]
-    ]
-    mine = jnp.concatenate(
-        [jnp.where(even, features(prompts, f), features(responses, f)) for f in there[2:]], axis=1
-    )
-    emb, columns, wanted, mine = tie((emb, columns, wanted, mine))
-    emb = project(
+    (emb,) = project(
         prompts,
         responses,
-        orders[1],
+        orders[2],
         [(first_y,), (inner, outer), (inner_y, outer_y), (middle, last)],
         emb,
         jnp.float32,
-    )
-    middle_y, last_y, emb = tie((send(middle_late, Y_MIDDLE), send(last, Y_ENDS), emb))
-    emb = project(prompts, responses, orders[2], [(middle_y, last_y)], emb, jnp.bfloat16)
-    prompt_emb, response_emb = emb[:row_count], emb[row_count:]
+        2.4,
+    )
+    middle_y, last_y, emb = tie(
+        (send(middle_late, Y_MIDDLE), send(last, Y_ENDS), emb)
+    )
+    prompt_emb, response_emb = project(
+        prompts, responses, orders[3], [(middle_y, last_y)], emb, jnp.bfloat16, 0.7, positive[None, :]
+    )
 
     pieces = []
     for k in range(SIDE * CORES):
-        piece = lax.dynamic_slice(response_emb, (places[k], zero), (quarter, width))
+        piece = lax.dynamic_slice(response_emb, (places[k], jnp.uint32(0)), (quarter, width))
         pieces.append(piece if k == 0 else send(piece, MIX[k]))
-    pieces[1], mine, prompt_emb = tie((pieces[1], mine, prompt_emb))
-    fetched = send(mine, ACROSS_Y)
+    emb_done, picked = tie((prompt_emb, picked))
+    fetched = send(picked, ACROSS_Y)
     prompt_pair = send(prompt_emb, PAIRS)
     response_rows = jnp.concatenate(pieces, axis=1)
-    response_rows, prompt_emb = tie((response_rows, prompt_emb))
-
-    held = [send(response_rows, table) for table in (FAR, ACROSS_Y, FAR_Y)]
-    groups = [prompt_emb, prompt_pair]
-    groups = [[block, send(block, ACROSS_C), send(block, ACROSS_X)] for block in groups]
-    held, fetched, *beside = tie((held, fetched, *[group[2] for group in groups]))
-    groups = [[*group[:2], x, send(x, ACROSS_C)] for group, x in zip(groups, beside)]
-    sibling = send(fetched, ACROSS_C)
-    losses, mine, away, *parts = compare(groups, [response_rows, *held], wanted, ids, row_count)
-
-    back = [send(part, table) for part, table in zip(parts[1:], (FAR, ACROSS_Y, FAR_Y))]
+
+    held = [send(response_rows, FAR), send(response_rows, FAR_Y), send(response_rows, ACROSS_Y)]
+    groups = [
+        [block, send(block, ACROSS_C), send(block, ACROSS_X)] for block in (prompt_emb, prompt_pair)
+    ]
+    beside = [group[2] for group in groups]
+    held = [held[0], held[2], held[1]]
+    held = stacked([response_rows, *held])
+    fetched_x = send(fetched, ACROSS_X)
+    features = slices(prompts, responses, tie((orders[4], prompt_emb))[0], depth)
+    cross = [send(x, ACROSS_C) for x in beside]
+    held, features, cross_tied, fetched_x = tie((held, features, cross, fetched_x))
+    cross = cross_tied
+    features = list(zip(features[:6], features[6:]))
+    groups = [[*group[:2], x, across] for group, x, across in zip(groups, beside, cross)]
+    losses, mine, away, *parts = compare(
+        groups, held, positive[None, :], starts, row_count, LINE
+    )
+
     mine, aside, losses = after_cores(mine, send(away, ACROSS_C), losses)
-    columns_y = [
-        jnp.concatenate(
-            [array[:, k * depth : (k + 1) * depth].T for array in (fetched, sibling)], axis=1
-        )
-        for k in range(2)
-    ]
-    back, aside, columns_y = tie((back, send(aside, ACROSS_X), columns_y))
-    grad = parts[0] + sum(part.astype(jnp.float32) for part in back)
-    grad = grad.astype(jnp.bfloat16)
+    back = [send(parts[1], FAR), send(parts[3], FAR_Y), send(parts[2], ACROSS_Y)]
+    pieces = summed([parts[0], *back], SIDE * CORES)
+    pieces, aside = tie((pieces, send(aside, ACROSS_X)))
+    sibling, sibling_x = send(fetched, ACROSS_C), send(fetched_x, ACROSS_C)
     mine, far, losses = after_sides(mine, aside, losses)
 
-    pieces = [grad[:, k * width : (k + 1) * width] for k in range(SIDE * CORES)]
     pieces = [pieces[0]] + [send(pieces[k], MIX[k]) for k in range(1, SIDE * CORES)]
     pieces, far = tie((pieces, send(far, PAIRS)))
-    swapped = [jnp.where(even, pieces[k], pieces[k ^ 1]) for k in range(SIDE * CORES)]
+    swapped = [jnp.where(swap, pieces[k], pieces[k ^ 1]) for k in range(SIDE * CORES)]
     swapped = [jnp.where(left, swapped[k], swapped[k ^ 2]) for k in range(SIDE * CORES)]
     grad_response = jnp.concatenate(swapped, axis=0)
-    grad_response_y = send(grad_response, ACROSS_Y)
     grad_prompt, losses = after_line(mine, far, losses)
-    grad_prompt_y = send(grad_prompt, ACROSS_Y)
-    grad_response_y, grad_prompt_y = tie((grad_response_y, grad_prompt_y))
-
-    grads = jnp.concatenate([grad_prompt, grad_response], axis=0)
-    grads_y = jnp.concatenate(
-        [
-            jnp.where(even, grad_prompt_y, grad_response_y),
-            jnp.where(even, grad_response_y, grad_prompt_y),
-        ],
-        axis=0,
-    )
-    third = matmul(columns[3], grads) + matmul(columns_y[1], grads_y)
-    third_b, grads = tie((third.astype(jnp.bfloat16), grads))
-    second = matmul(columns[2], grads) + matmul(columns_y[0], grads_y)
-    second_b, grads = tie((second.astype(jnp.bfloat16), grads))
-    first_y, own_y = [matmul(columns[k], grads).astype(jnp.bfloat16) for k in (5, 4)]
-    first, own = [matmul(columns[k], grads) for k in (1, 0)]
-    head_grad = line_reduce(own, first, second, third, second_b, third_b, own_y, first_y)
-    return (losses[0] / row_count, head_grad)
+    grads_y = [send(grad_prompt, ACROSS_Y), send(grad_response, ACROSS_Y)]
+
+    own_y, first_y, own, first, second, third = own_products(
+        features, (grad_prompt, grad_response)
+    )
+    far_features = in_order(orders[5], (fetched, fetched_x, sibling, sibling_x))
+    grads_y, own, first, second, third, far_features = tie(
+        (grads_y, own, first, second, third, far_features)
+    )
+    own_y, first_y = send(own_y, ACROSS_Y), send(first_y, ACROSS_Y)
+    second, third, second_b, third_b = far_products(
+        (second, third), far_features, grads_y
+    )
+    terms = line_reduce(own, first, second, third, second_b, third_b, own_y, first_y)
+    return (losses[0] / row_count, turned_sum(*terms))
 
 
 def per_device(prompts, responses, head_projection_matrix, positive):

time: 127 us -> 123 us (0.969)
  other arithmetic: 9.8 us -> 0.91 us
  Pallas kernels: 6.83 us -> 13.1 us
  starting transfers between devices: 56.1 us -> 50.2 us
  waiting for transfers between devices: 48.3 us -> 53.4 us
  matrix products: 2.73 us -> 0 us
  local copies, waits for them, and re-layouts: 0.83 us -> 3.32 us
    ppermute x45 -> x46, starting transfers between devices: 56.1 us -> 50.2 us  [send(): return lax.ppermute(block, ('dp', 'mp'), table)]
    ppermute x45 -> x46, waiting for transfers between devices: 48.3 us -> 53.4 us  [send(): return lax.ppermute(block, ('dp', 'mp'), table)]
    select_n x2 -> x1, other arithmetic: 4.98 us -> 0.02 us  [full_window(): jnp.where(left, swapped[k], swapped[k ^ 2])]
    pallas_call x3 -> x9, Pallas kernels: 0.27 us -> 3.79 us  [in_vmem(): pl.pallas_call(kernel, in_specs=[inside] * len(operands), out_specs=[insi...]
    concatenate x11 -> x0, other arithmetic: 2.77 us -> none  [the longest x6 2.61 us: full_window(): jnp.concatenate([features(prompts, start).T, features(responses, start).T...]
    dot_general x8 -> x0, matrix products: 2.73 us -> none  [matmul(): jnp.dot(left_side, righthand_term, preferred_element_type=jnp.float32)]
    unnamed x19 -> x12, local copies, waits for them, and re-layouts: 0.47 us -> 3.2 us
    pallas_call x1 -> x4, Pallas kernels: 1.53 us -> 4.23 us  [the longest x1 2.07 us: compare(): pl.pallas_call(kernel, in_specs=[pl.BlockSpec(memory_space=pltpu.SMEM)] +...]
  transfers between devices with their start and end apart: 45 -> 46, of which waited for: 22 -> 19; matrix products, arithmetic and copies ran while one was open for 8% -> 1% of each run, Pallas kernels for 4% -> 8%
where the time goes in v9:
time: 123 us; the launch traced here: 122 us
  waiting for transfers between devices  53.4 us (43%)
  starting transfers between devices  50.2 us (41%)
  Pallas kernels  13.1 us (11%)
  local copies, waits for them, and re-layouts  3.32 us (3%)
    ppermute x46, waiting for transfers between devices, send(): return lax.ppermute(block, ('dp', 'mp'), table)  53.4 us
    ppermute x46, starting transfers between devices, send(): return lax.ppermute(block, ('dp', 'mp'), table)  50.2 us
    pallas_call x3, Pallas kernels, project(): pl.pallas_call(kernel, in_specs=[pl.BlockSpec(memory_space=pltpu.SMEM)] +...  5.06 us
    pallas_call x9, Pallas kernels, in_vmem(): pl.pallas_call(kernel, in_specs=[inside] * len(operands), out_specs=[insi...  3.79 us
    unnamed x12, local copies, waits for them, and re-layouts  3.2 us
  transfers between devices with their start and end apart: 46, of which 19 were waited for; matrix products, arithmetic and copies ran while one was open for 1% of the time, Pallas kernels for 8%

profile of v9, /device:TPU:0, one launch (start us, length us, event | category | flops | bytes accessed | tf_op | source)
XLA Modules:
  0.0 121.9 jit_solution(26074655473114128)
XLA Ops:
  1.1 3.0 %collective-permute-start = (bf16[512,256]{1,0:T(8,128)(2,1)}, bf16[512,256]{1,0:T(8,128)(2,1)S(1)}, u32[]{:S(2)}, u32[]{:S(2)}) collective-permute-start(bf16[512,256]{1,0:T(8,128)(2,1)} %refs_2_), channel_id=1, source_target_pairs={{0,8},{1,9},{2,10},{3,11},{4,12},{5,13},{6,14},{7,15},{8,0},{9,1},... | collective-permute-start | bytes 786440 | tf_op jit(solution)/shard_map/ppermute | solution.py:106
  15.7 2.0 %shard_map.60.refs_9_ = f32[512,256]{1,0:T(8,128)S(1)} custom-call(s32[3]{0:T(128)S(1)} %pad_add_fusion.1.block_ref, bf16[256,4096]{1,0:T(8,128)(2,1)S(1)} %copy-done.1, bf16[256,4096]{1,0:T(8,128)(2,1)S(1)} %copy-done.3, bf16[512,256]{1,0:T(8,128)(2,1)S(1)} %copy-done.5, bf16[512,256]{1,0:T(8,128)(2,1)S(1)} %collective-permute-done.3.refs_3_, ...), custom_call_target="tpu_custom_call" | custom-call | flops 2000000000 | tf_op jit(solution)/shard_map/pallas_call | solution.py:286
  18.4 7.2 %collective-permute-done.8.refs_4_ = bf16[512,256]{1,0:T(8,128)(2,1)S(1)} collective-permute-done((bf16[512,256]{1,0:T(8,128)(2,1)S(1)}, bf16[512,256]{1,0:T(8,128)(2,1)S(1)}, u32[]{:S(2)}, u32[]{:S(2)}) %collective-permute-start.8) | collective-permute-done | bytes 262176 | tf_op jit(solution)/shard_map/ppermute | solution.py:106
  25.6 3.4 %collective-permute-start.10 = (bf16[512,256]{1,0:T(8,128)(2,1)S(1)}, bf16[512,256]{1,0:T(8,128)(2,1)S(1)}, u32[]{:S(2)}, u32[]{:S(2)}) collective-permute-start(bf16[512,256]{1,0:T(8,128)(2,1)S(1)} %collective-permute-done.8.refs_4_), channel_id=1, source_target_pairs={{0,4},{1,5},{2,6},{3,7},{4,0},{5,1},{6,2},{7,3},{24,28},{25,29},{2... | collective-permute-start | bytes 786440 | tf_op jit(solution)/shard_map/ppermute | solution.py:106
  30.8 3.4 %collective-permute-start.6 = (bf16[512,256]{1,0:T(8,128)(2,1)S(1)}, bf16[512,256]{1,0:T(8,128)(2,1)S(1)}, u32[]{:S(2)}, u32[]{:S(2)}) collective-permute-start(bf16[512,256]{1,0:T(8,128)(2,1)S(1)} %collective-permute-done.5.refs_8_), channel_id=1, source_target_pairs={{0,4},{1,5},{2,6},{3,7},{4,0},{5,1},{6,2},{7,3},{24,28},{25,29},{2... | collective-permute-start | bytes 786440 | tf_op jit(solution)/shard_map/ppermute | solution.py:106
  34.5 2.4 %shard_map.61.refs_4_ = f32[512,256]{1,0:T(8,128)S(1)} custom-call(s32[4]{0:T(128)S(1)} %get-tuple-element.120.block_ref, bf16[256,4096]{1,0:T(8,128)(2,1)S(1)} %copy-done.1, bf16[256,4096]{1,0:T(8,128)(2,1)S(1)} %copy-done.3, bf16[512,256]{1,0:T(8,128)(2,1)S(1)} %collective-permute-done.7.refs_2_, bf16[512,256]{1,0:T(8,128)(2,1)S(1)} %collective-permute-done.2.refs_3_, ...), custom_call_target="tpu_custom_call" | custom-call | flops 2400000000 | tf_op jit(solution)/shard_map/pallas_call | solution.py:286
  36.9 2.6 %collective-permute-done.6.refs_3_ = bf16[512,256]{1,0:T(8,128)(2,1)S(1)} collective-permute-done((bf16[512,256]{1,0:T(8,128)(2,1)S(1)}, bf16[512,256]{1,0:T(8,128)(2,1)S(1)}, u32[]{:S(2)}, u32[]{:S(2)}) %collective-permute-start.6) | collective-permute-done | bytes 262176 | tf_op jit(solution)/shard_map/ppermute | solution.py:106
  40.2 2.3 %collective-permute-start.20 = (bf16[272,256]{1,0:T(8,128)(2,1)S(1)}, bf16[272,256]{1,0:T(8,128)(2,1)S(1)}, u32[]{:S(2)}, u32[]{:S(2)}) collective-permute-start(bf16[272,256]{1,0:T(8,128)(2,1)S(1)} %get-tuple-element.126.refs_0_), channel_id=1, source_target_pairs={{0,8},{1,9},{2,10},{3,11},{4,12},{5,13},{6,14},{7,15},{8,0},{9,1},... | collective-permute-start | bytes 417800 | tf_op jit(solution)/shard_map/ppermute | solution.py:106
  45.8 1.8 %collective-permute-done.15 = bf16[64,256]{1,0:T(8,128)(2,1)S(1)} collective-permute-done((bf16[64,256]{1,0:T(8,128)(2,1)S(1)}, bf16[64,256]{1,0:T(8,128)(2,1)S(1)}, u32[]{:S(2)}, u32[]{:S(2)}) %collective-permute-start.15) | collective-permute-done | bytes 32800 | tf_op jit(solution)/shard_map/ppermute | solution.py:106
  51.2 2.9 %collective-permute-done.12.refs_2_ = bf16[272,256]{1,0:T(8,128)(2,1)S(1)} collective-permute-done((bf16[272,256]{1,0:T(8,128)(2,1)S(1)}, bf16[272,256]{1,0:T(8,128)(2,1)S(1)}, u32[]{:S(2)}, u32[]{:S(2)}) %collective-permute-start.12) | collective-permute-done | bytes 139296 | tf_op jit(solution)/shard_map/ppermute | solution.py:106
  56.1 4.8 %collective-permute-done.16.refs_1_ = bf16[64,1024]{1,0:T(8,128)(2,1)S(1)} collective-permute-done((bf16[64,1024]{1,0:T(8,128)(2,1)S(1)}, bf16[64,1024]{1,0:T(8,128)(2,1)S(1)}, u32[]{:S(2)}, u32[]{:S(2)}) %collective-permute-start.16) | collective-permute-done | bytes 131104 | tf_op jit(solution)/shard_map/ppermute | solution.py:106
  61.4 2.3 %collective-permute-done.18.refs_3_ = bf16[64,1024]{1,0:T(8,128)(2,1)S(1)} collective-permute-done((bf16[64,1024]{1,0:T(8,128)(2,1)S(1)}, bf16[64,1024]{1,0:T(8,128)(2,1)S(1)}, u32[]{:S(2)}, u32[]{:S(2)}) %collective-permute-start.18) | collective-permute-done | bytes 131104 | tf_op jit(solution)/shard_map/ppermute | solution.py:106
  65.1 2.1 %shard_map.65 = (f32[1,512]{1,0:T(1,128)S(1)}, f32[512,512]{1,0:T(8,128)S(1)}, bf16[528,512]{1,0:T(8,128)(2,1)S(1)}, f32[64,1024]{1,0:T(8,128)S(1)}, bf16[64,102...) custom-call(s32[4]{0:T(128)S(1)} %fusion.start_ref, s32[1,256]{1,0:T(1,128)S(1)} %bitcast.13, ...), custom_call_target="tpu_custom_call" | custom-call | flops 2000000000 | tf_op jit(solution)/shard_map/pallas_call | solution.py:522
  67.5 3.6 %collective-permute-start.28 = (bf16[64,1024]{1,0:T(8,128)(2,1)S(1)}, bf16[64,1024]{1,0:T(8,128)(2,1)S(1)}, u32[]{:S(2)}, u32[]{:S(2)}) collective-permute-start(bf16[64,1024]{1,0:T(8,128)(2,1)S(1)} %get-tuple-element.157), channel_id=1, source_target_pairs={{0,20},{1,21},{2,22},{3,23},{4,16},{5,17},{6,18},{7,19},{8,28},{9,... | collective-permute-start | bytes 393224 | tf_op jit(solution)/shard_map/ppermute | solution.py:106
  72.4 6.9 %collective-permute-done.27.refs_1_ = bf16[64,1024]{1,0:T(8,128)(2,1)S(1)} collective-permute-done((bf16[64,1024]{1,0:T(8,128)(2,1)S(1)}, bf16[64,1024]{1,0:T(8,128)(2,1)S(1)}, u32[]{:S(2)}, u32[]{:S(2)}) %collective-permute-start.27) | collective-permute-done | bytes 131104 | tf_op jit(solution)/shard_map/ppermute | solution.py:106
  79.3 3.3 %collective-permute-done.28.refs_2_ = bf16[64,1024]{1,0:T(8,128)(2,1)S(1)} collective-permute-done((bf16[64,1024]{1,0:T(8,128)(2,1)S(1)}, bf16[64,1024]{1,0:T(8,128)(2,1)S(1)}, u32[]{:S(2)}, u32[]{:S(2)}) %collective-permute-start.28) | collective-permute-done | bytes 131104 | tf_op jit(solution)/shard_map/ppermute | solution.py:106
  85.3 1.8 %collective-permute-done.32 = bf16[64,256]{1,0:T(8,128)(2,1)S(1)} collective-permute-done((bf16[64,256]{1,0:T(8,128)(2,1)S(1)}, bf16[64,256]{1,0:T(8,128)(2,1)S(1)}, u32[]{:S(2)}, u32[]{:S(2)}) %collective-permute-start.32) | collective-permute-done | bytes 32800 | tf_op jit(solution)/shard_map/ppermute | solution.py:106
  93.3 1.7 %collective-permute-done.35.prompt_ref = bf16[256,256]{1,0:T(8,128)(2,1)S(1)} collective-permute-done((bf16[256,256]{1,0:T(8,128)(2,1)S(1)}, bf16[256,256]{1,0:T(8,128)(2,1)S(1)}, u32[]{:S(2)}, u32[]{:S(2)}) %collective-permute-start.35) | collective-permute-done | bytes 131104 | tf_op jit(solution)/shard_map/ppermute | solution.py:106
  95.0 2.8 %collective-permute-done.36.response_ref = bf16[256,256]{1,0:T(8,128)(2,1)S(1)} collective-permute-done((bf16[256,256]{1,0:T(8,128)(2,1)S(1)}, bf16[256,256]{1,0:T(8,128)(2,1)S(1)}, u32[]{:S(2)}, u32[]{:S(2)}) %collective-permute-start.36) | collective-permute-done | bytes 131104 | tf_op jit(solution)/shard_map/ppermute | solution.py:106
  99.0 2.7 %collective-permute-start.40 = (bf16[256,512]{1,0:T(8,128)(2,1)S(1)}, bf16[256,512]{1,0:T(8,128)(2,1)S(1)}, u32[]{:S(2)}, u32[]{:S(2)}) collective-permute-start(bf16[256,512]{1,0:T(8,128)(2,1)S(1)} %get-tuple-element.208), channel_id=1, source_target_pairs={{0,16},{1,17},{2,18},{3,19},{4,20},{5,21},{6,22},{7,23},{24,8},{25... | collective-permute-start | bytes 786440 | tf_op jit(solution)/shard_map/ppermute | solution.py:106
  104.6 3.9 %collective-permute-done.40.refs_3_ = bf16[256,512]{1,0:T(8,128)(2,1)S(1)} collective-permute-done((bf16[256,512]{1,0:T(8,128)(2,1)S(1)}, bf16[256,512]{1,0:T(8,128)(2,1)S(1)}, u32[]{:S(2)}, u32[]{:S(2)}) %collective-permute-start.40) | collective-permute-done | bytes 262176 | tf_op jit(solution)/shard_map/ppermute | solution.py:106
  108.5 3.1 %collective-permute-done.41.refs_5_ = bf16[256,512]{1,0:T(8,128)(2,1)S(1)} collective-permute-done((bf16[256,512]{1,0:T(8,128)(2,1)S(1)}, bf16[256,512]{1,0:T(8,128)(2,1)S(1)}, u32[]{:S(2)}, u32[]{:S(2)}) %collective-permute-start.41) | collective-permute-done | bytes 262176 | tf_op jit(solution)/shard_map/ppermute | solution.py:106
  111.8 3.1 %collective-permute-start.44 = (bf16[256,512]{1,0:T(8,128)(2,1)S(1)}, bf16[256,512]{1,0:T(8,128)(2,1)S(1)}, u32[]{:S(2)}, u32[]{:S(2)}) collective-permute-start(bf16[256,512]{1,0:T(8,128)(2,1)S(1)} %get-tuple-element.216), channel_id=1, source_target_pairs={{0,8},{1,9},{2,10},{3,11},{4,12},{5,13},{6,14},{7,15},{8,0},{9,1},... | collective-permute-start | bytes 786440 | tf_op jit(solution)/shard_map/ppermute | solution.py:106
  116.1 4.8 %collective-permute-done.44.refs_2_ = bf16[256,512]{1,0:T(8,128)(2,1)S(1)} collective-permute-done((bf16[256,512]{1,0:T(8,128)(2,1)S(1)}, bf16[256,512]{1,0:T(8,128)(2,1)S(1)}, u32[]{:S(2)}, u32[]{:S(2)}) %collective-permute-start.44) | collective-permute-done | bytes 262176 | tf_op jit(solution)/shard_map/ppermute | solution.py:106
  (106 shorter events, 43.0 us)
Async XLA Ops:
  1.1 9.6 %collective-permute-start = (bf16[512,256]{1,0:T(8,128)(2,1)}, bf16[512,256]{1,0:T(8,128)(2,1)S(1)}, u32[]{:S(2)}, u32[]{:S(2)}) collective-permute-start(bf16[512,256]{1,0:T(8,128)(2,1)} %refs_2_), channel_id=1, source_target_pairs={{0,8},{1,9},{2,10},{3,11},{4,12},{5,13},{6,14},{7,15},{8,0},{9,1},... | collective-permute-start | bytes 786440 | tf_op jit(solution)/shard_map/ppermute | solution.py:106
  4.8 9.6 %collective-permute-start.3 = (bf16[512,256]{1,0:T(8,128)(2,1)}, bf16[512,256]{1,0:T(8,128)(2,1)S(1)}, u32[]{:S(2)}, u32[]{:S(2)}) collective-permute-start(bf16[512,256]{1,0:T(8,128)(2,1)} %refs_2_), channel_id=1, source_target_pairs={{0,4},{1,5},{2,6},{3,7},{4,0},{5,1},{6,2},{7,3},{8,12},{9,13},{10,... | collective-permute-start | bytes 786440 | tf_op jit(solution)/shard_map/ppermute | solution.py:106
  11.5 14.2 %collective-permute-start.8 = (bf16[512,256]{1,0:T(8,128)(2,1)S(1)}, bf16[512,256]{1,0:T(8,128)(2,1)S(1)}, u32[]{:S(2)}, u32[]{:S(2)}) collective-permute-start(bf16[512,256]{1,0:T(8,128)(2,1)S(1)} %collective-permute-done.1.refs_7_), channel_id=1, source_target_pairs={{8,0},{9,1},{10,2},{11,3},{12,4},{13,5},{14,6},{15,7},{16,24},{17,... | collective-permute-start | bytes 786440 | tf_op jit(solution)/shard_map/ppermute | solution.py:106
  12.8 21.4 %collective-permute-start.7 = (bf16[512,256]{1,0:T(8,128)(2,1)S(1)}, bf16[512,256]{1,0:T(8,128)(2,1)S(1)}, u32[]{:S(2)}, u32[]{:S(2)}) collective-permute-start(bf16[512,256]{1,0:T(8,128)(2,1)S(1)} %collective-permute-done.refs_4_), channel_id=1, source_target_pairs={{0,4},{1,5},{2,6},{3,7},{4,0},{5,1},{6,2},{7,3},{8,12},{9,13},{10,... | collective-permute-start | bytes 786440 | tf_op jit(solution)/shard_map/ppermute | solution.py:106
  14.4 16.4 %collective-permute-start.5 = (bf16[512,256]{1,0:T(8,128)(2,1)S(1)}, bf16[512,256]{1,0:T(8,128)(2,1)S(1)}, u32[]{:S(2)}, u32[]{:S(2)}) collective-permute-start(bf16[512,256]{1,0:T(8,128)(2,1)S(1)} %collective-permute-done.2.refs_3_), channel_id=1, source_target_pairs={{8,0},{9,1},{10,2},{11,3},{12,4},{13,5},{14,6},{15,7},{16,24},{17,... | collective-permute-start | bytes 786440 | tf_op jit(solution)/shard_map/ppermute | solution.py:106
  17.7 16.5 %collective-permute-start.9 = (bf16[512,256]{1,0:T(8,128)(2,1)S(1)}, bf16[512,256]{1,0:T(8,128)(2,1)S(1)}, u32[]{:S(2)}, u32[]{:S(2)}) collective-permute-start(bf16[512,256]{1,0:T(8,128)(2,1)S(1)} %collective-permute-done.2.refs_3_), channel_id=1, source_target_pairs={{8,12},{9,13},{10,14},{11,15},{12,8},{13,9},{14,10},{15,11},{16,20... | collective-permute-start | bytes 786440 | tf_op jit(solution)/shard_map/ppermute | solution.py:106
  25.6 8.9 %collective-permute-start.10 = (bf16[512,256]{1,0:T(8,128)(2,1)S(1)}, bf16[512,256]{1,0:T(8,128)(2,1)S(1)}, u32[]{:S(2)}, u32[]{:S(2)}) collective-permute-start(bf16[512,256]{1,0:T(8,128)(2,1)S(1)} %collective-permute-done.8.refs_4_), channel_id=1, source_target_pairs={{0,4},{1,5},{2,6},{3,7},{4,0},{5,1},{6,2},{7,3},{24,28},{25,29},{2... | collective-permute-start | bytes 786440 | tf_op jit(solution)/shard_map/ppermute | solution.py:106
  30.8 8.7 %collective-permute-start.6 = (bf16[512,256]{1,0:T(8,128)(2,1)S(1)}, bf16[512,256]{1,0:T(8,128)(2,1)S(1)}, u32[]{:S(2)}, u32[]{:S(2)}) collective-permute-start(bf16[512,256]{1,0:T(8,128)(2,1)S(1)} %collective-permute-done.5.refs_8_), channel_id=1, source_target_pairs={{0,4},{1,5},{2,6},{3,7},{4,0},{5,1},{6,2},{7,3},{24,28},{25,29},{2... | collective-permute-start | bytes 786440 | tf_op jit(solution)/shard_map/ppermute | solution.py:106
  40.2 8.6 %collective-permute-start.20 = (bf16[272,256]{1,0:T(8,128)(2,1)S(1)}, bf16[272,256]{1,0:T(8,128)(2,1)S(1)}, u32[]{:S(2)}, u32[]{:S(2)}) collective-permute-start(bf16[272,256]{1,0:T(8,128)(2,1)S(1)} %get-tuple-element.126.refs_0_), channel_id=1, source_target_pairs={{0,8},{1,9},{2,10},{3,11},{4,12},{5,13},{6,14},{7,15},{8,0},{9,1},... | collective-permute-start | bytes 417800 | tf_op jit(solution)/shard_map/ppermute | solution.py:106
  42.4 12.6 %collective-permute-start.23 = (bf16[128,1024]{1,0:T(8,128)(2,1)S(1)}, bf16[128,1024]{1,0:T(8,128)(2,1)S(1)}, u32[]{:S(2)}, u32[]{:S(2)}) collective-permute-start(bf16[128,1024]{1,0:T(8,128)(2,1)S(1)} %shard_map.59), channel_id=1, source_target_pairs={{0,4},{1,5},{2,6},{3,7},{4,0},{5,1},{6,2},{7,3},{8,12},{9,13},{10,... | collective-permute-start | bytes 786440 | tf_op jit(solution)/shard_map/ppermute | solution.py:106
  48.8 12.1 %collective-permute-start.21 = (bf16[272,256]{1,0:T(8,128)(2,1)S(1)}, bf16[272,256]{1,0:T(8,128)(2,1)S(1)}, u32[]{:S(2)}, u32[]{:S(2)}) collective-permute-start(bf16[272,256]{1,0:T(8,128)(2,1)S(1)} %collective-permute-done.20.refs_4_), channel_id=1, source_target_pairs={{0,2},{1,3},{2,0},{3,1},{4,6},{5,7},{6,4},{7,5},{8,10},{9,11},{10,... | collective-permute-start | bytes 417800 | tf_op jit(solution)/shard_map/ppermute | solution.py:106
  49.7 11.2 %collective-permute-start.16 = (bf16[64,1024]{1,0:T(8,128)(2,1)S(1)}, bf16[64,1024]{1,0:T(8,128)(2,1)S(1)}, u32[]{:S(2)}, u32[]{:S(2)}) collective-permute-start(bf16[64,1024]{1,0:T(8,128)(2,1)S(1)} %pad_maximum_fusion.refs_0_), channel_id=1, source_target_pairs={{0,16},{1,17},{2,18},{3,19},{4,20},{5,21},{6,22},{7,23},{8,24},{9,... | collective-permute-start | bytes 393224 | tf_op jit(solution)/shard_map/ppermute | solution.py:106
  50.3 11.0 %collective-permute-start.17 = (bf16[64,1024]{1,0:T(8,128)(2,1)S(1)}, bf16[64,1024]{1,0:T(8,128)(2,1)S(1)}, u32[]{:S(2)}, u32[]{:S(2)}) collective-permute-start(bf16[64,1024]{1,0:T(8,128)(2,1)S(1)} %pad_maximum_fusion.refs_0_), channel_id=1, source_target_pairs={{0,4},{1,5},{2,6},{3,7},{4,0},{5,1},{6,2},{7,3},{8,12},{9,13},{10,... | collective-permute-start | bytes 393224 | tf_op jit(solution)/shard_map/ppermute | solution.py:106
  54.1 9.6 %collective-permute-start.18 = (bf16[64,1024]{1,0:T(8,128)(2,1)S(1)}, bf16[64,1024]{1,0:T(8,128)(2,1)S(1)}, u32[]{:S(2)}, u32[]{:S(2)}) collective-permute-start(bf16[64,1024]{1,0:T(8,128)(2,1)S(1)} %pad_maximum_fusion.refs_0_), channel_id=1, source_target_pairs={{0,20},{1,21},{2,22},{3,23},{4,16},{5,17},{6,18},{7,19},{8,28},{9,... | collective-permute-start | bytes 393224 | tf_op jit(solution)/shard_map/ppermute | solution.py:106
  55.1 9.7 %collective-permute-start.24 = (bf16[128,1024]{1,0:T(8,128)(2,1)S(1)}, bf16[128,1024]{1,0:T(8,128)(2,1)S(1)}, u32[]{:S(2)}, u32[]{:S(2)}) collective-permute-start(bf16[128,1024]{1,0:T(8,128)(2,1)S(1)} %collective-permute-done.23.refs_0_), channel_id=1, source_target_pairs={{0,2},{1,3},{2,0},{3,1},{4,6},{5,7},{6,4},{7,5},{8,10},{9,11},{10,... | collective-permute-start | bytes 786440 | tf_op jit(solution)/shard_map/ppermute | solution.py:106
  67.5 11.8 %collective-permute-start.27 = (bf16[64,1024]{1,0:T(8,128)(2,1)S(1)}, bf16[64,1024]{1,0:T(8,128)(2,1)S(1)}, u32[]{:S(2)}, u32[]{:S(2)}) collective-permute-start(bf16[64,1024]{1,0:T(8,128)(2,1)S(1)} %get-tuple-element.156), channel_id=1, source_target_pairs={{0,16},{1,17},{2,18},{3,19},{4,20},{5,21},{6,22},{7,23},{8,24},{9,... | collective-permute-start | bytes 393224 | tf_op jit(solution)/shard_map/ppermute | solution.py:106
  67.5 15.1 %collective-permute-start.28 = (bf16[64,1024]{1,0:T(8,128)(2,1)S(1)}, bf16[64,1024]{1,0:T(8,128)(2,1)S(1)}, u32[]{:S(2)}, u32[]{:S(2)}) collective-permute-start(bf16[64,1024]{1,0:T(8,128)(2,1)S(1)} %get-tuple-element.157), channel_id=1, source_target_pairs={{0,20},{1,21},{2,22},{3,23},{4,16},{5,17},{6,18},{7,19},{8,28},{9,... | collective-permute-start | bytes 393224 | tf_op jit(solution)/shard_map/ppermute | solution.py:106
  71.1 11.5 %collective-permute-start.29 = (bf16[64,1024]{1,0:T(8,128)(2,1)S(1)}, bf16[64,1024]{1,0:T(8,128)(2,1)S(1)}, u32[]{:S(2)}, u32[]{:S(2)}) collective-permute-start(bf16[64,1024]{1,0:T(8,128)(2,1)S(1)} %get-tuple-element.158), channel_id=1, source_target_pairs={{0,4},{1,5},{2,6},{3,7},{4,0},{5,1},{6,2},{7,3},{8,12},{9,13},{10,... | collective-permute-start | bytes 393224 | tf_op jit(solution)/shard_map/ppermute | solution.py:106
  72.0 10.7 %collective-permute-start.30 = (bf16[528,256]{1,0:T(8,128)(2,1)S(1)}, bf16[528,256]{1,0:T(8,128)(2,1)S(1)}, u32[]{:S(2)}, u32[]{:S(2)}) collective-permute-start(bf16[528,256]{1,0:T(8,128)(2,1)S(1)} %get-tuple-element.163), channel_id=1, source_target_pairs={{0,2},{1,3},{2,0},{3,1},{4,6},{5,7},{6,4},{7,5},{8,10},{9,11},{10,... | collective-permute-start | bytes 811016 | tf_op jit(solution)/shard_map/ppermute | solution.py:106
  92.3 12.3 %collective-permute-start.43 = (bf16[256,512]{1,0:T(8,128)(2,1)S(1)}, bf16[256,512]{1,0:T(8,128)(2,1)S(1)}, u32[]{:S(2)}, u32[]{:S(2)}) collective-permute-start(bf16[256,512]{1,0:T(8,128)(2,1)S(1)} %get-tuple-element.210), channel_id=1, source_target_pairs={{0,4},{1,5},{2,6},{3,7},{4,0},{5,1},{6,2},{7,3},{8,12},{9,13},{10,... | collective-permute-start | bytes 786440 | tf_op jit(solution)/shard_map/ppermute | solution.py:106
  99.0 9.5 %collective-permute-start.40 = (bf16[256,512]{1,0:T(8,128)(2,1)S(1)}, bf16[256,512]{1,0:T(8,128)(2,1)S(1)}, u32[]{:S(2)}, u32[]{:S(2)}) collective-permute-start(bf16[256,512]{1,0:T(8,128)(2,1)S(1)} %get-tuple-element.208), channel_id=1, source_target_pairs={{0,16},{1,17},{2,18},{3,19},{4,20},{5,21},{6,22},{7,23},{24,8},{25... | collective-permute-start | bytes 786440 | tf_op jit(solution)/shard_map/ppermute | solution.py:106
  101.8 9.9 %collective-permute-start.41 = (bf16[256,512]{1,0:T(8,128)(2,1)S(1)}, bf16[256,512]{1,0:T(8,128)(2,1)S(1)}, u32[]{:S(2)}, u32[]{:S(2)}) collective-permute-start(bf16[256,512]{1,0:T(8,128)(2,1)S(1)} %get-tuple-element.209), channel_id=1, source_target_pairs={{0,8},{1,9},{2,10},{3,11},{4,12},{5,13},{6,14},{7,15},{24,16},{25,... | collective-permute-start | bytes 786440 | tf_op jit(solution)/shard_map/ppermute | solution.py:106
  103.8 12.4 %collective-permute-start.39 = (bf16[256,512]{1,0:T(8,128)(2,1)S(1)}, bf16[256,512]{1,0:T(8,128)(2,1)S(1)}, u32[]{:S(2)}, u32[]{:S(2)}) collective-permute-start(bf16[256,512]{1,0:T(8,128)(2,1)S(1)} %get-tuple-element.201), channel_id=1, source_target_pairs={{0,4},{1,5},{2,6},{3,7},{4,0},{5,1},{6,2},{7,3},{8,12},{9,13},{10,... | collective-permute-start | bytes 786440 | tf_op jit(solution)/shard_map/ppermute | solution.py:106
  111.8 9.1 %collective-permute-start.44 = (bf16[256,512]{1,0:T(8,128)(2,1)S(1)}, bf16[256,512]{1,0:T(8,128)(2,1)S(1)}, u32[]{:S(2)}, u32[]{:S(2)}) collective-permute-start(bf16[256,512]{1,0:T(8,128)(2,1)S(1)} %get-tuple-element.216), channel_id=1, source_target_pairs={{0,8},{1,9},{2,10},{3,11},{4,12},{5,13},{6,14},{7,15},{8,0},{9,1},... | collective-permute-start | bytes 786440 | tf_op jit(solution)/shard_map/ppermute | solution.py:106
  (28 other events, 155.4 us)

commit v10 on v9

--- a/solution.py
+++ b/solution.py
@@ -118,7 +118,8 @@
 TWO_OUT = along_line({1: 3, 2: 0})
 TWO_IN = along_line({3: 1, 0: 2})
 FAR = along_line({0: 2, 1: 3, 2: 0, 3: 1})
-FAR_Y = routes(lambda z, y, x, c: (z ^ 2, 1 - y, x, c))
+FAR_X = routes(lambda z, y, x, c: (z ^ 2, y, 1 - x, c))
+PAIRS_Y = routes(lambda z, y, x, c: (z ^ 1, 1 - y, x, c))
 MIX = [routes(lambda z, y, x, c, k=k: (z, y, x ^ (k >> 1), c ^ (k & 1))) for k in range(4)]
 
 
@@ -155,7 +156,7 @@
 
 
 def tail_of(message, row):
-    terms = message[-TAIL:].astype(jnp.float32)[3 * row : 3 * row + 3]
+    terms = message.astype(jnp.float32)[3 * row : 3 * row + 3]
     return terms[0:1] + terms[1:2] + terms[2:3]
 
 
@@ -171,57 +172,51 @@
     )(*operands)
 
 
-def after_cores(mine, message, loss):
-    rows, width = mine.shape[0], mine.shape[1] // 2
-    half = rows // 2
-
-    def kernel(mine_ref, message_ref, loss_ref, kept_ref, out_ref, total_ref):
-        kept_ref[...] = mine_ref[:, :width] + message_ref[:rows, :width].astype(jnp.float32)
-        sent = mine_ref[:, width:] + message_ref[:rows, width:].astype(jnp.float32)
-        out_ref[:rows] = sent.astype(jnp.bfloat16)
-        total = loss_ref[...] + tail_of(message_ref, 0)
-        total_ref[...] = total
-        out_ref[rows:] = tail_rows([total[:, :half], total[:, half:]])
-
-    results = [
-        jax.ShapeDtypeStruct((rows, width), jnp.float32),
-        jax.ShapeDtypeStruct((rows + TAIL, width), jnp.bfloat16),
-        jax.ShapeDtypeStruct((1, rows), jnp.float32),
-    ]
-    return in_vmem(kernel, results, mine, message, loss, time=0.5)
-
-
-def after_sides(kept, message, loss):
-    rows, width = kept.shape[0] // 2, kept.shape[1]
-
-    def kernel(kept_ref, message_ref, loss_ref, own_ref, out_ref, total_ref):
-        own_ref[...] = kept_ref[:rows] + message_ref[:rows].astype(jnp.float32)
-        sent = kept_ref[rows:] + message_ref[rows : 2 * rows].astype(jnp.float32)
-        out_ref[:rows] = sent.astype(jnp.bfloat16)
-        total_ref[...] = loss_ref[:, :rows] + tail_of(message_ref, 0)
-        out_ref[rows:] = tail_rows([loss_ref[:, rows:] + tail_of(message_ref, 1)])
-
-    results = [
-        jax.ShapeDtypeStruct((rows, width), jnp.float32),
-        jax.ShapeDtypeStruct((rows + TAIL, width), jnp.bfloat16),
-        jax.ShapeDtypeStruct((1, rows), jnp.float32),
-    ]
-    return in_vmem(kernel, results, kept, message, loss, time=0.5)
-
-
-def after_line(own, message, loss):
+def after_cores(mine, message, loss, fetched):
+    rows, width = mine.shape[0] // 2, mine.shape[1] // 2
+
+    below, blocks = fetched.shape[0], fetched.shape[1] // width
+
+    def kernel(
+        mine_ref, message_ref, loss_ref, fetched_ref, kept_ref, far_ref, far_x_ref, x_ref, total_ref
+    ):
+        total = loss_ref[...] + tail_of(message_ref[2 * rows :], 0)
+        total_ref[...] = total[:, :rows]
+        tails = [tail_rows([total[:, :rows]]), tail_rows([total[:, rows:]])]
+        for k, ref in enumerate((kept_ref, x_ref, far_ref, far_x_ref)):
+            place = slice(k // 2 * rows, (k // 2 + 1) * rows)
+            columns = slice(k % 2 * width, (k % 2 + 1) * width)
+            part = mine_ref[place, columns] + message_ref[place, columns].astype(jnp.float32)
+            ref[:rows] = part.astype(ref.dtype)
+            if k > 0:
+                ref[rows : rows + TAIL] = tails[k // 2]
+        for k in range(blocks):
+            place = slice(rows + TAIL + k * below, rows + TAIL + (k + 1) * below)
+            x_ref[place] = fetched_ref[:, k * width : (k + 1) * width]
+
+    results = [jax.ShapeDtypeStruct((rows, width), jnp.float32)]
+    heights = [rows + TAIL] * 2 + [rows + TAIL + below * blocks]
+    results += [jax.ShapeDtypeStruct((height, width), jnp.bfloat16) for height in heights]
+    results += [jax.ShapeDtypeStruct((1, rows), jnp.float32)]
+    return in_vmem(kernel, results, mine, message, loss, fetched, time=0.5)
+
+
+def after_line(own, messages, loss):
     rows, width = own.shape
 
-    def kernel(own_ref, message_ref, loss_ref, out_ref, total_ref):
-        total = own_ref[...] + message_ref[:rows].astype(jnp.float32)
+    def kernel(own_ref, far_ref, far_x_ref, x_ref, loss_ref, out_ref, total_ref):
+        total = own_ref[...]
+        for ref in (x_ref, far_ref, far_x_ref):
+            total += ref[:rows].astype(jnp.float32)
         out_ref[...] = total.astype(jnp.bfloat16)
-        total_ref[...] = loss_ref[...] + tail_of(message_ref, 0)
+        far = tail_of(far_ref[rows:], 0) + tail_of(far_x_ref[rows:], 0)
+        total_ref[...] = (loss_ref[...] + tail_of(x_ref[rows : rows + TAIL], 0)) + far
 
     results = [
         jax.ShapeDtypeStruct((rows, width), jnp.bfloat16),
         jax.ShapeDtypeStruct((1, rows), jnp.float32),
     ]
-    return in_vmem(kernel, results, own, message, loss, time=0.5)
+    return in_vmem(kernel, results, own, *messages, loss, time=0.5)
 
 
 def project(prompts, responses, blocks, weights, total, kind, time, digits=None):
@@ -381,42 +376,50 @@
     return in_vmem(kernel, results, *grads, *arrays, time=1)
 
 
-def in_order(order, fetched):
+def in_order(order, fetched, messages):
     half, columns = fetched[0].shape
+    height, width = messages[0].shape
+    blocks = columns // width
 
     def kernel(order_ref, *refs):
-        place = order_ref[1] * half
-        start = (1 - order_ref[0]) * 2 * half
-        for part, ref in enumerate(refs[:-1]):
-            first = start if part < 2 else 2 * half - start
-            row = first + (place if part % 2 == 0 else half - place)
-            refs[-1][pl.ds(pl.multiple_of(row, half), half)] = ref[...]
+        for k in range(2):
+            for array in range(2):
+
+                @pl.when(order_ref[0] == (array if k else 1 - array))
+                def _(ref=refs[k], message=refs[2 + k], out=refs[4 + array]):
+                    place = pl.multiple_of(order_ref[1] * half, half)
+                    out[pl.ds(place, half)] = ref[...]
+                    place = pl.multiple_of((1 - order_ref[1]) * half, half)
+                    for block in range(blocks):
+                        start = height - (blocks - block) * half
+                        columns = slice(block * width, (block + 1) * width)
+                        out[pl.ds(place, half), columns] = message[start : start + half]
 
     inside = pl.BlockSpec(memory_space=pltpu.VMEM)
     return pl.pallas_call(
         kernel,
         in_specs=[pl.BlockSpec(memory_space=pltpu.SMEM)] + [inside] * 4,
-        out_specs=inside,
-        out_shape=jax.ShapeDtypeStruct((4 * half, columns), fetched[0].dtype),
+        out_specs=[inside] * 2,
+        out_shape=[jax.ShapeDtypeStruct((2 * half, columns), fetched[0].dtype)] * 2,
         compiler_params=pltpu.CompilerParams(vmem_limit_bytes=8 * 1024 * 1024),
         cost_estimate=cost(0.5),
-    )(order, *fetched)
-
-
-def far_products(totals, features, grads):
-    (width, depth), rows = totals[0].shape, grads[0].shape[0]
-
-    def kernel(first_ref, second_ref, prompt_ref, response_ref, feature_ref, *outs):
+    )(order, *fetched, *messages)
+
+
+def far_products(totals, features, grad, time, last=False):
+    width, depth = totals[0].shape
+
+    def kernel(first_ref, second_ref, grad_ref, feature_ref, *outs):
         for k, ref in ((1, second_ref), (0, first_ref)):
             columns = slice(k * depth, (k + 1) * depth)
-            total = ref[...] + cross_rows(prompt_ref[...], feature_ref[:rows, columns])
-            total += cross_rows(response_ref[...], feature_ref[rows:, columns])
+            total = ref[...] + cross_rows(grad_ref[...], feature_ref[:, columns])
             outs[k][...] = total
-            outs[2 + k][...] = total.astype(jnp.bfloat16)
+            if last:
+                outs[2 + k][...] = total.astype(jnp.bfloat16)
 
     results = [jax.ShapeDtypeStruct((width, depth), jnp.float32)] * 2
-    results += [jax.ShapeDtypeStruct((width, depth), jnp.bfloat16)] * 2
-    return in_vmem(kernel, results, *totals, *grads, features, time=2)
+    results += [jax.ShapeDtypeStruct((width, depth), jnp.bfloat16)] * 2 * last
+    return in_vmem(kernel, results, *totals, grad, features, time=time)
 
 
 def second_round(*sums):
@@ -555,7 +558,7 @@
         there[:2] + here,
         [even, mp // CORES],
     )
-    starts = jnp.stack([here[0], here[2], there[0], there[2]]) * row_count + mp * quarter
+    starts = jnp.stack([here[0], here[1], there[1], there[0]]) * row_count + mp * quarter
     own, orders, places, swap, left, starts = tie(
         (
             head_projection_matrix,
@@ -600,54 +603,51 @@
     for k in range(SIDE * CORES):
         piece = lax.dynamic_slice(response_emb, (places[k], jnp.uint32(0)), (quarter, width))
         pieces.append(piece if k == 0 else send(piece, MIX[k]))
-    emb_done, picked = tie((prompt_emb, picked))
+    prompt_emb, picked = tie((prompt_emb, picked))
     fetched = send(picked, ACROSS_Y)
-    prompt_pair = send(prompt_emb, PAIRS)
+    prompt_far, prompt_far_x = send(prompt_emb, FAR), send(prompt_emb, FAR_X)
+    beside = [send(prompt_emb, ACROSS_X), prompt_far_x]
     response_rows = jnp.concatenate(pieces, axis=1)
 
-    held = [send(response_rows, FAR), send(response_rows, FAR_Y), send(response_rows, ACROSS_Y)]
-    groups = [
-        [block, send(block, ACROSS_C), send(block, ACROSS_X)] for block in (prompt_emb, prompt_pair)
-    ]
-    beside = [group[2] for group in groups]
-    held = [held[0], held[2], held[1]]
+    rows_late, fetched = tie((response_rows, fetched))
+    held = [send(response_rows, PAIRS), send(response_rows, PAIRS_Y), send(rows_late, ACROSS_Y)]
     held = stacked([response_rows, *held])
-    fetched_x = send(fetched, ACROSS_X)
-    features = slices(prompts, responses, tie((orders[4], prompt_emb))[0], depth)
+    groups = [[block, send(block, ACROSS_C)] for block in (prompt_emb, prompt_far)]
+    sibling = send(fetched, ACROSS_C)
+    features = slices(prompts, responses, tie((orders[4], response_rows))[0], depth)
     cross = [send(x, ACROSS_C) for x in beside]
-    held, features, cross_tied, fetched_x = tie((held, features, cross, fetched_x))
+    held, features, cross_tied, fetched = tie((held, features, cross, fetched))
     cross = cross_tied
     features = list(zip(features[:6], features[6:]))
-    groups = [[*group[:2], x, across] for group, x, across in zip(groups, beside, cross)]
+    groups = [[*group, x, across] for group, x, across in zip(groups, beside, cross)]
     losses, mine, away, *parts = compare(
         groups, held, positive[None, :], starts, row_count, LINE
     )
 
-    mine, aside, losses = after_cores(mine, send(away, ACROSS_C), losses)
-    back = [send(parts[1], FAR), send(parts[3], FAR_Y), send(parts[2], ACROSS_Y)]
+    back = [send(part, table) for part, table in zip(parts[1:], (PAIRS, PAIRS_Y, ACROSS_Y))]
+    mine, *messages, losses = after_cores(mine, send(away, ACROSS_C), losses, fetched)
+    messages = [send(part, table) for part, table in zip(messages, (FAR, FAR_X, ACROSS_X))]
     pieces = summed([parts[0], *back], SIDE * CORES)
-    pieces, aside = tie((pieces, send(aside, ACROSS_X)))
-    sibling, sibling_x = send(fetched, ACROSS_C), send(fetched_x, ACROSS_C)
-    mine, far, losses = after_sides(mine, aside, losses)
 
     pieces = [pieces[0]] + [send(pieces[k], MIX[k]) for k in range(1, SIDE * CORES)]
-    pieces, far = tie((pieces, send(far, PAIRS)))
+    pieces, messages = tie((pieces, messages))
     swapped = [jnp.where(swap, pieces[k], pieces[k ^ 1]) for k in range(SIDE * CORES)]
     swapped = [jnp.where(left, swapped[k], swapped[k ^ 2]) for k in range(SIDE * CORES)]
     grad_response = jnp.concatenate(swapped, axis=0)
-    grad_prompt, losses = after_line(mine, far, losses)
+    grad_prompt, losses = after_line(mine, messages, losses)
     grads_y = [send(grad_prompt, ACROSS_Y), send(grad_response, ACROSS_Y)]
 
     own_y, first_y, own, first, second, third = own_products(
         features, (grad_prompt, grad_response)
     )
-    far_features = in_order(orders[5], (fetched, fetched_x, sibling, sibling_x))
-    grads_y, own, first, second, third, far_features = tie(
-        (grads_y, own, first, second, third, far_features)
-    )
+    far_features = in_order(
+        orders[5], (fetched, sibling), (messages[2], send(messages[2], ACROSS_C))
+    )
+    own, first, second, third, far_features = tie((own, first, second, third, far_features))
+    second, third = far_products((second, third), far_features[1], grads_y[1], 4)
     own_y, first_y = send(own_y, ACROSS_Y), send(first_y, ACROSS_Y)
     second, third, second_b, third_b = far_products(
-        (second, third), far_features, grads_y
+        (second, third), far_features[0], grads_y[0], 1, last=True
     )
     terms = line_reduce(own, first, second, third, second_b, third_b, own_y, first_y)
     return (losses[0] / row_count, turned_sum(*terms))

time: 123 us -> 118 us (0.959)
  waiting for transfers between devices: 53.4 us -> 45.2 us
  starting transfers between devices: 50.2 us -> 53.6 us
    ppermute x46, waiting for transfers between devices: 53.4 us -> 45.2 us  [send(): return lax.ppermute(block, ('dp', 'mp'), table)]
    ppermute x46, starting transfers between devices: 50.2 us -> 53.6 us  [send(): return lax.ppermute(block, ('dp', 'mp'), table)]
  transfers between devices with their start and end apart: 46 -> 46, of which waited for: 19 -> 20; matrix products, arithmetic and copies ran while one was open for 1% -> 1% of each run, Pallas kernels for 8% -> 8%
where the time goes in v10:
time: 118 us; the launch traced here: 117 us
  starting transfers between devices  53.6 us (45%)
  waiting for transfers between devices  45.2 us (38%)
  Pallas kernels  13.3 us (11%)
  local copies, waits for them, and re-layouts  3.32 us (3%)
    ppermute x46, starting transfers between devices, send(): return lax.ppermute(block, ('dp', 'mp'), table)  53.6 us
    ppermute x46, waiting for transfers between devices, send(): return lax.ppermute(block, ('dp', 'mp'), table)  45.2 us
    pallas_call x3, Pallas kernels, project(): pl.pallas_call(kernel, in_specs=[pl.BlockSpec(memory_space=pltpu.SMEM)] +...  5.06 us
    pallas_call x9, Pallas kernels, in_vmem(): pl.pallas_call(kernel, in_specs=[inside] * len(operands), out_specs=[insi...  3.93 us
    unnamed x12, local copies, waits for them, and re-layouts  3.2 us
  transfers between devices with their start and end apart: 46, of which 20 were waited for; matrix products, arithmetic and copies ran while one was open for 1% of the time, Pallas kernels for 8%

profile of v10, /device:TPU:0, one launch (start us, length us, event | category | flops | bytes accessed | tf_op | source)
XLA Modules:
  0.0 117.4 jit_solution(13877203302091803758)
XLA Ops:
  1.1 3.0 %collective-permute-start = (bf16[512,256]{1,0:T(8,128)(2,1)}, bf16[512,256]{1,0:T(8,128)(2,1)S(1)}, u32[]{:S(2)}, u32[]{:S(2)}) collective-permute-start(bf16[512,256]{1,0:T(8,128)(2,1)} %refs_2_), channel_id=1, source_target_pairs={{0,8},{1,9},{2,10},{3,11},{4,12},{5,13},{6,14},{7,15},{8,0},{9,1},... | collective-permute-start | bytes 786440 | tf_op jit(solution)/shard_map/ppermute | solution.py:106
  12.7 1.6 %collective-permute-start.7 = (bf16[512,256]{1,0:T(8,128)(2,1)S(1)}, bf16[512,256]{1,0:T(8,128)(2,1)S(1)}, u32[]{:S(2)}, u32[]{:S(2)}) collective-permute-start(bf16[512,256]{1,0:T(8,128)(2,1)S(1)} %collective-permute-done.refs_4_), channel_id=1, source_target_pairs={{0,4},{1,5},{2,6},{3,7},{4,0},{5,1},{6,2},{7,3},{8,12},{9,13},{10,... | collective-permute-start | bytes 786440 | tf_op jit(solution)/shard_map/ppermute | solution.py:106
  15.7 2.0 %shard_map.60.refs_9_ = f32[512,256]{1,0:T(8,128)S(1)} custom-call(s32[3]{0:T(128)S(1)} %pad_add_fusion.1.block_ref, bf16[256,4096]{1,0:T(8,128)(2,1)S(1)} %copy-done.1, bf16[256,4096]{1,0:T(8,128)(2,1)S(1)} %copy-done.3, bf16[512,256]{1,0:T(8,128)(2,1)S(1)} %copy-done.5, bf16[512,256]{1,0:T(8,128)(2,1)S(1)} %collective-permute-done.3.refs_3_, ...), custom_call_target="tpu_custom_call" | custom-call | flops 2000000000 | tf_op jit(solution)/shard_map/pallas_call | solution.py:281
  18.4 7.2 %collective-permute-done.8.refs_4_ = bf16[512,256]{1,0:T(8,128)(2,1)S(1)} collective-permute-done((bf16[512,256]{1,0:T(8,128)(2,1)S(1)}, bf16[512,256]{1,0:T(8,128)(2,1)S(1)}, u32[]{:S(2)}, u32[]{:S(2)}) %collective-permute-start.8) | collective-permute-done | bytes 262176 | tf_op jit(solution)/shard_map/ppermute | solution.py:106
  25.6 3.4 %collective-permute-start.10 = (bf16[512,256]{1,0:T(8,128)(2,1)S(1)}, bf16[512,256]{1,0:T(8,128)(2,1)S(1)}, u32[]{:S(2)}, u32[]{:S(2)}) collective-permute-start(bf16[512,256]{1,0:T(8,128)(2,1)S(1)} %collective-permute-done.8.refs_4_), channel_id=1, source_target_pairs={{0,4},{1,5},{2,6},{3,7},{4,0},{5,1},{6,2},{7,3},{24,28},{25,29},{2... | collective-permute-start | bytes 786440 | tf_op jit(solution)/shard_map/ppermute | solution.py:106
  30.7 3.4 %collective-permute-start.6 = (bf16[512,256]{1,0:T(8,128)(2,1)S(1)}, bf16[512,256]{1,0:T(8,128)(2,1)S(1)}, u32[]{:S(2)}, u32[]{:S(2)}) collective-permute-start(bf16[512,256]{1,0:T(8,128)(2,1)S(1)} %collective-permute-done.5.refs_8_), channel_id=1, source_target_pairs={{0,4},{1,5},{2,6},{3,7},{4,0},{5,1},{6,2},{7,3},{24,28},{25,29},{2... | collective-permute-start | bytes 786440 | tf_op jit(solution)/shard_map/ppermute | solution.py:106
  34.5 2.4 %shard_map.61.refs_4_ = f32[512,256]{1,0:T(8,128)S(1)} custom-call(s32[4]{0:T(128)S(1)} %get-tuple-element.122.block_ref, bf16[256,4096]{1,0:T(8,128)(2,1)S(1)} %copy-done.1, bf16[256,4096]{1,0:T(8,128)(2,1)S(1)} %copy-done.3, bf16[512,256]{1,0:T(8,128)(2,1)S(1)} %collective-permute-done.7.refs_2_, bf16[512,256]{1,0:T(8,128)(2,1)S(1)} %collective-permute-done.2.refs_3_, ...), custom_call_target="tpu_custom_call" | custom-call | flops 2400000000 | tf_op jit(solution)/shard_map/pallas_call | solution.py:281
  36.9 2.6 %collective-permute-done.6.refs_3_ = bf16[512,256]{1,0:T(8,128)(2,1)S(1)} collective-permute-done((bf16[512,256]{1,0:T(8,128)(2,1)S(1)}, bf16[512,256]{1,0:T(8,128)(2,1)S(1)}, u32[]{:S(2)}, u32[]{:S(2)}) %collective-permute-start.6) | collective-permute-done | bytes 262176 | tf_op jit(solution)/shard_map/ppermute | solution.py:106
  45.2 2.6 %collective-permute-start.21 = (bf16[272,256]{1,0:T(8,128)(2,1)S(1)}, bf16[272,256]{1,0:T(8,128)(2,1)S(1)}, u32[]{:S(2)}, u32[]{:S(2)}) collective-permute-start(bf16[272,256]{1,0:T(8,128)(2,1)S(1)} %get-tuple-element.130.refs_0_), channel_id=1, source_target_pairs={{0,18},{1,19},{2,16},{3,17},{4,22},{5,23},{6,20},{7,21},{8,26},{9,... | collective-permute-start | bytes 417800 | tf_op jit(solution)/shard_map/ppermute | solution.py:106
  48.5 1.8 %collective-permute-start.16 = (bf16[64,1024]{1,0:T(8,128)(2,1)S(1)}, bf16[64,1024]{1,0:T(8,128)(2,1)S(1)}, u32[]{:S(2)}, u32[]{:S(2)}) collective-permute-start(bf16[64,1024]{1,0:T(8,128)(2,1)S(1)} %pad_maximum_fusion.refs_0_), channel_id=1, source_target_pairs={{0,8},{1,9},{2,10},{3,11},{4,12},{5,13},{6,14},{7,15},{8,0},{9,1},... | collective-permute-start | bytes 393224 | tf_op jit(solution)/shard_map/ppermute | solution.py:106
  52.3 7.2 %collective-permute-done.21.refs_6_ = bf16[272,256]{1,0:T(8,128)(2,1)S(1)} collective-permute-done((bf16[272,256]{1,0:T(8,128)(2,1)S(1)}, bf16[272,256]{1,0:T(8,128)(2,1)S(1)}, u32[]{:S(2)}, u32[]{:S(2)}) %collective-permute-start.21) | collective-permute-done | bytes 139296 | tf_op jit(solution)/shard_map/ppermute | solution.py:106
  62.7 2.1 %shard_map.65 = (f32[1,512]{1,0:T(1,128)S(1)}, f32[512,512]{1,0:T(8,128)S(1)}, bf16[528,512]{1,0:T(8,128)(2,1)S(1)}, f32[64,1024]{1,0:T(8,128)S(1)}, bf16[64,102...) custom-call(s32[4]{0:T(128)S(1)} %fusion.start_ref, s32[1,256]{1,0:T(1,128)S(1)} %bitcast.13, ...), custom_call_target="tpu_custom_call" | custom-call | flops 2000000000 | tf_op jit(solution)/shard_map/pallas_call | solution.py:525
  71.5 2.1 %collective-permute-start.33 = (bf16[272,256]{1,0:T(8,128)(2,1)S(1)}, bf16[272,256]{1,0:T(8,128)(2,1)S(1)}, u32[]{:S(2)}, u32[]{:S(2)}) collective-permute-start(bf16[272,256]{1,0:T(8,128)(2,1)S(1)} %get-tuple-element.170), channel_id=1, source_target_pairs={{0,18},{1,19},{2,16},{3,17},{4,22},{5,23},{6,20},{7,21},{8,26},{9,... | collective-permute-start | bytes 417800 | tf_op jit(solution)/shard_map/ppermute | solution.py:106
  73.6 2.5 %collective-permute-done.27.refs_2_ = bf16[64,1024]{1,0:T(8,128)(2,1)S(1)} collective-permute-done((bf16[64,1024]{1,0:T(8,128)(2,1)S(1)}, bf16[64,1024]{1,0:T(8,128)(2,1)S(1)}, u32[]{:S(2)}, u32[]{:S(2)}) %collective-permute-start.27) | collective-permute-done | bytes 131104 | tf_op jit(solution)/shard_map/ppermute | solution.py:106
  76.2 1.6 %collective-permute-start.30 = (bf16[64,256]{1,0:T(8,128)(2,1)S(1)}, bf16[64,256]{1,0:T(8,128)(2,1)S(1)}, u32[]{:S(2)}, u32[]{:S(2)}) collective-permute-start(bf16[64,256]{1,0:T(8,128)(2,1)S(1)} %get-tuple-element.167), channel_id=1, source_target_pairs={{0,2},{1,3},{2,0},{3,1},{4,6},{5,7},{6,4},{7,5},{8,10},{9,11},{10,... | collective-permute-start | bytes 98312 | tf_op jit(solution)/shard_map/ppermute | solution.py:106
  78.7 1.7 %collective-permute-done.30 = bf16[64,256]{1,0:T(8,128)(2,1)S(1)} collective-permute-done((bf16[64,256]{1,0:T(8,128)(2,1)S(1)}, bf16[64,256]{1,0:T(8,128)(2,1)S(1)}, u32[]{:S(2)}, u32[]{:S(2)}) %collective-permute-start.30) | collective-permute-done | bytes 32800 | tf_op jit(solution)/shard_map/ppermute | solution.py:106
  81.2 2.0 %collective-permute-done.32.far_ref = bf16[272,256]{1,0:T(8,128)(2,1)S(1)} collective-permute-done((bf16[272,256]{1,0:T(8,128)(2,1)S(1)}, bf16[272,256]{1,0:T(8,128)(2,1)S(1)}, u32[]{:S(2)}, u32[]{:S(2)}) %collective-permute-start.32) | collective-permute-done | bytes 139296 | tf_op jit(solution)/shard_map/ppermute | solution.py:106
  83.2 1.9 %collective-permute-done.33.far_x_ref = bf16[272,256]{1,0:T(8,128)(2,1)S(1)} collective-permute-done((bf16[272,256]{1,0:T(8,128)(2,1)S(1)}, bf16[272,256]{1,0:T(8,128)(2,1)S(1)}, u32[]{:S(2)}, u32[]{:S(2)}) %collective-permute-start.33) | collective-permute-done | bytes 139296 | tf_op jit(solution)/shard_map/ppermute | solution.py:106
  91.8 2.5 %collective-permute-done.39.grad_ref = bf16[256,256]{1,0:T(8,128)(2,1)S(1)} collective-permute-done((bf16[256,256]{1,0:T(8,128)(2,1)S(1)}, bf16[256,256]{1,0:T(8,128)(2,1)S(1)}, u32[]{:S(2)}, u32[]{:S(2)}) %collective-permute-start.39) | collective-permute-done | bytes 131104 | tf_op jit(solution)/shard_map/ppermute | solution.py:106
  95.4 2.2 %collective-permute-start.40 = (bf16[256,512]{1,0:T(8,128)(2,1)S(1)}, bf16[256,512]{1,0:T(8,128)(2,1)S(1)}, u32[]{:S(2)}, u32[]{:S(2)}) collective-permute-start(bf16[256,512]{1,0:T(8,128)(2,1)S(1)} %get-tuple-element.212), channel_id=1, source_target_pairs={{0,16},{1,17},{2,18},{3,19},{4,20},{5,21},{6,22},{7,23},{24,8},{25... | collective-permute-start | bytes 786440 | tf_op jit(solution)/shard_map/ppermute | solution.py:106
  101.0 3.4 %collective-permute-done.40.refs_3_ = bf16[256,512]{1,0:T(8,128)(2,1)S(1)} collective-permute-done((bf16[256,512]{1,0:T(8,128)(2,1)S(1)}, bf16[256,512]{1,0:T(8,128)(2,1)S(1)}, u32[]{:S(2)}, u32[]{:S(2)}) %collective-permute-start.40) | collective-permute-done | bytes 262176 | tf_op jit(solution)/shard_map/ppermute | solution.py:106
  104.4 3.3 %collective-permute-done.41.refs_5_ = bf16[256,512]{1,0:T(8,128)(2,1)S(1)} collective-permute-done((bf16[256,512]{1,0:T(8,128)(2,1)S(1)}, bf16[256,512]{1,0:T(8,128)(2,1)S(1)}, u32[]{:S(2)}, u32[]{:S(2)}) %collective-permute-start.41) | collective-permute-done | bytes 262176 | tf_op jit(solution)/shard_map/ppermute | solution.py:106
  107.9 2.8 %collective-permute-start.44 = (bf16[256,512]{1,0:T(8,128)(2,1)S(1)}, bf16[256,512]{1,0:T(8,128)(2,1)S(1)}, u32[]{:S(2)}, u32[]{:S(2)}) collective-permute-start(bf16[256,512]{1,0:T(8,128)(2,1)S(1)} %get-tuple-element.220), channel_id=1, source_target_pairs={{0,8},{1,9},{2,10},{3,11},{4,12},{5,13},{6,14},{7,15},{8,0},{9,1},... | collective-permute-start | bytes 786440 | tf_op jit(solution)/shard_map/ppermute | solution.py:106
  111.9 4.5 %collective-permute-done.44.refs_2_ = bf16[256,512]{1,0:T(8,128)(2,1)S(1)} collective-permute-done((bf16[256,512]{1,0:T(8,128)(2,1)S(1)}, bf16[256,512]{1,0:T(8,128)(2,1)S(1)}, u32[]{:S(2)}, u32[]{:S(2)}) %collective-permute-start.44) | collective-permute-done | bytes 262176 | tf_op jit(solution)/shard_map/ppermute | solution.py:106
  (106 shorter events, 46.6 us)
Async XLA Ops:
  1.1 9.6 %collective-permute-start = (bf16[512,256]{1,0:T(8,128)(2,1)}, bf16[512,256]{1,0:T(8,128)(2,1)S(1)}, u32[]{:S(2)}, u32[]{:S(2)}) collective-permute-start(bf16[512,256]{1,0:T(8,128)(2,1)} %refs_2_), channel_id=1, source_target_pairs={{0,8},{1,9},{2,10},{3,11},{4,12},{5,13},{6,14},{7,15},{8,0},{9,1},... | collective-permute-start | bytes 786440 | tf_op jit(solution)/shard_map/ppermute | solution.py:106
  4.8 9.6 %collective-permute-start.3 = (bf16[512,256]{1,0:T(8,128)(2,1)}, bf16[512,256]{1,0:T(8,128)(2,1)S(1)}, u32[]{:S(2)}, u32[]{:S(2)}) collective-permute-start(bf16[512,256]{1,0:T(8,128)(2,1)} %refs_2_), channel_id=1, source_target_pairs={{0,4},{1,5},{2,6},{3,7},{4,0},{5,1},{6,2},{7,3},{8,12},{9,13},{10,... | collective-permute-start | bytes 786440 | tf_op jit(solution)/shard_map/ppermute | solution.py:106
  11.4 14.2 %collective-permute-start.8 = (bf16[512,256]{1,0:T(8,128)(2,1)S(1)}, bf16[512,256]{1,0:T(8,128)(2,1)S(1)}, u32[]{:S(2)}, u32[]{:S(2)}) collective-permute-start(bf16[512,256]{1,0:T(8,128)(2,1)S(1)} %collective-permute-done.1.refs_7_), channel_id=1, source_target_pairs={{8,0},{9,1},{10,2},{11,3},{12,4},{13,5},{14,6},{15,7},{16,24},{17,... | collective-permute-start | bytes 786440 | tf_op jit(solution)/shard_map/ppermute | solution.py:106
  12.7 21.4 %collective-permute-start.7 = (bf16[512,256]{1,0:T(8,128)(2,1)S(1)}, bf16[512,256]{1,0:T(8,128)(2,1)S(1)}, u32[]{:S(2)}, u32[]{:S(2)}) collective-permute-start(bf16[512,256]{1,0:T(8,128)(2,1)S(1)} %collective-permute-done.refs_4_), channel_id=1, source_target_pairs={{0,4},{1,5},{2,6},{3,7},{4,0},{5,1},{6,2},{7,3},{8,12},{9,13},{10,... | collective-permute-start | bytes 786440 | tf_op jit(solution)/shard_map/ppermute | solution.py:106
  14.4 16.4 %collective-permute-start.5 = (bf16[512,256]{1,0:T(8,128)(2,1)S(1)}, bf16[512,256]{1,0:T(8,128)(2,1)S(1)}, u32[]{:S(2)}, u32[]{:S(2)}) collective-permute-start(bf16[512,256]{1,0:T(8,128)(2,1)S(1)} %collective-permute-done.2.refs_3_), channel_id=1, source_target_pairs={{8,0},{9,1},{10,2},{11,3},{12,4},{13,5},{14,6},{15,7},{16,24},{17,... | collective-permute-start | bytes 786440 | tf_op jit(solution)/shard_map/ppermute | solution.py:106
  17.7 16.5 %collective-permute-start.9 = (bf16[512,256]{1,0:T(8,128)(2,1)S(1)}, bf16[512,256]{1,0:T(8,128)(2,1)S(1)}, u32[]{:S(2)}, u32[]{:S(2)}) collective-permute-start(bf16[512,256]{1,0:T(8,128)(2,1)S(1)} %collective-permute-done.2.refs_3_), channel_id=1, source_target_pairs={{8,12},{9,13},{10,14},{11,15},{12,8},{13,9},{14,10},{15,11},{16,20... | collective-permute-start | bytes 786440 | tf_op jit(solution)/shard_map/ppermute | solution.py:106
  25.6 8.9 %collective-permute-start.10 = (bf16[512,256]{1,0:T(8,128)(2,1)S(1)}, bf16[512,256]{1,0:T(8,128)(2,1)S(1)}, u32[]{:S(2)}, u32[]{:S(2)}) collective-permute-start(bf16[512,256]{1,0:T(8,128)(2,1)S(1)} %collective-permute-done.8.refs_4_), channel_id=1, source_target_pairs={{0,4},{1,5},{2,6},{3,7},{4,0},{5,1},{6,2},{7,3},{24,28},{25,29},{2... | collective-permute-start | bytes 786440 | tf_op jit(solution)/shard_map/ppermute | solution.py:106
  30.7 8.7 %collective-permute-start.6 = (bf16[512,256]{1,0:T(8,128)(2,1)S(1)}, bf16[512,256]{1,0:T(8,128)(2,1)S(1)}, u32[]{:S(2)}, u32[]{:S(2)}) collective-permute-start(bf16[512,256]{1,0:T(8,128)(2,1)S(1)} %collective-permute-done.5.refs_8_), channel_id=1, source_target_pairs={{0,4},{1,5},{2,6},{3,7},{4,0},{5,1},{6,2},{7,3},{24,28},{25,29},{2... | collective-permute-start | bytes 786440 | tf_op jit(solution)/shard_map/ppermute | solution.py:106
  40.1 10.2 %collective-permute-start.18 = (bf16[128,1024]{1,0:T(8,128)(2,1)S(1)}, bf16[128,1024]{1,0:T(8,128)(2,1)S(1)}, u32[]{:S(2)}, u32[]{:S(2)}) collective-permute-start(bf16[128,1024]{1,0:T(8,128)(2,1)S(1)} %shard_map.59), channel_id=1, source_target_pairs={{0,4},{1,5},{2,6},{3,7},{4,0},{5,1},{6,2},{7,3},{8,12},{9,13},{10,... | collective-permute-start | bytes 786440 | tf_op jit(solution)/shard_map/ppermute | solution.py:106
  45.2 14.3 %collective-permute-start.21 = (bf16[272,256]{1,0:T(8,128)(2,1)S(1)}, bf16[272,256]{1,0:T(8,128)(2,1)S(1)}, u32[]{:S(2)}, u32[]{:S(2)}) collective-permute-start(bf16[272,256]{1,0:T(8,128)(2,1)S(1)} %get-tuple-element.130.refs_0_), channel_id=1, source_target_pairs={{0,18},{1,19},{2,16},{3,17},{4,22},{5,23},{6,20},{7,21},{8,26},{9,... | collective-permute-start | bytes 417800 | tf_op jit(solution)/shard_map/ppermute | solution.py:106
  47.8 12.9 %collective-permute-start.23 = (bf16[272,256]{1,0:T(8,128)(2,1)S(1)}, bf16[272,256]{1,0:T(8,128)(2,1)S(1)}, u32[]{:S(2)}, u32[]{:S(2)}) collective-permute-start(bf16[272,256]{1,0:T(8,128)(2,1)S(1)} %get-tuple-element.130.refs_0_), channel_id=1, source_target_pairs={{0,16},{1,17},{2,18},{3,19},{4,20},{5,21},{6,22},{7,23},{8,24},{9,... | collective-permute-start | bytes 417800 | tf_op jit(solution)/shard_map/ppermute | solution.py:106
  48.5 12.2 %collective-permute-start.16 = (bf16[64,1024]{1,0:T(8,128)(2,1)S(1)}, bf16[64,1024]{1,0:T(8,128)(2,1)S(1)}, u32[]{:S(2)}, u32[]{:S(2)}) collective-permute-start(bf16[64,1024]{1,0:T(8,128)(2,1)S(1)} %pad_maximum_fusion.refs_0_), channel_id=1, source_target_pairs={{0,8},{1,9},{2,10},{3,11},{4,12},{5,13},{6,14},{7,15},{8,0},{9,1},... | collective-permute-start | bytes 393224 | tf_op jit(solution)/shard_map/ppermute | solution.py:106
  50.3 11.1 %collective-permute-start.17 = (bf16[64,1024]{1,0:T(8,128)(2,1)S(1)}, bf16[64,1024]{1,0:T(8,128)(2,1)S(1)}, u32[]{:S(2)}, u32[]{:S(2)}) collective-permute-start(bf16[64,1024]{1,0:T(8,128)(2,1)S(1)} %pad_maximum_fusion.refs_0_), channel_id=1, source_target_pairs={{0,12},{1,13},{2,14},{3,15},{4,8},{5,9},{6,10},{7,11},{8,4},{9,5},... | collective-permute-start | bytes 393224 | tf_op jit(solution)/shard_map/ppermute | solution.py:106
  51.7 10.6 %collective-permute-start.19 = (bf16[64,1024]{1,0:T(8,128)(2,1)S(1)}, bf16[64,1024]{1,0:T(8,128)(2,1)S(1)}, u32[]{:S(2)}, u32[]{:S(2)}) collective-permute-start(bf16[64,1024]{1,0:T(8,128)(2,1)S(1)} %pad_maximum_fusion.refs_0_), channel_id=1, source_target_pairs={{0,4},{1,5},{2,6},{3,7},{4,0},{5,1},{6,2},{7,3},{8,12},{9,13},{10,... | collective-permute-start | bytes 393224 | tf_op jit(solution)/shard_map/ppermute | solution.py:106
  66.2 9.9 %collective-permute-start.27 = (bf16[64,1024]{1,0:T(8,128)(2,1)S(1)}, bf16[64,1024]{1,0:T(8,128)(2,1)S(1)}, u32[]{:S(2)}, u32[]{:S(2)}) collective-permute-start(bf16[64,1024]{1,0:T(8,128)(2,1)S(1)} %get-tuple-element.163), channel_id=1, source_target_pairs={{0,12},{1,13},{2,14},{3,15},{4,8},{5,9},{6,10},{7,11},{8,4},{9,5},... | collective-permute-start | bytes 393224 | tf_op jit(solution)/shard_map/ppermute | solution.py:106
  68.7 16.4 %collective-permute-start.34 = (bf16[784,256]{1,0:T(8,128)(2,1)S(1)}, bf16[784,256]{1,0:T(8,128)(2,1)S(1)}, u32[]{:S(2)}, u32[]{:S(2)}) collective-permute-start(bf16[784,256]{1,0:T(8,128)(2,1)S(1)} %get-tuple-element.171), channel_id=1, source_target_pairs={{0,2},{1,3},{2,0},{3,1},{4,6},{5,7},{6,4},{7,5},{8,10},{9,11},{10,... | collective-permute-start | bytes 1204232 | tf_op jit(solution)/shard_map/ppermute | solution.py:106
  70.1 13.1 %collective-permute-start.32 = (bf16[272,256]{1,0:T(8,128)(2,1)S(1)}, bf16[272,256]{1,0:T(8,128)(2,1)S(1)}, u32[]{:S(2)}, u32[]{:S(2)}) collective-permute-start(bf16[272,256]{1,0:T(8,128)(2,1)S(1)} %get-tuple-element.169), channel_id=1, source_target_pairs={{0,16},{1,17},{2,18},{3,19},{4,20},{5,21},{6,22},{7,23},{8,24},{9,... | collective-permute-start | bytes 417800 | tf_op jit(solution)/shard_map/ppermute | solution.py:106
  71.5 13.6 %collective-permute-start.33 = (bf16[272,256]{1,0:T(8,128)(2,1)S(1)}, bf16[272,256]{1,0:T(8,128)(2,1)S(1)}, u32[]{:S(2)}, u32[]{:S(2)}) collective-permute-start(bf16[272,256]{1,0:T(8,128)(2,1)S(1)} %get-tuple-element.170), channel_id=1, source_target_pairs={{0,18},{1,19},{2,16},{3,17},{4,22},{5,23},{6,20},{7,21},{8,26},{9,... | collective-permute-start | bytes 417800 | tf_op jit(solution)/shard_map/ppermute | solution.py:106
  80.5 8.9 %collective-permute-start.35 = (bf16[128,1024]{1,0:T(8,128)(2,1)S(1)}, bf16[128,1024]{1,0:T(8,128)(2,1)S(1)}, u32[]{:S(2)}, u32[]{:S(2)}) collective-permute-start(bf16[128,1024]{1,0:T(8,128)(2,1)S(1)} %collective-permute-done.18.fetched_ref.refs_0_), channel_id=1, source_target_pairs={{0,1},{1,0},{2,3},{3,2},{4,5},{5,4},{6,7},{7,6},{8,9},{9,8},{10,11... | collective-permute-start | bytes 786440 | tf_op jit(solution)/shard_map/ppermute | solution.py:106
  88.4 12.6 %collective-permute-start.43 = (bf16[256,512]{1,0:T(8,128)(2,1)S(1)}, bf16[256,512]{1,0:T(8,128)(2,1)S(1)}, u32[]{:S(2)}, u32[]{:S(2)}) collective-permute-start(bf16[256,512]{1,0:T(8,128)(2,1)S(1)} %get-tuple-element.214), channel_id=1, source_target_pairs={{0,4},{1,5},{2,6},{3,7},{4,0},{5,1},{6,2},{7,3},{8,12},{9,13},{10,... | collective-permute-start | bytes 786440 | tf_op jit(solution)/shard_map/ppermute | solution.py:106
  95.4 9.0 %collective-permute-start.40 = (bf16[256,512]{1,0:T(8,128)(2,1)S(1)}, bf16[256,512]{1,0:T(8,128)(2,1)S(1)}, u32[]{:S(2)}, u32[]{:S(2)}) collective-permute-start(bf16[256,512]{1,0:T(8,128)(2,1)S(1)} %get-tuple-element.212), channel_id=1, source_target_pairs={{0,16},{1,17},{2,18},{3,19},{4,20},{5,21},{6,22},{7,23},{24,8},{25... | collective-permute-start | bytes 786440 | tf_op jit(solution)/shard_map/ppermute | solution.py:106
  97.6 10.1 %collective-permute-start.41 = (bf16[256,512]{1,0:T(8,128)(2,1)S(1)}, bf16[256,512]{1,0:T(8,128)(2,1)S(1)}, u32[]{:S(2)}, u32[]{:S(2)}) collective-permute-start(bf16[256,512]{1,0:T(8,128)(2,1)S(1)} %get-tuple-element.213), channel_id=1, source_target_pairs={{0,8},{1,9},{2,10},{3,11},{4,12},{5,13},{6,14},{7,15},{24,16},{25,... | collective-permute-start | bytes 786440 | tf_op jit(solution)/shard_map/ppermute | solution.py:106
  99.0 8.8 %collective-permute-start.42 = (bf16[256,512]{1,0:T(8,128)(2,1)S(1)}, bf16[256,512]{1,0:T(8,128)(2,1)S(1)}, u32[]{:S(2)}, u32[]{:S(2)}) collective-permute-start(bf16[256,512]{1,0:T(8,128)(2,1)S(1)} %get-tuple-element.213), channel_id=1, source_target_pairs={{8,16},{9,17},{10,18},{11,19},{12,20},{13,21},{14,22},{15,23},{16,... | collective-permute-start | bytes 786440 | tf_op jit(solution)/shard_map/ppermute | solution.py:106
  99.6 12.2 %collective-permute-start.37 = (bf16[256,512]{1,0:T(8,128)(2,1)S(1)}, bf16[256,512]{1,0:T(8,128)(2,1)S(1)}, u32[]{:S(2)}, u32[]{:S(2)}) collective-permute-start(bf16[256,512]{1,0:T(8,128)(2,1)S(1)} %get-tuple-element.204), channel_id=1, source_target_pairs={{0,4},{1,5},{2,6},{3,7},{4,0},{5,1},{6,2},{7,3},{8,12},{9,13},{10,... | collective-permute-start | bytes 786440 | tf_op jit(solution)/shard_map/ppermute | solution.py:106
  (28 other events, 152.5 us)

commit v11 on v10

--- a/solution.py
+++ b/solution.py
@@ -108,15 +108,12 @@
 
 ACROSS_Y = routes(lambda z, y, x, c: (z, 1 - y, x, c))
 ACROSS_X = routes(lambda z, y, x, c: (z, y, 1 - x, c))
-Y_ENDS = routes(lambda z, y, x, c: (z, 1 - y, x, c) if z in (0, 3) else None)
-Y_MIDDLE = routes(lambda z, y, x, c: (z, 1 - y, x, c) if z in (1, 2) else None)
 ACROSS_C = routes(lambda z, y, x, c: (z, y, x, 1 - c))
 PAIRS = along_line({0: 1, 1: 0, 2: 3, 3: 2})
 MIDDLE = along_line({1: 2, 2: 1})
-OUTWARD = along_line({1: 0, 2: 3})
 INWARD = along_line({0: 1, 3: 2})
-TWO_OUT = along_line({1: 3, 2: 0})
 TWO_IN = along_line({3: 1, 0: 2})
+OPPOSITE = along_line({0: 3, 1: 2, 2: 1, 3: 0})
 FAR = along_line({0: 2, 1: 3, 2: 0, 3: 1})
 FAR_X = routes(lambda z, y, x, c: (z ^ 2, y, 1 - x, c))
 PAIRS_Y = routes(lambda z, y, x, c: (z ^ 1, 1 - y, x, c))
@@ -138,6 +135,7 @@
 
 TAIL = 16
 DIGIT_BITS = 8
+LANES = 128
 
 
 def cost(microseconds):
@@ -470,23 +468,23 @@
             out[...] = total.astype(jnp.bfloat16)
 
     result = jax.ShapeDtypeStruct((rows, width), jnp.bfloat16)
-    return in_vmem(kernel, [result] * count, *terms, time=5)
-
-
-def compare(groups, held, wanted, starts, row_count, blocks):
+    return in_vmem(kernel, [result] * count, *terms, time=4)
+
+
+def compare(groups, held, wanted, ids, row_count, blocks):
     rows, width = row_count, groups[0][0].shape[1]
     prompt_rows, across = rows * len(groups), len(groups[0])
     count, full = held.shape
     quarter = count // blocks
     factor = LOGIT_SCALE / math.sqrt(E)
-    operands = [wanted, *[piece for group in groups for piece in group], held]
-
-    def kernel(start_ref, wanted_ref, *refs):
+    operands = [wanted, ids, *[piece for group in groups for piece in group], held]
+
+    def kernel(wanted_ref, id_ref, *refs):
         group_refs = [refs[g * across : (g + 1) * across] for g in range(len(groups))]
         refs = refs[len(groups) * across :]
         rows_ref, loss_ref, mine_ref, away_ref, *part_refs = refs
-        count_up = lax.broadcasted_iota(jnp.int32, (quarter, 1), 0)
-        ids = jnp.concatenate([count_up + start_ref[k] for k in range(blocks)], axis=0)
+        ids = id_ref[...]
+        ids = jnp.concatenate([ids] * (rows // ids.shape[1]), axis=1)
         weights, losses = [], []
         for g, pieces in enumerate(group_refs):
             scores = jnp.zeros((count, rows), jnp.float32)
@@ -524,8 +522,7 @@
 
     return pl.pallas_call(
         kernel,
-        in_specs=[pl.BlockSpec(memory_space=pltpu.SMEM)]
-        + [pl.BlockSpec(memory_space=pltpu.VMEM)] * len(operands),
+        in_specs=[pl.BlockSpec(memory_space=pltpu.VMEM)] * len(operands),
         out_specs=[pl.BlockSpec(memory_space=pltpu.VMEM)] * (3 + blocks),
         out_shape=[
             jax.ShapeDtypeStruct((1, prompt_rows), jnp.float32),
@@ -536,7 +533,7 @@
         + [jax.ShapeDtypeStruct((quarter, full), jnp.bfloat16)] * (blocks - 1),
         compiler_params=pltpu.CompilerParams(vmem_limit_bytes=16 * 1024 * 1024),
         cost_estimate=cost(2),
-    )(starts, *operands)
+    )(*operands)
 
 
 def full_window(prompts, responses, head_projection_matrix, positive):
@@ -552,51 +549,56 @@
     even = (mp % CORES == 0).astype(jnp.int32)
     orders = (
         [there[2], there[3], even, mp // CORES],
-        [here[0], there[0], here[1]],
-        [there[1], here[2], there[2], here[3]],
-        [there[3]],
+        [here[0], there[0], here[1], there[1]],
+        [here[3], there[3], here[2]],
+        [there[2]],
         there[:2] + here,
         [even, mp // CORES],
     )
-    starts = jnp.stack([here[0], here[1], there[1], there[0]]) * row_count + mp * quarter
-    own, orders, places, swap, left, starts = tie(
+    ids = jnp.stack([here[0], here[1], there[1], there[0]]) * row_count + mp * quarter
+    ids = (ids.astype(jnp.int32)[:, None] + lax.iota(jnp.int32, quarter)).reshape(-1, 1)
+    ids = jnp.broadcast_to(ids, (LINE * quarter, LANES))
+    own, orders, places, swap, left, ids = tie(
         (
             head_projection_matrix,
             [jnp.stack(order).astype(jnp.int32) for order in orders],
             [((mp ^ k) * quarter).astype(jnp.uint32) for k in range(SIDE * CORES)],
             even == 1,
             mp < CORES,
-            starts.astype(jnp.int32),
+            ids,
         )
     )
 
     picked = pick(prompts, responses, orders[0], depth)
     own_y = send(own, ACROSS_Y)
-    first, middle, picked = tie(
-        (send(own, PAIRS), send(own, MIDDLE), picked)
-    )
-    inner, outer, first_y = send(first, MIDDLE), send(middle, OUTWARD), send(first, ACROSS_Y)
-    inner, own_y = tie((inner, own_y))
-    last = send(inner, OUTWARD)
+    first, picked = tie((send(own, PAIRS), picked))
+    third = send(own, OPPOSITE)
+    second = send(third, PAIRS)
+    first_y, third_y = send(first, ACROSS_Y), send(third, ACROSS_Y)
+    first, own_y = tie((first, own_y))
     (emb,) = project(
-        prompts, responses, orders[1], [(own,), (own_y,), (first,)], None, jnp.float32, 2
-    )
-    inner_late, middle_late, emb = tie((inner, middle, emb))
-    inner_y, outer_y = send(inner_late, Y_MIDDLE), send(outer, Y_ENDS)
+        prompts,
+        responses,
+        orders[1],
+        [(own,), (own_y,), (first,), (first_y,)],
+        None,
+        jnp.float32,
+        20,
+    )
+    second, emb = tie((second, emb))
+    second_y = send(second, ACROSS_Y)
     (emb,) = project(
         prompts,
         responses,
         orders[2],
-        [(first_y,), (inner, outer), (inner_y, outer_y), (middle, last)],
+        [(third,), (third_y,), (second,)],
         emb,
         jnp.float32,
         2.4,
     )
-    middle_y, last_y, emb = tie(
-        (send(middle_late, Y_MIDDLE), send(last, Y_ENDS), emb)
-    )
+    second_y, emb = tie((second_y, emb))
     prompt_emb, response_emb = project(
-        prompts, responses, orders[3], [(middle_y, last_y)], emb, jnp.bfloat16, 0.7, positive[None, :]
+        prompts, responses, orders[3], [(second_y,)], emb, jnp.bfloat16, 0.7, positive[None, :]
     )
 
     pieces = []
@@ -615,13 +617,14 @@
     groups = [[block, send(block, ACROSS_C)] for block in (prompt_emb, prompt_far)]
     sibling = send(fetched, ACROSS_C)
     features = slices(prompts, responses, tie((orders[4], response_rows))[0], depth)
+    held = tie(held)
     cross = [send(x, ACROSS_C) for x in beside]
     held, features, cross_tied, fetched = tie((held, features, cross, fetched))
     cross = cross_tied
     features = list(zip(features[:6], features[6:]))
     groups = [[*group, x, across] for group, x, across in zip(groups, beside, cross)]
     losses, mine, away, *parts = compare(
-        groups, held, positive[None, :], starts, row_count, LINE
+        groups, held, positive[None, :], ids, row_count, LINE
     )
 
     back = [send(part, table) for part, table in zip(parts[1:], (PAIRS, PAIRS_Y, ACROSS_Y))]

time: 118 us -> 116 us (0.983)
  waiting for transfers between devices: 45.2 us -> 42 us
  starting transfers between devices: 53.6 us -> 55.1 us
    ppermute x46 -> x42, waiting for transfers between devices: 45.2 us -> 42 us  [send(): return lax.ppermute(block, ('dp', 'mp'), table)]
    ppermute x46 -> x42, starting transfers between devices: 53.6 us -> 55.1 us  [send(): return lax.ppermute(block, ('dp', 'mp'), table)]
  transfers between devices with their start and end apart: 46 -> 42, of which waited for: 20 -> 19; matrix products, arithmetic and copies ran while one was open for 1% -> 1% of each run, Pallas kernels for 8% -> 8%
where the time goes in v11:
time: 116 us; the launch traced here: 115 us
  starting transfers between devices  55.1 us (48%)
  waiting for transfers between devices  42 us (36%)
  Pallas kernels  12.7 us (11%)
  local copies, waits for them, and re-layouts  3.5 us (3%)
    ppermute x42, starting transfers between devices, send(): return lax.ppermute(block, ('dp', 'mp'), table)  55.1 us
    ppermute x42, waiting for transfers between devices, send(): return lax.ppermute(block, ('dp', 'mp'), table)  42 us
    pallas_call x3, Pallas kernels, project(): pl.pallas_call(kernel, in_specs=[pl.BlockSpec(memory_space=pltpu.SMEM)] +...  5.03 us
    pallas_call x9, Pallas kernels, in_vmem(): pl.pallas_call(kernel, in_specs=[inside] * len(operands), out_specs=[insi...  3.93 us
    unnamed x12, local copies, waits for them, and re-layouts  3.2 us
  transfers between devices with their start and end apart: 42, of which 19 were waited for; matrix products, arithmetic and copies ran while one was open for 1% of the time, Pallas kernels for 8%

profile of v11, /device:TPU:0, one launch (start us, length us, event | category | flops | bytes accessed | tf_op | source)
XLA Modules:
  0.0 115.2 jit_solution(10323695976231804207)
XLA Ops:
  1.3 3.1 %collective-permute-start.2 = (bf16[512,256]{1,0:T(8,128)(2,1)}, bf16[512,256]{1,0:T(8,128)(2,1)S(1)}, u32[]{:S(2)}, u32[]{:S(2)}) collective-permute-start(bf16[512,256]{1,0:T(8,128)(2,1)} %refs_2_), channel_id=1, source_target_pairs={{0,8},{1,9},{2,10},{3,11},{4,12},{5,13},{6,14},{7,15},{8,0},{9,1},... | collective-permute-start | bytes 786440 | tf_op jit(solution)/shard_map/ppermute | solution.py:106
  5.9 2.5 %collective-permute-start = (bf16[512,256]{1,0:T(8,128)(2,1)}, bf16[512,256]{1,0:T(8,128)(2,1)S(1)}, u32[]{:S(2)}, u32[]{:S(2)}) collective-permute-start(bf16[512,256]{1,0:T(8,128)(2,1)} %refs_2_), channel_id=1, source_target_pairs={{0,24},{1,25},{2,26},{3,27},{4,28},{5,29},{6,30},{7,31},{8,16},{9,... | collective-permute-start | bytes 786440 | tf_op jit(solution)/shard_map/ppermute | solution.py:106
  13.0 5.9 %collective-permute-done.refs_2_ = bf16[512,256]{1,0:T(8,128)(2,1)S(1)} collective-permute-done((bf16[512,256]{1,0:T(8,128)(2,1)}, bf16[512,256]{1,0:T(8,128)(2,1)S(1)}, u32[]{:S(2)}, u32[]{:S(2)}) %collective-permute-start) | collective-permute-done | bytes 262176 | tf_op jit(solution)/shard_map/ppermute | solution.py:106
  18.8 1.8 %collective-permute-start.1 = (bf16[512,256]{1,0:T(8,128)(2,1)S(1)}, bf16[512,256]{1,0:T(8,128)(2,1)S(1)}, u32[]{:S(2)}, u32[]{:S(2)}) collective-permute-start(bf16[512,256]{1,0:T(8,128)(2,1)S(1)} %collective-permute-done.refs_2_), channel_id=1, source_target_pairs={{0,8},{1,9},{2,10},{3,11},{4,12},{5,13},{6,14},{7,15},{8,0},{9,1},... | collective-permute-start | bytes 786440 | tf_op jit(solution)/shard_map/ppermute | solution.py:106
  21.2 2.4 %shard_map.60.refs_5_ = f32[512,256]{1,0:T(8,128)S(1)} custom-call(s32[4]{0:T(128)S(1)} %get-tuple-element.112.block_ref, bf16[256,4096]{1,0:T(8,128)(2,1)S(1)} %copy-done.1, bf16[256,4096]{1,0:T(8,128)(2,1)S(1)} %copy-done.3, bf16[512,256]{1,0:T(8,128)(2,1)S(1)} %copy-done.5, bf16[512,256]{1,0:T(8,128)(2,1)S(1)} %collective-permute-done.3.refs_3_, ...), custom_call_target="tpu_custom_call" | custom-call | flops 20000000000 | tf_op jit(solution)/shard_map/pallas_call | solution.py:279
  23.6 2.3 %collective-permute-done.1.refs_4_ = bf16[512,256]{1,0:T(8,128)(2,1)S(1)} collective-permute-done((bf16[512,256]{1,0:T(8,128)(2,1)S(1)}, bf16[512,256]{1,0:T(8,128)(2,1)S(1)}, u32[]{:S(2)}, u32[]{:S(2)}) %collective-permute-start.1) | collective-permute-done | bytes 262176 | tf_op jit(solution)/shard_map/ppermute | solution.py:106
  27.5 2.0 %shard_map.61.refs_3_ = f32[512,256]{1,0:T(8,128)S(1)} custom-call(s32[3]{0:T(128)S(1)} %pad_add_fusion.2.block_ref, bf16[256,4096]{1,0:T(8,128)(2,1)S(1)} %copy-done.1, bf16[256,4096]{1,0:T(8,128)(2,1)S(1)} %copy-done.3, bf16[512,256]{1,0:T(8,128)(2,1)S(1)} %collective-permute-done.refs_2_, bf16[512,256]{1,0:T(8,128)(2,1)S(1)} %collective-permute-done.6.refs_3_, ...), custom_call_target="tpu_custom_call" | custom-call | flops 2400000000 | tf_op jit(solution)/shard_map/pallas_call | solution.py:279
  29.5 3.2 %collective-permute-done.5.refs_2_ = bf16[512,256]{1,0:T(8,128)(2,1)S(1)} collective-permute-done((bf16[512,256]{1,0:T(8,128)(2,1)S(1)}, bf16[512,256]{1,0:T(8,128)(2,1)S(1)}, u32[]{:S(2)}, u32[]{:S(2)}) %collective-permute-start.5) | collective-permute-done | bytes 262176 | tf_op jit(solution)/shard_map/ppermute | solution.py:106
  38.6 2.5 %collective-permute-start.17 = (bf16[272,256]{1,0:T(8,128)(2,1)S(1)}, bf16[272,256]{1,0:T(8,128)(2,1)S(1)}, u32[]{:S(2)}, u32[]{:S(2)}) collective-permute-start(bf16[272,256]{1,0:T(8,128)(2,1)S(1)} %get-tuple-element.124.refs_0_), channel_id=1, source_target_pairs={{0,18},{1,19},{2,16},{3,17},{4,22},{5,23},{6,20},{7,21},{8,26},{9,... | collective-permute-start | bytes 417800 | tf_op jit(solution)/shard_map/ppermute | solution.py:106
  42.8 4.6 %collective-permute-start.12 = (bf16[64,1024]{1,0:T(8,128)(2,1)S(1)}, bf16[64,1024]{1,0:T(8,128)(2,1)S(1)}, u32[]{:S(2)}, u32[]{:S(2)}) collective-permute-start(bf16[64,1024]{1,0:T(8,128)(2,1)S(1)} %pad_maximum_fusion.refs_0_), channel_id=1, source_target_pairs={{0,8},{1,9},{2,10},{3,11},{4,12},{5,13},{6,14},{7,15},{8,0},{9,1},... | collective-permute-start | bytes 393224 | tf_op jit(solution)/shard_map/ppermute | solution.py:106
  48.9 2.9 %collective-permute-done.17.refs_6_ = bf16[272,256]{1,0:T(8,128)(2,1)S(1)} collective-permute-done((bf16[272,256]{1,0:T(8,128)(2,1)S(1)}, bf16[272,256]{1,0:T(8,128)(2,1)S(1)}, u32[]{:S(2)}, u32[]{:S(2)}) %collective-permute-start.17) | collective-permute-done | bytes 139296 | tf_op jit(solution)/shard_map/ppermute | solution.py:106
  53.2 2.2 %collective-permute-done.13.refs_2_ = bf16[64,1024]{1,0:T(8,128)(2,1)S(1)} collective-permute-done((bf16[64,1024]{1,0:T(8,128)(2,1)S(1)}, bf16[64,1024]{1,0:T(8,128)(2,1)S(1)}, u32[]{:S(2)}, u32[]{:S(2)}) %collective-permute-start.13) | collective-permute-done | bytes 131104 | tf_op jit(solution)/shard_map/ppermute | solution.py:106
  58.5 1.9 %collective-permute-start.23 = (bf16[64,1024]{1,0:T(8,128)(2,1)S(1)}, bf16[64,1024]{1,0:T(8,128)(2,1)S(1)}, u32[]{:S(2)}, u32[]{:S(2)}) collective-permute-start(bf16[64,1024]{1,0:T(8,128)(2,1)S(1)} %get-tuple-element.157), channel_id=1, source_target_pairs={{0,12},{1,13},{2,14},{3,15},{4,8},{5,9},{6,10},{7,11},{8,4},{9,5},... | collective-permute-start | bytes 393224 | tf_op jit(solution)/shard_map/ppermute | solution.py:106
  63.3 4.8 %collective-permute-start.28 = (bf16[272,256]{1,0:T(8,128)(2,1)S(1)}, bf16[272,256]{1,0:T(8,128)(2,1)S(1)}, u32[]{:S(2)}, u32[]{:S(2)}) collective-permute-start(bf16[272,256]{1,0:T(8,128)(2,1)S(1)} %get-tuple-element.163), channel_id=1, source_target_pairs={{0,16},{1,17},{2,18},{3,19},{4,20},{5,21},{6,22},{7,23},{8,24},{9,... | collective-permute-start | bytes 417800 | tf_op jit(solution)/shard_map/ppermute | solution.py:106
  71.6 2.6 %collective-permute-done.26 = bf16[64,256]{1,0:T(8,128)(2,1)S(1)} collective-permute-done((bf16[64,256]{1,0:T(8,128)(2,1)S(1)}, bf16[64,256]{1,0:T(8,128)(2,1)S(1)}, u32[]{:S(2)}, u32[]{:S(2)}) %collective-permute-start.26) | collective-permute-done | bytes 32800 | tf_op jit(solution)/shard_map/ppermute | solution.py:106
  74.6 3.7 %collective-permute-done.28.far_ref = bf16[272,256]{1,0:T(8,128)(2,1)S(1)} collective-permute-done((bf16[272,256]{1,0:T(8,128)(2,1)S(1)}, bf16[272,256]{1,0:T(8,128)(2,1)S(1)}, u32[]{:S(2)}, u32[]{:S(2)}) %collective-permute-start.28) | collective-permute-done | bytes 139296 | tf_op jit(solution)/shard_map/ppermute | solution.py:106
  78.3 2.0 %collective-permute-done.29.far_x_ref = bf16[272,256]{1,0:T(8,128)(2,1)S(1)} collective-permute-done((bf16[272,256]{1,0:T(8,128)(2,1)S(1)}, bf16[272,256]{1,0:T(8,128)(2,1)S(1)}, u32[]{:S(2)}, u32[]{:S(2)}) %collective-permute-start.29) | collective-permute-done | bytes 139296 | tf_op jit(solution)/shard_map/ppermute | solution.py:106
  80.4 1.8 %collective-permute-start.34 = (bf16[256,256]{1,0:T(8,128)(2,1)S(1)}, bf16[256,256]{1,0:T(8,128)(2,1)S(1)}, u32[]{:S(2)}, u32[]{:S(2)}) collective-permute-start(bf16[256,256]{1,0:T(8,128)(2,1)S(1)} %pad_maximum_fusion.1.refs_1_), channel_id=1, source_target_pairs={{0,4},{1,5},{2,6},{3,7},{4,0},{5,1},{6,2},{7,3},{8,12},{9,13},{10,... | collective-permute-start | bytes 393224 | tf_op jit(solution)/shard_map/ppermute | solution.py:106
  87.1 2.5 %collective-permute-done.35.grad_ref = bf16[256,256]{1,0:T(8,128)(2,1)S(1)} collective-permute-done((bf16[256,256]{1,0:T(8,128)(2,1)S(1)}, bf16[256,256]{1,0:T(8,128)(2,1)S(1)}, u32[]{:S(2)}, u32[]{:S(2)}) %collective-permute-start.35) | collective-permute-done | bytes 131104 | tf_op jit(solution)/shard_map/ppermute | solution.py:106
  90.7 3.8 %collective-permute-start.36 = (bf16[256,512]{1,0:T(8,128)(2,1)S(1)}, bf16[256,512]{1,0:T(8,128)(2,1)S(1)}, u32[]{:S(2)}, u32[]{:S(2)}) collective-permute-start(bf16[256,512]{1,0:T(8,128)(2,1)S(1)} %get-tuple-element.206), channel_id=1, source_target_pairs={{0,16},{1,17},{2,18},{3,19},{4,20},{5,21},{6,22},{7,23},{24,8},{25... | collective-permute-start | bytes 786440 | tf_op jit(solution)/shard_map/ppermute | solution.py:106
  98.1 3.2 %collective-permute-done.36.refs_3_ = bf16[256,512]{1,0:T(8,128)(2,1)S(1)} collective-permute-done((bf16[256,512]{1,0:T(8,128)(2,1)S(1)}, bf16[256,512]{1,0:T(8,128)(2,1)S(1)}, u32[]{:S(2)}, u32[]{:S(2)}) %collective-permute-start.36) | collective-permute-done | bytes 262176 | tf_op jit(solution)/shard_map/ppermute | solution.py:106
  101.3 2.8 %collective-permute-done.37.refs_5_ = bf16[256,512]{1,0:T(8,128)(2,1)S(1)} collective-permute-done((bf16[256,512]{1,0:T(8,128)(2,1)S(1)}, bf16[256,512]{1,0:T(8,128)(2,1)S(1)}, u32[]{:S(2)}, u32[]{:S(2)}) %collective-permute-start.37) | collective-permute-done | bytes 262176 | tf_op jit(solution)/shard_map/ppermute | solution.py:106
  104.3 3.5 %collective-permute-start.40 = (bf16[256,512]{1,0:T(8,128)(2,1)S(1)}, bf16[256,512]{1,0:T(8,128)(2,1)S(1)}, u32[]{:S(2)}, u32[]{:S(2)}) collective-permute-start(bf16[256,512]{1,0:T(8,128)(2,1)S(1)} %get-tuple-element.214), channel_id=1, source_target_pairs={{0,8},{1,9},{2,10},{3,11},{4,12},{5,13},{6,14},{7,15},{8,0},{9,1},... | collective-permute-start | bytes 786440 | tf_op jit(solution)/shard_map/ppermute | solution.py:106
  109.0 5.2 %collective-permute-done.40.refs_2_ = bf16[256,512]{1,0:T(8,128)(2,1)S(1)} collective-permute-done((bf16[256,512]{1,0:T(8,128)(2,1)S(1)}, bf16[256,512]{1,0:T(8,128)(2,1)S(1)}, u32[]{:S(2)}, u32[]{:S(2)}) %collective-permute-start.40) | collective-permute-done | bytes 262176 | tf_op jit(solution)/shard_map/ppermute | solution.py:106
  (101 shorter events, 41.0 us)
Async XLA Ops:
  1.3 10.9 %collective-permute-start.2 = (bf16[512,256]{1,0:T(8,128)(2,1)}, bf16[512,256]{1,0:T(8,128)(2,1)S(1)}, u32[]{:S(2)}, u32[]{:S(2)}) collective-permute-start(bf16[512,256]{1,0:T(8,128)(2,1)} %refs_2_), channel_id=1, source_target_pairs={{0,8},{1,9},{2,10},{3,11},{4,12},{5,13},{6,14},{7,15},{8,0},{9,1},... | collective-permute-start | bytes 786440 | tf_op jit(solution)/shard_map/ppermute | solution.py:106
  4.4 8.6 %collective-permute-start.3 = (bf16[512,256]{1,0:T(8,128)(2,1)}, bf16[512,256]{1,0:T(8,128)(2,1)S(1)}, u32[]{:S(2)}, u32[]{:S(2)}) collective-permute-start(bf16[512,256]{1,0:T(8,128)(2,1)} %refs_2_), channel_id=1, source_target_pairs={{0,4},{1,5},{2,6},{3,7},{4,0},{5,1},{6,2},{7,3},{8,12},{9,13},{10,... | collective-permute-start | bytes 786440 | tf_op jit(solution)/shard_map/ppermute | solution.py:106
  5.9 12.9 %collective-permute-start = (bf16[512,256]{1,0:T(8,128)(2,1)}, bf16[512,256]{1,0:T(8,128)(2,1)S(1)}, u32[]{:S(2)}, u32[]{:S(2)}) collective-permute-start(bf16[512,256]{1,0:T(8,128)(2,1)} %refs_2_), channel_id=1, source_target_pairs={{0,24},{1,25},{2,26},{3,27},{4,28},{5,29},{6,30},{7,31},{8,16},{9,... | collective-permute-start | bytes 786440 | tf_op jit(solution)/shard_map/ppermute | solution.py:106
  12.2 9.0 %collective-permute-start.4 = (bf16[512,256]{1,0:T(8,128)(2,1)S(1)}, bf16[512,256]{1,0:T(8,128)(2,1)S(1)}, u32[]{:S(2)}, u32[]{:S(2)}) collective-permute-start(bf16[512,256]{1,0:T(8,128)(2,1)S(1)} %collective-permute-done.2.refs_4_), channel_id=1, source_target_pairs={{0,4},{1,5},{2,6},{3,7},{4,0},{5,1},{6,2},{7,3},{8,12},{9,13},{10,... | collective-permute-start | bytes 786440 | tf_op jit(solution)/shard_map/ppermute | solution.py:106
  33.3 14.0 %collective-permute-start.14 = (bf16[128,1024]{1,0:T(8,128)(2,1)S(1)}, bf16[128,1024]{1,0:T(8,128)(2,1)S(1)}, u32[]{:S(2)}, u32[]{:S(2)}) collective-permute-start(bf16[128,1024]{1,0:T(8,128)(2,1)S(1)} %shard_map.59), channel_id=1, source_target_pairs={{0,4},{1,5},{2,6},{3,7},{4,0},{5,1},{6,2},{7,3},{8,12},{9,13},{10,... | collective-permute-start | bytes 786440 | tf_op jit(solution)/shard_map/ppermute | solution.py:106
  36.8 10.6 %collective-permute-start.8 = (bf16[272,256]{1,0:T(8,128)(2,1)S(1)}, bf16[272,256]{1,0:T(8,128)(2,1)S(1)}, u32[]{:S(2)}, u32[]{:S(2)}) collective-permute-start(bf16[272,256]{1,0:T(8,128)(2,1)S(1)} %get-tuple-element.124.refs_0_), channel_id=1, source_target_pairs={{0,2},{1,3},{2,0},{3,1},{4,6},{5,7},{6,4},{7,5},{8,10},{9,11},{10,... | collective-permute-start | bytes 417800 | tf_op jit(solution)/shard_map/ppermute | solution.py:106
  38.6 13.3 %collective-permute-start.17 = (bf16[272,256]{1,0:T(8,128)(2,1)S(1)}, bf16[272,256]{1,0:T(8,128)(2,1)S(1)}, u32[]{:S(2)}, u32[]{:S(2)}) collective-permute-start(bf16[272,256]{1,0:T(8,128)(2,1)S(1)} %get-tuple-element.124.refs_0_), channel_id=1, source_target_pairs={{0,18},{1,19},{2,16},{3,17},{4,22},{5,23},{6,20},{7,21},{8,26},{9,... | collective-permute-start | bytes 417800 | tf_op jit(solution)/shard_map/ppermute | solution.py:106
  41.1 11.6 %collective-permute-start.19 = (bf16[272,256]{1,0:T(8,128)(2,1)S(1)}, bf16[272,256]{1,0:T(8,128)(2,1)S(1)}, u32[]{:S(2)}, u32[]{:S(2)}) collective-permute-start(bf16[272,256]{1,0:T(8,128)(2,1)S(1)} %get-tuple-element.124.refs_0_), channel_id=1, source_target_pairs={{0,16},{1,17},{2,18},{3,19},{4,20},{5,21},{6,22},{7,23},{8,24},{9,... | collective-permute-start | bytes 417800 | tf_op jit(solution)/shard_map/ppermute | solution.py:106
  42.8 10.2 %collective-permute-start.12 = (bf16[64,1024]{1,0:T(8,128)(2,1)S(1)}, bf16[64,1024]{1,0:T(8,128)(2,1)S(1)}, u32[]{:S(2)}, u32[]{:S(2)}) collective-permute-start(bf16[64,1024]{1,0:T(8,128)(2,1)S(1)} %pad_maximum_fusion.refs_0_), channel_id=1, source_target_pairs={{0,8},{1,9},{2,10},{3,11},{4,12},{5,13},{6,14},{7,15},{8,0},{9,1},... | collective-permute-start | bytes 393224 | tf_op jit(solution)/shard_map/ppermute | solution.py:106
  47.4 8.0 %collective-permute-start.13 = (bf16[64,1024]{1,0:T(8,128)(2,1)S(1)}, bf16[64,1024]{1,0:T(8,128)(2,1)S(1)}, u32[]{:S(2)}, u32[]{:S(2)}) collective-permute-start(bf16[64,1024]{1,0:T(8,128)(2,1)S(1)} %pad_maximum_fusion.refs_0_), channel_id=1, source_target_pairs={{0,12},{1,13},{2,14},{3,15},{4,8},{5,9},{6,10},{7,11},{8,4},{9,5},... | collective-permute-start | bytes 393224 | tf_op jit(solution)/shard_map/ppermute | solution.py:106
  47.4 8.9 %collective-permute-start.15 = (bf16[64,1024]{1,0:T(8,128)(2,1)S(1)}, bf16[64,1024]{1,0:T(8,128)(2,1)S(1)}, u32[]{:S(2)}, u32[]{:S(2)}) collective-permute-start(bf16[64,1024]{1,0:T(8,128)(2,1)S(1)} %pad_maximum_fusion.refs_0_), channel_id=1, source_target_pairs={{0,4},{1,5},{2,6},{3,7},{4,0},{5,1},{6,2},{7,3},{8,12},{9,13},{10,... | collective-permute-start | bytes 393224 | tf_op jit(solution)/shard_map/ppermute | solution.py:106
  58.5 9.6 %collective-permute-start.22 = (bf16[64,1024]{1,0:T(8,128)(2,1)S(1)}, bf16[64,1024]{1,0:T(8,128)(2,1)S(1)}, u32[]{:S(2)}, u32[]{:S(2)}) collective-permute-start(bf16[64,1024]{1,0:T(8,128)(2,1)S(1)} %get-tuple-element.156), channel_id=1, source_target_pairs={{0,8},{1,9},{2,10},{3,11},{4,12},{5,13},{6,14},{7,15},{8,0},{9,1},... | collective-permute-start | bytes 393224 | tf_op jit(solution)/shard_map/ppermute | solution.py:106
  58.5 11.1 %collective-permute-start.23 = (bf16[64,1024]{1,0:T(8,128)(2,1)S(1)}, bf16[64,1024]{1,0:T(8,128)(2,1)S(1)}, u32[]{:S(2)}, u32[]{:S(2)}) collective-permute-start(bf16[64,1024]{1,0:T(8,128)(2,1)S(1)} %get-tuple-element.157), channel_id=1, source_target_pairs={{0,12},{1,13},{2,14},{3,15},{4,8},{5,9},{6,10},{7,11},{8,4},{9,5},... | collective-permute-start | bytes 393224 | tf_op jit(solution)/shard_map/ppermute | solution.py:106
  60.4 9.1 %collective-permute-start.24 = (bf16[64,1024]{1,0:T(8,128)(2,1)S(1)}, bf16[64,1024]{1,0:T(8,128)(2,1)S(1)}, u32[]{:S(2)}, u32[]{:S(2)}) collective-permute-start(bf16[64,1024]{1,0:T(8,128)(2,1)S(1)} %get-tuple-element.158), channel_id=1, source_target_pairs={{0,4},{1,5},{2,6},{3,7},{4,0},{5,1},{6,2},{7,3},{8,12},{9,13},{10,... | collective-permute-start | bytes 393224 | tf_op jit(solution)/shard_map/ppermute | solution.py:106
  62.1 18.2 %collective-permute-start.30 = (bf16[784,256]{1,0:T(8,128)(2,1)S(1)}, bf16[784,256]{1,0:T(8,128)(2,1)S(1)}, u32[]{:S(2)}, u32[]{:S(2)}) collective-permute-start(bf16[784,256]{1,0:T(8,128)(2,1)S(1)} %get-tuple-element.165), channel_id=1, source_target_pairs={{0,2},{1,3},{2,0},{3,1},{4,6},{5,7},{6,4},{7,5},{8,10},{9,11},{10,... | collective-permute-start | bytes 1204232 | tf_op jit(solution)/shard_map/ppermute | solution.py:106
  63.3 15.0 %collective-permute-start.28 = (bf16[272,256]{1,0:T(8,128)(2,1)S(1)}, bf16[272,256]{1,0:T(8,128)(2,1)S(1)}, u32[]{:S(2)}, u32[]{:S(2)}) collective-permute-start(bf16[272,256]{1,0:T(8,128)(2,1)S(1)} %get-tuple-element.163), channel_id=1, source_target_pairs={{0,16},{1,17},{2,18},{3,19},{4,20},{5,21},{6,22},{7,23},{8,24},{9,... | collective-permute-start | bytes 417800 | tf_op jit(solution)/shard_map/ppermute | solution.py:106
  68.1 12.3 %collective-permute-start.29 = (bf16[272,256]{1,0:T(8,128)(2,1)S(1)}, bf16[272,256]{1,0:T(8,128)(2,1)S(1)}, u32[]{:S(2)}, u32[]{:S(2)}) collective-permute-start(bf16[272,256]{1,0:T(8,128)(2,1)S(1)} %get-tuple-element.164), channel_id=1, source_target_pairs={{0,18},{1,19},{2,16},{3,17},{4,22},{5,23},{6,20},{7,21},{8,26},{9,... | collective-permute-start | bytes 417800 | tf_op jit(solution)/shard_map/ppermute | solution.py:106
  74.2 11.3 %collective-permute-start.31 = (bf16[128,1024]{1,0:T(8,128)(2,1)S(1)}, bf16[128,1024]{1,0:T(8,128)(2,1)S(1)}, u32[]{:S(2)}, u32[]{:S(2)}) collective-permute-start(bf16[128,1024]{1,0:T(8,128)(2,1)S(1)} %collective-permute-done.14.fetched_ref.refs_0_), channel_id=1, source_target_pairs={{0,1},{1,0},{2,3},{3,2},{4,5},{5,4},{6,7},{7,6},{8,9},{9,8},{10,11... | collective-permute-start | bytes 786440 | tf_op jit(solution)/shard_map/ppermute | solution.py:106
  83.7 14.4 %collective-permute-start.39 = (bf16[256,512]{1,0:T(8,128)(2,1)S(1)}, bf16[256,512]{1,0:T(8,128)(2,1)S(1)}, u32[]{:S(2)}, u32[]{:S(2)}) collective-permute-start(bf16[256,512]{1,0:T(8,128)(2,1)S(1)} %get-tuple-element.208), channel_id=1, source_target_pairs={{0,4},{1,5},{2,6},{3,7},{4,0},{5,1},{6,2},{7,3},{8,12},{9,13},{10,... | collective-permute-start | bytes 786440 | tf_op jit(solution)/shard_map/ppermute | solution.py:106
  90.7 10.6 %collective-permute-start.36 = (bf16[256,512]{1,0:T(8,128)(2,1)S(1)}, bf16[256,512]{1,0:T(8,128)(2,1)S(1)}, u32[]{:S(2)}, u32[]{:S(2)}) collective-permute-start(bf16[256,512]{1,0:T(8,128)(2,1)S(1)} %get-tuple-element.206), channel_id=1, source_target_pairs={{0,16},{1,17},{2,18},{3,19},{4,20},{5,21},{6,22},{7,23},{24,8},{25... | collective-permute-start | bytes 786440 | tf_op jit(solution)/shard_map/ppermute | solution.py:106
  94.5 9.5 %collective-permute-start.37 = (bf16[256,512]{1,0:T(8,128)(2,1)S(1)}, bf16[256,512]{1,0:T(8,128)(2,1)S(1)}, u32[]{:S(2)}, u32[]{:S(2)}) collective-permute-start(bf16[256,512]{1,0:T(8,128)(2,1)S(1)} %get-tuple-element.207), channel_id=1, source_target_pairs={{0,8},{1,9},{2,10},{3,11},{4,12},{5,13},{6,14},{7,15},{24,16},{25,... | collective-permute-start | bytes 786440 | tf_op jit(solution)/shard_map/ppermute | solution.py:106
  95.9 8.2 %collective-permute-start.38 = (bf16[256,512]{1,0:T(8,128)(2,1)S(1)}, bf16[256,512]{1,0:T(8,128)(2,1)S(1)}, u32[]{:S(2)}, u32[]{:S(2)}) collective-permute-start(bf16[256,512]{1,0:T(8,128)(2,1)S(1)} %get-tuple-element.207), channel_id=1, source_target_pairs={{8,16},{9,17},{10,18},{11,19},{12,20},{13,21},{14,22},{15,23},{16,... | collective-permute-start | bytes 786440 | tf_op jit(solution)/shard_map/ppermute | solution.py:106
  96.5 12.4 %collective-permute-start.33 = (bf16[256,512]{1,0:T(8,128)(2,1)S(1)}, bf16[256,512]{1,0:T(8,128)(2,1)S(1)}, u32[]{:S(2)}, u32[]{:S(2)}) collective-permute-start(bf16[256,512]{1,0:T(8,128)(2,1)S(1)} %get-tuple-element.198), channel_id=1, source_target_pairs={{0,4},{1,5},{2,6},{3,7},{4,0},{5,1},{6,2},{7,3},{8,12},{9,13},{10,... | collective-permute-start | bytes 786440 | tf_op jit(solution)/shard_map/ppermute | solution.py:106
  104.3 10.0 %collective-permute-start.40 = (bf16[256,512]{1,0:T(8,128)(2,1)S(1)}, bf16[256,512]{1,0:T(8,128)(2,1)S(1)}, u32[]{:S(2)}, u32[]{:S(2)}) collective-permute-start(bf16[256,512]{1,0:T(8,128)(2,1)S(1)} %get-tuple-element.214), channel_id=1, source_target_pairs={{0,8},{1,9},{2,10},{3,11},{4,12},{5,13},{6,14},{7,15},{8,0},{9,1},... | collective-permute-start | bytes 786440 | tf_op jit(solution)/shard_map/ppermute | solution.py:106
  (24 other events, 128.5 us)

commit v12 on v11

--- a/solution.py
+++ b/solution.py
@@ -121,13 +121,8 @@
 
 
 def line_reduce(own, first, second, third, second_b, third_b, own_y, first_y):
-    jumped, inward, across, first_y = lax.optimization_barrier(
-        (
-            send(third_b, TWO_IN),
-            send(second_b, INWARD),
-            send(second_b, MIDDLE),
-            first_y,
-        )
+    inward, jumped, across, first_y = lax.optimization_barrier(
+        (send(second_b, INWARD), send(third_b, TWO_IN), send(second_b, MIDDLE), first_y)
     )
     paired, last = second_round((first, first_y, across, jumped), (third, inward))
     return own, own_y, send(paired, PAIRS), send(last, MIDDLE)
@@ -291,6 +286,28 @@
         compiler_params=pltpu.CompilerParams(vmem_limit_bytes=12 * 1024 * 1024),
         cost_estimate=cost(time),
     )(blocks, prompts, responses, *operands)
+
+
+def finish(features, weight, total, wanted):
+    (rows, _), width = features[0].shape, weight.shape[1]
+
+    def kernel(prompt_ref, response_ref, weight_ref, total_ref, wanted_ref, out_ref, other_ref):
+        block = weight_ref[...]
+        prompt_part = total_ref[:rows] + matmul(prompt_ref[...], block)
+        out_ref[:rows] = prompt_part.astype(jnp.bfloat16)
+        response_part = total_ref[rows:] + matmul(response_ref[...], block)
+        other_ref[...] = response_part.astype(jnp.bfloat16)
+        high = wanted_ref[...] >> DIGIT_BITS
+        low = wanted_ref[...] - (high << DIGIT_BITS)
+        digits = [high.astype(jnp.float32), low.astype(jnp.float32)]
+        digits.append(jnp.zeros((TAIL - 2, wanted_ref.shape[1]), jnp.float32))
+        out_ref[rows:] = jnp.concatenate(digits, axis=0).astype(jnp.bfloat16)
+
+    results = [
+        jax.ShapeDtypeStruct((rows + TAIL, width), jnp.bfloat16),
+        jax.ShapeDtypeStruct((rows, width), jnp.bfloat16),
+    ]
+    return in_vmem(kernel, results, *features, weight, total, wanted, time=0.7)
 
 
 def pick(prompts, responses, order, depth):
@@ -596,10 +613,9 @@
         jnp.float32,
         2.4,
     )
-    second_y, emb = tie((second_y, emb))
-    prompt_emb, response_emb = project(
-        prompts, responses, orders[3], [(second_y,)], emb, jnp.bfloat16, 0.7, positive[None, :]
-    )
+    features = slices(prompts, responses, tie((orders[3], second))[0], depth)
+    second_y, emb, features = tie((second_y, emb, features))
+    prompt_emb, response_emb = finish(features, second_y, emb, positive[None, :])
 
     pieces = []
     for k in range(SIDE * CORES):

time: 116 us -> 116 us (level)
  waiting for transfers between devices: 42 us -> 39.7 us
  starting transfers between devices: 55.1 us -> 56.9 us
    ppermute x42, waiting for transfers between devices: 42 us -> 39.7 us  [send(): return lax.ppermute(block, ('dp', 'mp'), table)]
    ppermute x42, starting transfers between devices: 55.1 us -> 56.9 us  [send(): return lax.ppermute(block, ('dp', 'mp'), table)]
    pallas_call x3 -> x2, Pallas kernels: 5.03 us -> 4.39 us  [project(): pl.pallas_call(kernel, in_specs=[pl.BlockSpec(memory_space=pltpu.SMEM)] +...]
    pallas_call x9 -> x10, Pallas kernels: 3.93 us -> 4.23 us  [in_vmem(): pl.pallas_call(kernel, in_specs=[inside] * len(operands), out_specs=[insi...]
  transfers between devices with their start and end apart: 42 -> 42, of which waited for: 19 -> 18; matrix products, arithmetic and copies ran while one was open for 1% -> 1% of each run, Pallas kernels for 8% -> 8%
where the time goes in v12:
time: 116 us; the launch traced here: 114 us
  starting transfers between devices  56.9 us (49%)
  waiting for transfers between devices  39.7 us (34%)
  Pallas kernels  12.4 us (11%)
  local copies, waits for them, and re-layouts  3.5 us (3%)
    ppermute x42, starting transfers between devices, send(): return lax.ppermute(block, ('dp', 'mp'), table)  56.9 us
    ppermute x42, waiting for transfers between devices, send(): return lax.ppermute(block, ('dp', 'mp'), table)  39.7 us
    pallas_call x2, Pallas kernels, project(): pl.pallas_call(kernel, in_specs=[pl.BlockSpec(memory_space=pltpu.SMEM)] +...  4.39 us
    pallas_call x10, Pallas kernels, in_vmem(): pl.pallas_call(kernel, in_specs=[inside] * len(operands), out_specs=[insi...  4.23 us
    unnamed x12, local copies, waits for them, and re-layouts  3.2 us
  transfers between devices with their start and end apart: 42, of which 18 were waited for; matrix products, arithmetic and copies ran while one was open for 1% of the time, Pallas kernels for 8%

profile of v12, /device:TPU:0, one launch (start us, length us, event | category | flops | bytes accessed | tf_op | source)
XLA Modules:
  0.0 114.5 jit_solution(8638703118853317206)
XLA Ops:
  1.3 3.1 %collective-permute-start.2 = (bf16[512,256]{1,0:T(8,128)(2,1)}, bf16[512,256]{1,0:T(8,128)(2,1)S(1)}, u32[]{:S(2)}, u32[]{:S(2)}) collective-permute-start(bf16[512,256]{1,0:T(8,128)(2,1)} %refs_2_), channel_id=1, source_target_pairs={{0,8},{1,9},{2,10},{3,11},{4,12},{5,13},{6,14},{7,15},{8,0},{9,1},... | collective-permute-start | bytes 786440 | tf_op jit(solution)/shard_map/ppermute | solution.py:106
  5.9 2.5 %collective-permute-start = (bf16[512,256]{1,0:T(8,128)(2,1)}, bf16[512,256]{1,0:T(8,128)(2,1)S(1)}, u32[]{:S(2)}, u32[]{:S(2)}) collective-permute-start(bf16[512,256]{1,0:T(8,128)(2,1)} %refs_2_), channel_id=1, source_target_pairs={{0,24},{1,25},{2,26},{3,27},{4,28},{5,29},{6,30},{7,31},{8,16},{9,... | collective-permute-start | bytes 786440 | tf_op jit(solution)/shard_map/ppermute | solution.py:106
  13.0 5.9 %collective-permute-done.refs_2_ = bf16[512,256]{1,0:T(8,128)(2,1)S(1)} collective-permute-done((bf16[512,256]{1,0:T(8,128)(2,1)}, bf16[512,256]{1,0:T(8,128)(2,1)S(1)}, u32[]{:S(2)}, u32[]{:S(2)}) %collective-permute-start) | collective-permute-done | bytes 262176 | tf_op jit(solution)/shard_map/ppermute | solution.py:106
  18.8 1.8 %collective-permute-start.1 = (bf16[512,256]{1,0:T(8,128)(2,1)S(1)}, bf16[512,256]{1,0:T(8,128)(2,1)S(1)}, u32[]{:S(2)}, u32[]{:S(2)}) collective-permute-start(bf16[512,256]{1,0:T(8,128)(2,1)S(1)} %collective-permute-done.refs_2_), channel_id=1, source_target_pairs={{0,8},{1,9},{2,10},{3,11},{4,12},{5,13},{6,14},{7,15},{8,0},{9,1},... | collective-permute-start | bytes 786440 | tf_op jit(solution)/shard_map/ppermute | solution.py:106
  21.2 2.4 %shard_map.60.refs_5_ = f32[512,256]{1,0:T(8,128)S(1)} custom-call(s32[4]{0:T(128)S(1)} %get-tuple-element.116.block_ref, bf16[256,4096]{1,0:T(8,128)(2,1)S(1)} %copy-done.1, bf16[256,4096]{1,0:T(8,128)(2,1)S(1)} %copy-done.3, bf16[512,256]{1,0:T(8,128)(2,1)S(1)} %copy-done.4, bf16[512,256]{1,0:T(8,128)(2,1)S(1)} %collective-permute-done.3.refs_3_, ...), custom_call_target="tpu_custom_call" | custom-call | flops 20000000000 | tf_op jit(solution)/shard_map/pallas_call | solution.py:274
  23.6 2.3 %collective-permute-done.1.refs_4_ = bf16[512,256]{1,0:T(8,128)(2,1)S(1)} collective-permute-done((bf16[512,256]{1,0:T(8,128)(2,1)S(1)}, bf16[512,256]{1,0:T(8,128)(2,1)S(1)}, u32[]{:S(2)}, u32[]{:S(2)}) %collective-permute-start.1) | collective-permute-done | bytes 262176 | tf_op jit(solution)/shard_map/ppermute | solution.py:106
  27.6 2.0 %shard_map.61.total_ref = f32[512,256]{1,0:T(8,128)S(1)} custom-call(s32[3]{0:T(128)S(1)} %pad_add_fusion.2.block_ref, bf16[256,4096]{1,0:T(8,128)(2,1)S(1)} %copy-done.1, bf16[256,4096]{1,0:T(8,128)(2,1)S(1)} %copy-done.3, bf16[512,256]{1,0:T(8,128)(2,1)S(1)} %collective-permute-done.refs_2_, bf16[512,256]{1,0:T(8,128)(2,1)S(1)} %collective-permute-done.6.refs_3_, ...), custom_call_target="tpu_custom_call" | custom-call | flops 2400000000 | tf_op jit(solution)/shard_map/pallas_call | solution.py:274
  29.6 3.1 %collective-permute-done.5.weight_ref = bf16[512,256]{1,0:T(8,128)(2,1)S(1)} collective-permute-done((bf16[512,256]{1,0:T(8,128)(2,1)S(1)}, bf16[512,256]{1,0:T(8,128)(2,1)S(1)}, u32[]{:S(2)}, u32[]{:S(2)}) %collective-permute-start.5) | collective-permute-done | bytes 262176 | tf_op jit(solution)/shard_map/ppermute | solution.py:106
  38.4 2.5 %collective-permute-start.17 = (bf16[272,256]{1,0:T(8,128)(2,1)S(1)}, bf16[272,256]{1,0:T(8,128)(2,1)S(1)}, u32[]{:S(2)}, u32[]{:S(2)}) collective-permute-start(bf16[272,256]{1,0:T(8,128)(2,1)S(1)} %get-tuple-element.134.refs_0_), channel_id=1, source_target_pairs={{0,18},{1,19},{2,16},{3,17},{4,22},{5,23},{6,20},{7,21},{8,26},{9,... | collective-permute-start | bytes 417800 | tf_op jit(solution)/shard_map/ppermute | solution.py:106
  42.6 4.8 %collective-permute-start.12 = (bf16[64,1024]{1,0:T(8,128)(2,1)S(1)}, bf16[64,1024]{1,0:T(8,128)(2,1)S(1)}, u32[]{:S(2)}, u32[]{:S(2)}) collective-permute-start(bf16[64,1024]{1,0:T(8,128)(2,1)S(1)} %pad_maximum_fusion.refs_0_), channel_id=1, source_target_pairs={{0,8},{1,9},{2,10},{3,11},{4,12},{5,13},{6,14},{7,15},{8,0},{9,1},... | collective-permute-start | bytes 393224 | tf_op jit(solution)/shard_map/ppermute | solution.py:106
  48.9 3.3 %collective-permute-done.19.refs_4_ = bf16[272,256]{1,0:T(8,128)(2,1)S(1)} collective-permute-done((bf16[272,256]{1,0:T(8,128)(2,1)S(1)}, bf16[272,256]{1,0:T(8,128)(2,1)S(1)}, u32[]{:S(2)}, u32[]{:S(2)}) %collective-permute-start.19) | collective-permute-done | bytes 139296 | tf_op jit(solution)/shard_map/ppermute | solution.py:106
  52.8 2.6 %collective-permute-done.13.refs_2_ = bf16[64,1024]{1,0:T(8,128)(2,1)S(1)} collective-permute-done((bf16[64,1024]{1,0:T(8,128)(2,1)S(1)}, bf16[64,1024]{1,0:T(8,128)(2,1)S(1)}, u32[]{:S(2)}, u32[]{:S(2)}) %collective-permute-start.13) | collective-permute-done | bytes 131104 | tf_op jit(solution)/shard_map/ppermute | solution.py:106
  63.0 4.9 %collective-permute-start.28 = (bf16[272,256]{1,0:T(8,128)(2,1)S(1)}, bf16[272,256]{1,0:T(8,128)(2,1)S(1)}, u32[]{:S(2)}, u32[]{:S(2)}) collective-permute-start(bf16[272,256]{1,0:T(8,128)(2,1)S(1)} %get-tuple-element.173), channel_id=1, source_target_pairs={{0,16},{1,17},{2,18},{3,19},{4,20},{5,21},{6,22},{7,23},{8,24},{9,... | collective-permute-start | bytes 417800 | tf_op jit(solution)/shard_map/ppermute | solution.py:106
  67.9 1.9 %collective-permute-start.29 = (bf16[272,256]{1,0:T(8,128)(2,1)S(1)}, bf16[272,256]{1,0:T(8,128)(2,1)S(1)}, u32[]{:S(2)}, u32[]{:S(2)}) collective-permute-start(bf16[272,256]{1,0:T(8,128)(2,1)S(1)} %get-tuple-element.174), channel_id=1, source_target_pairs={{0,18},{1,19},{2,16},{3,17},{4,22},{5,23},{6,20},{7,21},{8,26},{9,... | collective-permute-start | bytes 417800 | tf_op jit(solution)/shard_map/ppermute | solution.py:106
  71.8 2.4 %collective-permute-done.26 = bf16[64,256]{1,0:T(8,128)(2,1)S(1)} collective-permute-done((bf16[64,256]{1,0:T(8,128)(2,1)S(1)}, bf16[64,256]{1,0:T(8,128)(2,1)S(1)}, u32[]{:S(2)}, u32[]{:S(2)}) %collective-permute-start.26) | collective-permute-done | bytes 32800 | tf_op jit(solution)/shard_map/ppermute | solution.py:106
  74.6 3.4 %collective-permute-done.28.far_ref = bf16[272,256]{1,0:T(8,128)(2,1)S(1)} collective-permute-done((bf16[272,256]{1,0:T(8,128)(2,1)S(1)}, bf16[272,256]{1,0:T(8,128)(2,1)S(1)}, u32[]{:S(2)}, u32[]{:S(2)}) %collective-permute-start.28) | collective-permute-done | bytes 139296 | tf_op jit(solution)/shard_map/ppermute | solution.py:106
  78.0 2.3 %collective-permute-done.29.far_x_ref = bf16[272,256]{1,0:T(8,128)(2,1)S(1)} collective-permute-done((bf16[272,256]{1,0:T(8,128)(2,1)S(1)}, bf16[272,256]{1,0:T(8,128)(2,1)S(1)}, u32[]{:S(2)}, u32[]{:S(2)}) %collective-permute-start.29) | collective-permute-done | bytes 139296 | tf_op jit(solution)/shard_map/ppermute | solution.py:106
  87.0 2.5 %collective-permute-done.35.grad_ref = bf16[256,256]{1,0:T(8,128)(2,1)S(1)} collective-permute-done((bf16[256,256]{1,0:T(8,128)(2,1)S(1)}, bf16[256,256]{1,0:T(8,128)(2,1)S(1)}, u32[]{:S(2)}, u32[]{:S(2)}) %collective-permute-start.35) | collective-permute-done | bytes 131104 | tf_op jit(solution)/shard_map/ppermute | solution.py:106
  90.6 2.6 %collective-permute-start.36 = (bf16[256,512]{1,0:T(8,128)(2,1)S(1)}, bf16[256,512]{1,0:T(8,128)(2,1)S(1)}, u32[]{:S(2)}, u32[]{:S(2)}) collective-permute-start(bf16[256,512]{1,0:T(8,128)(2,1)S(1)} %get-tuple-element.216), channel_id=1, source_target_pairs={{0,8},{1,9},{2,10},{3,11},{4,12},{5,13},{6,14},{7,15},{24,16},{25,... | collective-permute-start | bytes 786440 | tf_op jit(solution)/shard_map/ppermute | solution.py:106
  93.2 2.5 %collective-permute-start.37 = (bf16[256,512]{1,0:T(8,128)(2,1)S(1)}, bf16[256,512]{1,0:T(8,128)(2,1)S(1)}, u32[]{:S(2)}, u32[]{:S(2)}) collective-permute-start(bf16[256,512]{1,0:T(8,128)(2,1)S(1)} %get-tuple-element.217), channel_id=1, source_target_pairs={{0,16},{1,17},{2,18},{3,19},{4,20},{5,21},{6,22},{7,23},{24,8},{25... | collective-permute-start | bytes 786440 | tf_op jit(solution)/shard_map/ppermute | solution.py:106
  97.9 2.0 %collective-permute-done.36.refs_5_ = bf16[256,512]{1,0:T(8,128)(2,1)S(1)} collective-permute-done((bf16[256,512]{1,0:T(8,128)(2,1)S(1)}, bf16[256,512]{1,0:T(8,128)(2,1)S(1)}, u32[]{:S(2)}, u32[]{:S(2)}) %collective-permute-start.36) | collective-permute-done | bytes 262176 | tf_op jit(solution)/shard_map/ppermute | solution.py:106
  99.9 3.9 %collective-permute-done.37.refs_3_ = bf16[256,512]{1,0:T(8,128)(2,1)S(1)} collective-permute-done((bf16[256,512]{1,0:T(8,128)(2,1)S(1)}, bf16[256,512]{1,0:T(8,128)(2,1)S(1)}, u32[]{:S(2)}, u32[]{:S(2)}) %collective-permute-start.37) | collective-permute-done | bytes 262176 | tf_op jit(solution)/shard_map/ppermute | solution.py:106
  104.0 5.1 %collective-permute-start.40 = (bf16[256,512]{1,0:T(8,128)(2,1)S(1)}, bf16[256,512]{1,0:T(8,128)(2,1)S(1)}, u32[]{:S(2)}, u32[]{:S(2)}) collective-permute-start(bf16[256,512]{1,0:T(8,128)(2,1)S(1)} %get-tuple-element.224), channel_id=1, source_target_pairs={{0,8},{1,9},{2,10},{3,11},{4,12},{5,13},{6,14},{7,15},{8,0},{9,1},... | collective-permute-start | bytes 786440 | tf_op jit(solution)/shard_map/ppermute | solution.py:106
  110.3 3.1 %collective-permute-done.40.refs_2_ = bf16[256,512]{1,0:T(8,128)(2,1)S(1)} collective-permute-done((bf16[256,512]{1,0:T(8,128)(2,1)S(1)}, bf16[256,512]{1,0:T(8,128)(2,1)S(1)}, u32[]{:S(2)}, u32[]{:S(2)}) %collective-permute-start.40) | collective-permute-done | bytes 262176 | tf_op jit(solution)/shard_map/ppermute | solution.py:106
  (102 shorter events, 40.7 us)
Async XLA Ops:
  1.3 10.9 %collective-permute-start.2 = (bf16[512,256]{1,0:T(8,128)(2,1)}, bf16[512,256]{1,0:T(8,128)(2,1)S(1)}, u32[]{:S(2)}, u32[]{:S(2)}) collective-permute-start(bf16[512,256]{1,0:T(8,128)(2,1)} %refs_2_), channel_id=1, source_target_pairs={{0,8},{1,9},{2,10},{3,11},{4,12},{5,13},{6,14},{7,15},{8,0},{9,1},... | collective-permute-start | bytes 786440 | tf_op jit(solution)/shard_map/ppermute | solution.py:106
  4.4 8.6 %collective-permute-start.3 = (bf16[512,256]{1,0:T(8,128)(2,1)}, bf16[512,256]{1,0:T(8,128)(2,1)S(1)}, u32[]{:S(2)}, u32[]{:S(2)}) collective-permute-start(bf16[512,256]{1,0:T(8,128)(2,1)} %refs_2_), channel_id=1, source_target_pairs={{0,4},{1,5},{2,6},{3,7},{4,0},{5,1},{6,2},{7,3},{8,12},{9,13},{10,... | collective-permute-start | bytes 786440 | tf_op jit(solution)/shard_map/ppermute | solution.py:106
  5.9 12.9 %collective-permute-start = (bf16[512,256]{1,0:T(8,128)(2,1)}, bf16[512,256]{1,0:T(8,128)(2,1)S(1)}, u32[]{:S(2)}, u32[]{:S(2)}) collective-permute-start(bf16[512,256]{1,0:T(8,128)(2,1)} %refs_2_), channel_id=1, source_target_pairs={{0,24},{1,25},{2,26},{3,27},{4,28},{5,29},{6,30},{7,31},{8,16},{9,... | collective-permute-start | bytes 786440 | tf_op jit(solution)/shard_map/ppermute | solution.py:106
  12.2 9.0 %collective-permute-start.4 = (bf16[512,256]{1,0:T(8,128)(2,1)S(1)}, bf16[512,256]{1,0:T(8,128)(2,1)S(1)}, u32[]{:S(2)}, u32[]{:S(2)}) collective-permute-start(bf16[512,256]{1,0:T(8,128)(2,1)S(1)} %collective-permute-done.2.refs_4_), channel_id=1, source_target_pairs={{0,4},{1,5},{2,6},{3,7},{4,0},{5,1},{6,2},{7,3},{8,12},{9,13},{10,... | collective-permute-start | bytes 786440 | tf_op jit(solution)/shard_map/ppermute | solution.py:106
  33.0 14.4 %collective-permute-start.14 = (bf16[128,1024]{1,0:T(8,128)(2,1)S(1)}, bf16[128,1024]{1,0:T(8,128)(2,1)S(1)}, u32[]{:S(2)}, u32[]{:S(2)}) collective-permute-start(bf16[128,1024]{1,0:T(8,128)(2,1)S(1)} %shard_map.59), channel_id=1, source_target_pairs={{0,4},{1,5},{2,6},{3,7},{4,0},{5,1},{6,2},{7,3},{8,12},{9,13},{10,... | collective-permute-start | bytes 786440 | tf_op jit(solution)/shard_map/ppermute | solution.py:106
  36.6 10.8 %collective-permute-start.8 = (bf16[272,256]{1,0:T(8,128)(2,1)S(1)}, bf16[272,256]{1,0:T(8,128)(2,1)S(1)}, u32[]{:S(2)}, u32[]{:S(2)}) collective-permute-start(bf16[272,256]{1,0:T(8,128)(2,1)S(1)} %get-tuple-element.134.refs_0_), channel_id=1, source_target_pairs={{0,2},{1,3},{2,0},{3,1},{4,6},{5,7},{6,4},{7,5},{8,10},{9,11},{10,... | collective-permute-start | bytes 417800 | tf_op jit(solution)/shard_map/ppermute | solution.py:106
  38.4 10.5 %collective-permute-start.17 = (bf16[272,256]{1,0:T(8,128)(2,1)S(1)}, bf16[272,256]{1,0:T(8,128)(2,1)S(1)}, u32[]{:S(2)}, u32[]{:S(2)}) collective-permute-start(bf16[272,256]{1,0:T(8,128)(2,1)S(1)} %get-tuple-element.134.refs_0_), channel_id=1, source_target_pairs={{0,18},{1,19},{2,16},{3,17},{4,22},{5,23},{6,20},{7,21},{8,26},{9,... | collective-permute-start | bytes 417800 | tf_op jit(solution)/shard_map/ppermute | solution.py:106
  40.9 11.4 %collective-permute-start.19 = (bf16[272,256]{1,0:T(8,128)(2,1)S(1)}, bf16[272,256]{1,0:T(8,128)(2,1)S(1)}, u32[]{:S(2)}, u32[]{:S(2)}) collective-permute-start(bf16[272,256]{1,0:T(8,128)(2,1)S(1)} %get-tuple-element.134.refs_0_), channel_id=1, source_target_pairs={{0,16},{1,17},{2,18},{3,19},{4,20},{5,21},{6,22},{7,23},{8,24},{9,... | collective-permute-start | bytes 417800 | tf_op jit(solution)/shard_map/ppermute | solution.py:106
  42.6 10.2 %collective-permute-start.12 = (bf16[64,1024]{1,0:T(8,128)(2,1)S(1)}, bf16[64,1024]{1,0:T(8,128)(2,1)S(1)}, u32[]{:S(2)}, u32[]{:S(2)}) collective-permute-start(bf16[64,1024]{1,0:T(8,128)(2,1)S(1)} %pad_maximum_fusion.refs_0_), channel_id=1, source_target_pairs={{0,8},{1,9},{2,10},{3,11},{4,12},{5,13},{6,14},{7,15},{8,0},{9,1},... | collective-permute-start | bytes 393224 | tf_op jit(solution)/shard_map/ppermute | solution.py:106
  47.4 8.0 %collective-permute-start.13 = (bf16[64,1024]{1,0:T(8,128)(2,1)S(1)}, bf16[64,1024]{1,0:T(8,128)(2,1)S(1)}, u32[]{:S(2)}, u32[]{:S(2)}) collective-permute-start(bf16[64,1024]{1,0:T(8,128)(2,1)S(1)} %pad_maximum_fusion.refs_0_), channel_id=1, source_target_pairs={{0,12},{1,13},{2,14},{3,15},{4,8},{5,9},{6,10},{7,11},{8,4},{9,5},... | collective-permute-start | bytes 393224 | tf_op jit(solution)/shard_map/ppermute | solution.py:106
  47.4 8.9 %collective-permute-start.15 = (bf16[64,1024]{1,0:T(8,128)(2,1)S(1)}, bf16[64,1024]{1,0:T(8,128)(2,1)S(1)}, u32[]{:S(2)}, u32[]{:S(2)}) collective-permute-start(bf16[64,1024]{1,0:T(8,128)(2,1)S(1)} %pad_maximum_fusion.refs_0_), channel_id=1, source_target_pairs={{0,4},{1,5},{2,6},{3,7},{4,0},{5,1},{6,2},{7,3},{8,12},{9,13},{10,... | collective-permute-start | bytes 393224 | tf_op jit(solution)/shard_map/ppermute | solution.py:106
  58.5 9.4 %collective-permute-start.22 = (bf16[64,1024]{1,0:T(8,128)(2,1)S(1)}, bf16[64,1024]{1,0:T(8,128)(2,1)S(1)}, u32[]{:S(2)}, u32[]{:S(2)}) collective-permute-start(bf16[64,1024]{1,0:T(8,128)(2,1)S(1)} %get-tuple-element.166), channel_id=1, source_target_pairs={{0,8},{1,9},{2,10},{3,11},{4,12},{5,13},{6,14},{7,15},{8,0},{9,1},... | collective-permute-start | bytes 393224 | tf_op jit(solution)/shard_map/ppermute | solution.py:106
  58.5 11.3 %collective-permute-start.23 = (bf16[64,1024]{1,0:T(8,128)(2,1)S(1)}, bf16[64,1024]{1,0:T(8,128)(2,1)S(1)}, u32[]{:S(2)}, u32[]{:S(2)}) collective-permute-start(bf16[64,1024]{1,0:T(8,128)(2,1)S(1)} %get-tuple-element.167), channel_id=1, source_target_pairs={{0,12},{1,13},{2,14},{3,15},{4,8},{5,9},{6,10},{7,11},{8,4},{9,5},... | collective-permute-start | bytes 393224 | tf_op jit(solution)/shard_map/ppermute | solution.py:106
  60.2 9.5 %collective-permute-start.24 = (bf16[64,1024]{1,0:T(8,128)(2,1)S(1)}, bf16[64,1024]{1,0:T(8,128)(2,1)S(1)}, u32[]{:S(2)}, u32[]{:S(2)}) collective-permute-start(bf16[64,1024]{1,0:T(8,128)(2,1)S(1)} %get-tuple-element.168), channel_id=1, source_target_pairs={{0,4},{1,5},{2,6},{3,7},{4,0},{5,1},{6,2},{7,3},{8,12},{9,13},{10,... | collective-permute-start | bytes 393224 | tf_op jit(solution)/shard_map/ppermute | solution.py:106
  62.1 18.1 %collective-permute-start.30 = (bf16[784,256]{1,0:T(8,128)(2,1)S(1)}, bf16[784,256]{1,0:T(8,128)(2,1)S(1)}, u32[]{:S(2)}, u32[]{:S(2)}) collective-permute-start(bf16[784,256]{1,0:T(8,128)(2,1)S(1)} %get-tuple-element.175), channel_id=1, source_target_pairs={{0,2},{1,3},{2,0},{3,1},{4,6},{5,7},{6,4},{7,5},{8,10},{9,11},{10,... | collective-permute-start | bytes 1204232 | tf_op jit(solution)/shard_map/ppermute | solution.py:106
  63.0 15.0 %collective-permute-start.28 = (bf16[272,256]{1,0:T(8,128)(2,1)S(1)}, bf16[272,256]{1,0:T(8,128)(2,1)S(1)}, u32[]{:S(2)}, u32[]{:S(2)}) collective-permute-start(bf16[272,256]{1,0:T(8,128)(2,1)S(1)} %get-tuple-element.173), channel_id=1, source_target_pairs={{0,16},{1,17},{2,18},{3,19},{4,20},{5,21},{6,22},{7,23},{8,24},{9,... | collective-permute-start | bytes 417800 | tf_op jit(solution)/shard_map/ppermute | solution.py:106
  67.9 12.4 %collective-permute-start.29 = (bf16[272,256]{1,0:T(8,128)(2,1)S(1)}, bf16[272,256]{1,0:T(8,128)(2,1)S(1)}, u32[]{:S(2)}, u32[]{:S(2)}) collective-permute-start(bf16[272,256]{1,0:T(8,128)(2,1)S(1)} %get-tuple-element.174), channel_id=1, source_target_pairs={{0,18},{1,19},{2,16},{3,17},{4,22},{5,23},{6,20},{7,21},{8,26},{9,... | collective-permute-start | bytes 417800 | tf_op jit(solution)/shard_map/ppermute | solution.py:106
  74.2 11.1 %collective-permute-start.31 = (bf16[128,1024]{1,0:T(8,128)(2,1)S(1)}, bf16[128,1024]{1,0:T(8,128)(2,1)S(1)}, u32[]{:S(2)}, u32[]{:S(2)}) collective-permute-start(bf16[128,1024]{1,0:T(8,128)(2,1)S(1)} %collective-permute-done.14.fetched_ref.refs_0_), channel_id=1, source_target_pairs={{0,1},{1,0},{2,3},{3,2},{4,5},{5,4},{6,7},{7,6},{8,9},{9,8},{10,11... | collective-permute-start | bytes 786440 | tf_op jit(solution)/shard_map/ppermute | solution.py:106
  83.5 14.3 %collective-permute-start.39 = (bf16[256,512]{1,0:T(8,128)(2,1)S(1)}, bf16[256,512]{1,0:T(8,128)(2,1)S(1)}, u32[]{:S(2)}, u32[]{:S(2)}) collective-permute-start(bf16[256,512]{1,0:T(8,128)(2,1)S(1)} %get-tuple-element.218), channel_id=1, source_target_pairs={{0,4},{1,5},{2,6},{3,7},{4,0},{5,1},{6,2},{7,3},{8,12},{9,13},{10,... | collective-permute-start | bytes 786440 | tf_op jit(solution)/shard_map/ppermute | solution.py:106
  90.6 9.3 %collective-permute-start.36 = (bf16[256,512]{1,0:T(8,128)(2,1)S(1)}, bf16[256,512]{1,0:T(8,128)(2,1)S(1)}, u32[]{:S(2)}, u32[]{:S(2)}) collective-permute-start(bf16[256,512]{1,0:T(8,128)(2,1)S(1)} %get-tuple-element.216), channel_id=1, source_target_pairs={{0,8},{1,9},{2,10},{3,11},{4,12},{5,13},{6,14},{7,15},{24,16},{25,... | collective-permute-start | bytes 786440 | tf_op jit(solution)/shard_map/ppermute | solution.py:106
  93.2 10.7 %collective-permute-start.37 = (bf16[256,512]{1,0:T(8,128)(2,1)S(1)}, bf16[256,512]{1,0:T(8,128)(2,1)S(1)}, u32[]{:S(2)}, u32[]{:S(2)}) collective-permute-start(bf16[256,512]{1,0:T(8,128)(2,1)S(1)} %get-tuple-element.217), channel_id=1, source_target_pairs={{0,16},{1,17},{2,18},{3,19},{4,20},{5,21},{6,22},{7,23},{24,8},{25... | collective-permute-start | bytes 786440 | tf_op jit(solution)/shard_map/ppermute | solution.py:106
  95.6 8.2 %collective-permute-start.38 = (bf16[256,512]{1,0:T(8,128)(2,1)S(1)}, bf16[256,512]{1,0:T(8,128)(2,1)S(1)}, u32[]{:S(2)}, u32[]{:S(2)}) collective-permute-start(bf16[256,512]{1,0:T(8,128)(2,1)S(1)} %get-tuple-element.216), channel_id=1, source_target_pairs={{8,16},{9,17},{10,18},{11,19},{12,20},{13,21},{14,22},{15,23},{16,... | collective-permute-start | bytes 786440 | tf_op jit(solution)/shard_map/ppermute | solution.py:106
  96.3 14.0 %collective-permute-start.33 = (bf16[256,512]{1,0:T(8,128)(2,1)S(1)}, bf16[256,512]{1,0:T(8,128)(2,1)S(1)}, u32[]{:S(2)}, u32[]{:S(2)}) collective-permute-start(bf16[256,512]{1,0:T(8,128)(2,1)S(1)} %get-tuple-element.208), channel_id=1, source_target_pairs={{0,4},{1,5},{2,6},{3,7},{4,0},{5,1},{6,2},{7,3},{8,12},{9,13},{10,... | collective-permute-start | bytes 786440 | tf_op jit(solution)/shard_map/ppermute | solution.py:106
  104.0 9.4 %collective-permute-start.40 = (bf16[256,512]{1,0:T(8,128)(2,1)S(1)}, bf16[256,512]{1,0:T(8,128)(2,1)S(1)}, u32[]{:S(2)}, u32[]{:S(2)}) collective-permute-start(bf16[256,512]{1,0:T(8,128)(2,1)S(1)} %get-tuple-element.224), channel_id=1, source_target_pairs={{0,8},{1,9},{2,10},{3,11},{4,12},{5,13},{6,14},{7,15},{8,0},{9,1},... | collective-permute-start | bytes 786440 | tf_op jit(solution)/shard_map/ppermute | solution.py:106
  (24 other events, 125.7 us)

commit v13 on v12

--- a/solution.py
+++ b/solution.py
@@ -621,7 +621,7 @@
     for k in range(SIDE * CORES):
         piece = lax.dynamic_slice(response_emb, (places[k], jnp.uint32(0)), (quarter, width))
         pieces.append(piece if k == 0 else send(piece, MIX[k]))
-    prompt_emb, picked = tie((prompt_emb, picked))
+    pieces, picked = tie((pieces, picked))
     fetched = send(picked, ACROSS_Y)
     prompt_far, prompt_far_x = send(prompt_emb, FAR), send(prompt_emb, FAR_X)
     beside = [send(prompt_emb, ACROSS_X), prompt_far_x]

time: 116 us -> 114 us (0.983)
  waiting for transfers between devices: 39.7 us -> 36.5 us
  starting transfers between devices: 56.9 us -> 59 us
    ppermute x42, waiting for transfers between devices: 39.7 us -> 36.5 us  [send(): return lax.ppermute(block, ('dp', 'mp'), table)]
    ppermute x42, starting transfers between devices: 56.9 us -> 59 us  [send(): return lax.ppermute(block, ('dp', 'mp'), table)]
    unnamed x12 -> x15, local copies, waits for them, and re-layouts: 3.2 us -> 3.21 us
  transfers between devices with their start and end apart: 42 -> 42, of which waited for: 18 -> 16; matrix products, arithmetic and copies ran while one was open for 1% -> 1% of each run, Pallas kernels for 8% -> 8%
where the time goes in v13:
time: 114 us; the launch traced here: 113 us
  starting transfers between devices  59 us (52%)
  waiting for transfers between devices  36.5 us (32%)
  Pallas kernels  12.4 us (11%)
  local copies, waits for them, and re-layouts  3.52 us (3%)
    ppermute x42, starting transfers between devices, send(): return lax.ppermute(block, ('dp', 'mp'), table)  59 us
    ppermute x42, waiting for transfers between devices, send(): return lax.ppermute(block, ('dp', 'mp'), table)  36.5 us
    pallas_call x2, Pallas kernels, project(): pl.pallas_call(kernel, in_specs=[pl.BlockSpec(memory_space=pltpu.SMEM)] +...  4.39 us
    pallas_call x10, Pallas kernels, in_vmem(): pl.pallas_call(kernel, in_specs=[inside] * len(operands), out_specs=[insi...  4.23 us
    unnamed x15, local copies, waits for them, and re-layouts  3.21 us
  transfers between devices with their start and end apart: 42, of which 16 were waited for; matrix products, arithmetic and copies ran while one was open for 1% of the time, Pallas kernels for 8%

profile of v13, /device:TPU:0, one launch (start us, length us, event | category | flops | bytes accessed | tf_op | source)
XLA Modules:
  0.0 113.4 jit_solution(16536016997647239115)
XLA Ops:
  1.3 3.1 %collective-permute-start.2 = (bf16[512,256]{1,0:T(8,128)(2,1)}, bf16[512,256]{1,0:T(8,128)(2,1)S(1)}, u32[]{:S(2)}, u32[]{:S(2)}) collective-permute-start(bf16[512,256]{1,0:T(8,128)(2,1)} %refs_2_), channel_id=1, source_target_pairs={{0,8},{1,9},{2,10},{3,11},{4,12},{5,13},{6,14},{7,15},{8,0},{9,1},... | collective-permute-start | bytes 786440 | tf_op jit(solution)/shard_map/ppermute | solution.py:106
  5.9 2.5 %collective-permute-start = (bf16[512,256]{1,0:T(8,128)(2,1)}, bf16[512,256]{1,0:T(8,128)(2,1)S(1)}, u32[]{:S(2)}, u32[]{:S(2)}) collective-permute-start(bf16[512,256]{1,0:T(8,128)(2,1)} %refs_2_), channel_id=1, source_target_pairs={{0,24},{1,25},{2,26},{3,27},{4,28},{5,29},{6,30},{7,31},{8,16},{9,... | collective-permute-start | bytes 786440 | tf_op jit(solution)/shard_map/ppermute | solution.py:106
  13.0 5.9 %collective-permute-done.refs_2_ = bf16[512,256]{1,0:T(8,128)(2,1)S(1)} collective-permute-done((bf16[512,256]{1,0:T(8,128)(2,1)}, bf16[512,256]{1,0:T(8,128)(2,1)S(1)}, u32[]{:S(2)}, u32[]{:S(2)}) %collective-permute-start) | collective-permute-done | bytes 262176 | tf_op jit(solution)/shard_map/ppermute | solution.py:106
  18.8 1.8 %collective-permute-start.1 = (bf16[512,256]{1,0:T(8,128)(2,1)S(1)}, bf16[512,256]{1,0:T(8,128)(2,1)S(1)}, u32[]{:S(2)}, u32[]{:S(2)}) collective-permute-start(bf16[512,256]{1,0:T(8,128)(2,1)S(1)} %collective-permute-done.refs_2_), channel_id=1, source_target_pairs={{0,8},{1,9},{2,10},{3,11},{4,12},{5,13},{6,14},{7,15},{8,0},{9,1},... | collective-permute-start | bytes 786440 | tf_op jit(solution)/shard_map/ppermute | solution.py:106
  21.2 2.4 %shard_map.60.refs_5_ = f32[512,256]{1,0:T(8,128)S(1)} custom-call(s32[4]{0:T(128)S(1)} %get-tuple-element.119.block_ref, bf16[256,4096]{1,0:T(8,128)(2,1)S(1)} %copy-done.1, bf16[256,4096]{1,0:T(8,128)(2,1)S(1)} %copy-done.3, bf16[512,256]{1,0:T(8,128)(2,1)S(1)} %copy-done.4, bf16[512,256]{1,0:T(8,128)(2,1)S(1)} %collective-permute-done.3.refs_3_, ...), custom_call_target="tpu_custom_call" | custom-call | flops 20000000000 | tf_op jit(solution)/shard_map/pallas_call | solution.py:274
  23.6 2.3 %collective-permute-done.1.refs_4_ = bf16[512,256]{1,0:T(8,128)(2,1)S(1)} collective-permute-done((bf16[512,256]{1,0:T(8,128)(2,1)S(1)}, bf16[512,256]{1,0:T(8,128)(2,1)S(1)}, u32[]{:S(2)}, u32[]{:S(2)}) %collective-permute-start.1) | collective-permute-done | bytes 262176 | tf_op jit(solution)/shard_map/ppermute | solution.py:106
  27.6 2.0 %shard_map.61.total_ref = f32[512,256]{1,0:T(8,128)S(1)} custom-call(s32[3]{0:T(128)S(1)} %pad_add_fusion.2.block_ref, bf16[256,4096]{1,0:T(8,128)(2,1)S(1)} %copy-done.1, bf16[256,4096]{1,0:T(8,128)(2,1)S(1)} %copy-done.3, bf16[512,256]{1,0:T(8,128)(2,1)S(1)} %collective-permute-done.refs_2_, bf16[512,256]{1,0:T(8,128)(2,1)S(1)} %collective-permute-done.6.refs_3_, ...), custom_call_target="tpu_custom_call" | custom-call | flops 2400000000 | tf_op jit(solution)/shard_map/pallas_call | solution.py:274
  29.6 3.1 %collective-permute-done.5.weight_ref = bf16[512,256]{1,0:T(8,128)(2,1)S(1)} collective-permute-done((bf16[512,256]{1,0:T(8,128)(2,1)S(1)}, bf16[512,256]{1,0:T(8,128)(2,1)S(1)}, u32[]{:S(2)}, u32[]{:S(2)}) %collective-permute-start.5) | collective-permute-done | bytes 262176 | tf_op jit(solution)/shard_map/ppermute | solution.py:106
  36.7 2.1 %collective-permute-start.17 = (bf16[272,256]{1,0:T(8,128)(2,1)S(1)}, bf16[272,256]{1,0:T(8,128)(2,1)S(1)}, u32[]{:S(2)}, u32[]{:S(2)}) collective-permute-start(bf16[272,256]{1,0:T(8,128)(2,1)S(1)} %get-tuple-element.135.refs_0_), channel_id=1, source_target_pairs={{0,18},{1,19},{2,16},{3,17},{4,22},{5,23},{6,20},{7,21},{8,26},{9,... | collective-permute-start | bytes 417800 | tf_op jit(solution)/shard_map/ppermute | solution.py:106
  40.9 3.9 %collective-permute-start.12 = (bf16[64,1024]{1,0:T(8,128)(2,1)S(1)}, bf16[64,1024]{1,0:T(8,128)(2,1)S(1)}, u32[]{:S(2)}, u32[]{:S(2)}) collective-permute-start(bf16[64,1024]{1,0:T(8,128)(2,1)S(1)} %constant_dynamic-update-slice_fusion.refs_0_), channel_id=1, source_target_pairs={{0,8},{1,9},{2,10},{3,11},{4,12},{5,13},{6,14},{7,15},{8,0},{9,1},... | collective-permute-start | bytes 393224 | tf_op jit(solution)/shard_map/ppermute | solution.py:106
  44.8 2.3 %collective-permute-done.14.fetched_ref.refs_0_ = bf16[128,1024]{1,0:T(8,128)(2,1)S(1)} collective-permute-done((bf16[128,1024]{1,0:T(8,128)(2,1)S(1)}, bf16[128,1024]{1,0:T(8,128)(2,1)S(1)}, u32[]{:S(2)}, u32[]{:S(2)}) %collective-permute-start.14) | collective-permute-done | bytes 262176 | tf_op jit(solution)/shard_map/ppermute | solution.py:106
  47.1 4.5 %collective-permute-start.13 = (bf16[64,1024]{1,0:T(8,128)(2,1)S(1)}, bf16[64,1024]{1,0:T(8,128)(2,1)S(1)}, u32[]{:S(2)}, u32[]{:S(2)}) collective-permute-start(bf16[64,1024]{1,0:T(8,128)(2,1)S(1)} %constant_dynamic-update-slice_fusion.refs_0_), channel_id=1, source_target_pairs={{0,12},{1,13},{2,14},{3,15},{4,8},{5,9},{6,10},{7,11},{8,4},{9,5},... | collective-permute-start | bytes 393224 | tf_op jit(solution)/shard_map/ppermute | solution.py:106
  52.7 2.6 %collective-permute-done.13.refs_2_ = bf16[64,1024]{1,0:T(8,128)(2,1)S(1)} collective-permute-done((bf16[64,1024]{1,0:T(8,128)(2,1)S(1)}, bf16[64,1024]{1,0:T(8,128)(2,1)S(1)}, u32[]{:S(2)}, u32[]{:S(2)}) %collective-permute-start.13) | collective-permute-done | bytes 131104 | tf_op jit(solution)/shard_map/ppermute | solution.py:106
  64.2 2.6 %collective-permute-start.28 = (bf16[272,256]{1,0:T(8,128)(2,1)S(1)}, bf16[272,256]{1,0:T(8,128)(2,1)S(1)}, u32[]{:S(2)}, u32[]{:S(2)}) collective-permute-start(bf16[272,256]{1,0:T(8,128)(2,1)S(1)} %get-tuple-element.179), channel_id=1, source_target_pairs={{0,16},{1,17},{2,18},{3,19},{4,20},{5,21},{6,22},{7,23},{8,24},{9,... | collective-permute-start | bytes 417800 | tf_op jit(solution)/shard_map/ppermute | solution.py:106
  66.8 2.0 %collective-permute-start.29 = (bf16[272,256]{1,0:T(8,128)(2,1)S(1)}, bf16[272,256]{1,0:T(8,128)(2,1)S(1)}, u32[]{:S(2)}, u32[]{:S(2)}) collective-permute-start(bf16[272,256]{1,0:T(8,128)(2,1)S(1)} %get-tuple-element.180), channel_id=1, source_target_pairs={{0,18},{1,19},{2,16},{3,17},{4,22},{5,23},{6,20},{7,21},{8,26},{9,... | collective-permute-start | bytes 417800 | tf_op jit(solution)/shard_map/ppermute | solution.py:106
  69.6 3.3 %collective-permute-start.26 = (bf16[64,256]{1,0:T(8,128)(2,1)S(1)}, bf16[64,256]{1,0:T(8,128)(2,1)S(1)}, u32[]{:S(2)}, u32[]{:S(2)}) collective-permute-start(bf16[64,256]{1,0:T(8,128)(2,1)S(1)} %get-tuple-element.177), channel_id=1, source_target_pairs={{0,2},{1,3},{2,0},{3,1},{4,6},{5,7},{6,4},{7,5},{8,10},{9,11},{10,... | collective-permute-start | bytes 98312 | tf_op jit(solution)/shard_map/ppermute | solution.py:106
  76.9 2.5 %collective-permute-done.29.far_x_ref = bf16[272,256]{1,0:T(8,128)(2,1)S(1)} collective-permute-done((bf16[272,256]{1,0:T(8,128)(2,1)S(1)}, bf16[272,256]{1,0:T(8,128)(2,1)S(1)}, u32[]{:S(2)}, u32[]{:S(2)}) %collective-permute-start.29) | collective-permute-done | bytes 139296 | tf_op jit(solution)/shard_map/ppermute | solution.py:106
  86.2 2.5 %collective-permute-done.35.grad_ref = bf16[256,256]{1,0:T(8,128)(2,1)S(1)} collective-permute-done((bf16[256,256]{1,0:T(8,128)(2,1)S(1)}, bf16[256,256]{1,0:T(8,128)(2,1)S(1)}, u32[]{:S(2)}, u32[]{:S(2)}) %collective-permute-start.35) | collective-permute-done | bytes 131104 | tf_op jit(solution)/shard_map/ppermute | solution.py:106
  89.8 2.3 %collective-permute-start.36 = (bf16[256,512]{1,0:T(8,128)(2,1)S(1)}, bf16[256,512]{1,0:T(8,128)(2,1)S(1)}, u32[]{:S(2)}, u32[]{:S(2)}) collective-permute-start(bf16[256,512]{1,0:T(8,128)(2,1)S(1)} %get-tuple-element.222), channel_id=1, source_target_pairs={{0,8},{1,9},{2,10},{3,11},{4,12},{5,13},{6,14},{7,15},{24,16},{25,... | collective-permute-start | bytes 786440 | tf_op jit(solution)/shard_map/ppermute | solution.py:106
  92.1 2.4 %collective-permute-start.37 = (bf16[256,512]{1,0:T(8,128)(2,1)S(1)}, bf16[256,512]{1,0:T(8,128)(2,1)S(1)}, u32[]{:S(2)}, u32[]{:S(2)}) collective-permute-start(bf16[256,512]{1,0:T(8,128)(2,1)S(1)} %get-tuple-element.223), channel_id=1, source_target_pairs={{0,16},{1,17},{2,18},{3,19},{4,20},{5,21},{6,22},{7,23},{24,8},{25... | collective-permute-start | bytes 786440 | tf_op jit(solution)/shard_map/ppermute | solution.py:106
  96.7 2.1 %collective-permute-done.36.refs_5_ = bf16[256,512]{1,0:T(8,128)(2,1)S(1)} collective-permute-done((bf16[256,512]{1,0:T(8,128)(2,1)S(1)}, bf16[256,512]{1,0:T(8,128)(2,1)S(1)}, u32[]{:S(2)}, u32[]{:S(2)}) %collective-permute-start.36) | collective-permute-done | bytes 262176 | tf_op jit(solution)/shard_map/ppermute | solution.py:106
  98.8 3.9 %collective-permute-done.37.refs_3_ = bf16[256,512]{1,0:T(8,128)(2,1)S(1)} collective-permute-done((bf16[256,512]{1,0:T(8,128)(2,1)S(1)}, bf16[256,512]{1,0:T(8,128)(2,1)S(1)}, u32[]{:S(2)}, u32[]{:S(2)}) %collective-permute-start.37) | collective-permute-done | bytes 262176 | tf_op jit(solution)/shard_map/ppermute | solution.py:106
  102.9 5.1 %collective-permute-start.40 = (bf16[256,512]{1,0:T(8,128)(2,1)S(1)}, bf16[256,512]{1,0:T(8,128)(2,1)S(1)}, u32[]{:S(2)}, u32[]{:S(2)}) collective-permute-start(bf16[256,512]{1,0:T(8,128)(2,1)S(1)} %get-tuple-element.230), channel_id=1, source_target_pairs={{0,8},{1,9},{2,10},{3,11},{4,12},{5,13},{6,14},{7,15},{8,0},{9,1},... | collective-permute-start | bytes 786440 | tf_op jit(solution)/shard_map/ppermute | solution.py:106
  109.2 3.1 %collective-permute-done.40.refs_2_ = bf16[256,512]{1,0:T(8,128)(2,1)S(1)} collective-permute-done((bf16[256,512]{1,0:T(8,128)(2,1)S(1)}, bf16[256,512]{1,0:T(8,128)(2,1)S(1)}, u32[]{:S(2)}, u32[]{:S(2)}) %collective-permute-start.40) | collective-permute-done | bytes 262176 | tf_op jit(solution)/shard_map/ppermute | solution.py:106
  (105 shorter events, 42.0 us)
Async XLA Ops:
  1.3 10.9 %collective-permute-start.2 = (bf16[512,256]{1,0:T(8,128)(2,1)}, bf16[512,256]{1,0:T(8,128)(2,1)S(1)}, u32[]{:S(2)}, u32[]{:S(2)}) collective-permute-start(bf16[512,256]{1,0:T(8,128)(2,1)} %refs_2_), channel_id=1, source_target_pairs={{0,8},{1,9},{2,10},{3,11},{4,12},{5,13},{6,14},{7,15},{8,0},{9,1},... | collective-permute-start | bytes 786440 | tf_op jit(solution)/shard_map/ppermute | solution.py:106
  4.4 8.6 %collective-permute-start.3 = (bf16[512,256]{1,0:T(8,128)(2,1)}, bf16[512,256]{1,0:T(8,128)(2,1)S(1)}, u32[]{:S(2)}, u32[]{:S(2)}) collective-permute-start(bf16[512,256]{1,0:T(8,128)(2,1)} %refs_2_), channel_id=1, source_target_pairs={{0,4},{1,5},{2,6},{3,7},{4,0},{5,1},{6,2},{7,3},{8,12},{9,13},{10,... | collective-permute-start | bytes 786440 | tf_op jit(solution)/shard_map/ppermute | solution.py:106
  5.9 12.9 %collective-permute-start = (bf16[512,256]{1,0:T(8,128)(2,1)}, bf16[512,256]{1,0:T(8,128)(2,1)S(1)}, u32[]{:S(2)}, u32[]{:S(2)}) collective-permute-start(bf16[512,256]{1,0:T(8,128)(2,1)} %refs_2_), channel_id=1, source_target_pairs={{0,24},{1,25},{2,26},{3,27},{4,28},{5,29},{6,30},{7,31},{8,16},{9,... | collective-permute-start | bytes 786440 | tf_op jit(solution)/shard_map/ppermute | solution.py:106
  12.2 9.0 %collective-permute-start.4 = (bf16[512,256]{1,0:T(8,128)(2,1)S(1)}, bf16[512,256]{1,0:T(8,128)(2,1)S(1)}, u32[]{:S(2)}, u32[]{:S(2)}) collective-permute-start(bf16[512,256]{1,0:T(8,128)(2,1)S(1)} %collective-permute-done.2.refs_4_), channel_id=1, source_target_pairs={{0,4},{1,5},{2,6},{3,7},{4,0},{5,1},{6,2},{7,3},{8,12},{9,13},{10,... | collective-permute-start | bytes 786440 | tf_op jit(solution)/shard_map/ppermute | solution.py:106
  35.3 16.3 %collective-permute-start.8 = (bf16[272,256]{1,0:T(8,128)(2,1)S(1)}, bf16[272,256]{1,0:T(8,128)(2,1)S(1)}, u32[]{:S(2)}, u32[]{:S(2)}) collective-permute-start(bf16[272,256]{1,0:T(8,128)(2,1)S(1)} %get-tuple-element.135.refs_0_), channel_id=1, source_target_pairs={{0,2},{1,3},{2,0},{3,1},{4,6},{5,7},{6,4},{7,5},{8,10},{9,11},{10,... | collective-permute-start | bytes 417800 | tf_op jit(solution)/shard_map/ppermute | solution.py:106
  36.7 15.4 %collective-permute-start.17 = (bf16[272,256]{1,0:T(8,128)(2,1)S(1)}, bf16[272,256]{1,0:T(8,128)(2,1)S(1)}, u32[]{:S(2)}, u32[]{:S(2)}) collective-permute-start(bf16[272,256]{1,0:T(8,128)(2,1)S(1)} %get-tuple-element.135.refs_0_), channel_id=1, source_target_pairs={{0,18},{1,19},{2,16},{3,17},{4,22},{5,23},{6,20},{7,21},{8,26},{9,... | collective-permute-start | bytes 417800 | tf_op jit(solution)/shard_map/ppermute | solution.py:106
  38.8 13.3 %collective-permute-start.19 = (bf16[272,256]{1,0:T(8,128)(2,1)S(1)}, bf16[272,256]{1,0:T(8,128)(2,1)S(1)}, u32[]{:S(2)}, u32[]{:S(2)}) collective-permute-start(bf16[272,256]{1,0:T(8,128)(2,1)S(1)} %get-tuple-element.135.refs_0_), channel_id=1, source_target_pairs={{0,16},{1,17},{2,18},{3,19},{4,20},{5,21},{6,22},{7,23},{8,24},{9,... | collective-permute-start | bytes 417800 | tf_op jit(solution)/shard_map/ppermute | solution.py:106
  39.7 7.4 %collective-permute-start.14 = (bf16[128,1024]{1,0:T(8,128)(2,1)S(1)}, bf16[128,1024]{1,0:T(8,128)(2,1)S(1)}, u32[]{:S(2)}, u32[]{:S(2)}) collective-permute-start(bf16[128,1024]{1,0:T(8,128)(2,1)S(1)} %shard_map.59), channel_id=1, source_target_pairs={{0,4},{1,5},{2,6},{3,7},{4,0},{5,1},{6,2},{7,3},{8,12},{9,13},{10,... | collective-permute-start | bytes 786440 | tf_op jit(solution)/shard_map/ppermute | solution.py:106
  40.9 11.7 %collective-permute-start.12 = (bf16[64,1024]{1,0:T(8,128)(2,1)S(1)}, bf16[64,1024]{1,0:T(8,128)(2,1)S(1)}, u32[]{:S(2)}, u32[]{:S(2)}) collective-permute-start(bf16[64,1024]{1,0:T(8,128)(2,1)S(1)} %constant_dynamic-update-slice_fusion.refs_0_), channel_id=1, source_target_pairs={{0,8},{1,9},{2,10},{3,11},{4,12},{5,13},{6,14},{7,15},{8,0},{9,1},... | collective-permute-start | bytes 393224 | tf_op jit(solution)/shard_map/ppermute | solution.py:106
  47.1 8.2 %collective-permute-start.13 = (bf16[64,1024]{1,0:T(8,128)(2,1)S(1)}, bf16[64,1024]{1,0:T(8,128)(2,1)S(1)}, u32[]{:S(2)}, u32[]{:S(2)}) collective-permute-start(bf16[64,1024]{1,0:T(8,128)(2,1)S(1)} %constant_dynamic-update-slice_fusion.refs_0_), channel_id=1, source_target_pairs={{0,12},{1,13},{2,14},{3,15},{4,8},{5,9},{6,10},{7,11},{8,4},{9,5},... | collective-permute-start | bytes 393224 | tf_op jit(solution)/shard_map/ppermute | solution.py:106
  59.3 7.5 %collective-permute-start.22 = (bf16[64,1024]{1,0:T(8,128)(2,1)S(1)}, bf16[64,1024]{1,0:T(8,128)(2,1)S(1)}, u32[]{:S(2)}, u32[]{:S(2)}) collective-permute-start(bf16[64,1024]{1,0:T(8,128)(2,1)S(1)} %get-tuple-element.172), channel_id=1, source_target_pairs={{0,8},{1,9},{2,10},{3,11},{4,12},{5,13},{6,14},{7,15},{8,0},{9,1},... | collective-permute-start | bytes 393224 | tf_op jit(solution)/shard_map/ppermute | solution.py:106
  59.8 9.1 %collective-permute-start.23 = (bf16[64,1024]{1,0:T(8,128)(2,1)S(1)}, bf16[64,1024]{1,0:T(8,128)(2,1)S(1)}, u32[]{:S(2)}, u32[]{:S(2)}) collective-permute-start(bf16[64,1024]{1,0:T(8,128)(2,1)S(1)} %get-tuple-element.173), channel_id=1, source_target_pairs={{0,12},{1,13},{2,14},{3,15},{4,8},{5,9},{6,10},{7,11},{8,4},{9,5},... | collective-permute-start | bytes 393224 | tf_op jit(solution)/shard_map/ppermute | solution.py:106
  61.4 8.1 %collective-permute-start.24 = (bf16[64,1024]{1,0:T(8,128)(2,1)S(1)}, bf16[64,1024]{1,0:T(8,128)(2,1)S(1)}, u32[]{:S(2)}, u32[]{:S(2)}) collective-permute-start(bf16[64,1024]{1,0:T(8,128)(2,1)S(1)} %get-tuple-element.174), channel_id=1, source_target_pairs={{0,4},{1,5},{2,6},{3,7},{4,0},{5,1},{6,2},{7,3},{8,12},{9,13},{10,... | collective-permute-start | bytes 393224 | tf_op jit(solution)/shard_map/ppermute | solution.py:106
  63.0 16.4 %collective-permute-start.30 = (bf16[784,256]{1,0:T(8,128)(2,1)S(1)}, bf16[784,256]{1,0:T(8,128)(2,1)S(1)}, u32[]{:S(2)}, u32[]{:S(2)}) collective-permute-start(bf16[784,256]{1,0:T(8,128)(2,1)S(1)} %get-tuple-element.181), channel_id=1, source_target_pairs={{0,2},{1,3},{2,0},{3,1},{4,6},{5,7},{6,4},{7,5},{8,10},{9,11},{10,... | collective-permute-start | bytes 1204232 | tf_op jit(solution)/shard_map/ppermute | solution.py:106
  64.2 12.7 %collective-permute-start.28 = (bf16[272,256]{1,0:T(8,128)(2,1)S(1)}, bf16[272,256]{1,0:T(8,128)(2,1)S(1)}, u32[]{:S(2)}, u32[]{:S(2)}) collective-permute-start(bf16[272,256]{1,0:T(8,128)(2,1)S(1)} %get-tuple-element.179), channel_id=1, source_target_pairs={{0,16},{1,17},{2,18},{3,19},{4,20},{5,21},{6,22},{7,23},{8,24},{9,... | collective-permute-start | bytes 417800 | tf_op jit(solution)/shard_map/ppermute | solution.py:106
  66.8 12.6 %collective-permute-start.29 = (bf16[272,256]{1,0:T(8,128)(2,1)S(1)}, bf16[272,256]{1,0:T(8,128)(2,1)S(1)}, u32[]{:S(2)}, u32[]{:S(2)}) collective-permute-start(bf16[272,256]{1,0:T(8,128)(2,1)S(1)} %get-tuple-element.180), channel_id=1, source_target_pairs={{0,18},{1,19},{2,16},{3,17},{4,22},{5,23},{6,20},{7,21},{8,26},{9,... | collective-permute-start | bytes 417800 | tf_op jit(solution)/shard_map/ppermute | solution.py:106
  75.0 9.2 %collective-permute-start.31 = (bf16[128,1024]{1,0:T(8,128)(2,1)S(1)}, bf16[128,1024]{1,0:T(8,128)(2,1)S(1)}, u32[]{:S(2)}, u32[]{:S(2)}) collective-permute-start(bf16[128,1024]{1,0:T(8,128)(2,1)S(1)} %collective-permute-done.14.fetched_ref.refs_0_), channel_id=1, source_target_pairs={{0,1},{1,0},{2,3},{3,2},{4,5},{5,4},{6,7},{7,6},{8,9},{9,8},{10,11... | collective-permute-start | bytes 786440 | tf_op jit(solution)/shard_map/ppermute | solution.py:106
  81.0 7.7 %collective-permute-start.35 = (bf16[256,256]{1,0:T(8,128)(2,1)S(1)}, bf16[256,256]{1,0:T(8,128)(2,1)S(1)}, u32[]{:S(2)}, u32[]{:S(2)}) collective-permute-start(bf16[256,256]{1,0:T(8,128)(2,1)S(1)} %get-tuple-element.187.refs_0_), channel_id=1, source_target_pairs={{0,4},{1,5},{2,6},{3,7},{4,0},{5,1},{6,2},{7,3},{8,12},{9,13},{10,... | collective-permute-start | bytes 393224 | tf_op jit(solution)/shard_map/ppermute | solution.py:106
  82.7 14.0 %collective-permute-start.39 = (bf16[256,512]{1,0:T(8,128)(2,1)S(1)}, bf16[256,512]{1,0:T(8,128)(2,1)S(1)}, u32[]{:S(2)}, u32[]{:S(2)}) collective-permute-start(bf16[256,512]{1,0:T(8,128)(2,1)S(1)} %get-tuple-element.224), channel_id=1, source_target_pairs={{0,4},{1,5},{2,6},{3,7},{4,0},{5,1},{6,2},{7,3},{8,12},{9,13},{10,... | collective-permute-start | bytes 786440 | tf_op jit(solution)/shard_map/ppermute | solution.py:106
  89.8 9.0 %collective-permute-start.36 = (bf16[256,512]{1,0:T(8,128)(2,1)S(1)}, bf16[256,512]{1,0:T(8,128)(2,1)S(1)}, u32[]{:S(2)}, u32[]{:S(2)}) collective-permute-start(bf16[256,512]{1,0:T(8,128)(2,1)S(1)} %get-tuple-element.222), channel_id=1, source_target_pairs={{0,8},{1,9},{2,10},{3,11},{4,12},{5,13},{6,14},{7,15},{24,16},{25,... | collective-permute-start | bytes 786440 | tf_op jit(solution)/shard_map/ppermute | solution.py:106
  92.1 10.7 %collective-permute-start.37 = (bf16[256,512]{1,0:T(8,128)(2,1)S(1)}, bf16[256,512]{1,0:T(8,128)(2,1)S(1)}, u32[]{:S(2)}, u32[]{:S(2)}) collective-permute-start(bf16[256,512]{1,0:T(8,128)(2,1)S(1)} %get-tuple-element.223), channel_id=1, source_target_pairs={{0,16},{1,17},{2,18},{3,19},{4,20},{5,21},{6,22},{7,23},{24,8},{25... | collective-permute-start | bytes 786440 | tf_op jit(solution)/shard_map/ppermute | solution.py:106
  94.5 8.2 %collective-permute-start.38 = (bf16[256,512]{1,0:T(8,128)(2,1)S(1)}, bf16[256,512]{1,0:T(8,128)(2,1)S(1)}, u32[]{:S(2)}, u32[]{:S(2)}) collective-permute-start(bf16[256,512]{1,0:T(8,128)(2,1)S(1)} %get-tuple-element.222), channel_id=1, source_target_pairs={{8,16},{9,17},{10,18},{11,19},{12,20},{13,21},{14,22},{15,23},{16,... | collective-permute-start | bytes 786440 | tf_op jit(solution)/shard_map/ppermute | solution.py:106
  95.2 14.0 %collective-permute-start.33 = (bf16[256,512]{1,0:T(8,128)(2,1)S(1)}, bf16[256,512]{1,0:T(8,128)(2,1)S(1)}, u32[]{:S(2)}, u32[]{:S(2)}) collective-permute-start(bf16[256,512]{1,0:T(8,128)(2,1)S(1)} %get-tuple-element.214), channel_id=1, source_target_pairs={{0,4},{1,5},{2,6},{3,7},{4,0},{5,1},{6,2},{7,3},{8,12},{9,13},{10,... | collective-permute-start | bytes 786440 | tf_op jit(solution)/shard_map/ppermute | solution.py:106
  102.9 9.4 %collective-permute-start.40 = (bf16[256,512]{1,0:T(8,128)(2,1)S(1)}, bf16[256,512]{1,0:T(8,128)(2,1)S(1)}, u32[]{:S(2)}, u32[]{:S(2)}) collective-permute-start(bf16[256,512]{1,0:T(8,128)(2,1)S(1)} %get-tuple-element.230), channel_id=1, source_target_pairs={{0,8},{1,9},{2,10},{3,11},{4,12},{5,13},{6,14},{7,15},{8,0},{9,1},... | collective-permute-start | bytes 786440 | tf_op jit(solution)/shard_map/ppermute | solution.py:106
  (24 other events, 129.4 us)

commit v14 on v13

--- a/solution.py
+++ b/solution.py
@@ -621,10 +621,10 @@
     for k in range(SIDE * CORES):
         piece = lax.dynamic_slice(response_emb, (places[k], jnp.uint32(0)), (quarter, width))
         pieces.append(piece if k == 0 else send(piece, MIX[k]))
-    pieces, picked = tie((pieces, picked))
+    pieces, picked, prompt_late = tie((pieces, picked, prompt_emb))
     fetched = send(picked, ACROSS_Y)
     prompt_far, prompt_far_x = send(prompt_emb, FAR), send(prompt_emb, FAR_X)
-    beside = [send(prompt_emb, ACROSS_X), prompt_far_x]
+    beside = [send(prompt_late, ACROSS_X), prompt_far_x]
     response_rows = jnp.concatenate(pieces, axis=1)
 
     rows_late, fetched = tie((response_rows, fetched))

time: 114 us -> 114 us (level)
  starting transfers between devices: 59 us -> 53.9 us
  waiting for transfers between devices: 36.5 us -> 40.8 us
    ppermute x42, starting transfers between devices: 59 us -> 53.9 us  [send(): return lax.ppermute(block, ('dp', 'mp'), table)]
    ppermute x42, waiting for transfers between devices: 36.5 us -> 40.8 us  [send(): return lax.ppermute(block, ('dp', 'mp'), table)]
where the time goes in v14:
time: 114 us; the launch traced here: 113 us
  starting transfers between devices  53.9 us (47%)
  waiting for transfers between devices  40.8 us (36%)
  Pallas kernels  12.4 us (11%)
  local copies, waits for them, and re-layouts  3.52 us (3%)
    ppermute x42, starting transfers between devices, send(): return lax.ppermute(block, ('dp', 'mp'), table)  53.9 us
    ppermute x42, waiting for transfers between devices, send(): return lax.ppermute(block, ('dp', 'mp'), table)  40.8 us
    pallas_call x2, Pallas kernels, project(): pl.pallas_call(kernel, in_specs=[pl.BlockSpec(memory_space=pltpu.SMEM)] +...  4.39 us
    pallas_call x10, Pallas kernels, in_vmem(): pl.pallas_call(kernel, in_specs=[inside] * len(operands), out_specs=[insi...  4.23 us
    unnamed x15, local copies, waits for them, and re-layouts  3.21 us
  transfers between devices with their start and end apart: 42, of which 16 were waited for; matrix products, arithmetic and copies ran while one was open for 1% of the time, Pallas kernels for 8%

profile of v14, /device:TPU:0, one launch (start us, length us, event | category | flops | bytes accessed | tf_op | source)
XLA Modules:
  0.0 112.6 jit_solution(15955741177804820950)
XLA Ops:
  1.3 3.1 %collective-permute-start.2 = (bf16[512,256]{1,0:T(8,128)(2,1)}, bf16[512,256]{1,0:T(8,128)(2,1)S(1)}, u32[]{:S(2)}, u32[]{:S(2)}) collective-permute-start(bf16[512,256]{1,0:T(8,128)(2,1)} %refs_2_), channel_id=1, source_target_pairs={{0,8},{1,9},{2,10},{3,11},{4,12},{5,13},{6,14},{7,15},{8,0},{9,1},... | collective-permute-start | bytes 786440 | tf_op jit(solution)/shard_map/ppermute | solution.py:106
  5.9 2.5 %collective-permute-start = (bf16[512,256]{1,0:T(8,128)(2,1)}, bf16[512,256]{1,0:T(8,128)(2,1)S(1)}, u32[]{:S(2)}, u32[]{:S(2)}) collective-permute-start(bf16[512,256]{1,0:T(8,128)(2,1)} %refs_2_), channel_id=1, source_target_pairs={{0,24},{1,25},{2,26},{3,27},{4,28},{5,29},{6,30},{7,31},{8,16},{9,... | collective-permute-start | bytes 786440 | tf_op jit(solution)/shard_map/ppermute | solution.py:106
  13.0 5.9 %collective-permute-done.refs_2_ = bf16[512,256]{1,0:T(8,128)(2,1)S(1)} collective-permute-done((bf16[512,256]{1,0:T(8,128)(2,1)}, bf16[512,256]{1,0:T(8,128)(2,1)S(1)}, u32[]{:S(2)}, u32[]{:S(2)}) %collective-permute-start) | collective-permute-done | bytes 262176 | tf_op jit(solution)/shard_map/ppermute | solution.py:106
  18.8 1.8 %collective-permute-start.1 = (bf16[512,256]{1,0:T(8,128)(2,1)S(1)}, bf16[512,256]{1,0:T(8,128)(2,1)S(1)}, u32[]{:S(2)}, u32[]{:S(2)}) collective-permute-start(bf16[512,256]{1,0:T(8,128)(2,1)S(1)} %collective-permute-done.refs_2_), channel_id=1, source_target_pairs={{0,8},{1,9},{2,10},{3,11},{4,12},{5,13},{6,14},{7,15},{8,0},{9,1},... | collective-permute-start | bytes 786440 | tf_op jit(solution)/shard_map/ppermute | solution.py:106
  21.2 2.4 %shard_map.60.refs_5_ = f32[512,256]{1,0:T(8,128)S(1)} custom-call(s32[4]{0:T(128)S(1)} %get-tuple-element.120.block_ref, bf16[256,4096]{1,0:T(8,128)(2,1)S(1)} %copy-done.1, bf16[256,4096]{1,0:T(8,128)(2,1)S(1)} %copy-done.3, bf16[512,256]{1,0:T(8,128)(2,1)S(1)} %copy-done.4, bf16[512,256]{1,0:T(8,128)(2,1)S(1)} %collective-permute-done.3.refs_3_, ...), custom_call_target="tpu_custom_call" | custom-call | flops 20000000000 | tf_op jit(solution)/shard_map/pallas_call | solution.py:274
  23.6 2.3 %collective-permute-done.1.refs_4_ = bf16[512,256]{1,0:T(8,128)(2,1)S(1)} collective-permute-done((bf16[512,256]{1,0:T(8,128)(2,1)S(1)}, bf16[512,256]{1,0:T(8,128)(2,1)S(1)}, u32[]{:S(2)}, u32[]{:S(2)}) %collective-permute-start.1) | collective-permute-done | bytes 262176 | tf_op jit(solution)/shard_map/ppermute | solution.py:106
  27.6 2.0 %shard_map.61.total_ref = f32[512,256]{1,0:T(8,128)S(1)} custom-call(s32[3]{0:T(128)S(1)} %pad_add_fusion.2.block_ref, bf16[256,4096]{1,0:T(8,128)(2,1)S(1)} %copy-done.1, bf16[256,4096]{1,0:T(8,128)(2,1)S(1)} %copy-done.3, bf16[512,256]{1,0:T(8,128)(2,1)S(1)} %collective-permute-done.refs_2_, bf16[512,256]{1,0:T(8,128)(2,1)S(1)} %collective-permute-done.6.refs_3_, ...), custom_call_target="tpu_custom_call" | custom-call | flops 2400000000 | tf_op jit(solution)/shard_map/pallas_call | solution.py:274
  29.6 3.1 %collective-permute-done.5.weight_ref = bf16[512,256]{1,0:T(8,128)(2,1)S(1)} collective-permute-done((bf16[512,256]{1,0:T(8,128)(2,1)S(1)}, bf16[512,256]{1,0:T(8,128)(2,1)S(1)}, u32[]{:S(2)}, u32[]{:S(2)}) %collective-permute-start.5) | collective-permute-done | bytes 262176 | tf_op jit(solution)/shard_map/ppermute | solution.py:106
  35.3 3.0 %collective-permute-start.17 = (bf16[272,256]{1,0:T(8,128)(2,1)S(1)}, bf16[272,256]{1,0:T(8,128)(2,1)S(1)}, u32[]{:S(2)}, u32[]{:S(2)}) collective-permute-start(bf16[272,256]{1,0:T(8,128)(2,1)S(1)} %get-tuple-element.143.refs_0_), channel_id=1, source_target_pairs={{0,18},{1,19},{2,16},{3,17},{4,22},{5,23},{6,20},{7,21},{8,26},{9,... | collective-permute-start | bytes 417800 | tf_op jit(solution)/shard_map/ppermute | solution.py:106
  40.9 3.6 %collective-permute-start.12 = (bf16[64,1024]{1,0:T(8,128)(2,1)S(1)}, bf16[64,1024]{1,0:T(8,128)(2,1)S(1)}, u32[]{:S(2)}, u32[]{:S(2)}) collective-permute-start(bf16[64,1024]{1,0:T(8,128)(2,1)S(1)} %constant_dynamic-update-slice_fusion.refs_0_), channel_id=1, source_target_pairs={{0,8},{1,9},{2,10},{3,11},{4,12},{5,13},{6,14},{7,15},{8,0},{9,1},... | collective-permute-start | bytes 393224 | tf_op jit(solution)/shard_map/ppermute | solution.py:106
  44.6 2.0 %collective-permute-done.14.fetched_ref.refs_0_ = bf16[128,1024]{1,0:T(8,128)(2,1)S(1)} collective-permute-done((bf16[128,1024]{1,0:T(8,128)(2,1)S(1)}, bf16[128,1024]{1,0:T(8,128)(2,1)S(1)}, u32[]{:S(2)}, u32[]{:S(2)}) %collective-permute-start.14) | collective-permute-done | bytes 262176 | tf_op jit(solution)/shard_map/ppermute | solution.py:106
  46.6 4.4 %collective-permute-start.13 = (bf16[64,1024]{1,0:T(8,128)(2,1)S(1)}, bf16[64,1024]{1,0:T(8,128)(2,1)S(1)}, u32[]{:S(2)}, u32[]{:S(2)}) collective-permute-start(bf16[64,1024]{1,0:T(8,128)(2,1)S(1)} %constant_dynamic-update-slice_fusion.refs_0_), channel_id=1, source_target_pairs={{0,12},{1,13},{2,14},{3,15},{4,8},{5,9},{6,10},{7,11},{8,4},{9,5},... | collective-permute-start | bytes 393224 | tf_op jit(solution)/shard_map/ppermute | solution.py:106
  52.1 2.7 %collective-permute-done.13.refs_2_ = bf16[64,1024]{1,0:T(8,128)(2,1)S(1)} collective-permute-done((bf16[64,1024]{1,0:T(8,128)(2,1)S(1)}, bf16[64,1024]{1,0:T(8,128)(2,1)S(1)}, u32[]{:S(2)}, u32[]{:S(2)}) %collective-permute-start.13) | collective-permute-done | bytes 131104 | tf_op jit(solution)/shard_map/ppermute | solution.py:106
  59.3 2.0 %collective-permute-start.23 = (bf16[64,1024]{1,0:T(8,128)(2,1)S(1)}, bf16[64,1024]{1,0:T(8,128)(2,1)S(1)}, u32[]{:S(2)}, u32[]{:S(2)}) collective-permute-start(bf16[64,1024]{1,0:T(8,128)(2,1)S(1)} %get-tuple-element.175), channel_id=1, source_target_pairs={{0,12},{1,13},{2,14},{3,15},{4,8},{5,9},{6,10},{7,11},{8,4},{9,5},... | collective-permute-start | bytes 393224 | tf_op jit(solution)/shard_map/ppermute | solution.py:106
  63.4 2.5 %collective-permute-start.28 = (bf16[272,256]{1,0:T(8,128)(2,1)S(1)}, bf16[272,256]{1,0:T(8,128)(2,1)S(1)}, u32[]{:S(2)}, u32[]{:S(2)}) collective-permute-start(bf16[272,256]{1,0:T(8,128)(2,1)S(1)} %get-tuple-element.181), channel_id=1, source_target_pairs={{0,16},{1,17},{2,18},{3,19},{4,20},{5,21},{6,22},{7,23},{8,24},{9,... | collective-permute-start | bytes 417800 | tf_op jit(solution)/shard_map/ppermute | solution.py:106
  65.9 1.8 %collective-permute-start.29 = (bf16[272,256]{1,0:T(8,128)(2,1)S(1)}, bf16[272,256]{1,0:T(8,128)(2,1)S(1)}, u32[]{:S(2)}, u32[]{:S(2)}) collective-permute-start(bf16[272,256]{1,0:T(8,128)(2,1)S(1)} %get-tuple-element.182), channel_id=1, source_target_pairs={{0,18},{1,19},{2,16},{3,17},{4,22},{5,23},{6,20},{7,21},{8,26},{9,... | collective-permute-start | bytes 417800 | tf_op jit(solution)/shard_map/ppermute | solution.py:106
  67.8 3.6 %collective-permute-done.23.refs_2_ = bf16[64,1024]{1,0:T(8,128)(2,1)S(1)} collective-permute-done((bf16[64,1024]{1,0:T(8,128)(2,1)S(1)}, bf16[64,1024]{1,0:T(8,128)(2,1)S(1)}, u32[]{:S(2)}, u32[]{:S(2)}) %collective-permute-start.23) | collective-permute-done | bytes 131104 | tf_op jit(solution)/shard_map/ppermute | solution.py:106
  73.4 2.1 %collective-permute-done.26 = bf16[64,256]{1,0:T(8,128)(2,1)S(1)} collective-permute-done((bf16[64,256]{1,0:T(8,128)(2,1)S(1)}, bf16[64,256]{1,0:T(8,128)(2,1)S(1)}, u32[]{:S(2)}, u32[]{:S(2)}) %collective-permute-start.26) | collective-permute-done | bytes 32800 | tf_op jit(solution)/shard_map/ppermute | solution.py:106
  76.4 2.9 %collective-permute-done.29.far_x_ref = bf16[272,256]{1,0:T(8,128)(2,1)S(1)} collective-permute-done((bf16[272,256]{1,0:T(8,128)(2,1)S(1)}, bf16[272,256]{1,0:T(8,128)(2,1)S(1)}, u32[]{:S(2)}, u32[]{:S(2)}) %collective-permute-start.29) | collective-permute-done | bytes 139296 | tf_op jit(solution)/shard_map/ppermute | solution.py:106
  86.0 2.5 %collective-permute-done.35.grad_ref = bf16[256,256]{1,0:T(8,128)(2,1)S(1)} collective-permute-done((bf16[256,256]{1,0:T(8,128)(2,1)S(1)}, bf16[256,256]{1,0:T(8,128)(2,1)S(1)}, u32[]{:S(2)}, u32[]{:S(2)}) %collective-permute-start.35) | collective-permute-done | bytes 131104 | tf_op jit(solution)/shard_map/ppermute | solution.py:106
  91.2 3.0 %collective-permute-start.37 = (bf16[256,512]{1,0:T(8,128)(2,1)S(1)}, bf16[256,512]{1,0:T(8,128)(2,1)S(1)}, u32[]{:S(2)}, u32[]{:S(2)}) collective-permute-start(bf16[256,512]{1,0:T(8,128)(2,1)S(1)} %get-tuple-element.225), channel_id=1, source_target_pairs={{0,16},{1,17},{2,18},{3,19},{4,20},{5,21},{6,22},{7,23},{24,8},{25... | collective-permute-start | bytes 786440 | tf_op jit(solution)/shard_map/ppermute | solution.py:106
  98.0 4.0 %collective-permute-done.37.refs_3_ = bf16[256,512]{1,0:T(8,128)(2,1)S(1)} collective-permute-done((bf16[256,512]{1,0:T(8,128)(2,1)S(1)}, bf16[256,512]{1,0:T(8,128)(2,1)S(1)}, u32[]{:S(2)}, u32[]{:S(2)}) %collective-permute-start.37) | collective-permute-done | bytes 262176 | tf_op jit(solution)/shard_map/ppermute | solution.py:106
  102.1 5.1 %collective-permute-start.40 = (bf16[256,512]{1,0:T(8,128)(2,1)S(1)}, bf16[256,512]{1,0:T(8,128)(2,1)S(1)}, u32[]{:S(2)}, u32[]{:S(2)}) collective-permute-start(bf16[256,512]{1,0:T(8,128)(2,1)S(1)} %get-tuple-element.232), channel_id=1, source_target_pairs={{0,8},{1,9},{2,10},{3,11},{4,12},{5,13},{6,14},{7,15},{8,0},{9,1},... | collective-permute-start | bytes 786440 | tf_op jit(solution)/shard_map/ppermute | solution.py:106
  108.4 3.1 %collective-permute-done.40.refs_2_ = bf16[256,512]{1,0:T(8,128)(2,1)S(1)} collective-permute-done((bf16[256,512]{1,0:T(8,128)(2,1)S(1)}, bf16[256,512]{1,0:T(8,128)(2,1)S(1)}, u32[]{:S(2)}, u32[]{:S(2)}) %collective-permute-start.40) | collective-permute-done | bytes 262176 | tf_op jit(solution)/shard_map/ppermute | solution.py:106
  (105 shorter events, 40.0 us)
Async XLA Ops:
  1.3 10.9 %collective-permute-start.2 = (bf16[512,256]{1,0:T(8,128)(2,1)}, bf16[512,256]{1,0:T(8,128)(2,1)S(1)}, u32[]{:S(2)}, u32[]{:S(2)}) collective-permute-start(bf16[512,256]{1,0:T(8,128)(2,1)} %refs_2_), channel_id=1, source_target_pairs={{0,8},{1,9},{2,10},{3,11},{4,12},{5,13},{6,14},{7,15},{8,0},{9,1},... | collective-permute-start | bytes 786440 | tf_op jit(solution)/shard_map/ppermute | solution.py:106
  4.4 8.6 %collective-permute-start.3 = (bf16[512,256]{1,0:T(8,128)(2,1)}, bf16[512,256]{1,0:T(8,128)(2,1)S(1)}, u32[]{:S(2)}, u32[]{:S(2)}) collective-permute-start(bf16[512,256]{1,0:T(8,128)(2,1)} %refs_2_), channel_id=1, source_target_pairs={{0,4},{1,5},{2,6},{3,7},{4,0},{5,1},{6,2},{7,3},{8,12},{9,13},{10,... | collective-permute-start | bytes 786440 | tf_op jit(solution)/shard_map/ppermute | solution.py:106
  5.9 12.9 %collective-permute-start = (bf16[512,256]{1,0:T(8,128)(2,1)}, bf16[512,256]{1,0:T(8,128)(2,1)S(1)}, u32[]{:S(2)}, u32[]{:S(2)}) collective-permute-start(bf16[512,256]{1,0:T(8,128)(2,1)} %refs_2_), channel_id=1, source_target_pairs={{0,24},{1,25},{2,26},{3,27},{4,28},{5,29},{6,30},{7,31},{8,16},{9,... | collective-permute-start | bytes 786440 | tf_op jit(solution)/shard_map/ppermute | solution.py:106
  12.2 9.0 %collective-permute-start.4 = (bf16[512,256]{1,0:T(8,128)(2,1)S(1)}, bf16[512,256]{1,0:T(8,128)(2,1)S(1)}, u32[]{:S(2)}, u32[]{:S(2)}) collective-permute-start(bf16[512,256]{1,0:T(8,128)(2,1)S(1)} %collective-permute-done.2.refs_4_), channel_id=1, source_target_pairs={{0,4},{1,5},{2,6},{3,7},{4,0},{5,1},{6,2},{7,3},{8,12},{9,13},{10,... | collective-permute-start | bytes 786440 | tf_op jit(solution)/shard_map/ppermute | solution.py:106
  18.8 7.1 %collective-permute-start.1 = (bf16[512,256]{1,0:T(8,128)(2,1)S(1)}, bf16[512,256]{1,0:T(8,128)(2,1)S(1)}, u32[]{:S(2)}, u32[]{:S(2)}) collective-permute-start(bf16[512,256]{1,0:T(8,128)(2,1)S(1)} %collective-permute-done.refs_2_), channel_id=1, source_target_pairs={{0,8},{1,9},{2,10},{3,11},{4,12},{5,13},{6,14},{7,15},{8,0},{9,1},... | collective-permute-start | bytes 786440 | tf_op jit(solution)/shard_map/ppermute | solution.py:106
  35.3 15.8 %collective-permute-start.17 = (bf16[272,256]{1,0:T(8,128)(2,1)S(1)}, bf16[272,256]{1,0:T(8,128)(2,1)S(1)}, u32[]{:S(2)}, u32[]{:S(2)}) collective-permute-start(bf16[272,256]{1,0:T(8,128)(2,1)S(1)} %get-tuple-element.143.refs_0_), channel_id=1, source_target_pairs={{0,18},{1,19},{2,16},{3,17},{4,22},{5,23},{6,20},{7,21},{8,26},{9,... | collective-permute-start | bytes 417800 | tf_op jit(solution)/shard_map/ppermute | solution.py:106
  38.3 13.3 %collective-permute-start.19 = (bf16[272,256]{1,0:T(8,128)(2,1)S(1)}, bf16[272,256]{1,0:T(8,128)(2,1)S(1)}, u32[]{:S(2)}, u32[]{:S(2)}) collective-permute-start(bf16[272,256]{1,0:T(8,128)(2,1)S(1)} %get-tuple-element.143.refs_0_), channel_id=1, source_target_pairs={{0,16},{1,17},{2,18},{3,19},{4,20},{5,21},{6,22},{7,23},{8,24},{9,... | collective-permute-start | bytes 417800 | tf_op jit(solution)/shard_map/ppermute | solution.py:106
  39.1 7.4 %collective-permute-start.14 = (bf16[128,1024]{1,0:T(8,128)(2,1)S(1)}, bf16[128,1024]{1,0:T(8,128)(2,1)S(1)}, u32[]{:S(2)}, u32[]{:S(2)}) collective-permute-start(bf16[128,1024]{1,0:T(8,128)(2,1)S(1)} %shard_map.59), channel_id=1, source_target_pairs={{0,4},{1,5},{2,6},{3,7},{4,0},{5,1},{6,2},{7,3},{8,12},{9,13},{10,... | collective-permute-start | bytes 786440 | tf_op jit(solution)/shard_map/ppermute | solution.py:106
  40.4 11.2 %collective-permute-start.11 = (bf16[272,256]{1,0:T(8,128)(2,1)S(1)}, bf16[272,256]{1,0:T(8,128)(2,1)S(1)}, u32[]{:S(2)}, u32[]{:S(2)}) collective-permute-start(bf16[272,256]{1,0:T(8,128)(2,1)S(1)} %get-tuple-element.143.refs_0_), channel_id=1, source_target_pairs={{0,2},{1,3},{2,0},{3,1},{4,6},{5,7},{6,4},{7,5},{8,10},{9,11},{10,... | collective-permute-start | bytes 417800 | tf_op jit(solution)/shard_map/ppermute | solution.py:106
  40.9 11.2 %collective-permute-start.12 = (bf16[64,1024]{1,0:T(8,128)(2,1)S(1)}, bf16[64,1024]{1,0:T(8,128)(2,1)S(1)}, u32[]{:S(2)}, u32[]{:S(2)}) collective-permute-start(bf16[64,1024]{1,0:T(8,128)(2,1)S(1)} %constant_dynamic-update-slice_fusion.refs_0_), channel_id=1, source_target_pairs={{0,8},{1,9},{2,10},{3,11},{4,12},{5,13},{6,14},{7,15},{8,0},{9,1},... | collective-permute-start | bytes 393224 | tf_op jit(solution)/shard_map/ppermute | solution.py:106
  46.6 8.3 %collective-permute-start.13 = (bf16[64,1024]{1,0:T(8,128)(2,1)S(1)}, bf16[64,1024]{1,0:T(8,128)(2,1)S(1)}, u32[]{:S(2)}, u32[]{:S(2)}) collective-permute-start(bf16[64,1024]{1,0:T(8,128)(2,1)S(1)} %constant_dynamic-update-slice_fusion.refs_0_), channel_id=1, source_target_pairs={{0,12},{1,13},{2,14},{3,15},{4,8},{5,9},{6,10},{7,11},{8,4},{9,5},... | collective-permute-start | bytes 393224 | tf_op jit(solution)/shard_map/ppermute | solution.py:106
  59.3 12.1 %collective-permute-start.23 = (bf16[64,1024]{1,0:T(8,128)(2,1)S(1)}, bf16[64,1024]{1,0:T(8,128)(2,1)S(1)}, u32[]{:S(2)}, u32[]{:S(2)}) collective-permute-start(bf16[64,1024]{1,0:T(8,128)(2,1)S(1)} %get-tuple-element.175), channel_id=1, source_target_pairs={{0,12},{1,13},{2,14},{3,15},{4,8},{5,9},{6,10},{7,11},{8,4},{9,5},... | collective-permute-start | bytes 393224 | tf_op jit(solution)/shard_map/ppermute | solution.py:106
  61.2 10.1 %collective-permute-start.24 = (bf16[64,1024]{1,0:T(8,128)(2,1)S(1)}, bf16[64,1024]{1,0:T(8,128)(2,1)S(1)}, u32[]{:S(2)}, u32[]{:S(2)}) collective-permute-start(bf16[64,1024]{1,0:T(8,128)(2,1)S(1)} %get-tuple-element.176), channel_id=1, source_target_pairs={{0,4},{1,5},{2,6},{3,7},{4,0},{5,1},{6,2},{7,3},{8,12},{9,13},{10,... | collective-permute-start | bytes 393224 | tf_op jit(solution)/shard_map/ppermute | solution.py:106
  62.9 16.4 %collective-permute-start.30 = (bf16[784,256]{1,0:T(8,128)(2,1)S(1)}, bf16[784,256]{1,0:T(8,128)(2,1)S(1)}, u32[]{:S(2)}, u32[]{:S(2)}) collective-permute-start(bf16[784,256]{1,0:T(8,128)(2,1)S(1)} %get-tuple-element.183), channel_id=1, source_target_pairs={{0,2},{1,3},{2,0},{3,1},{4,6},{5,7},{6,4},{7,5},{8,10},{9,11},{10,... | collective-permute-start | bytes 1204232 | tf_op jit(solution)/shard_map/ppermute | solution.py:106
  63.4 13.0 %collective-permute-start.28 = (bf16[272,256]{1,0:T(8,128)(2,1)S(1)}, bf16[272,256]{1,0:T(8,128)(2,1)S(1)}, u32[]{:S(2)}, u32[]{:S(2)}) collective-permute-start(bf16[272,256]{1,0:T(8,128)(2,1)S(1)} %get-tuple-element.181), channel_id=1, source_target_pairs={{0,16},{1,17},{2,18},{3,19},{4,20},{5,21},{6,22},{7,23},{8,24},{9,... | collective-permute-start | bytes 417800 | tf_op jit(solution)/shard_map/ppermute | solution.py:106
  65.9 13.4 %collective-permute-start.29 = (bf16[272,256]{1,0:T(8,128)(2,1)S(1)}, bf16[272,256]{1,0:T(8,128)(2,1)S(1)}, u32[]{:S(2)}, u32[]{:S(2)}) collective-permute-start(bf16[272,256]{1,0:T(8,128)(2,1)S(1)} %get-tuple-element.182), channel_id=1, source_target_pairs={{0,18},{1,19},{2,16},{3,17},{4,22},{5,23},{6,20},{7,21},{8,26},{9,... | collective-permute-start | bytes 417800 | tf_op jit(solution)/shard_map/ppermute | solution.py:106
  75.5 8.3 %collective-permute-start.31 = (bf16[128,1024]{1,0:T(8,128)(2,1)S(1)}, bf16[128,1024]{1,0:T(8,128)(2,1)S(1)}, u32[]{:S(2)}, u32[]{:S(2)}) collective-permute-start(bf16[128,1024]{1,0:T(8,128)(2,1)S(1)} %collective-permute-done.14.fetched_ref.refs_0_), channel_id=1, source_target_pairs={{0,1},{1,0},{2,3},{3,2},{4,5},{5,4},{6,7},{7,6},{8,9},{9,8},{10,11... | collective-permute-start | bytes 786440 | tf_op jit(solution)/shard_map/ppermute | solution.py:106
  80.6 7.9 %collective-permute-start.35 = (bf16[256,256]{1,0:T(8,128)(2,1)S(1)}, bf16[256,256]{1,0:T(8,128)(2,1)S(1)}, u32[]{:S(2)}, u32[]{:S(2)}) collective-permute-start(bf16[256,256]{1,0:T(8,128)(2,1)S(1)} %get-tuple-element.189.refs_0_), channel_id=1, source_target_pairs={{0,4},{1,5},{2,6},{3,7},{4,0},{5,1},{6,2},{7,3},{8,12},{9,13},{10,... | collective-permute-start | bytes 393224 | tf_op jit(solution)/shard_map/ppermute | solution.py:106
  82.6 13.9 %collective-permute-start.39 = (bf16[256,512]{1,0:T(8,128)(2,1)S(1)}, bf16[256,512]{1,0:T(8,128)(2,1)S(1)}, u32[]{:S(2)}, u32[]{:S(2)}) collective-permute-start(bf16[256,512]{1,0:T(8,128)(2,1)S(1)} %get-tuple-element.226), channel_id=1, source_target_pairs={{0,4},{1,5},{2,6},{3,7},{4,0},{5,1},{6,2},{7,3},{8,12},{9,13},{10,... | collective-permute-start | bytes 786440 | tf_op jit(solution)/shard_map/ppermute | solution.py:106
  89.6 8.3 %collective-permute-start.36 = (bf16[256,512]{1,0:T(8,128)(2,1)S(1)}, bf16[256,512]{1,0:T(8,128)(2,1)S(1)}, u32[]{:S(2)}, u32[]{:S(2)}) collective-permute-start(bf16[256,512]{1,0:T(8,128)(2,1)S(1)} %get-tuple-element.224), channel_id=1, source_target_pairs={{0,8},{1,9},{2,10},{3,11},{4,12},{5,13},{6,14},{7,15},{24,16},{25,... | collective-permute-start | bytes 786440 | tf_op jit(solution)/shard_map/ppermute | solution.py:106
  91.2 10.7 %collective-permute-start.37 = (bf16[256,512]{1,0:T(8,128)(2,1)S(1)}, bf16[256,512]{1,0:T(8,128)(2,1)S(1)}, u32[]{:S(2)}, u32[]{:S(2)}) collective-permute-start(bf16[256,512]{1,0:T(8,128)(2,1)S(1)} %get-tuple-element.225), channel_id=1, source_target_pairs={{0,16},{1,17},{2,18},{3,19},{4,20},{5,21},{6,22},{7,23},{24,8},{25... | collective-permute-start | bytes 786440 | tf_op jit(solution)/shard_map/ppermute | solution.py:106
  94.2 7.7 %collective-permute-start.38 = (bf16[256,512]{1,0:T(8,128)(2,1)S(1)}, bf16[256,512]{1,0:T(8,128)(2,1)S(1)}, u32[]{:S(2)}, u32[]{:S(2)}) collective-permute-start(bf16[256,512]{1,0:T(8,128)(2,1)S(1)} %get-tuple-element.224), channel_id=1, source_target_pairs={{8,16},{9,17},{10,18},{11,19},{12,20},{13,21},{14,22},{15,23},{16,... | collective-permute-start | bytes 786440 | tf_op jit(solution)/shard_map/ppermute | solution.py:106
  94.9 13.5 %collective-permute-start.33 = (bf16[256,512]{1,0:T(8,128)(2,1)S(1)}, bf16[256,512]{1,0:T(8,128)(2,1)S(1)}, u32[]{:S(2)}, u32[]{:S(2)}) collective-permute-start(bf16[256,512]{1,0:T(8,128)(2,1)S(1)} %get-tuple-element.216), channel_id=1, source_target_pairs={{0,4},{1,5},{2,6},{3,7},{4,0},{5,1},{6,2},{7,3},{8,12},{9,13},{10,... | collective-permute-start | bytes 786440 | tf_op jit(solution)/shard_map/ppermute | solution.py:106
  102.1 9.5 %collective-permute-start.40 = (bf16[256,512]{1,0:T(8,128)(2,1)S(1)}, bf16[256,512]{1,0:T(8,128)(2,1)S(1)}, u32[]{:S(2)}, u32[]{:S(2)}) collective-permute-start(bf16[256,512]{1,0:T(8,128)(2,1)S(1)} %get-tuple-element.232), channel_id=1, source_target_pairs={{0,8},{1,9},{2,10},{3,11},{4,12},{5,13},{6,14},{7,15},{8,0},{9,1},... | collective-permute-start | bytes 786440 | tf_op jit(solution)/shard_map/ppermute | solution.py:106
  (24 other events, 128.2 us)
